TPU v7x, 32 devices: a whole 2x2x4 slice. The times are simulated.
32 devices in a mesh: groups: 2 (over x), blk: 16 (over z, y, core).
Axes of the slice: x: 2, y: 2, z: 4, core: 2. Of those that a mesh axis runs over, the one named last changes fastest.
Arguments:
- points: bfloat16 [8192, 128], P(('groups', 'blk')), parts along dimension 0, may hold values from -4 to 4
- lengthscale: float32 [8], P('groups'), parts along dimension 0, may hold values from 0.6 to 2.5
- noise: float32 [8], P('groups'), parts along dimension 0, may hold values from 0.1 to 1
- solution: float32 [4, 8192], P(None, ('groups', 'blk')), parts along dimension 1, may hold values from -6 to 6
- residual: float32 [4, 8192], P(None, ('groups', 'blk')), parts along dimension 1, may hold values from -16 to 16
- direction: float32 [4, 8192], P(None, ('groups', 'blk')), parts along dimension 1, may hold values from -16 to 16
Outputs:
- next_solution: float32 [4, 8192], P(None, ('groups', 'blk')), parts along dimension 1
- next_residual: float32 [4, 8192], P(None, ('groups', 'blk')), parts along dimension 1
- next_direction: float32 [4, 8192], P(None, ('groups', 'blk')), parts along dimension 1
There are 2 independent parts, one for each index of `groups`. A program takes and returns all parts, laid end to end along the dimension named above; each array names one. Nothing has to cross between parts.
All inputs are finite; a program needn't handle non-finite values.
Results may differ from a plain program's by a relative error of at most 0.0075.
Values may be sent and summed in bfloat16 or wider, within the bound.
No kernel may reach another device: no remote copies, remote signals or barrier semaphores. Data moves between devices by JAX's collectives and lax.ppermute only.
A program may use at most 128 MiB of HBM per device.

v0:
```python
import jax
import jax.numpy as jnp
from jax import lax
from jax.sharding import PartitionSpec as P


def tile_kernel(target, target_sq, source, inverse):
    source_sq = jnp.sum(jnp.square(source.astype(jnp.float32)), axis=1)
    cross = jnp.dot(target, source.T, preferred_element_type=jnp.float32)
    dist = target_sq[:, None] + source_sq[None, :] - 2.0 * cross
    return jnp.exp(-inverse[:, None, None] * dist[None]).astype(jnp.bfloat16)


def per_device(points, lengthscale, noise, solution, residual, direction):
    inverse = 0.5 / (lengthscale * lengthscale)
    target_sq = jnp.sum(jnp.square(points.astype(jnp.float32)), axis=1)
    dir_rows = direction.astype(jnp.bfloat16).T
    kern = tile_kernel(
        points, target_sq, lax.all_gather(points, "blk", axis=0, tiled=True), inverse
    )
    product = jnp.einsum(
        "cij,jc->ci",
        kern,
        lax.all_gather(dir_rows, "blk", axis=0, tiled=True),
        preferred_element_type=jnp.float32,
    )
    image = product + noise[:, None] * direction
    local_norm = jnp.sum(residual * residual, axis=1)
    local_curve = jnp.sum(direction * image, axis=1)
    norm_now, curve = lax.psum((local_norm, local_curve), "blk")
    alpha = norm_now / curve
    next_solution = solution + alpha[:, None] * direction
    next_residual = residual - alpha[:, None] * image
    norm_next = lax.psum(jnp.sum(next_residual * next_residual, axis=1), "blk")
    beta = norm_next / norm_now
    next_direction = next_residual + beta[:, None] * direction
    return (next_solution, next_residual, next_direction)


def solution(mesh):
    return jax.shard_map(
        per_device,
        mesh=mesh,
        in_specs=(
            P(("groups", "blk"), None),
            P("groups"),
            P("groups"),
            P(None, ("groups", "blk")),
            P(None, ("groups", "blk")),
            P(None, ("groups", "blk")),
        ),
        out_specs=(
            P(None, ("groups", "blk")),
            P(None, ("groups", "blk")),
            P(None, ("groups", "blk")),
        ),
        check_vma=False,
    )
```

profile of v0, /device:TPU:0, one launch (start us, length us, event | category | flops | bytes accessed | tf_op | source)
XLA Modules:
  0.0 126.7 jit_solution(14237697257973716281)
XLA Ops:
  7.2 0.0 all-gather.2.cloned.1.call-start
  7.2 0.7 all-gather.2.cloned.1.call-update
  7.9 0.7 convert_bitcast_fusion
  8.6 23.2 %all_gather.7 = bf16[4096,4]{0,1:T(4,128)(2,1)S(1)} all-gather(bf16[256,4]{0,1:T(4,128)(2,1)S(1)} %convert_bitcast_fusion), channel_id=1, replica_groups=mesh['groups'=2,'blk'=16] {'blk'}, dimensions={0}, use_global_device_ids=true | all-gather | bytes 34816 | tf_op jit(solution)/shard_map/all_gather | solution.py:24
  31.7 0.9 multiply_reduce_fusion.1
  32.7 0.7 divide_negate_fusion
  33.4 17.5 %all-gather.2.cloned.1.call-done = bf16[4096,128]{1,0:T(8,128)(2,1)} async-done(((bf16[256,128]{1,0:T(8,128)(2,1)}), bf16[4096,128]{1,0:T(8,128)(2,1)}) %all-gather.2.cloned.1.call-update) | async-done | bytes 1048592 | tf_op jit(solution)/shard_map/all_gather | solution.py:19
  50.8 1.8 %multiply_reduce_fusion = f32[4096]{0:T(1024)S(1)} fusion(bf16[4096,128]{1,0:T(8,128)(2,1)} %all-gather.2.cloned.1.call-done), kind=kLoop, calls=%fused_computation.6 | loop fusion | flops 1568768 | bytes 1064960 | tf_op jit(solution)/shard_map/reduce_sum | solution.py:8
  52.7 2.0 %fusion.3 = f32[256,4096]{1,0:T(8,128)S(1)} fusion(bf16[256,128]{1,0:T(8,128)(2,1)} %param.6, bf16[4096,128]{1,0:T(8,128)(2,1)} %all-gather.2.cloned.1.call-done, f32[4096]{0:T(1024)S(1)} %multiply_reduce_fusion, f32[256]{0:T(256)S(1)} %multiply_reduce_fusion.1), kind=kOutput, calls=%fused_computation.5 | convolution fusion | flops 271581184 | bytes 5325824 | tf_op jit(solution)/shard_map/dot_general | solution.py:9
  54.7 0.0 copy-start
  54.7 0.0 copy-start.1
  54.7 0.0 copy-start.4
  54.7 0.0 copy-start.3
  54.7 2.4 %fusion = f32[4,1,256]{2,1,0:T(1,128)S(1)} fusion(f32[256,4096]{1,0:T(8,128)S(1)} %fusion.3, f32[4]{0:T(128)S(1)} %divide_negate_fusion, bf16[4096,4,1]{0,1,2:T(4,128)(2,1)S(1)} %bitcast.12), kind=kOutput, calls=%fused_computation.1 | convolution fusion | flops 16777216 | bytes 4231184 | tf_op jit(solution)/shard_map/cij,jc->ci/dot_general | solution.py:21
  57.1 0.0 copy-done
  57.1 0.0 copy-done.1
  57.1 0.0 copy-done.4
  57.1 0.2 multiply_reduce_fusion.3
  57.3 31.6 %all-reduce = (f32[4]{0:T(128)S(1)}, f32[4]{0:T(128)S(1)}) all-reduce(f32[4]{0:T(128)S(1)} %get-tuple-element.9, f32[4]{0:T(128)S(1)} %get-tuple-element.8), channel_id=1, replica_groups=mesh['groups'=2,'blk'=16] {'blk'}, use_global_device_ids=true, to_apply=%region_1.0 | all-reduce | flops 8 | bytes 64 | tf_op jit(solution)/shard_map/psum | solution.py:30
  88.9 0.0 copy-done.3
  88.9 0.8 multiply_reduce_fusion.2
  89.7 29.5 %psum.23 = f32[4]{0:T(128)S(1)} all-reduce(f32[4]{0:T(128)S(1)} %get-tuple-element.5), channel_id=1, replica_groups=mesh['groups'=2,'blk'=16] {'blk'}, use_global_device_ids=true, to_apply=%region_7.0 | all-reduce | flops 4 | bytes 32 | tf_op jit(solution)/shard_map/psum | solution.py:34
  119.2 0.7 multiply_add_fusion
  119.8 0.0 copy-done.2
  (3 shorter events, 0.0 us)
Async XLA Ops:
  7.2 43.7 %all-gather.2.cloned.1.call-start = ((), (), s32[]{:S(2)}) async-start(), calls=%async_computation | async-start | bytes 1114112 | tf_op jit(solution)/shard_map/all_gather | solution.py:19
  54.7 2.4 %copy-start = (f32[4,256]{1,0:T(4,128)S(1)}, f32[4,256]{1,0:T(4,128)}, u32[]{:S(2)}) copy-start(f32[4,256]{1,0:T(4,128)} %param.11) | copy-start | bytes 12292
  54.7 2.4 %copy-start.1 = (f32[4,256]{1,0:T(4,128)S(1)}, f32[4,256]{1,0:T(4,128)}, u32[]{:S(2)}) copy-start(f32[4,256]{1,0:T(4,128)} %param.10) | copy-start | bytes 12292
  54.7 2.4 %copy-start.4 = (f32[4]{0:T(128)S(1)}, f32[4]{0:T(128)}, u32[]{:S(2)}) copy-start(f32[4]{0:T(128)} %param.8) | copy-start | bytes 52
  54.7 34.2 %copy-start.3 = (f32[4,256]{1,0:T(4,128)S(1)}, f32[4,256]{1,0:T(4,128)}, u32[]{:S(2)}) copy-start(f32[4,256]{1,0:T(4,128)} %param.9) | copy-start | bytes 12292
  89.6 30.2 %copy-start.2 = (f32[4,256]{1,0:T(4,128)}, f32[4,256]{1,0:T(4,128)S(1)}, u32[]{:S(2)}) copy-start(f32[4,256]{1,0:T(4,128)S(1)} %get-tuple-element.6) | copy-start | bytes 12292
Sparse Core Ops, SparseCore 0:
  10.2 40.6 all-gather.1
where the time goes:
time: 127 us
  blocking collectives  84.2 us (66%)
  waiting for transfers between devices  18.2 us (14%)
  between operations  14.1 us (11%)
  other arithmetic  5.79 us (5%)
  matrix products  4.32 us (3%)
    psum x1, blocking collectives, per_device(): norm_now, curve = lax.psum((local_norm, local_curve), 'blk')  31.6 us
    psum x1, blocking collectives, per_device(): norm_next = lax.psum(jnp.sum(next_residual * next_residual, axis=1), 'blk')  29.5 us
    all_gather x1, blocking collectives, per_device(): lax.all_gather(dir_rows, 'blk', axis=0, tiled=True)  23.2 us
    all_gather x1, waiting for transfers between devices, per_device(): lax.all_gather(points, 'blk', axis=0, tiled=True)  17.5 us
  transfers between devices with their start and end apart: 1, of which 1 were waited for; matrix products, arithmetic and copies ran while one was open for 2% of the time, Pallas kernels for 0%

commit v1 on v0

v1 whole, which is shorter than its diff:
```python
import functools
import math

import jax
import jax.numpy as jnp
from jax import lax
from jax.experimental import pallas as pl
from jax.experimental.pallas import tpu as pltpu
from jax.sharding import PartitionSpec as P

LOG2E = 1.4426950408889634


def split_sizes(devices):
    lo = max(d for d in range(1, math.isqrt(devices) + 1) if devices % d == 0)
    return devices // lo, lo


def squares(block):
    wide = block.astype(jnp.float32)
    return jnp.sum(wide * wide, axis=1, keepdims=True)


def widen(block, scale, first):
    sq = squares(block)
    high = sq.astype(jnp.bfloat16).astype(jnp.float32)
    middle = (sq - high).astype(jnp.bfloat16).astype(jnp.float32)
    low = sq - high - middle
    lane = lax.broadcasted_iota(jnp.int32, block.shape, 1)
    base = 0 if first else 3
    one = 3 - base
    extra = jnp.where(lane == base, high, 0.0)
    extra = jnp.where(lane == base + 1, middle, extra)
    extra = jnp.where(lane == base + 2, low, extra)
    extra = jnp.where((lane >= one) & (lane < one + 3), 1.0, extra)
    scaled = block.astype(jnp.float32) * scale
    return jnp.concatenate(
        [scaled.astype(jnp.bfloat16), extra.astype(jnp.bfloat16)], axis=1
    )


def product_kernel(lo, hi, *refs):
    rows, refs = refs[:lo], refs[lo:]
    cols, refs = refs[:hi], refs[hi:]
    dirs, refs = refs[:hi], refs[hi:]
    length, out, row_wide = refs
    size = rows[0].shape[0]
    cands = length.shape[0]
    for k in range(lo):
        row_wide[pl.ds(k * size, size), :] = widen(rows[k][...], 1.0, True)
    rates = [
        (-0.5 * LOG2E) / (length[c] * length[c]) for c in range(cands)
    ]
    total = [None] * lo
    for h in range(hi):
        col_wide = widen(cols[h][...], -2.0, False)
        low = dirs[h][...].astype(jnp.bfloat16)
        which = lax.broadcasted_iota(jnp.int32, low.shape, 0)
        only = [jnp.where(which == c, low, jnp.zeros_like(low)) for c in range(cands)]
        for k in range(lo):
            dist = lax.dot_general(
                col_wide,
                row_wide[pl.ds(k * size, size), :],
                (((1,), (1,)), ((), ())),
                preferred_element_type=jnp.float32,
            )
            for c in range(cands):
                kern = jnp.exp2(dist * rates[c]).astype(jnp.bfloat16)
                part = jnp.dot(only[c], kern, preferred_element_type=jnp.float32)
                total[k] = part if total[k] is None else total[k] + part
    for k in range(lo):
        out[:, pl.ds(k * size, size)] = total[k]


def sums_kernel(lo, *refs):
    parts, refs = refs[:lo], refs[lo:]
    dirs, refs = refs[:lo], refs[lo:]
    ress, refs = refs[:lo], refs[lo:]
    noise, image_out, sums_out = refs
    cands, size = dirs[0].shape
    row = lax.broadcasted_iota(jnp.int32, (cands, 1), 0)
    sigma = jnp.zeros((cands, 1), jnp.float32)
    for c in range(cands):
        sigma = jnp.where(row == c, noise[c], sigma)
    sums = [jnp.zeros((cands, 1), jnp.float32)] * 4
    for k in range(lo):
        image = sigma * dirs[k][...]
        for m in range(lo):
            image += parts[m][:, pl.ds(((k - m) % lo) * size, size)]
        if k == 0:
            image_out[...] = image
        direction, residual = dirs[k][...], ress[k][...]
        terms = (
            residual * residual,
            direction * image,
            residual * image,
            image * image,
        )
        sums = [
            s + jnp.sum(t, axis=1, keepdims=True) for s, t in zip(sums, terms)
        ]
    lane = lax.broadcasted_iota(jnp.int32, (cands, 128), 1)
    packed = jnp.zeros((cands, 128), jnp.float32)
    for t in range(4):
        packed = jnp.where(lane == t, sums[t], packed)
    sums_out[...] = packed


def update_kernel(hi, *refs):
    sums, refs = refs[:hi], refs[hi:]
    image, solution, residual, direction, out_s, out_r, out_d = refs
    total = sums[0][...]
    for h in range(1, hi):
        total = total + sums[h][...]
    norm, curve, cross, square = (total[:, t : t + 1] for t in range(4))
    alpha = norm / curve
    norm_next = norm - 2.0 * alpha * cross + alpha * (alpha * square)
    beta = norm_next / norm
    step = direction[...]
    fresh = residual[...] - alpha * image[...]
    out_s[...] = solution[...] + alpha * step
    out_r[...] = fresh
    out_d[...] = fresh + beta * step


def per_device(devices, points, lengthscale, noise, solution, residual, direction):
    hi, lo = split_sizes(devices)
    size = points.shape[0]
    cands = direction.shape[0]

    def near(x):
        return [x] + [
            lax.ppermute(
                x,
                "blk",
                [
                    (h * lo + (l + k) % lo, h * lo + l)
                    for h in range(hi)
                    for l in range(lo)
                ],
            )
            for k in range(1, lo)
        ]

    def far(x):
        return [x] + [
            lax.ppermute(
                x,
                "blk",
                [
                    (((h + k) % hi) * lo + l, h * lo + l)
                    for h in range(hi)
                    for l in range(lo)
                ],
            )
            for k in range(1, hi)
        ]

    vmem = pl.BlockSpec(memory_space=pltpu.VMEM)
    smem = pl.BlockSpec(memory_space=pltpu.SMEM)
    params = pltpu.CompilerParams(vmem_limit_bytes=48 * 1024 * 1024)

    cols = far(points)
    col_dirs = far(direction)
    rows = near(points)
    row_dirs = near(direction)
    row_ress = near(residual)

    partial = pl.pallas_call(
        functools.partial(product_kernel, lo, hi),
        out_shape=jax.ShapeDtypeStruct((cands, lo * size), jnp.float32),
        in_specs=[vmem] * (lo + 2 * hi) + [smem],
        out_specs=vmem,
        scratch_shapes=[pltpu.VMEM((lo * size, 2 * points.shape[1]), jnp.bfloat16)],
        compiler_params=params,
        name="product",
    )(*rows, *cols, *col_dirs, lengthscale)

    image, sums = pl.pallas_call(
        functools.partial(sums_kernel, lo),
        out_shape=(
            jax.ShapeDtypeStruct((cands, size), jnp.float32),
            jax.ShapeDtypeStruct((cands, 128), jnp.float32),
        ),
        in_specs=[vmem] * (3 * lo) + [smem],
        out_specs=(vmem, vmem),
        compiler_params=params,
        name="sums",
    )(*near(partial), *row_dirs, *row_ress, noise)

    return pl.pallas_call(
        functools.partial(update_kernel, hi),
        out_shape=(jax.ShapeDtypeStruct((cands, size), jnp.float32),) * 3,
        in_specs=[vmem] * (hi + 4),
        out_specs=(vmem,) * 3,
        compiler_params=params,
        name="update",
    )(*far(sums), image, solution, residual, direction)


def solution(mesh):
    split = P(None, ("groups", "blk"))
    return jax.shard_map(
        functools.partial(per_device, mesh.shape["blk"]),
        mesh=mesh,
        in_specs=(P(("groups", "blk"), None), P("groups"), P("groups"), split, split, split),
        out_specs=(split, split, split),
        check_vma=False,
    )
```

time: 127 us -> 46.8 us (0.37)
  blocking collectives: 84.2 us -> 0 us
  starting transfers between devices: 0.04 us -> 20.3 us
  between operations: 14.1 us -> 0.68 us
  Pallas kernels: 0 us -> 5.87 us
  other arithmetic: 5.79 us -> 0 us
  matrix products: 4.32 us -> 0 us
  local copies, waits for them, and re-layouts: 0.03 us -> 2.2 us
    psum x2 -> x0, blocking collectives: 61.1 us -> none  [the longest x1 31.6 us: per_device(): norm_now, curve = lax.psum((local_norm, local_curve), 'blk')]
    all_gather x1 -> x0, blocking collectives: 23.2 us -> none  [per_device(): lax.all_gather(dir_rows, 'blk', axis=0, tiled=True)]
    ppermute x0 -> x21, starting transfers between devices: none -> 20.3 us  [the longest x9 10.4 us: far(): lax.ppermute(x, 'blk', [((h + k) % hi * lo + l, h * lo + l) for h in rang...]
    ppermute x0 -> x21, waiting for transfers between devices: none -> 17.5 us  [the longest x9 13 us: far(): lax.ppermute(x, 'blk', [((h + k) % hi * lo + l, h * lo + l) for h in rang...]
    all_gather x1 -> x0, waiting for transfers between devices: 17.5 us -> none  [per_device(): lax.all_gather(points, 'blk', axis=0, tiled=True)]
    pallas_call x0 -> x3, Pallas kernels: none -> 5.87 us  [the longest x1 4.48 us: per_device(): pl.pallas_call(functools.partial(product_kernel, lo, hi), out_shape=jax.S...]
    dot_general x2 -> x0, matrix products: 4.32 us -> none  [the longest x1 2.35 us: per_device(): jnp.einsum('cij,jc->ci', kern, lax.all_gather(dir_rows, 'blk', axis=0, ti...]
    reduce_sum x4 -> x0, other arithmetic: 3.75 us -> none  [the longest x1 1.84 us: tile_kernel(): source_sq = jnp.sum(jnp.square(source.astype(jnp.float32)), axis=1)]
  transfers between devices with their start and end apart: 1 -> 21, of which waited for: 1 -> 10; matrix products, arithmetic and copies ran while one was open for 2% -> 0% of each run, Pallas kernels for 0% -> 0%
where the time goes in v1:
time: 46.8 us; the launch traced here: 46.6 us
  starting transfers between devices  20.3 us (43%)
  waiting for transfers between devices  17.5 us (37%)
  Pallas kernels  5.87 us (13%)
  local copies, waits for them, and re-layouts  2.2 us (5%)
  between operations  0.68 us (1%)
    ppermute x9, waiting for transfers between devices, far(): lax.ppermute(x, 'blk', [((h + k) % hi * lo + l, h * lo + l) for h in rang...  13 us
    ppermute x9, starting transfers between devices, far(): lax.ppermute(x, 'blk', [((h + k) % hi * lo + l, h * lo + l) for h in rang...  10.4 us
    ppermute x12, starting transfers between devices, near(): lax.ppermute(x, 'blk', [(h * lo + (l + k) % lo, h * lo + l) for h in rang...  9.92 us
    ppermute x12, waiting for transfers between devices, near(): lax.ppermute(x, 'blk', [(h * lo + (l + k) % lo, h * lo + l) for h in rang...  4.51 us
    pallas_call x1, Pallas kernels, per_device(): pl.pallas_call(functools.partial(product_kernel, lo, hi), out_shape=jax.S...  4.48 us
    unnamed x12, local copies, waits for them, and re-layouts  2.2 us
  transfers between devices with their start and end apart: 21, of which 10 were waited for; matrix products, arithmetic and copies ran while one was open for 0% of the time, Pallas kernels for 0%

profile of v1, /device:TPU:0, one launch (start us, length us, event | category | flops | bytes accessed | tf_op | source)
XLA Modules:
  0.0 46.6 jit_solution(4431338085677331908)
XLA Ops:
  0.6 2.5 %collective-permute-start = (bf16[256,128]{1,0:T(8,128)(2,1)}, bf16[256,128]{1,0:T(8,128)(2,1)S(1)}, u32[]{:S(2)}, u32[]{:S(2)}) collective-permute-start(bf16[256,128]{1,0:T(8,128)(2,1)} %refs_4_.2), channel_id=1, source_target_pairs={{1,0},{2,1},{3,2},{0,3},{5,4},{6,5},{7,6},{4,7},{9,8},{10,9},{11,1... | collective-permute-start | bytes 196616 | tf_op jit(solution)/shard_map/ppermute | solution.py:133
  3.1 3.6 %collective-permute-start.6 = (f32[4,256]{1,0:T(4,128)}, f32[4,256]{1,0:T(4,128)S(1)}, u32[]{:S(2)}, u32[]{:S(2)}) collective-permute-start(f32[4,256]{1,0:T(4,128)} %refs_7_.1), channel_id=1, source_target_pairs={{4,0},{5,1},{6,2},{7,3},{8,4},{9,5},{10,6},{11,7},{12,8},{13,9},{1... | collective-permute-start | bytes 12296 | tf_op jit(solution)/shard_map/ppermute | solution.py:147
  6.7 1.0 %collective-permute-start.8 = (f32[4,256]{1,0:T(4,128)}, f32[4,256]{1,0:T(4,128)S(1)}, u32[]{:S(2)}, u32[]{:S(2)}) collective-permute-start(f32[4,256]{1,0:T(4,128)} %refs_7_.1), channel_id=1, source_target_pairs={{12,0},{13,1},{14,2},{15,3},{0,4},{1,5},{2,6},{3,7},{4,8},{5,9},{6... | collective-permute-start | bytes 12296 | tf_op jit(solution)/shard_map/ppermute | solution.py:147
  8.3 3.1 %collective-permute-done.7.refs_10_ = f32[4,256]{1,0:T(4,128)S(1)} collective-permute-done((f32[4,256]{1,0:T(4,128)}, f32[4,256]{1,0:T(4,128)S(1)}, u32[]{:S(2)}, u32[]{:S(2)}) %collective-permute-start.7) | collective-permute-done | bytes 4128 | tf_op jit(solution)/shard_map/ppermute | solution.py:147
  11.4 0.9 %collective-permute-start.3 = (bf16[256,128]{1,0:T(8,128)(2,1)}, bf16[256,128]{1,0:T(8,128)(2,1)S(1)}, u32[]{:S(2)}, u32[]{:S(2)}) collective-permute-start(bf16[256,128]{1,0:T(8,128)(2,1)} %refs_4_.2), channel_id=1, source_target_pairs={{4,0},{5,1},{6,2},{7,3},{8,4},{9,5},{10,6},{11,7},{12,8},{13,9},{1... | collective-permute-start | bytes 196616 | tf_op jit(solution)/shard_map/ppermute | solution.py:147
  12.3 1.1 %collective-permute-start.4 = (bf16[256,128]{1,0:T(8,128)(2,1)}, bf16[256,128]{1,0:T(8,128)(2,1)S(1)}, u32[]{:S(2)}, u32[]{:S(2)}) collective-permute-start(bf16[256,128]{1,0:T(8,128)(2,1)} %refs_4_.2), channel_id=1, source_target_pairs={{8,0},{9,1},{10,2},{11,3},{12,4},{13,5},{14,6},{15,7},{0,8},{1,9},... | collective-permute-start | bytes 196616 | tf_op jit(solution)/shard_map/ppermute | solution.py:147
  13.5 2.4 %collective-permute-done.3.refs_5_ = bf16[256,128]{1,0:T(8,128)(2,1)S(1)} collective-permute-done((bf16[256,128]{1,0:T(8,128)(2,1)}, bf16[256,128]{1,0:T(8,128)(2,1)S(1)}, u32[]{:S(2)}, u32[]{:S(2)}) %collective-permute-start.3) | collective-permute-done | bytes 65568 | tf_op jit(solution)/shard_map/ppermute | solution.py:147
  15.9 4.1 %collective-permute-done.4.refs_6_ = bf16[256,128]{1,0:T(8,128)(2,1)S(1)} collective-permute-done((bf16[256,128]{1,0:T(8,128)(2,1)}, bf16[256,128]{1,0:T(8,128)(2,1)S(1)}, u32[]{:S(2)}, u32[]{:S(2)}) %collective-permute-start.4) | collective-permute-done | bytes 65568 | tf_op jit(solution)/shard_map/ppermute | solution.py:147
  20.0 0.8 %copy-done = bf16[256,128]{1,0:T(8,128)(2,1)S(1)} copy-done((bf16[256,128]{1,0:T(8,128)(2,1)S(1)}, bf16[256,128]{1,0:T(8,128)(2,1)}, u32[]{:S(2)}) %copy-start) | copy-done | bytes 65560
  20.8 0.7 %copy-done.1 = f32[4,256]{1,0:T(4,128)S(1)} copy-done((f32[4,256]{1,0:T(4,128)S(1)}, f32[4,256]{1,0:T(4,128)}, u32[]{:S(2)}) %copy-start.1) | copy-done | bytes 4120
  22.2 4.5 %product.1.refs_0_ = f32[4,1024]{1,0:T(4,128)S(1)} custom-call(bf16[256,128]{1,0:T(8,128)(2,1)S(1)} %copy-done, bf16[256,128]{1,0:T(8,128)(2,1)S(1)} %collective-permute-done.refs_1_, bf16[256,128]{1,0:T(8,128)(2,1)S(1)} %collective-permute-done.1.refs_2_, bf16[256,128]{1,0:T(8,128)(2,1)S(1)} %collective-permute-done.2.refs_3_, ...), custom_call_target="tpu_custom_call" | custom-call | tf_op jit(solution)/shard_map/product/pallas_call | solution.py:169
  26.7 0.9 %collective-permute-start.10 = (f32[4,1024]{1,0:T(4,128)S(1)}, f32[4,1024]{1,0:T(4,128)S(1)}, u32[]{:S(2)}, u32[]{:S(2)}) collective-permute-start(f32[4,1024]{1,0:T(4,128)S(1)} %product.1.refs_0_), channel_id=1, source_target_pairs={{2,0},{3,1},{0,2},{1,3},{6,4},{7,5},{4,6},{5,7},{10,8},{11,9},{8,1... | collective-permute-start | bytes 49160 | tf_op jit(solution)/shard_map/ppermute | solution.py:133
  27.6 1.7 %collective-permute-start.9 = (f32[4,1024]{1,0:T(4,128)S(1)}, f32[4,1024]{1,0:T(4,128)S(1)}, u32[]{:S(2)}, u32[]{:S(2)}) collective-permute-start(f32[4,1024]{1,0:T(4,128)S(1)} %product.1.refs_0_), channel_id=1, source_target_pairs={{1,0},{2,1},{3,2},{0,3},{5,4},{6,5},{7,6},{4,7},{9,8},{10,9},{11,1... | collective-permute-start | bytes 49160 | tf_op jit(solution)/shard_map/ppermute | solution.py:133
  29.3 1.2 %collective-permute-start.13 = (f32[4,256]{1,0:T(4,128)S(1)}, f32[4,256]{1,0:T(4,128)S(1)}, u32[]{:S(2)}, u32[]{:S(2)}) collective-permute-start(f32[4,256]{1,0:T(4,128)S(1)} %copy-done.1), channel_id=1, source_target_pairs={{2,0},{3,1},{0,2},{1,3},{6,4},{7,5},{4,6},{5,7},{10,8},{11,9},{8,1... | collective-permute-start | bytes 12296 | tf_op jit(solution)/shard_map/ppermute | solution.py:133
  30.8 1.2 %collective-permute-start.14 = (f32[4,256]{1,0:T(4,128)S(1)}, f32[4,256]{1,0:T(4,128)S(1)}, u32[]{:S(2)}, u32[]{:S(2)}) collective-permute-start(f32[4,256]{1,0:T(4,128)S(1)} %copy-done.1), channel_id=1, source_target_pairs={{3,0},{0,1},{1,2},{2,3},{7,4},{4,5},{5,6},{6,7},{11,8},{8,9},{9,10... | collective-permute-start | bytes 12296 | tf_op jit(solution)/shard_map/ppermute | solution.py:133
  32.0 0.9 %collective-permute-done.13.refs_6_ = f32[4,256]{1,0:T(4,128)S(1)} collective-permute-done((f32[4,256]{1,0:T(4,128)S(1)}, f32[4,256]{1,0:T(4,128)S(1)}, u32[]{:S(2)}, u32[]{:S(2)}) %collective-permute-start.13) | collective-permute-done | bytes 4128 | tf_op jit(solution)/shard_map/ppermute | solution.py:133
  33.0 0.8 %collective-permute-done.14.refs_7_ = f32[4,256]{1,0:T(4,128)S(1)} collective-permute-done((f32[4,256]{1,0:T(4,128)S(1)}, f32[4,256]{1,0:T(4,128)S(1)}, u32[]{:S(2)}, u32[]{:S(2)}) %collective-permute-start.14) | collective-permute-done | bytes 4128 | tf_op jit(solution)/shard_map/ppermute | solution.py:133
  33.8 1.2 %collective-permute-start.16 = (f32[4,256]{1,0:T(4,128)S(1)}, f32[4,256]{1,0:T(4,128)S(1)}, u32[]{:S(2)}, u32[]{:S(2)}) collective-permute-start(f32[4,256]{1,0:T(4,128)S(1)} %copy-done.2), channel_id=1, source_target_pairs={{2,0},{3,1},{0,2},{1,3},{6,4},{7,5},{4,6},{5,7},{10,8},{11,9},{8,1... | collective-permute-start | bytes 12296 | tf_op jit(solution)/shard_map/ppermute | solution.py:133
  35.5 1.9 %collective-permute-done.16.refs_10_ = f32[4,256]{1,0:T(4,128)S(1)} collective-permute-done((f32[4,256]{1,0:T(4,128)S(1)}, f32[4,256]{1,0:T(4,128)S(1)}, u32[]{:S(2)}, u32[]{:S(2)}) %collective-permute-start.16) | collective-permute-done | bytes 4128 | tf_op jit(solution)/shard_map/ppermute | solution.py:133
  38.7 1.8 %collective-permute-start.18 = (f32[4,128]{1,0:T(4,128)S(1)}, f32[4,128]{1,0:T(4,128)S(1)}, u32[]{:S(2)}, u32[]{:S(2)}) collective-permute-start(f32[4,128]{1,0:T(4,128)S(1)} %get-tuple-element.5.refs_0_), channel_id=1, source_target_pairs={{4,0},{5,1},{6,2},{7,3},{8,4},{9,5},{10,6},{11,7},{12,8},{13,9},{1... | collective-permute-start | bytes 6152 | tf_op jit(solution)/shard_map/ppermute | solution.py:147
  40.5 1.9 %collective-permute-start.20 = (f32[4,128]{1,0:T(4,128)S(1)}, f32[4,128]{1,0:T(4,128)S(1)}, u32[]{:S(2)}, u32[]{:S(2)}) collective-permute-start(f32[4,128]{1,0:T(4,128)S(1)} %get-tuple-element.5.refs_0_), channel_id=1, source_target_pairs={{12,0},{13,1},{14,2},{15,3},{0,4},{1,5},{2,6},{3,7},{4,8},{5,9},{6... | collective-permute-start | bytes 6152 | tf_op jit(solution)/shard_map/ppermute | solution.py:147
  42.4 2.5 %collective-permute-done.19.refs_2_ = f32[4,128]{1,0:T(4,128)S(1)} collective-permute-done((f32[4,128]{1,0:T(4,128)S(1)}, f32[4,128]{1,0:T(4,128)S(1)}, u32[]{:S(2)}, u32[]{:S(2)}) %collective-permute-start.19) | collective-permute-done | bytes 2080 | tf_op jit(solution)/shard_map/ppermute | solution.py:147
  44.9 0.9 %collective-permute-done.20.refs_3_ = f32[4,128]{1,0:T(4,128)S(1)} collective-permute-done((f32[4,128]{1,0:T(4,128)S(1)}, f32[4,128]{1,0:T(4,128)S(1)}, u32[]{:S(2)}, u32[]{:S(2)}) %collective-permute-start.20) | collective-permute-done | bytes 2080 | tf_op jit(solution)/shard_map/ppermute | solution.py:147
  45.9 0.8 %update.1 = (f32[4,256]{1,0:T(4,128)}, f32[4,256]{1,0:T(4,128)}, f32[4,256]{1,0:T(4,128)}) custom-call(f32[4,128]{1,0:T(4,128)S(1)} %get-tuple-element.5.refs_0_, f32[4,128]{1,0:T(4,128)S(1)} %collective-permute-done.18.refs_1_, f32[4,128]{1,0:T(4,128)S(1)} %collective-permute-done.19.refs_2_, f32[4,128]{1,0:T(4,128)S(1)} %collective-permute-done.20.refs_3_, ...), custom_call_target="tpu_custom_call" | custom-call | tf_op jit(solution)/shard_map/update/pallas_call | solution.py:191
  (33 shorter events, 3.6 us)
Async XLA Ops:
  0.6 12.8 %collective-permute-start = (bf16[256,128]{1,0:T(8,128)(2,1)}, bf16[256,128]{1,0:T(8,128)(2,1)S(1)}, u32[]{:S(2)}, u32[]{:S(2)}) collective-permute-start(bf16[256,128]{1,0:T(8,128)(2,1)} %refs_4_.2), channel_id=1, source_target_pairs={{1,0},{2,1},{3,2},{0,3},{5,4},{6,5},{7,6},{4,7},{9,8},{10,9},{11,1... | collective-permute-start | bytes 196616 | tf_op jit(solution)/shard_map/ppermute | solution.py:133
  3.1 5.2 %collective-permute-start.6 = (f32[4,256]{1,0:T(4,128)}, f32[4,256]{1,0:T(4,128)S(1)}, u32[]{:S(2)}, u32[]{:S(2)}) collective-permute-start(f32[4,256]{1,0:T(4,128)} %refs_7_.1), channel_id=1, source_target_pairs={{4,0},{5,1},{6,2},{7,3},{8,4},{9,5},{10,6},{11,7},{12,8},{13,9},{1... | collective-permute-start | bytes 12296 | tf_op jit(solution)/shard_map/ppermute | solution.py:147
  6.7 4.7 %collective-permute-start.7 = (f32[4,256]{1,0:T(4,128)}, f32[4,256]{1,0:T(4,128)S(1)}, u32[]{:S(2)}, u32[]{:S(2)}) collective-permute-start(f32[4,256]{1,0:T(4,128)} %refs_7_.1), channel_id=1, source_target_pairs={{8,0},{9,1},{10,2},{11,3},{12,4},{13,5},{14,6},{15,7},{0,8},{1,9},... | collective-permute-start | bytes 12296 | tf_op jit(solution)/shard_map/ppermute | solution.py:147
  6.7 5.6 %collective-permute-start.8 = (f32[4,256]{1,0:T(4,128)}, f32[4,256]{1,0:T(4,128)S(1)}, u32[]{:S(2)}, u32[]{:S(2)}) collective-permute-start(f32[4,256]{1,0:T(4,128)} %refs_7_.1), channel_id=1, source_target_pairs={{12,0},{13,1},{14,2},{15,3},{0,4},{1,5},{2,6},{3,7},{4,8},{5,9},{6... | collective-permute-start | bytes 12296 | tf_op jit(solution)/shard_map/ppermute | solution.py:147
  7.7 5.8 %collective-permute-start.1 = (bf16[256,128]{1,0:T(8,128)(2,1)}, bf16[256,128]{1,0:T(8,128)(2,1)S(1)}, u32[]{:S(2)}, u32[]{:S(2)}) collective-permute-start(bf16[256,128]{1,0:T(8,128)(2,1)} %refs_4_.2), channel_id=1, source_target_pairs={{2,0},{3,1},{0,2},{1,3},{6,4},{7,5},{4,6},{5,7},{10,8},{11,9},{8,1... | collective-permute-start | bytes 196616 | tf_op jit(solution)/shard_map/ppermute | solution.py:133
  8.3 5.2 %collective-permute-start.2 = (bf16[256,128]{1,0:T(8,128)(2,1)}, bf16[256,128]{1,0:T(8,128)(2,1)S(1)}, u32[]{:S(2)}, u32[]{:S(2)}) collective-permute-start(bf16[256,128]{1,0:T(8,128)(2,1)} %refs_4_.2), channel_id=1, source_target_pairs={{3,0},{0,1},{1,2},{2,3},{7,4},{4,5},{5,6},{6,7},{11,8},{8,9},{9,10... | collective-permute-start | bytes 196616 | tf_op jit(solution)/shard_map/ppermute | solution.py:133
  11.4 4.5 %collective-permute-start.3 = (bf16[256,128]{1,0:T(8,128)(2,1)}, bf16[256,128]{1,0:T(8,128)(2,1)S(1)}, u32[]{:S(2)}, u32[]{:S(2)}) collective-permute-start(bf16[256,128]{1,0:T(8,128)(2,1)} %refs_4_.2), channel_id=1, source_target_pairs={{4,0},{5,1},{6,2},{7,3},{8,4},{9,5},{10,6},{11,7},{12,8},{13,9},{1... | collective-permute-start | bytes 196616 | tf_op jit(solution)/shard_map/ppermute | solution.py:147
  12.3 7.7 %collective-permute-start.4 = (bf16[256,128]{1,0:T(8,128)(2,1)}, bf16[256,128]{1,0:T(8,128)(2,1)S(1)}, u32[]{:S(2)}, u32[]{:S(2)}) collective-permute-start(bf16[256,128]{1,0:T(8,128)(2,1)} %refs_4_.2), channel_id=1, source_target_pairs={{8,0},{9,1},{10,2},{11,3},{12,4},{13,5},{14,6},{15,7},{0,8},{1,9},... | collective-permute-start | bytes 196616 | tf_op jit(solution)/shard_map/ppermute | solution.py:147
  13.4 6.6 %collective-permute-start.5 = (bf16[256,128]{1,0:T(8,128)(2,1)}, bf16[256,128]{1,0:T(8,128)(2,1)S(1)}, u32[]{:S(2)}, u32[]{:S(2)}) collective-permute-start(bf16[256,128]{1,0:T(8,128)(2,1)} %refs_4_.2), channel_id=1, source_target_pairs={{12,0},{13,1},{14,2},{15,3},{0,4},{1,5},{2,6},{3,7},{4,8},{5,9},{6... | collective-permute-start | bytes 196616 | tf_op jit(solution)/shard_map/ppermute | solution.py:147
  22.2 10.8 %copy-start.2 = (f32[4,256]{1,0:T(4,128)S(1)}, f32[4,256]{1,0:T(4,128)}, u32[]{:S(2)}) copy-start(f32[4,256]{1,0:T(4,128)} %refs_6_.1) | copy-start | bytes 12292
  22.2 15.8 %copy-start.5 = (f32[4]{0:T(128)S(1)}, f32[4]{0:T(128)}, u32[]{:S(2)}) copy-start(f32[4]{0:T(128)} %refs_12_.3) | copy-start | bytes 52
  26.7 11.3 %collective-permute-start.10 = (f32[4,1024]{1,0:T(4,128)S(1)}, f32[4,1024]{1,0:T(4,128)S(1)}, u32[]{:S(2)}, u32[]{:S(2)}) collective-permute-start(f32[4,1024]{1,0:T(4,128)S(1)} %product.1.refs_0_), channel_id=1, source_target_pairs={{2,0},{3,1},{0,2},{1,3},{6,4},{7,5},{4,6},{5,7},{10,8},{11,9},{8,1... | collective-permute-start | bytes 49160 | tf_op jit(solution)/shard_map/ppermute | solution.py:133
  27.6 10.5 %collective-permute-start.11 = (f32[4,1024]{1,0:T(4,128)S(1)}, f32[4,1024]{1,0:T(4,128)S(1)}, u32[]{:S(2)}, u32[]{:S(2)}) collective-permute-start(f32[4,1024]{1,0:T(4,128)S(1)} %product.1.refs_0_), channel_id=1, source_target_pairs={{3,0},{0,1},{1,2},{2,3},{7,4},{4,5},{5,6},{6,7},{11,8},{8,9},{9,10... | collective-permute-start | bytes 49160 | tf_op jit(solution)/shard_map/ppermute | solution.py:133
  27.6 10.5 %collective-permute-start.9 = (f32[4,1024]{1,0:T(4,128)S(1)}, f32[4,1024]{1,0:T(4,128)S(1)}, u32[]{:S(2)}, u32[]{:S(2)}) collective-permute-start(f32[4,1024]{1,0:T(4,128)S(1)} %product.1.refs_0_), channel_id=1, source_target_pairs={{1,0},{2,1},{3,2},{0,3},{5,4},{6,5},{7,6},{4,7},{9,8},{10,9},{11,1... | collective-permute-start | bytes 49160 | tf_op jit(solution)/shard_map/ppermute | solution.py:133
  29.3 1.5 %collective-permute-start.12 = (f32[4,256]{1,0:T(4,128)S(1)}, f32[4,256]{1,0:T(4,128)S(1)}, u32[]{:S(2)}, u32[]{:S(2)}) collective-permute-start(f32[4,256]{1,0:T(4,128)S(1)} %copy-done.1), channel_id=1, source_target_pairs={{1,0},{2,1},{3,2},{0,3},{5,4},{6,5},{7,6},{4,7},{9,8},{10,9},{11,1... | collective-permute-start | bytes 12296 | tf_op jit(solution)/shard_map/ppermute | solution.py:133
  29.3 3.6 %collective-permute-start.13 = (f32[4,256]{1,0:T(4,128)S(1)}, f32[4,256]{1,0:T(4,128)S(1)}, u32[]{:S(2)}, u32[]{:S(2)}) collective-permute-start(f32[4,256]{1,0:T(4,128)S(1)} %copy-done.1), channel_id=1, source_target_pairs={{2,0},{3,1},{0,2},{1,3},{6,4},{7,5},{4,6},{5,7},{10,8},{11,9},{8,1... | collective-permute-start | bytes 12296 | tf_op jit(solution)/shard_map/ppermute | solution.py:133
  30.8 3.0 %collective-permute-start.14 = (f32[4,256]{1,0:T(4,128)S(1)}, f32[4,256]{1,0:T(4,128)S(1)}, u32[]{:S(2)}, u32[]{:S(2)}) collective-permute-start(f32[4,256]{1,0:T(4,128)S(1)} %copy-done.1), channel_id=1, source_target_pairs={{3,0},{0,1},{1,2},{2,3},{7,4},{4,5},{5,6},{6,7},{11,8},{8,9},{9,10... | collective-permute-start | bytes 12296 | tf_op jit(solution)/shard_map/ppermute | solution.py:133
  32.9 2.0 %collective-permute-start.15 = (f32[4,256]{1,0:T(4,128)S(1)}, f32[4,256]{1,0:T(4,128)S(1)}, u32[]{:S(2)}, u32[]{:S(2)}) collective-permute-start(f32[4,256]{1,0:T(4,128)S(1)} %copy-done.2), channel_id=1, source_target_pairs={{1,0},{2,1},{3,2},{0,3},{5,4},{6,5},{7,6},{4,7},{9,8},{10,9},{11,1... | collective-permute-start | bytes 12296 | tf_op jit(solution)/shard_map/ppermute | solution.py:133
  33.8 3.6 %collective-permute-start.16 = (f32[4,256]{1,0:T(4,128)S(1)}, f32[4,256]{1,0:T(4,128)S(1)}, u32[]{:S(2)}, u32[]{:S(2)}) collective-permute-start(f32[4,256]{1,0:T(4,128)S(1)} %copy-done.2), channel_id=1, source_target_pairs={{2,0},{3,1},{0,2},{1,3},{6,4},{7,5},{4,6},{5,7},{10,8},{11,9},{8,1... | collective-permute-start | bytes 12296 | tf_op jit(solution)/shard_map/ppermute | solution.py:133
  35.0 3.0 %collective-permute-start.17 = (f32[4,256]{1,0:T(4,128)S(1)}, f32[4,256]{1,0:T(4,128)S(1)}, u32[]{:S(2)}, u32[]{:S(2)}) collective-permute-start(f32[4,256]{1,0:T(4,128)S(1)} %copy-done.2), channel_id=1, source_target_pairs={{3,0},{0,1},{1,2},{2,3},{7,4},{4,5},{5,6},{6,7},{11,8},{8,9},{9,10... | collective-permute-start | bytes 12296 | tf_op jit(solution)/shard_map/ppermute | solution.py:133
  38.0 7.8 %copy-start.3 = (f32[4,256]{1,0:T(4,128)S(1)}, f32[4,256]{1,0:T(4,128)}, u32[]{:S(2)}) copy-start(f32[4,256]{1,0:T(4,128)} %refs_5_.1) | copy-start | bytes 12292
  38.7 3.7 %collective-permute-start.18 = (f32[4,128]{1,0:T(4,128)S(1)}, f32[4,128]{1,0:T(4,128)S(1)}, u32[]{:S(2)}, u32[]{:S(2)}) collective-permute-start(f32[4,128]{1,0:T(4,128)S(1)} %get-tuple-element.5.refs_0_), channel_id=1, source_target_pairs={{4,0},{5,1},{6,2},{7,3},{8,4},{9,5},{10,6},{11,7},{12,8},{13,9},{1... | collective-permute-start | bytes 6152 | tf_op jit(solution)/shard_map/ppermute | solution.py:147
  40.4 4.5 %collective-permute-start.19 = (f32[4,128]{1,0:T(4,128)S(1)}, f32[4,128]{1,0:T(4,128)S(1)}, u32[]{:S(2)}, u32[]{:S(2)}) collective-permute-start(f32[4,128]{1,0:T(4,128)S(1)} %get-tuple-element.5.refs_0_), channel_id=1, source_target_pairs={{8,0},{9,1},{10,2},{11,3},{12,4},{13,5},{14,6},{15,7},{0,8},{1,9},... | collective-permute-start | bytes 6152 | tf_op jit(solution)/shard_map/ppermute | solution.py:147
  40.5 5.4 %collective-permute-start.20 = (f32[4,128]{1,0:T(4,128)S(1)}, f32[4,128]{1,0:T(4,128)S(1)}, u32[]{:S(2)}, u32[]{:S(2)}) collective-permute-start(f32[4,128]{1,0:T(4,128)S(1)} %get-tuple-element.5.refs_0_), channel_id=1, source_target_pairs={{12,0},{13,1},{14,2},{15,3},{0,4},{1,5},{2,6},{3,7},{4,8},{5,9},{6... | collective-permute-start | bytes 6152 | tf_op jit(solution)/shard_map/ppermute | solution.py:147
  (3 other events, 2.2 us)

commit v2 on v1

v2 whole, which is shorter than its diff:
```python
import functools
import math

import jax
import jax.numpy as jnp
from jax import lax
from jax.experimental import pallas as pl
from jax.experimental.pallas import tpu as pltpu
from jax.sharding import PartitionSpec as P

LOG2E = 1.4426950408889634


def split_sizes(devices):
    lo = max(d for d in range(1, math.isqrt(devices) + 1) if devices % d == 0)
    return devices // lo, lo


def squares(block):
    wide = block.astype(jnp.float32)
    return jnp.sum(wide * wide, axis=1, keepdims=True)


def widen(block, scale, first):
    sq = squares(block)
    high = sq.astype(jnp.bfloat16).astype(jnp.float32)
    middle = (sq - high).astype(jnp.bfloat16).astype(jnp.float32)
    low = sq - high - middle
    lane = lax.broadcasted_iota(jnp.int32, block.shape, 1)
    base = 0 if first else 3
    one = 3 - base
    extra = jnp.where(lane == base, high, 0.0)
    extra = jnp.where(lane == base + 1, middle, extra)
    extra = jnp.where(lane == base + 2, low, extra)
    extra = jnp.where((lane >= one) & (lane < one + 3), 1.0, extra)
    scaled = block.astype(jnp.float32) * scale
    return jnp.concatenate(
        [scaled.astype(jnp.bfloat16), extra.astype(jnp.bfloat16)], axis=1
    )


def pack_kernel(points, direction, to_cols, to_rows):
    size, dims = points.shape
    extra = to_cols.shape[1] - size
    pieces = [direction[:, pl.ds(p * dims, dims)] for p in range(size // dims)]
    spare = extra - sum(p.shape[0] for p in pieces)
    if spare:
        pieces.append(jnp.zeros((spare, dims), jnp.float32))
    tail = jnp.concatenate(pieces, axis=0).astype(jnp.bfloat16)
    for h in range(to_cols.shape[0]):
        to_cols[h, :size, :] = points[...]
        to_cols[h, size:, :] = tail
    for l in range(to_rows.shape[0]):
        to_rows[l] = points[...]


def product_kernel(rows, cols, length, out, row_wide):
    lo, size, dims = rows.shape
    hi = cols.shape[0]
    cands = length.shape[0]
    for k in range(lo):
        row_wide[pl.ds(k * size, size), :] = widen(rows[k], 1.0, True)
    rates = [
        (-0.5 * LOG2E) / (length[c] * length[c]) for c in range(cands)
    ]
    total = [None] * lo
    for h in range(hi):
        col_wide = widen(cols[h, :size, :], -2.0, False)
        tail = cols[h, size:, :].astype(jnp.float32)
        low = jnp.concatenate(
            [tail[p * cands : (p + 1) * cands] for p in range(size // dims)], axis=1
        )
        which = lax.broadcasted_iota(jnp.int32, low.shape, 0)
        only = [
            jnp.where(which == c, low, 0.0).astype(jnp.bfloat16) for c in range(cands)
        ]
        for k in range(lo):
            dist = lax.dot_general(
                col_wide,
                row_wide[pl.ds(k * size, size), :],
                (((1,), (1,)), ((), ())),
                preferred_element_type=jnp.float32,
            )
            for c in range(cands):
                kern = jnp.exp2(dist * rates[c]).astype(jnp.bfloat16)
                part = jnp.dot(only[c], kern, preferred_element_type=jnp.float32)
                total[k] = part if total[k] is None else total[k] + part
    for k in range(lo):
        out[k] = total[k]


def sums_kernel(parts, direction, residual, noise, image_out, sums_out):
    cands, size = direction.shape
    row = lax.broadcasted_iota(jnp.int32, (cands, 1), 0)
    sigma = jnp.zeros((cands, 1), jnp.float32)
    for c in range(cands):
        sigma = jnp.where(row == c, noise[c], sigma)
    step, rest = direction[...], residual[...]
    image = sigma * step
    for m in range(parts.shape[0]):
        image += parts[m]
    image_out[...] = image
    terms = (rest * rest, step * image, rest * image, image * image)
    lane = lax.broadcasted_iota(jnp.int32, (cands, 128), 1)
    packed = jnp.zeros((cands, 128), jnp.float32)
    for t in range(4):
        packed = jnp.where(lane == t, jnp.sum(terms[t], axis=1, keepdims=True), packed)
    for n in range(sums_out.shape[0]):
        sums_out[n] = packed


def update_kernel(sums, image, solution, residual, direction, out_s, out_r, out_d):
    total = sums[0]
    for n in range(1, sums.shape[0]):
        total = total + sums[n]
    norm, curve, cross, square = (total[:, t : t + 1] for t in range(4))
    alpha = norm / curve
    norm_next = norm - 2.0 * alpha * cross + alpha * (alpha * square)
    beta = norm_next / norm
    step = direction[...]
    fresh = residual[...] - alpha * image[...]
    out_s[...] = solution[...] + alpha * step
    out_r[...] = fresh
    out_d[...] = fresh + beta * step


def per_device(devices, points, lengthscale, noise, solution, residual, direction):
    hi, lo = split_sizes(devices)
    size, dims = points.shape
    cands = direction.shape[0]
    row_groups = [[h * lo + l for l in range(lo)] for h in range(hi)]
    col_groups = [[h * lo + l for h in range(hi)] for l in range(lo)]

    def exchange(x, groups):
        return lax.all_to_all(
            x, "blk", split_axis=0, concat_axis=0, axis_index_groups=groups
        )

    vmem = pl.BlockSpec(memory_space=pltpu.VMEM)
    smem = pl.BlockSpec(memory_space=pltpu.SMEM)
    params = pltpu.CompilerParams(vmem_limit_bytes=48 * 1024 * 1024)

    extra = -(-cands * (size // dims) // 16) * 16
    to_cols, to_rows = pl.pallas_call(
        pack_kernel,
        out_shape=(
            jax.ShapeDtypeStruct((hi, size + extra, dims), jnp.bfloat16),
            jax.ShapeDtypeStruct((lo, size, dims), jnp.bfloat16),
        ),
        in_specs=[vmem, vmem],
        out_specs=(vmem, vmem),
        compiler_params=params,
        name="pack",
    )(points, direction)
    cols = exchange(to_cols, col_groups)
    rows = exchange(to_rows, row_groups)

    partial = pl.pallas_call(
        product_kernel,
        out_shape=jax.ShapeDtypeStruct((lo, cands, size), jnp.float32),
        in_specs=[vmem, vmem, smem],
        out_specs=vmem,
        scratch_shapes=[pltpu.VMEM((lo * size, 2 * dims), jnp.bfloat16)],
        compiler_params=params,
        name="product",
    )(rows, cols, lengthscale)

    image, sums = pl.pallas_call(
        sums_kernel,
        out_shape=(
            jax.ShapeDtypeStruct((cands, size), jnp.float32),
            jax.ShapeDtypeStruct((devices, cands, 128), jnp.float32),
        ),
        in_specs=[vmem, vmem, vmem, smem],
        out_specs=(vmem, vmem),
        compiler_params=params,
        name="sums",
    )(exchange(partial, row_groups), direction, residual, noise)

    return pl.pallas_call(
        update_kernel,
        out_shape=(jax.ShapeDtypeStruct((cands, size), jnp.float32),) * 3,
        in_specs=[vmem] * 5,
        out_specs=(vmem,) * 3,
        compiler_params=params,
        name="update",
    )(exchange(sums, None), image, solution, residual, direction)


def solution(mesh):
    split = P(None, ("groups", "blk"))
    return jax.shard_map(
        functools.partial(per_device, mesh.shape["blk"]),
        mesh=mesh,
        in_specs=(P(("groups", "blk"), None), P("groups"), P("groups"), split, split, split),
        out_specs=(split, split, split),
        check_vma=False,
    )
```

time: 46.8 us -> 48 us (1.026)
  blocking collectives: 0 us -> 39.5 us
  starting transfers between devices: 20.3 us -> 0 us
  waiting for transfers between devices: 17.5 us -> 0 us
  local copies, waits for them, and re-layouts: 2.2 us -> 1.54 us
    all_to_all x0 -> x4, blocking collectives: none -> 39.5 us  [exchange(): lax.all_to_all(x, 'blk', split_axis=0, concat_axis=0, axis_index_groups=g...]
    ppermute x21 -> x0, starting transfers between devices: 20.3 us -> none  [the longest x9 10.4 us: far(): lax.ppermute(x, 'blk', [((h + k) % hi * lo + l, h * lo + l) for h in rang...]
    ppermute x21 -> x0, waiting for transfers between devices: 17.5 us -> none  [the longest x9 13 us: far(): lax.ppermute(x, 'blk', [((h + k) % hi * lo + l, h * lo + l) for h in rang...]
    unnamed x12 -> x14, local copies, waits for them, and re-layouts: 2.2 us -> 1.54 us
    pallas_call x3 -> x4, Pallas kernels: 5.87 us -> 5.95 us  [the longest x1 4.48 us: per_device(): pl.pallas_call(product_kernel, out_shape=jax.ShapeDtypeStruct((lo, cands,...]
  transfers between devices with their start and end apart: 21 -> 0, of which waited for: 10 -> 0; matrix products, arithmetic and copies ran while one was open for 0% -> 0% of each run, Pallas kernels for 0% -> 0%
where the time goes in v2:
time: 48 us; the launch traced here: 47.6 us
  blocking collectives  39.5 us (82%)
  Pallas kernels  5.95 us (12%)
  local copies, waits for them, and re-layouts  1.54 us (3%)
  between operations  0.66 us (1%)
    all_to_all x4, blocking collectives, exchange(): lax.all_to_all(x, 'blk', split_axis=0, concat_axis=0, axis_index_groups=g...  39.5 us
    pallas_call x1, Pallas kernels, per_device(): pl.pallas_call(product_kernel, out_shape=jax.ShapeDtypeStruct((lo, cands,...  4.48 us
    unnamed x14, local copies, waits for them, and re-layouts  1.54 us

profile of v2, /device:TPU:0, one launch (start us, length us, event | category | flops | bytes accessed | tf_op | source)
XLA Modules:
  0.0 47.6 jit_solution(2216468919552868203)
XLA Ops:
  0.6 0.0 copy-start
  0.6 0.8 %copy-done = bf16[256,128]{1,0:T(8,128)(2,1)S(1)} copy-done((bf16[256,128]{1,0:T(8,128)(2,1)S(1)}, bf16[256,128]{1,0:T(8,128)(2,1)}, u32[]{:S(2)}) %copy-start) | copy-done | bytes 65560
  1.5 0.0 copy-start.1
  1.5 0.7 %copy-done.1 = f32[4,256]{1,0:T(4,128)S(1)} copy-done((f32[4,256]{1,0:T(4,128)S(1)}, f32[4,256]{1,0:T(4,128)}, u32[]{:S(2)}) %copy-start.1) | copy-done | bytes 4120
  2.2 0.1 pack.1
  2.2 10.1 %all_to_all.20.rows = bf16[4,256,128]{2,1,0:T(8,128)(2,1)S(1)} all-to-all(bf16[4,256,128]{2,1,0:T(8,128)(2,1)S(1)} %get-tuple-element.7), channel_id=1, replica_groups={{0,1,2,3},{4,5,6,7},{8,9,10,11},{12,13,14,15},{16,17,18,19},{20,21,22,2..., dimensions={0} | all-to-all | bytes 524288 | tf_op jit(solution)/shard_map/all_to_all | solution.py:135
  12.3 0.0 copy-start.5
  12.3 13.6 %all_to_all.21.cols = bf16[4,272,128]{2,1,0:T(8,128)(2,1)S(1)} all-to-all(bf16[4,272,128]{2,1,0:T(8,128)(2,1)S(1)} %get-tuple-element.8), channel_id=1, replica_groups={{0,4,8,12},{1,5,9,13},{2,6,10,14},{3,7,11,15},{16,20,24,28},{17,21,25,2..., dimensions={0} | all-to-all | bytes 557056 | tf_op jit(solution)/shard_map/all_to_all | solution.py:135
  26.0 0.0 copy-done.5
  26.0 4.5 %product.1 = f32[4,4,256]{2,1,0:T(4,128)S(1)} custom-call(bf16[4,256,128]{2,1,0:T(8,128)(2,1)S(1)} %all_to_all.20.rows, bf16[4,272,128]{2,1,0:T(8,128)(2,1)S(1)} %all_to_all.21.cols, f32[4]{0:T(128)S(1)} %copy-done.5), custom_call_target="tpu_custom_call" | custom-call | tf_op jit(solution)/shard_map/product/pallas_call | solution.py:158
  30.4 0.0 copy-start.2
  30.4 0.0 copy-start.3
  30.4 0.0 copy-start.6
  30.5 6.3 %all_to_all.22.parts = f32[4,4,256]{2,1,0:T(4,128)S(1)} all-to-all(f32[4,4,256]{2,1,0:T(4,128)S(1)} %product.1), channel_id=1, replica_groups={{0,1,2,3},{4,5,6,7},{8,9,10,11},{12,13,14,15},{16,17,18,19},{20,21,22,2..., dimensions={0} | all-to-all | bytes 32768 | tf_op jit(solution)/shard_map/all_to_all | solution.py:135
  36.8 0.0 copy-done.2
  36.8 0.0 copy-done.3
  36.8 0.0 copy-done.6
  36.8 0.6 %sums.1 = (f32[4,256]{1,0:T(4,128)S(1)}, f32[16,4,128]{2,1,0:T(4,128)S(1)}) custom-call(f32[4,4,256]{2,1,0:T(4,128)S(1)} %all_to_all.22.parts, f32[4,256]{1,0:T(4,128)S(1)} %copy-done.2, f32[4,256]{1,0:T(4,128)S(1)} %copy-done.3, f32[4]{0:T(128)S(1)} %copy-done.6), custom_call_target="tpu_custom_call" | custom-call | tf_op jit(solution)/shard_map/sums/pallas_call | solution.py:168
  37.4 0.0 copy-start.4
  37.4 9.4 %all_to_all.23.sums = f32[16,4,128]{2,1,0:T(4,128)S(1)} all-to-all(f32[16,4,128]{2,1,0:T(4,128)S(1)} %get-tuple-element.9), channel_id=1, replica_groups=mesh['groups'=2,'blk'=16] {'blk'}, dimensions={0} | all-to-all | bytes 65536 | tf_op jit(solution)/shard_map/all_to_all | solution.py:135
  46.9 0.0 copy-done.4
  46.9 0.8 %update.1 = (f32[4,256]{1,0:T(4,128)}, f32[4,256]{1,0:T(4,128)}, f32[4,256]{1,0:T(4,128)}) custom-call(f32[16,4,128]{2,1,0:T(4,128)S(1)} %all_to_all.23.sums, f32[4,256]{1,0:T(4,128)S(1)} %get-tuple-element.10.image, f32[4,256]{1,0:T(4,128)S(1)} %copy-done.4, f32[4,256]{1,0:T(4,128)S(1)} %copy-done.3, f32[4,256]{1,0:T(4,128)S(1)} %copy-done.2), custom_call_target="tpu_custom_call" | custom-call | tf_op jit(solution)/shard_map/update/pallas_call | solution.py:180
Async XLA Ops:
  0.6 0.8 %copy-start = (bf16[256,128]{1,0:T(8,128)(2,1)S(1)}, bf16[256,128]{1,0:T(8,128)(2,1)}, u32[]{:S(2)}) copy-start(bf16[256,128]{1,0:T(8,128)(2,1)} %points.1) | copy-start | bytes 196612
  1.5 0.7 %copy-start.1 = (f32[4,256]{1,0:T(4,128)S(1)}, f32[4,256]{1,0:T(4,128)}, u32[]{:S(2)}) copy-start(f32[4,256]{1,0:T(4,128)} %direction.5) | copy-start | bytes 12292
  12.3 13.7 %copy-start.5 = (f32[4]{0:T(128)S(1)}, f32[4]{0:T(128)}, u32[]{:S(2)}) copy-start(f32[4]{0:T(128)} %length.1) | copy-start | bytes 52
  30.4 6.4 %copy-start.2 = (f32[4,256]{1,0:T(4,128)S(1)}, f32[4,256]{1,0:T(4,128)}, u32[]{:S(2)}) copy-start(f32[4,256]{1,0:T(4,128)} %direction.5) | copy-start | bytes 12292
  30.4 6.4 %copy-start.3 = (f32[4,256]{1,0:T(4,128)S(1)}, f32[4,256]{1,0:T(4,128)}, u32[]{:S(2)}) copy-start(f32[4,256]{1,0:T(4,128)} %residual.3) | copy-start | bytes 12292
  30.4 6.4 %copy-start.6 = (f32[4]{0:T(128)S(1)}, f32[4]{0:T(128)}, u32[]{:S(2)}) copy-start(f32[4]{0:T(128)} %noise.1) | copy-start | bytes 52
  37.4 9.4 %copy-start.4 = (f32[4,256]{1,0:T(4,128)S(1)}, f32[4,256]{1,0:T(4,128)}, u32[]{:S(2)}) copy-start(f32[4,256]{1,0:T(4,128)} %solution.1) | copy-start | bytes 12292

commit v3 on v1

v3 whole, which is shorter than its diff:
```python
import functools
import math

import jax
import jax.numpy as jnp
from jax import lax
from jax.experimental import pallas as pl
from jax.experimental.pallas import tpu as pltpu
from jax.sharding import PartitionSpec as P

LOG2E = 1.4426950408889634


def split_sizes(devices):
    lo = max(d for d in range(1, math.isqrt(devices) + 1) if devices % d == 0)
    return devices // lo, lo


def peer(index, step, count):
    return index ^ step if count & (count - 1) == 0 else (step - index) % count


def pieces_of(wide):
    high = wide.astype(jnp.bfloat16).astype(jnp.float32)
    middle = (wide - high).astype(jnp.bfloat16).astype(jnp.float32)
    return high, middle, wide - high - middle


def fold(wide, dims):
    return jnp.concatenate(
        [wide[:, p : p + dims] for p in range(0, wide.shape[1], dims)], axis=0
    )


def unfold(tall, cands):
    return jnp.concatenate(
        [tall[p : p + cands] for p in range(0, tall.shape[0], cands)], axis=1
    )


def squares(block):
    wide = block.astype(jnp.float32)
    return jnp.sum(wide * wide, axis=1, keepdims=True)


def widen(block, scale, first):
    sq = squares(block)
    high, middle, low = pieces_of(sq)
    lane = lax.broadcasted_iota(jnp.int32, block.shape, 1)
    base = 0 if first else 3
    one = 3 - base
    extra = jnp.where(lane == base, high, 0.0)
    extra = jnp.where(lane == base + 1, middle, extra)
    extra = jnp.where(lane == base + 2, low, extra)
    extra = jnp.where((lane >= one) & (lane < one + 3), 1.0, extra)
    scaled = block.astype(jnp.float32) * scale
    return jnp.concatenate(
        [scaled.astype(jnp.bfloat16), extra.astype(jnp.bfloat16)], axis=1
    )


def pack_kernel(points, direction, residual, to_col, to_row):
    size, dims = points.shape
    step = fold(direction[...], dims)
    rest = fold(residual[...], dims)
    zero = jnp.zeros_like(step)
    to_col[:size, :] = points[...]
    to_row[:size, :] = points[...]
    to_col[size:, :] = jnp.concatenate([step, zero], axis=0).astype(jnp.bfloat16)
    to_row[size:, :] = jnp.concatenate(
        [*pieces_of(step), *pieces_of(rest)], axis=0
    ).astype(jnp.bfloat16)


def product_kernel(lo, hi, *refs):
    rows, refs = refs[:lo], refs[lo:]
    cols, refs = refs[:hi], refs[hi:]
    length, out, row_wide = refs
    cands = length.shape[0]
    size = out.shape[1] // lo
    dims = rows[0].shape[1]
    tall = cands * size // dims
    for k in range(lo):
        row_wide[pl.ds(k * size, size), :] = widen(rows[k][:size, :], 1.0, True)
    rates = [
        (-0.5 * LOG2E) / (length[c] * length[c]) for c in range(cands)
    ]
    total = [None] * lo
    for h in range(hi):
        col_wide = widen(cols[h][:size, :], -2.0, False)
        tail = cols[h][size:, :].astype(jnp.float32)
        low = unfold(tail[:tall], cands)
        which = lax.broadcasted_iota(jnp.int32, low.shape, 0)
        only = [
            jnp.where(which == c, low, 0.0).astype(jnp.bfloat16) for c in range(cands)
        ]
        for k in range(lo):
            dist = lax.dot_general(
                col_wide,
                row_wide[pl.ds(k * size, size), :],
                (((1,), (1,)), ((), ())),
                preferred_element_type=jnp.float32,
            )
            for c in range(cands):
                kern = jnp.exp2(dist * rates[c]).astype(jnp.bfloat16)
                part = jnp.dot(only[c], kern, preferred_element_type=jnp.float32)
                total[k] = part if total[k] is None else total[k] + part
    for k in range(lo):
        out[:, pl.ds(k * size, size)] = total[k]


def sums_kernel(lo, *refs):
    parts, refs = refs[:lo], refs[lo:]
    rows, refs = refs[:lo], refs[lo:]
    noise, image_out, sums_out = refs
    cands, size = image_out.shape
    dims = rows[0].shape[1]
    tall = cands * size // dims
    row = lax.broadcasted_iota(jnp.int32, (cands, 1), 0)
    sigma = jnp.zeros((cands, 1), jnp.float32)
    for c in range(cands):
        sigma = jnp.where(row == c, noise[c], sigma)
    sums = [jnp.zeros((cands, 1), jnp.float32)] * 4
    for k in range(lo):
        tail = rows[k][size:, :].astype(jnp.float32)
        step, rest = (
            unfold(sum(tail[p * tall : (p + 1) * tall] for p in three), cands)
            for three in ((0, 1, 2), (3, 4, 5))
        )
        image = sigma * step
        for m in range(lo):
            image += parts[m][:, pl.ds(peer(m, k, lo) * size, size)]
        if k == 0:
            image_out[...] = image
        terms = (rest * rest, step * image, rest * image, image * image)
        sums = [
            s + jnp.sum(t, axis=1, keepdims=True) for s, t in zip(sums, terms)
        ]
    lane = lax.broadcasted_iota(jnp.int32, (cands, 128), 1)
    packed = jnp.zeros((cands, 128), jnp.float32)
    for t in range(4):
        packed = jnp.where(lane == t, sums[t], packed)
    sums_out[...] = packed


def update_kernel(sums, image, solution, residual, direction, out_s, out_r, out_d):
    total = sums[0]
    for n in range(1, sums.shape[0]):
        total = total + sums[n]
    norm, curve, cross, square = (total[:, t : t + 1] for t in range(4))
    alpha = norm / curve
    norm_next = norm - 2.0 * alpha * cross + alpha * (alpha * square)
    beta = norm_next / norm
    step = direction[...]
    fresh = residual[...] - alpha * image[...]
    out_s[...] = solution[...] + alpha * step
    out_r[...] = fresh
    out_d[...] = fresh + beta * step


def per_device(devices, points, lengthscale, noise, solution, residual, direction):
    hi, lo = split_sizes(devices)
    size, dims = points.shape
    cands = direction.shape[0]
    tall = cands * size // dims

    def row_peers(x):
        return [x] + [
            lax.ppermute(
                x,
                "blk",
                [
                    (h * lo + l, h * lo + peer(l, k, lo))
                    for h in range(hi)
                    for l in range(lo)
                ],
            )
            for k in range(1, lo)
        ]

    def col_peers(x):
        return [x] + [
            lax.ppermute(
                x,
                "blk",
                [
                    (h * lo + l, peer(h, k, hi) * lo + l)
                    for h in range(hi)
                    for l in range(lo)
                ],
            )
            for k in range(1, hi)
        ]

    vmem = pl.BlockSpec(memory_space=pltpu.VMEM)
    smem = pl.BlockSpec(memory_space=pltpu.SMEM)
    params = pltpu.CompilerParams(vmem_limit_bytes=48 * 1024 * 1024)

    to_col, to_row = pl.pallas_call(
        pack_kernel,
        out_shape=(
            jax.ShapeDtypeStruct((size + 2 * tall, dims), jnp.bfloat16),
            jax.ShapeDtypeStruct((size + 6 * tall, dims), jnp.bfloat16),
        ),
        in_specs=[vmem] * 3,
        out_specs=(vmem, vmem),
        compiler_params=params,
        name="pack",
    )(points, direction, residual)
    cols = col_peers(to_col)
    rows = row_peers(to_row)

    partial = pl.pallas_call(
        functools.partial(product_kernel, lo, hi),
        out_shape=jax.ShapeDtypeStruct((cands, lo * size), jnp.float32),
        in_specs=[vmem] * (lo + hi) + [smem],
        out_specs=vmem,
        scratch_shapes=[pltpu.VMEM((lo * size, 2 * dims), jnp.bfloat16)],
        compiler_params=params,
        name="product",
    )(*rows, *cols, lengthscale)

    image, sums = pl.pallas_call(
        functools.partial(sums_kernel, lo),
        out_shape=(
            jax.ShapeDtypeStruct((cands, size), jnp.float32),
            jax.ShapeDtypeStruct((cands, 128), jnp.float32),
        ),
        in_specs=[vmem] * (2 * lo) + [smem],
        out_specs=(vmem, vmem),
        compiler_params=params,
        name="sums",
    )(*row_peers(partial), *rows, noise)

    all_sums = lax.all_gather(
        sums,
        "blk",
        axis_index_groups=[[h * lo + l for h in range(hi)] for l in range(lo)],
    )
    return pl.pallas_call(
        update_kernel,
        out_shape=(jax.ShapeDtypeStruct((cands, size), jnp.float32),) * 3,
        in_specs=[vmem] * 5,
        out_specs=(vmem,) * 3,
        compiler_params=params,
        name="update",
    )(all_sums, image, solution, residual, direction)


def solution(mesh):
    split = P(None, ("groups", "blk"))
    return jax.shard_map(
        functools.partial(per_device, mesh.shape["blk"]),
        mesh=mesh,
        in_specs=(P(("groups", "blk"), None), P("groups"), P("groups"), split, split, split),
        out_specs=(split, split, split),
        check_vma=False,
    )
```

time: 46.8 us -> 38.4 us (0.82)
  blocking collectives: 0 us -> 11.9 us
  starting transfers between devices: 20.3 us -> 10 us
  waiting for transfers between devices: 17.5 us -> 7.43 us
    all_gather x0 -> x1, blocking collectives: none -> 11.9 us  [per_device(): lax.all_gather(sums, 'blk', axis_index_groups=[[h * lo + l for h in range...]
    ppermute x21 -> x9, starting transfers between devices: 20.3 us -> 10 us  [the longest x3 6.26 us: col_peers(): lax.ppermute(x, 'blk', [(h * lo + l, peer(h, k, hi) * lo + l) for h in ra...]
    ppermute x21 -> x9, waiting for transfers between devices: 17.5 us -> 7.43 us  [the longest x3 5.1 us: col_peers(): lax.ppermute(x, 'blk', [(h * lo + l, peer(h, k, hi) * lo + l) for h in ra...]
    unnamed x12 -> x14, local copies, waits for them, and re-layouts: 2.2 us -> 2.23 us
  transfers between devices with their start and end apart: 21 -> 9, of which waited for: 10 -> 5; matrix products, arithmetic and copies ran while one was open for 0% -> 0% of each run, Pallas kernels for 0% -> 0%
where the time goes in v3:
time: 38.4 us; the launch traced here: 38.2 us
  blocking collectives  11.9 us (31%)
  starting transfers between devices  10 us (26%)
  waiting for transfers between devices  7.43 us (19%)
  Pallas kernels  5.9 us (15%)
  local copies, waits for them, and re-layouts  2.23 us (6%)
  between operations  0.7 us (2%)
    all_gather x1, blocking collectives, per_device(): lax.all_gather(sums, 'blk', axis_index_groups=[[h * lo + l for h in range...  11.9 us
    ppermute x3, starting transfers between devices, col_peers(): lax.ppermute(x, 'blk', [(h * lo + l, peer(h, k, hi) * lo + l) for h in ra...  6.26 us
    ppermute x3, waiting for transfers between devices, col_peers(): lax.ppermute(x, 'blk', [(h * lo + l, peer(h, k, hi) * lo + l) for h in ra...  5.1 us
    pallas_call x1, Pallas kernels, per_device(): pl.pallas_call(functools.partial(product_kernel, lo, hi), out_shape=jax.S...  4.49 us
    ppermute x6, starting transfers between devices, row_peers(): lax.ppermute(x, 'blk', [(h * lo + l, h * lo + peer(l, k, lo)) for h in ra...  3.75 us
    ppermute x6, waiting for transfers between devices, row_peers(): lax.ppermute(x, 'blk', [(h * lo + l, h * lo + peer(l, k, lo)) for h in ra...  2.34 us
    unnamed x14, local copies, waits for them, and re-layouts  2.23 us
  transfers between devices with their start and end apart: 9, of which 5 were waited for; matrix products, arithmetic and copies ran while one was open for 0% of the time, Pallas kernels for 0%

profile of v3, /device:TPU:0, one launch (start us, length us, event | category | flops | bytes accessed | tf_op | source)
XLA Modules:
  0.0 38.2 jit_solution(8600450784902129785)
XLA Ops:
  0.6 0.8 %copy-done = bf16[256,128]{1,0:T(8,128)(2,1)S(1)} copy-done((bf16[256,128]{1,0:T(8,128)(2,1)S(1)}, bf16[256,128]{1,0:T(8,128)(2,1)}, u32[]{:S(2)}) %copy-start) | copy-done | bytes 65560
  1.5 0.7 %copy-done.1 = f32[4,256]{1,0:T(4,128)S(1)} copy-done((f32[4,256]{1,0:T(4,128)S(1)}, f32[4,256]{1,0:T(4,128)}, u32[]{:S(2)}) %copy-start.1) | copy-done | bytes 4120
  2.2 0.7 %copy-done.3 = f32[4,256]{1,0:T(4,128)S(1)} copy-done((f32[4,256]{1,0:T(4,128)S(1)}, f32[4,256]{1,0:T(4,128)}, u32[]{:S(2)}) %copy-start.3) | copy-done | bytes 4120
  2.9 0.0 copy-start.6
  2.9 5.1 %collective-permute-start.5 = (bf16[272,128]{1,0:T(8,128)(2,1)S(1)}, bf16[272,128]{1,0:T(8,128)(2,1)S(1)}, u32[]{:S(2)}, u32[]{:S(2)}) collective-permute-start(bf16[272,128]{1,0:T(8,128)(2,1)S(1)} %get-tuple-element.8.refs_4_), channel_id=1, source_target_pairs={{0,12},{1,13},{2,14},{3,15},{4,8},{5,9},{6,10},{7,11},{8,4},{9,5},... | collective-permute-start | bytes 208904 | tf_op jit(solution)/shard_map/ppermute | solution.py:183
  8.0 0.7 %collective-permute-start.2 = (bf16[304,128]{1,0:T(8,128)(2,1)S(1)}, bf16[304,128]{1,0:T(8,128)(2,1)S(1)}, u32[]{:S(2)}, u32[]{:S(2)}) collective-permute-start(bf16[304,128]{1,0:T(8,128)(2,1)S(1)} %get-tuple-element.7.refs_0_.refs_4_), channel_id=1, source_target_pairs={{0,3},{1,2},{2,1},{3,0},{4,7},{5,6},{6,5},{7,4},{8,11},{9,10},{10,... | collective-permute-start | bytes 233480 | tf_op jit(solution)/shard_map/ppermute | solution.py:169
  8.7 0.9 %collective-permute-start.1 = (bf16[304,128]{1,0:T(8,128)(2,1)S(1)}, bf16[304,128]{1,0:T(8,128)(2,1)S(1)}, u32[]{:S(2)}, u32[]{:S(2)}) collective-permute-start(bf16[304,128]{1,0:T(8,128)(2,1)S(1)} %get-tuple-element.7.refs_0_.refs_4_), channel_id=1, source_target_pairs={{0,2},{1,3},{2,0},{3,1},{4,6},{5,7},{6,4},{7,5},{8,10},{9,11},{10,... | collective-permute-start | bytes 233480 | tf_op jit(solution)/shard_map/ppermute | solution.py:169
  9.6 0.3 collective-permute-start
  9.9 0.5 %collective-permute-done.5.refs_7_ = bf16[272,128]{1,0:T(8,128)(2,1)S(1)} collective-permute-done((bf16[272,128]{1,0:T(8,128)(2,1)S(1)}, bf16[272,128]{1,0:T(8,128)(2,1)S(1)}, u32[]{:S(2)}, u32[]{:S(2)}) %collective-permute-start.5) | collective-permute-done | bytes 69664 | tf_op jit(solution)/shard_map/ppermute | solution.py:183
  10.3 1.1 %collective-permute-start.3 = (bf16[272,128]{1,0:T(8,128)(2,1)S(1)}, bf16[272,128]{1,0:T(8,128)(2,1)S(1)}, u32[]{:S(2)}, u32[]{:S(2)}) collective-permute-start(bf16[272,128]{1,0:T(8,128)(2,1)S(1)} %get-tuple-element.8.refs_4_), channel_id=1, source_target_pairs={{0,4},{1,5},{2,6},{3,7},{4,0},{5,1},{6,2},{7,3},{8,12},{9,13},{10,... | collective-permute-start | bytes 208904 | tf_op jit(solution)/shard_map/ppermute | solution.py:183
  11.5 4.2 %collective-permute-done.4.refs_6_ = bf16[272,128]{1,0:T(8,128)(2,1)S(1)} collective-permute-done((bf16[272,128]{1,0:T(8,128)(2,1)S(1)}, bf16[272,128]{1,0:T(8,128)(2,1)S(1)}, u32[]{:S(2)}, u32[]{:S(2)}) %collective-permute-start.4) | collective-permute-done | bytes 69664 | tf_op jit(solution)/shard_map/ppermute | solution.py:183
  15.7 0.5 %collective-permute-done.3.refs_5_ = bf16[272,128]{1,0:T(8,128)(2,1)S(1)} collective-permute-done((bf16[272,128]{1,0:T(8,128)(2,1)S(1)}, bf16[272,128]{1,0:T(8,128)(2,1)S(1)}, u32[]{:S(2)}, u32[]{:S(2)}) %collective-permute-start.3) | collective-permute-done | bytes 69664 | tf_op jit(solution)/shard_map/ppermute | solution.py:183
  16.1 0.0 collective-permute-done.2.refs_3_.refs_7_
  16.1 4.5 %product.1.refs_0_ = f32[4,1024]{1,0:T(4,128)S(1)} custom-call(bf16[304,128]{1,0:T(8,128)(2,1)S(1)} %get-tuple-element.7.refs_0_.refs_4_, bf16[304,128]{1,0:T(8,128)(2,1)S(1)} %collective-permute-done.refs_1_.refs_5_, bf16[304,128]{1,0:T(8,128)(2,1)S(1)} %collective-permute-done.1.refs_2_.refs_6_, ...), custom_call_target="tpu_custom_call" | custom-call | tf_op jit(solution)/shard_map/product/pallas_call | solution.py:213
  20.6 0.5 %collective-permute-start.8 = (f32[4,1024]{1,0:T(4,128)S(1)}, f32[4,1024]{1,0:T(4,128)S(1)}, u32[]{:S(2)}, u32[]{:S(2)}) collective-permute-start(f32[4,1024]{1,0:T(4,128)S(1)} %product.1.refs_0_), channel_id=1, source_target_pairs={{0,3},{1,2},{2,1},{3,0},{4,7},{5,6},{6,5},{7,4},{8,11},{9,10},{10,... | collective-permute-start | bytes 49160 | tf_op jit(solution)/shard_map/ppermute | solution.py:169
  21.1 1.3 %collective-permute-start.7 = (f32[4,1024]{1,0:T(4,128)S(1)}, f32[4,1024]{1,0:T(4,128)S(1)}, u32[]{:S(2)}, u32[]{:S(2)}) collective-permute-start(f32[4,1024]{1,0:T(4,128)S(1)} %product.1.refs_0_), channel_id=1, source_target_pairs={{0,2},{1,3},{2,0},{3,1},{4,6},{5,7},{6,4},{7,5},{8,10},{9,11},{10,... | collective-permute-start | bytes 49160 | tf_op jit(solution)/shard_map/ppermute | solution.py:169
  22.4 0.1 collective-permute-start.6
  22.5 1.3 %collective-permute-done.8.refs_3_ = f32[4,1024]{1,0:T(4,128)S(1)} collective-permute-done((f32[4,1024]{1,0:T(4,128)S(1)}, f32[4,1024]{1,0:T(4,128)S(1)}, u32[]{:S(2)}, u32[]{:S(2)}) %collective-permute-start.8) | collective-permute-done | bytes 16416 | tf_op jit(solution)/shard_map/ppermute | solution.py:169
  23.8 1.0 %collective-permute-done.7.refs_2_ = f32[4,1024]{1,0:T(4,128)S(1)} collective-permute-done((f32[4,1024]{1,0:T(4,128)S(1)}, f32[4,1024]{1,0:T(4,128)S(1)}, u32[]{:S(2)}, u32[]{:S(2)}) %collective-permute-start.7) | collective-permute-done | bytes 16416 | tf_op jit(solution)/shard_map/ppermute | solution.py:169
  24.8 0.6 %sums.1 = (f32[4,256]{1,0:T(4,128)S(1)}, f32[4,128]{1,0:T(4,128)S(1)}) custom-call(f32[4,1024]{1,0:T(4,128)S(1)} %product.1.refs_0_, f32[4,1024]{1,0:T(4,128)S(1)} %collective-permute-done.6.refs_1_, f32[4,1024]{1,0:T(4,128)S(1)} %collective-permute-done.7.refs_2_, f32[4,1024]{1,0:T(4,128)S(1)} %collective-permute-done.8.refs_3_, ...), custom_call_target="tpu_custom_call" | custom-call | tf_op jit(solution)/shard_map/sums/pallas_call | solution.py:223
  25.5 0.0 copy-start.2
  25.5 0.0 copy-start.4
  25.5 11.9 %all-gather.1.sums = f32[4,4,128]{2,1,0:T(4,128)S(1)} all-gather(f32[1,4,128]{2,1,0:T(4,128)S(1)} %bitcast.1), channel_id=2, replica_groups={{0,4,8,12},{1,5,9,13},{2,6,10,14},{3,7,11,15},{16,20,24,28},{17,21,25,2..., dimensions={0}, use_global_device_ids=true | all-gather | bytes 10240 | tf_op jit(solution)/shard_map/all_gather | solution.py:235
  37.4 0.8 %update.1 = (f32[4,256]{1,0:T(4,128)}, f32[4,256]{1,0:T(4,128)}, f32[4,256]{1,0:T(4,128)}) custom-call(f32[4,4,128]{2,1,0:T(4,128)S(1)} %all-gather.1.sums, f32[4,256]{1,0:T(4,128)S(1)} %get-tuple-element.10.image, f32[4,256]{1,0:T(4,128)S(1)} %copy-done.4, f32[4,256]{1,0:T(4,128)S(1)} %copy-done.3, f32[4,256]{1,0:T(4,128)S(1)} %copy-done.2), custom_call_target="tpu_custom_call" | custom-call | tf_op jit(solution)/shard_map/update/pallas_call | solution.py:240
  (13 shorter events, 0.0 us)
Async XLA Ops:
  0.6 0.8 %copy-start = (bf16[256,128]{1,0:T(8,128)(2,1)S(1)}, bf16[256,128]{1,0:T(8,128)(2,1)}, u32[]{:S(2)}) copy-start(bf16[256,128]{1,0:T(8,128)(2,1)} %points.1) | copy-start | bytes 196612
  1.5 0.7 %copy-start.1 = (f32[4,256]{1,0:T(4,128)S(1)}, f32[4,256]{1,0:T(4,128)}, u32[]{:S(2)}) copy-start(f32[4,256]{1,0:T(4,128)} %direction.3) | copy-start | bytes 12292
  2.2 0.7 %copy-start.3 = (f32[4,256]{1,0:T(4,128)S(1)}, f32[4,256]{1,0:T(4,128)}, u32[]{:S(2)}) copy-start(f32[4,256]{1,0:T(4,128)} %residual.3) | copy-start | bytes 12292
  2.9 13.3 %copy-start.6 = (f32[4]{0:T(128)S(1)}, f32[4]{0:T(128)}, u32[]{:S(2)}) copy-start(f32[4]{0:T(128)} %refs_8_.2) | copy-start | bytes 52
  2.9 7.5 %collective-permute-start.5 = (bf16[272,128]{1,0:T(8,128)(2,1)S(1)}, bf16[272,128]{1,0:T(8,128)(2,1)S(1)}, u32[]{:S(2)}, u32[]{:S(2)}) collective-permute-start(bf16[272,128]{1,0:T(8,128)(2,1)S(1)} %get-tuple-element.8.refs_4_), channel_id=1, source_target_pairs={{0,12},{1,13},{2,14},{3,15},{4,8},{5,9},{6,10},{7,11},{8,4},{9,5},... | collective-permute-start | bytes 208904 | tf_op jit(solution)/shard_map/ppermute | solution.py:183
  8.0 16.9 %copy-start.5 = (f32[4]{0:T(128)S(1)}, f32[4]{0:T(128)}, u32[]{:S(2)}) copy-start(f32[4]{0:T(128)} %refs_8_.3) | copy-start | bytes 52
  8.0 8.1 %collective-permute-start.2 = (bf16[304,128]{1,0:T(8,128)(2,1)S(1)}, bf16[304,128]{1,0:T(8,128)(2,1)S(1)}, u32[]{:S(2)}, u32[]{:S(2)}) collective-permute-start(bf16[304,128]{1,0:T(8,128)(2,1)S(1)} %get-tuple-element.7.refs_0_.refs_4_), channel_id=1, source_target_pairs={{0,3},{1,2},{2,1},{3,0},{4,7},{5,6},{6,5},{7,4},{8,11},{9,10},{10,... | collective-permute-start | bytes 233480 | tf_op jit(solution)/shard_map/ppermute | solution.py:169
  8.7 7.4 %collective-permute-start.1 = (bf16[304,128]{1,0:T(8,128)(2,1)S(1)}, bf16[304,128]{1,0:T(8,128)(2,1)S(1)}, u32[]{:S(2)}, u32[]{:S(2)}) collective-permute-start(bf16[304,128]{1,0:T(8,128)(2,1)S(1)} %get-tuple-element.7.refs_0_.refs_4_), channel_id=1, source_target_pairs={{0,2},{1,3},{2,0},{3,1},{4,6},{5,7},{6,4},{7,5},{8,10},{9,11},{10,... | collective-permute-start | bytes 233480 | tf_op jit(solution)/shard_map/ppermute | solution.py:169
  9.6 6.6 %collective-permute-start = (bf16[304,128]{1,0:T(8,128)(2,1)S(1)}, bf16[304,128]{1,0:T(8,128)(2,1)S(1)}, u32[]{:S(2)}, u32[]{:S(2)}) collective-permute-start(bf16[304,128]{1,0:T(8,128)(2,1)S(1)} %get-tuple-element.7.refs_0_.refs_4_), channel_id=1, source_target_pairs={{0,1},{1,0},{2,3},{3,2},{4,5},{5,4},{6,7},{7,6},{8,9},{9,8},{10,11... | collective-permute-start | bytes 233480 | tf_op jit(solution)/shard_map/ppermute | solution.py:169
  9.9 5.8 %collective-permute-start.4 = (bf16[272,128]{1,0:T(8,128)(2,1)S(1)}, bf16[272,128]{1,0:T(8,128)(2,1)S(1)}, u32[]{:S(2)}, u32[]{:S(2)}) collective-permute-start(bf16[272,128]{1,0:T(8,128)(2,1)S(1)} %get-tuple-element.8.refs_4_), channel_id=1, source_target_pairs={{0,8},{1,9},{2,10},{3,11},{4,12},{5,13},{6,14},{7,15},{8,0},{9,1},... | collective-permute-start | bytes 208904 | tf_op jit(solution)/shard_map/ppermute | solution.py:183
  10.3 5.8 %collective-permute-start.3 = (bf16[272,128]{1,0:T(8,128)(2,1)S(1)}, bf16[272,128]{1,0:T(8,128)(2,1)S(1)}, u32[]{:S(2)}, u32[]{:S(2)}) collective-permute-start(bf16[272,128]{1,0:T(8,128)(2,1)S(1)} %get-tuple-element.8.refs_4_), channel_id=1, source_target_pairs={{0,4},{1,5},{2,6},{3,7},{4,0},{5,1},{6,2},{7,3},{8,12},{9,13},{10,... | collective-permute-start | bytes 208904 | tf_op jit(solution)/shard_map/ppermute | solution.py:183
  20.6 3.2 %collective-permute-start.8 = (f32[4,1024]{1,0:T(4,128)S(1)}, f32[4,1024]{1,0:T(4,128)S(1)}, u32[]{:S(2)}, u32[]{:S(2)}) collective-permute-start(f32[4,1024]{1,0:T(4,128)S(1)} %product.1.refs_0_), channel_id=1, source_target_pairs={{0,3},{1,2},{2,1},{3,0},{4,7},{5,6},{6,5},{7,4},{8,11},{9,10},{10,... | collective-permute-start | bytes 49160 | tf_op jit(solution)/shard_map/ppermute | solution.py:169
  21.1 3.7 %collective-permute-start.7 = (f32[4,1024]{1,0:T(4,128)S(1)}, f32[4,1024]{1,0:T(4,128)S(1)}, u32[]{:S(2)}, u32[]{:S(2)}) collective-permute-start(f32[4,1024]{1,0:T(4,128)S(1)} %product.1.refs_0_), channel_id=1, source_target_pairs={{0,2},{1,3},{2,0},{3,1},{4,6},{5,7},{6,4},{7,5},{8,10},{9,11},{10,... | collective-permute-start | bytes 49160 | tf_op jit(solution)/shard_map/ppermute | solution.py:169
  22.4 2.5 %collective-permute-start.6 = (f32[4,1024]{1,0:T(4,128)S(1)}, f32[4,1024]{1,0:T(4,128)S(1)}, u32[]{:S(2)}, u32[]{:S(2)}) collective-permute-start(f32[4,1024]{1,0:T(4,128)S(1)} %product.1.refs_0_), channel_id=1, source_target_pairs={{0,1},{1,0},{2,3},{3,2},{4,5},{5,4},{6,7},{7,6},{8,9},{9,8},{10,11... | collective-permute-start | bytes 49160 | tf_op jit(solution)/shard_map/ppermute | solution.py:169
  25.5 11.9 %copy-start.2 = (f32[4,256]{1,0:T(4,128)S(1)}, f32[4,256]{1,0:T(4,128)}, u32[]{:S(2)}) copy-start(f32[4,256]{1,0:T(4,128)} %direction.3) | copy-start | bytes 12292
  25.5 11.9 %copy-start.4 = (f32[4,256]{1,0:T(4,128)S(1)}, f32[4,256]{1,0:T(4,128)}, u32[]{:S(2)}) copy-start(f32[4,256]{1,0:T(4,128)} %solution.1) | copy-start | bytes 12292

commit v4 on v3

--- a/solution.py
+++ b/solution.py
@@ -59,17 +59,32 @@
     )
 
 
-def pack_kernel(points, direction, residual, to_col, to_row):
+def pack_kernel(points, direction, residual, to_col, to_row, step_in, rest_in, sems):
     size, dims = points.shape
-    step = fold(direction[...], dims)
-    rest = fold(residual[...], dims)
+    copies = [
+        pltpu.make_async_copy(source, target, sems.at[i])
+        for i, (source, target) in enumerate(
+            (
+                (direction, step_in),
+                (residual, rest_in),
+                (points, to_col.at[pl.ds(0, size), :]),
+                (points, to_row.at[pl.ds(0, size), :]),
+            )
+        )
+    ]
+    for copy in copies:
+        copy.start()
+    for copy in copies[:2]:
+        copy.wait()
+    step = fold(step_in[...], dims)
+    rest = fold(rest_in[...], dims)
     zero = jnp.zeros_like(step)
-    to_col[:size, :] = points[...]
-    to_row[:size, :] = points[...]
     to_col[size:, :] = jnp.concatenate([step, zero], axis=0).astype(jnp.bfloat16)
     to_row[size:, :] = jnp.concatenate(
         [*pieces_of(step), *pieces_of(rest)], axis=0
     ).astype(jnp.bfloat16)
+    for copy in copies[2:]:
+        copy.wait()
 
 
 def product_kernel(lo, hi, *refs):
@@ -77,9 +92,9 @@
     cols, refs = refs[:hi], refs[hi:]
     length, out, row_wide = refs
     cands = length.shape[0]
-    size = out.shape[1] // lo
     dims = rows[0].shape[1]
-    tall = cands * size // dims
+    tall = out.shape[0] // lo
+    size = tall * dims // cands
     for k in range(lo):
         row_wide[pl.ds(k * size, size), :] = widen(rows[k][:size, :], 1.0, True)
     rates = [
@@ -106,53 +121,55 @@
                 part = jnp.dot(only[c], kern, preferred_element_type=jnp.float32)
                 total[k] = part if total[k] is None else total[k] + part
     for k in range(lo):
-        out[:, pl.ds(k * size, size)] = total[k]
+        out[pl.ds(k * tall, tall), :] = fold(total[k], dims)
 
 
 def sums_kernel(lo, *refs):
     parts, refs = refs[:lo], refs[lo:]
     rows, refs = refs[:lo], refs[lo:]
     noise, image_out, sums_out = refs
-    cands, size = image_out.shape
-    dims = rows[0].shape[1]
-    tall = cands * size // dims
-    row = lax.broadcasted_iota(jnp.int32, (cands, 1), 0)
-    sigma = jnp.zeros((cands, 1), jnp.float32)
+    cands = noise.shape[0]
+    tall, dims = image_out.shape
+    size = rows[0].shape[0] - 6 * tall
+    which = lax.broadcasted_iota(jnp.int32, (tall, 1), 0) % cands
+    sigma = jnp.zeros((tall, 1), jnp.float32)
     for c in range(cands):
-        sigma = jnp.where(row == c, noise[c], sigma)
-    sums = [jnp.zeros((cands, 1), jnp.float32)] * 4
+        sigma = jnp.where(which == c, noise[c], sigma)
+    sums = [jnp.zeros((tall, dims), jnp.float32)] * 4
     for k in range(lo):
         tail = rows[k][size:, :].astype(jnp.float32)
-        step, rest = (
-            unfold(sum(tail[p * tall : (p + 1) * tall] for p in three), cands)
-            for three in ((0, 1, 2), (3, 4, 5))
-        )
+        tail = [tail[p * tall : (p + 1) * tall] for p in range(6)]
+        step = tail[0] + tail[1] + tail[2]
+        rest = tail[3] + tail[4] + tail[5]
         image = sigma * step
         for m in range(lo):
-            image += parts[m][:, pl.ds(peer(m, k, lo) * size, size)]
+            image += parts[m][pl.ds(peer(m, k, lo) * tall, tall), :]
         if k == 0:
             image_out[...] = image
         terms = (rest * rest, step * image, rest * image, image * image)
-        sums = [
-            s + jnp.sum(t, axis=1, keepdims=True) for s, t in zip(sums, terms)
-        ]
-    lane = lax.broadcasted_iota(jnp.int32, (cands, 128), 1)
-    packed = jnp.zeros((cands, 128), jnp.float32)
-    for t in range(4):
-        packed = jnp.where(lane == t, sums[t], packed)
-    sums_out[...] = packed
-
-
-def update_kernel(sums, image, solution, residual, direction, out_s, out_r, out_d):
-    total = sums[0]
-    for n in range(1, sums.shape[0]):
-        total = total + sums[n]
-    norm, curve, cross, square = (total[:, t : t + 1] for t in range(4))
+        sums = [s + t for s, t in zip(sums, terms)]
+    for i, s in enumerate(sums):
+        sums_out[pl.ds(i * cands, cands), :] = sum(
+            s[p : p + cands] for p in range(0, tall, cands)
+        )
+
+
+def update_kernel(hi, *refs):
+    sums, refs = refs[:hi], refs[hi:]
+    image, solution, residual, direction, out_s, out_r, out_d = refs
+    cands = solution.shape[0]
+    total = sums[0][...]
+    for h in range(1, hi):
+        total = total + sums[h][...]
+    total = jnp.sum(total, axis=1, keepdims=True)
+    norm, curve, cross, square = (
+        total[i * cands : (i + 1) * cands] for i in range(4)
+    )
     alpha = norm / curve
     norm_next = norm - 2.0 * alpha * cross + alpha * (alpha * square)
     beta = norm_next / norm
     step = direction[...]
-    fresh = residual[...] - alpha * image[...]
+    fresh = residual[...] - alpha * unfold(image[...], cands)
     out_s[...] = solution[...] + alpha * step
     out_r[...] = fresh
     out_d[...] = fresh + beta * step
@@ -202,8 +219,13 @@
             jax.ShapeDtypeStruct((size + 2 * tall, dims), jnp.bfloat16),
             jax.ShapeDtypeStruct((size + 6 * tall, dims), jnp.bfloat16),
         ),
-        in_specs=[vmem] * 3,
+        in_specs=[pl.BlockSpec(memory_space=pl.ANY)] * 3,
         out_specs=(vmem, vmem),
+        scratch_shapes=[
+            pltpu.VMEM((cands, size), jnp.float32),
+            pltpu.VMEM((cands, size), jnp.float32),
+            pltpu.SemaphoreType.DMA((4,)),
+        ],
         compiler_params=params,
         name="pack",
     )(points, direction, residual)
@@ -212,7 +234,7 @@
 
     partial = pl.pallas_call(
         functools.partial(product_kernel, lo, hi),
-        out_shape=jax.ShapeDtypeStruct((cands, lo * size), jnp.float32),
+        out_shape=jax.ShapeDtypeStruct((lo * tall, dims), jnp.float32),
         in_specs=[vmem] * (lo + hi) + [smem],
         out_specs=vmem,
         scratch_shapes=[pltpu.VMEM((lo * size, 2 * dims), jnp.bfloat16)],
@@ -223,8 +245,8 @@
     image, sums = pl.pallas_call(
         functools.partial(sums_kernel, lo),
         out_shape=(
-            jax.ShapeDtypeStruct((cands, size), jnp.float32),
-            jax.ShapeDtypeStruct((cands, 128), jnp.float32),
+            jax.ShapeDtypeStruct((tall, dims), jnp.float32),
+            jax.ShapeDtypeStruct((4 * cands, dims), jnp.float32),
         ),
         in_specs=[vmem] * (2 * lo) + [smem],
         out_specs=(vmem, vmem),
@@ -232,19 +254,14 @@
         name="sums",
     )(*row_peers(partial), *rows, noise)
 
-    all_sums = lax.all_gather(
-        sums,
-        "blk",
-        axis_index_groups=[[h * lo + l for h in range(hi)] for l in range(lo)],
-    )
     return pl.pallas_call(
-        update_kernel,
+        functools.partial(update_kernel, hi),
         out_shape=(jax.ShapeDtypeStruct((cands, size), jnp.float32),) * 3,
-        in_specs=[vmem] * 5,
+        in_specs=[vmem] * (hi + 4),
         out_specs=(vmem,) * 3,
         compiler_params=params,
         name="update",
-    )(all_sums, image, solution, residual, direction)
+    )(*col_peers(sums), image, solution, residual, direction)
 
 
 def solution(mesh):

time: 38.4 us -> 33.2 us (0.86)
  blocking collectives: 11.9 us -> 0 us
  starting transfers between devices: 10 us -> 14.5 us
  waiting for transfers between devices: 7.43 us -> 9.51 us
    all_gather x1 -> x0, blocking collectives: 11.9 us -> none  [per_device(): lax.all_gather(sums, 'blk', axis_index_groups=[[h * lo + l for h in range...]
    ppermute x3 -> x6, starting transfers between devices: 6.26 us -> 10.7 us  [col_peers(): lax.ppermute(x, 'blk', [(h * lo + l, peer(h, k, hi) * lo + l) for h in ra...]
    ppermute x3 -> x6, waiting for transfers between devices: 5.1 us -> 7.18 us  [col_peers(): lax.ppermute(x, 'blk', [(h * lo + l, peer(h, k, hi) * lo + l) for h in ra...]
  transfers between devices with their start and end apart: 9 -> 12, of which waited for: 5 -> 7; matrix products, arithmetic and copies ran while one was open for 0% -> 0% of each run, Pallas kernels for 0% -> 0%
where the time goes in v4:
time: 33.2 us; the launch traced here: 32.9 us
  starting transfers between devices  14.5 us (44%)
  waiting for transfers between devices  9.51 us (29%)
  Pallas kernels  6.03 us (18%)
  local copies, waits for them, and re-layouts  2.23 us (7%)
  between operations  0.7 us (2%)
    ppermute x6, starting transfers between devices, col_peers(): lax.ppermute(x, 'blk', [(h * lo + l, peer(h, k, hi) * lo + l) for h in ra...  10.7 us
    ppermute x6, waiting for transfers between devices, col_peers(): lax.ppermute(x, 'blk', [(h * lo + l, peer(h, k, hi) * lo + l) for h in ra...  7.18 us
    pallas_call x1, Pallas kernels, per_device(): pl.pallas_call(functools.partial(product_kernel, lo, hi), out_shape=jax.S...  4.49 us
    ppermute x6, starting transfers between devices, row_peers(): lax.ppermute(x, 'blk', [(h * lo + l, h * lo + peer(l, k, lo)) for h in ra...  3.76 us
    ppermute x6, waiting for transfers between devices, row_peers(): lax.ppermute(x, 'blk', [(h * lo + l, h * lo + peer(l, k, lo)) for h in ra...  2.33 us
    unnamed x14, local copies, waits for them, and re-layouts  2.23 us
    pallas_call x1, Pallas kernels, per_device(): pl.pallas_call(functools.partial(update_kernel, hi), out_shape=(jax.Shape...  0.78 us
  transfers between devices with their start and end apart: 12, of which 7 were waited for; matrix products, arithmetic and copies ran while one was open for 0% of the time, Pallas kernels for 0%

profile of v4, /device:TPU:0, one launch (start us, length us, event | category | flops | bytes accessed | tf_op | source)
XLA Modules:
  0.0 32.9 jit_solution(17336600518335597565)
XLA Ops:
  0.6 0.8 %copy-done = bf16[256,128]{1,0:T(8,128)(2,1)S(1)} copy-done((bf16[256,128]{1,0:T(8,128)(2,1)S(1)}, bf16[256,128]{1,0:T(8,128)(2,1)}, u32[]{:S(2)}) %copy-start) | copy-done | bytes 65560
  1.5 0.7 %copy-done.1 = f32[4,256]{1,0:T(4,128)S(1)} copy-done((f32[4,256]{1,0:T(4,128)S(1)}, f32[4,256]{1,0:T(4,128)}, u32[]{:S(2)}) %copy-start.1) | copy-done | bytes 4120
  2.2 0.7 %copy-done.3 = f32[4,256]{1,0:T(4,128)S(1)} copy-done((f32[4,256]{1,0:T(4,128)S(1)}, f32[4,256]{1,0:T(4,128)}, u32[]{:S(2)}) %copy-start.3) | copy-done | bytes 4120
  2.8 0.2 pack.1
  3.1 5.1 %collective-permute-start.5 = (bf16[272,128]{1,0:T(8,128)(2,1)S(1)}, bf16[272,128]{1,0:T(8,128)(2,1)S(1)}, u32[]{:S(2)}, u32[]{:S(2)}) collective-permute-start(bf16[272,128]{1,0:T(8,128)(2,1)S(1)} %get-tuple-element.8.refs_4_), channel_id=1, source_target_pairs={{0,12},{1,13},{2,14},{3,15},{4,8},{5,9},{6,10},{7,11},{8,4},{9,5},... | collective-permute-start | bytes 208904 | tf_op jit(solution)/shard_map/ppermute | solution.py:200
  8.2 0.7 %collective-permute-start.2 = (bf16[304,128]{1,0:T(8,128)(2,1)S(1)}, bf16[304,128]{1,0:T(8,128)(2,1)S(1)}, u32[]{:S(2)}, u32[]{:S(2)}) collective-permute-start(bf16[304,128]{1,0:T(8,128)(2,1)S(1)} %get-tuple-element.7.refs_0_.refs_4_), channel_id=1, source_target_pairs={{0,3},{1,2},{2,1},{3,0},{4,7},{5,6},{6,5},{7,4},{8,11},{9,10},{10,... | collective-permute-start | bytes 233480 | tf_op jit(solution)/shard_map/ppermute | solution.py:186
  8.9 0.9 %collective-permute-start.1 = (bf16[304,128]{1,0:T(8,128)(2,1)S(1)}, bf16[304,128]{1,0:T(8,128)(2,1)S(1)}, u32[]{:S(2)}, u32[]{:S(2)}) collective-permute-start(bf16[304,128]{1,0:T(8,128)(2,1)S(1)} %get-tuple-element.7.refs_0_.refs_4_), channel_id=1, source_target_pairs={{0,2},{1,3},{2,0},{3,1},{4,6},{5,7},{6,4},{7,5},{8,10},{9,11},{10,... | collective-permute-start | bytes 233480 | tf_op jit(solution)/shard_map/ppermute | solution.py:186
  9.7 0.3 collective-permute-start
  10.0 0.5 %collective-permute-done.5.refs_7_ = bf16[272,128]{1,0:T(8,128)(2,1)S(1)} collective-permute-done((bf16[272,128]{1,0:T(8,128)(2,1)S(1)}, bf16[272,128]{1,0:T(8,128)(2,1)S(1)}, u32[]{:S(2)}, u32[]{:S(2)}) %collective-permute-start.5) | collective-permute-done | bytes 69664 | tf_op jit(solution)/shard_map/ppermute | solution.py:200
  10.5 1.1 %collective-permute-start.3 = (bf16[272,128]{1,0:T(8,128)(2,1)S(1)}, bf16[272,128]{1,0:T(8,128)(2,1)S(1)}, u32[]{:S(2)}, u32[]{:S(2)}) collective-permute-start(bf16[272,128]{1,0:T(8,128)(2,1)S(1)} %get-tuple-element.8.refs_4_), channel_id=1, source_target_pairs={{0,4},{1,5},{2,6},{3,7},{4,0},{5,1},{6,2},{7,3},{8,12},{9,13},{10,... | collective-permute-start | bytes 208904 | tf_op jit(solution)/shard_map/ppermute | solution.py:200
  11.7 4.2 %collective-permute-done.4.refs_6_ = bf16[272,128]{1,0:T(8,128)(2,1)S(1)} collective-permute-done((bf16[272,128]{1,0:T(8,128)(2,1)S(1)}, bf16[272,128]{1,0:T(8,128)(2,1)S(1)}, u32[]{:S(2)}, u32[]{:S(2)}) %collective-permute-start.4) | collective-permute-done | bytes 69664 | tf_op jit(solution)/shard_map/ppermute | solution.py:200
  15.8 0.5 %collective-permute-done.3.refs_5_ = bf16[272,128]{1,0:T(8,128)(2,1)S(1)} collective-permute-done((bf16[272,128]{1,0:T(8,128)(2,1)S(1)}, bf16[272,128]{1,0:T(8,128)(2,1)S(1)}, u32[]{:S(2)}, u32[]{:S(2)}) %collective-permute-start.3) | collective-permute-done | bytes 69664 | tf_op jit(solution)/shard_map/ppermute | solution.py:200
  16.3 4.5 %product.1.refs_0_ = f32[32,128]{1,0:T(8,128)S(1)} custom-call(bf16[304,128]{1,0:T(8,128)(2,1)S(1)} %get-tuple-element.7.refs_0_.refs_4_, bf16[304,128]{1,0:T(8,128)(2,1)S(1)} %collective-permute-done.refs_1_.refs_5_, bf16[304,128]{1,0:T(8,128)(2,1)S(1)} %collective-permute-done.1.refs_2_.refs_6_, ...), custom_call_target="tpu_custom_call" | custom-call | tf_op jit(solution)/shard_map/product/pallas_call | solution.py:235
  20.8 0.5 %collective-permute-start.8 = (f32[32,128]{1,0:T(8,128)S(1)}, f32[32,128]{1,0:T(8,128)S(1)}, u32[]{:S(2)}, u32[]{:S(2)}) collective-permute-start(f32[32,128]{1,0:T(8,128)S(1)} %product.1.refs_0_), channel_id=1, source_target_pairs={{0,3},{1,2},{2,1},{3,0},{4,7},{5,6},{6,5},{7,4},{8,11},{9,10},{10,... | collective-permute-start | bytes 49160 | tf_op jit(solution)/shard_map/ppermute | solution.py:186
  21.3 1.3 %collective-permute-start.7 = (f32[32,128]{1,0:T(8,128)S(1)}, f32[32,128]{1,0:T(8,128)S(1)}, u32[]{:S(2)}, u32[]{:S(2)}) collective-permute-start(f32[32,128]{1,0:T(8,128)S(1)} %product.1.refs_0_), channel_id=1, source_target_pairs={{0,2},{1,3},{2,0},{3,1},{4,6},{5,7},{6,4},{7,5},{8,10},{9,11},{10,... | collective-permute-start | bytes 49160 | tf_op jit(solution)/shard_map/ppermute | solution.py:186
  22.6 0.1 collective-permute-start.6
  22.7 1.3 %collective-permute-done.8.refs_3_ = f32[32,128]{1,0:T(8,128)S(1)} collective-permute-done((f32[32,128]{1,0:T(8,128)S(1)}, f32[32,128]{1,0:T(8,128)S(1)}, u32[]{:S(2)}, u32[]{:S(2)}) %collective-permute-start.8) | collective-permute-done | bytes 16416 | tf_op jit(solution)/shard_map/ppermute | solution.py:186
  24.0 1.0 %collective-permute-done.7.refs_2_ = f32[32,128]{1,0:T(8,128)S(1)} collective-permute-done((f32[32,128]{1,0:T(8,128)S(1)}, f32[32,128]{1,0:T(8,128)S(1)}, u32[]{:S(2)}, u32[]{:S(2)}) %collective-permute-start.7) | collective-permute-done | bytes 16416 | tf_op jit(solution)/shard_map/ppermute | solution.py:186
  25.0 0.6 %sums.1 = (f32[8,128]{1,0:T(8,128)S(1)}, f32[16,128]{1,0:T(8,128)S(1)}) custom-call(f32[32,128]{1,0:T(8,128)S(1)} %product.1.refs_0_, f32[32,128]{1,0:T(8,128)S(1)} %collective-permute-done.6.refs_1_, f32[32,128]{1,0:T(8,128)S(1)} %collective-permute-done.7.refs_2_, f32[32,128]{1,0:T(8,128)S(1)} %collective-permute-done.8.refs_3_, ...), custom_call_target="tpu_custom_call" | custom-call | tf_op jit(solution)/shard_map/sums/pallas_call | solution.py:245
  25.6 2.0 %collective-permute-start.11 = (f32[16,128]{1,0:T(8,128)S(1)}, f32[16,128]{1,0:T(8,128)S(1)}, u32[]{:S(2)}, u32[]{:S(2)}) collective-permute-start(f32[16,128]{1,0:T(8,128)S(1)} %get-tuple-element.9.refs_0_), channel_id=1, source_target_pairs={{0,12},{1,13},{2,14},{3,15},{4,8},{5,9},{6,10},{7,11},{8,4},{9,5},... | collective-permute-start | bytes 24584 | tf_op jit(solution)/shard_map/ppermute | solution.py:200
  27.6 2.5 %collective-permute-start.9 = (f32[16,128]{1,0:T(8,128)S(1)}, f32[16,128]{1,0:T(8,128)S(1)}, u32[]{:S(2)}, u32[]{:S(2)}) collective-permute-start(f32[16,128]{1,0:T(8,128)S(1)} %get-tuple-element.9.refs_0_), channel_id=1, source_target_pairs={{0,4},{1,5},{2,6},{3,7},{4,0},{5,1},{6,2},{7,3},{8,12},{9,13},{10,... | collective-permute-start | bytes 24584 | tf_op jit(solution)/shard_map/ppermute | solution.py:200
  30.1 1.1 %collective-permute-done.11.refs_3_ = f32[16,128]{1,0:T(8,128)S(1)} collective-permute-done((f32[16,128]{1,0:T(8,128)S(1)}, f32[16,128]{1,0:T(8,128)S(1)}, u32[]{:S(2)}, u32[]{:S(2)}) %collective-permute-start.11) | collective-permute-done | bytes 8224 | tf_op jit(solution)/shard_map/ppermute | solution.py:200
  31.1 1.0 %collective-permute-done.10.refs_2_ = f32[16,128]{1,0:T(8,128)S(1)} collective-permute-done((f32[16,128]{1,0:T(8,128)S(1)}, f32[16,128]{1,0:T(8,128)S(1)}, u32[]{:S(2)}, u32[]{:S(2)}) %collective-permute-start.10) | collective-permute-done | bytes 8224 | tf_op jit(solution)/shard_map/ppermute | solution.py:200
  32.2 0.8 %update.1 = (f32[4,256]{1,0:T(4,128)}, f32[4,256]{1,0:T(4,128)}, f32[4,256]{1,0:T(4,128)}) custom-call(f32[16,128]{1,0:T(8,128)S(1)} %get-tuple-element.9.refs_0_, f32[16,128]{1,0:T(8,128)S(1)} %collective-permute-done.9.refs_1_, f32[16,128]{1,0:T(8,128)S(1)} %collective-permute-done.10.refs_2_, f32[16,128]{1,0:T(8,128)S(1)} %collective-permute-done.11.refs_3_, ...), custom_call_target="tpu_custom_call" | custom-call | tf_op jit(solution)/shard_map/update/pallas_call | solution.py:257
  (18 shorter events, 0.0 us)
Async XLA Ops:
  0.6 0.8 %copy-start = (bf16[256,128]{1,0:T(8,128)(2,1)S(1)}, bf16[256,128]{1,0:T(8,128)(2,1)}, u32[]{:S(2)}) copy-start(bf16[256,128]{1,0:T(8,128)(2,1)} %points.1) | copy-start | bytes 196612
  1.5 0.7 %copy-start.1 = (f32[4,256]{1,0:T(4,128)S(1)}, f32[4,256]{1,0:T(4,128)}, u32[]{:S(2)}) copy-start(f32[4,256]{1,0:T(4,128)} %refs_7_.1) | copy-start | bytes 12292
  2.2 0.7 %copy-start.3 = (f32[4,256]{1,0:T(4,128)S(1)}, f32[4,256]{1,0:T(4,128)}, u32[]{:S(2)}) copy-start(f32[4,256]{1,0:T(4,128)} %refs_6_.1) | copy-start | bytes 12292
  3.1 13.3 %copy-start.6 = (f32[4]{0:T(128)S(1)}, f32[4]{0:T(128)}, u32[]{:S(2)}) copy-start(f32[4]{0:T(128)} %refs_8_.2) | copy-start | bytes 52
  3.1 7.5 %collective-permute-start.5 = (bf16[272,128]{1,0:T(8,128)(2,1)S(1)}, bf16[272,128]{1,0:T(8,128)(2,1)S(1)}, u32[]{:S(2)}, u32[]{:S(2)}) collective-permute-start(bf16[272,128]{1,0:T(8,128)(2,1)S(1)} %get-tuple-element.8.refs_4_), channel_id=1, source_target_pairs={{0,12},{1,13},{2,14},{3,15},{4,8},{5,9},{6,10},{7,11},{8,4},{9,5},... | collective-permute-start | bytes 208904 | tf_op jit(solution)/shard_map/ppermute | solution.py:200
  8.2 16.9 %copy-start.5 = (f32[4]{0:T(128)S(1)}, f32[4]{0:T(128)}, u32[]{:S(2)}) copy-start(f32[4]{0:T(128)} %refs_8_.3) | copy-start | bytes 52
  8.2 8.1 %collective-permute-start.2 = (bf16[304,128]{1,0:T(8,128)(2,1)S(1)}, bf16[304,128]{1,0:T(8,128)(2,1)S(1)}, u32[]{:S(2)}, u32[]{:S(2)}) collective-permute-start(bf16[304,128]{1,0:T(8,128)(2,1)S(1)} %get-tuple-element.7.refs_0_.refs_4_), channel_id=1, source_target_pairs={{0,3},{1,2},{2,1},{3,0},{4,7},{5,6},{6,5},{7,4},{8,11},{9,10},{10,... | collective-permute-start | bytes 233480 | tf_op jit(solution)/shard_map/ppermute | solution.py:186
  8.9 7.4 %collective-permute-start.1 = (bf16[304,128]{1,0:T(8,128)(2,1)S(1)}, bf16[304,128]{1,0:T(8,128)(2,1)S(1)}, u32[]{:S(2)}, u32[]{:S(2)}) collective-permute-start(bf16[304,128]{1,0:T(8,128)(2,1)S(1)} %get-tuple-element.7.refs_0_.refs_4_), channel_id=1, source_target_pairs={{0,2},{1,3},{2,0},{3,1},{4,6},{5,7},{6,4},{7,5},{8,10},{9,11},{10,... | collective-permute-start | bytes 233480 | tf_op jit(solution)/shard_map/ppermute | solution.py:186
  9.7 6.6 %collective-permute-start = (bf16[304,128]{1,0:T(8,128)(2,1)S(1)}, bf16[304,128]{1,0:T(8,128)(2,1)S(1)}, u32[]{:S(2)}, u32[]{:S(2)}) collective-permute-start(bf16[304,128]{1,0:T(8,128)(2,1)S(1)} %get-tuple-element.7.refs_0_.refs_4_), channel_id=1, source_target_pairs={{0,1},{1,0},{2,3},{3,2},{4,5},{5,4},{6,7},{7,6},{8,9},{9,8},{10,11... | collective-permute-start | bytes 233480 | tf_op jit(solution)/shard_map/ppermute | solution.py:186
  10.0 5.8 %collective-permute-start.4 = (bf16[272,128]{1,0:T(8,128)(2,1)S(1)}, bf16[272,128]{1,0:T(8,128)(2,1)S(1)}, u32[]{:S(2)}, u32[]{:S(2)}) collective-permute-start(bf16[272,128]{1,0:T(8,128)(2,1)S(1)} %get-tuple-element.8.refs_4_), channel_id=1, source_target_pairs={{0,8},{1,9},{2,10},{3,11},{4,12},{5,13},{6,14},{7,15},{8,0},{9,1},... | collective-permute-start | bytes 208904 | tf_op jit(solution)/shard_map/ppermute | solution.py:200
  10.5 5.8 %collective-permute-start.3 = (bf16[272,128]{1,0:T(8,128)(2,1)S(1)}, bf16[272,128]{1,0:T(8,128)(2,1)S(1)}, u32[]{:S(2)}, u32[]{:S(2)}) collective-permute-start(bf16[272,128]{1,0:T(8,128)(2,1)S(1)} %get-tuple-element.8.refs_4_), channel_id=1, source_target_pairs={{0,4},{1,5},{2,6},{3,7},{4,0},{5,1},{6,2},{7,3},{8,12},{9,13},{10,... | collective-permute-start | bytes 208904 | tf_op jit(solution)/shard_map/ppermute | solution.py:200
  20.8 3.2 %collective-permute-start.8 = (f32[32,128]{1,0:T(8,128)S(1)}, f32[32,128]{1,0:T(8,128)S(1)}, u32[]{:S(2)}, u32[]{:S(2)}) collective-permute-start(f32[32,128]{1,0:T(8,128)S(1)} %product.1.refs_0_), channel_id=1, source_target_pairs={{0,3},{1,2},{2,1},{3,0},{4,7},{5,6},{6,5},{7,4},{8,11},{9,10},{10,... | collective-permute-start | bytes 49160 | tf_op jit(solution)/shard_map/ppermute | solution.py:186
  21.3 3.7 %collective-permute-start.7 = (f32[32,128]{1,0:T(8,128)S(1)}, f32[32,128]{1,0:T(8,128)S(1)}, u32[]{:S(2)}, u32[]{:S(2)}) collective-permute-start(f32[32,128]{1,0:T(8,128)S(1)} %product.1.refs_0_), channel_id=1, source_target_pairs={{0,2},{1,3},{2,0},{3,1},{4,6},{5,7},{6,4},{7,5},{8,10},{9,11},{10,... | collective-permute-start | bytes 49160 | tf_op jit(solution)/shard_map/ppermute | solution.py:186
  22.6 2.5 %collective-permute-start.6 = (f32[32,128]{1,0:T(8,128)S(1)}, f32[32,128]{1,0:T(8,128)S(1)}, u32[]{:S(2)}, u32[]{:S(2)}) collective-permute-start(f32[32,128]{1,0:T(8,128)S(1)} %product.1.refs_0_), channel_id=1, source_target_pairs={{0,1},{1,0},{2,3},{3,2},{4,5},{5,4},{6,7},{7,6},{8,9},{9,8},{10,11... | collective-permute-start | bytes 49160 | tf_op jit(solution)/shard_map/ppermute | solution.py:186
  25.0 7.1 %copy-start.2 = (f32[4,256]{1,0:T(4,128)S(1)}, f32[4,256]{1,0:T(4,128)}, u32[]{:S(2)}) copy-start(f32[4,256]{1,0:T(4,128)} %refs_7_.1) | copy-start | bytes 12292
  25.0 7.1 %copy-start.4 = (f32[4,256]{1,0:T(4,128)S(1)}, f32[4,256]{1,0:T(4,128)}, u32[]{:S(2)}) copy-start(f32[4,256]{1,0:T(4,128)} %refs_5_.1) | copy-start | bytes 12292
  25.6 5.5 %collective-permute-start.11 = (f32[16,128]{1,0:T(8,128)S(1)}, f32[16,128]{1,0:T(8,128)S(1)}, u32[]{:S(2)}, u32[]{:S(2)}) collective-permute-start(f32[16,128]{1,0:T(8,128)S(1)} %get-tuple-element.9.refs_0_), channel_id=1, source_target_pairs={{0,12},{1,13},{2,14},{3,15},{4,8},{5,9},{6,10},{7,11},{8,4},{9,5},... | collective-permute-start | bytes 24584 | tf_op jit(solution)/shard_map/ppermute | solution.py:200
  27.6 4.5 %collective-permute-start.10 = (f32[16,128]{1,0:T(8,128)S(1)}, f32[16,128]{1,0:T(8,128)S(1)}, u32[]{:S(2)}, u32[]{:S(2)}) collective-permute-start(f32[16,128]{1,0:T(8,128)S(1)} %get-tuple-element.9.refs_0_), channel_id=1, source_target_pairs={{0,8},{1,9},{2,10},{3,11},{4,12},{5,13},{6,14},{7,15},{8,0},{9,1},... | collective-permute-start | bytes 24584 | tf_op jit(solution)/shard_map/ppermute | solution.py:200
  27.6 4.5 %collective-permute-start.9 = (f32[16,128]{1,0:T(8,128)S(1)}, f32[16,128]{1,0:T(8,128)S(1)}, u32[]{:S(2)}, u32[]{:S(2)}) collective-permute-start(f32[16,128]{1,0:T(8,128)S(1)} %get-tuple-element.9.refs_0_), channel_id=1, source_target_pairs={{0,4},{1,5},{2,6},{3,7},{4,0},{5,1},{6,2},{7,3},{8,12},{9,13},{10,... | collective-permute-start | bytes 24584 | tf_op jit(solution)/shard_map/ppermute | solution.py:200

commit v5 on v4

--- a/solution.py
+++ b/solution.py
@@ -14,10 +14,6 @@
 def split_sizes(devices):
     lo = max(d for d in range(1, math.isqrt(devices) + 1) if devices % d == 0)
     return devices // lo, lo
-
-
-def peer(index, step, count):
-    return index ^ step if count & (count - 1) == 0 else (step - index) % count
 
 
 def pieces_of(wide):
@@ -90,42 +86,53 @@
 def product_kernel(lo, hi, *refs):
     rows, refs = refs[:lo], refs[lo:]
     cols, refs = refs[:hi], refs[hi:]
-    length, out, row_wide = refs
+    length, out, row_wide, weights, dist = refs
     cands = length.shape[0]
     dims = rows[0].shape[1]
     tall = out.shape[0] // lo
     size = tall * dims // cands
-    for k in range(lo):
-        row_wide[pl.ds(k * size, size), :] = widen(rows[k][:size, :], 1.0, True)
+    chunk = 32
     rates = [
         (-0.5 * LOG2E) / (length[c] * length[c]) for c in range(cands)
     ]
-    total = [None] * lo
+    for k in range(lo):
+        row_wide[pl.ds(k * size, size), :] = widen(rows[k][:size, :], 1.0, True)
+    total = [[jnp.zeros((8, size), jnp.float32)] * cands for _ in range(lo)]
     for h in range(hi):
-        col_wide = widen(cols[h][:size, :], -2.0, False)
         tail = cols[h][size:, :].astype(jnp.float32)
-        low = unfold(tail[:tall], cands)
-        which = lax.broadcasted_iota(jnp.int32, low.shape, 0)
-        only = [
-            jnp.where(which == c, low, 0.0).astype(jnp.bfloat16) for c in range(cands)
-        ]
+        step = unfold(tail[:tall], cands)
+        step = jnp.concatenate([step, jnp.zeros((8 - cands, size), jnp.float32)]).T
+        for c in range(cands):
+            weights[c] = jnp.broadcast_to(step[:, c : c + 1], (size, dims))
+        dist[...] = lax.dot_general(
+            widen(cols[h][:size, :], -2.0, False),
+            row_wide[...],
+            (((1,), (1,)), ((), ())),
+            preferred_element_type=jnp.float32,
+        )
         for k in range(lo):
-            dist = lax.dot_general(
-                col_wide,
-                row_wide[pl.ds(k * size, size), :],
-                (((1,), (1,)), ((), ())),
-                preferred_element_type=jnp.float32,
-            )
-            for c in range(cands):
-                kern = jnp.exp2(dist * rates[c]).astype(jnp.bfloat16)
-                part = jnp.dot(only[c], kern, preferred_element_type=jnp.float32)
-                total[k] = part if total[k] is None else total[k] + part
+            for j in range(0, size, chunk):
+                here = dist[pl.ds(j, chunk), pl.ds(k * size, size)]
+                for c in range(cands):
+                    weight = weights[c, pl.ds(j, chunk), :]
+                    weight = jnp.concatenate([weight] * (size // dims), axis=1)
+                    kern = jnp.exp2(here * rates[c]) * weight
+                    total[k][c] = total[k][c] + jnp.sum(
+                        kern.reshape(chunk // 8, 8, size), axis=0
+                    )
     for k in range(lo):
-        out[pl.ds(k * tall, tall), :] = fold(total[k], dims)
+        part = [jnp.sum(total[k][c], axis=0, keepdims=True) for c in range(cands)]
+        out[pl.ds(k * tall, tall), :] = fold(jnp.concatenate(part, axis=0), dims)
+
+
+def add_kernel(step, tall, mine, other, out):
+    for k in range(mine.shape[0] // tall):
+        at = pl.ds(k * tall, tall)
+        out[at, :] = mine[at, :] + other[pl.ds((k ^ step) * tall, tall), :]
 
 
 def sums_kernel(lo, *refs):
-    parts, refs = refs[:lo], refs[lo:]
+    parts, refs = refs[:2], refs[2:]
     rows, refs = refs[:lo], refs[lo:]
     noise, image_out, sums_out = refs
     cands = noise.shape[0]
@@ -142,8 +149,8 @@
         step = tail[0] + tail[1] + tail[2]
         rest = tail[3] + tail[4] + tail[5]
         image = sigma * step
-        for m in range(lo):
-            image += parts[m][pl.ds(peer(m, k, lo) * tall, tall), :]
+        image += parts[0][pl.ds(k * tall, tall), :]
+        image += parts[1][pl.ds((k ^ (lo // 2)) * tall, tall), :]
         if k == 0:
             image_out[...] = image
         terms = (rest * rest, step * image, rest * image, image * image)
@@ -154,13 +161,11 @@
         )
 
 
-def update_kernel(hi, *refs):
-    sums, refs = refs[:hi], refs[hi:]
+def update_kernel(*refs):
+    sums, refs = refs[:2], refs[2:]
     image, solution, residual, direction, out_s, out_r, out_d = refs
     cands = solution.shape[0]
-    total = sums[0][...]
-    for h in range(1, hi):
-        total = total + sums[h][...]
+    total = sums[0][...] + sums[1][...]
     total = jnp.sum(total, axis=1, keepdims=True)
     norm, curve, cross, square = (
         total[i * cands : (i + 1) * cands] for i in range(4)
@@ -177,37 +182,36 @@
 
 def per_device(devices, points, lengthscale, noise, solution, residual, direction):
     hi, lo = split_sizes(devices)
+    assert hi & (hi - 1) == lo & (lo - 1) == 0
     size, dims = points.shape
     cands = direction.shape[0]
     tall = cands * size // dims
 
-    def row_peers(x):
-        return [x] + [
-            lax.ppermute(
-                x,
-                "blk",
-                [
-                    (h * lo + l, h * lo + peer(l, k, lo))
-                    for h in range(hi)
-                    for l in range(lo)
-                ],
-            )
-            for k in range(1, lo)
+    def from_row(x, k):
+        pairs = [
+            (h * lo + l, h * lo + (l ^ k)) for h in range(hi) for l in range(lo)
         ]
-
-    def col_peers(x):
-        return [x] + [
-            lax.ppermute(
-                x,
-                "blk",
-                [
-                    (h * lo + l, peer(h, k, hi) * lo + l)
-                    for h in range(hi)
-                    for l in range(lo)
-                ],
-            )
-            for k in range(1, hi)
+        return lax.ppermute(x, "blk", pairs)
+
+    def from_col(x, k):
+        pairs = [
+            (h * lo + l, (h ^ k) * lo + l) for h in range(hi) for l in range(lo)
         ]
+        return lax.ppermute(x, "blk", pairs)
+
+    def butterfly(x, fetch, count, tall, swaps):
+        k = 1
+        while 2 * k < count:
+            x = pl.pallas_call(
+                functools.partial(add_kernel, k if swaps else 0, tall),
+                out_shape=jax.ShapeDtypeStruct(x.shape, x.dtype),
+                in_specs=[vmem, vmem],
+                out_specs=vmem,
+                compiler_params=params,
+                name="add",
+            )(x, fetch(x, k))
+            k *= 2
+        return x, fetch(x, k)
 
     vmem = pl.BlockSpec(memory_space=pltpu.VMEM)
     smem = pl.BlockSpec(memory_space=pltpu.SMEM)
@@ -219,7 +223,7 @@
             jax.ShapeDtypeStruct((size + 2 * tall, dims), jnp.bfloat16),
             jax.ShapeDtypeStruct((size + 6 * tall, dims), jnp.bfloat16),
         ),
-        in_specs=[pl.BlockSpec(memory_space=pl.ANY)] * 3,
+        in_specs=[pl.BlockSpec(memory_space=pltpu.HBM)] * 3,
         out_specs=(vmem, vmem),
         scratch_shapes=[
             pltpu.VMEM((cands, size), jnp.float32),
@@ -228,16 +232,20 @@
         ],
         compiler_params=params,
         name="pack",
-    )(points, direction, residual)
-    cols = col_peers(to_col)
-    rows = row_peers(to_row)
+    )(*(pltpu.with_memory_space_constraint(x, pltpu.HBM) for x in (points, direction, residual)))
+    cols = [to_col] + [from_col(to_col, k) for k in range(1, hi)]
+    rows = [to_row] + [from_row(to_row, k) for k in range(1, lo)]
 
     partial = pl.pallas_call(
         functools.partial(product_kernel, lo, hi),
         out_shape=jax.ShapeDtypeStruct((lo * tall, dims), jnp.float32),
         in_specs=[vmem] * (lo + hi) + [smem],
         out_specs=vmem,
-        scratch_shapes=[pltpu.VMEM((lo * size, 2 * dims), jnp.bfloat16)],
+        scratch_shapes=[
+            pltpu.VMEM((lo * size, 2 * dims), jnp.bfloat16),
+            pltpu.VMEM((cands, size, dims), jnp.float32),
+            pltpu.VMEM((size, lo * size), jnp.float32),
+        ],
         compiler_params=params,
         name="product",
     )(*rows, *cols, lengthscale)
@@ -248,20 +256,20 @@
             jax.ShapeDtypeStruct((tall, dims), jnp.float32),
             jax.ShapeDtypeStruct((4 * cands, dims), jnp.float32),
         ),
-        in_specs=[vmem] * (2 * lo) + [smem],
+        in_specs=[vmem] * (2 + lo) + [smem],
         out_specs=(vmem, vmem),
         compiler_params=params,
         name="sums",
-    )(*row_peers(partial), *rows, noise)
+    )(*butterfly(partial, from_row, lo, tall, True), *rows, noise)
 
     return pl.pallas_call(
-        functools.partial(update_kernel, hi),
+        update_kernel,
         out_shape=(jax.ShapeDtypeStruct((cands, size), jnp.float32),) * 3,
-        in_specs=[vmem] * (hi + 4),
+        in_specs=[vmem] * 6,
         out_specs=(vmem,) * 3,
         compiler_params=params,
         name="update",
-    )(*col_peers(sums), image, solution, residual, direction)
+    )(*butterfly(sums, from_col, hi, 4 * cands, False), image, solution, residual, direction)
 
 
 def solution(mesh):

time: 33.2 us -> 33.5 us (level)
  waiting for transfers between devices: 9.51 us -> 15.5 us
  starting transfers between devices: 14.5 us -> 11 us
  local copies, waits for them, and re-layouts: 2.23 us -> 0.02 us
    ppermute x12 -> x10, waiting for transfers between devices: 9.51 us -> 15.5 us  [the longest x5 12.3 us: from_col(): return lax.ppermute(x, 'blk', pairs)]
    ppermute x12 -> x10, starting transfers between devices: 14.5 us -> 11 us  [the longest x5 7.38 us: from_col(): return lax.ppermute(x, 'blk', pairs)]
    unnamed x14 -> x10, local copies, waits for them, and re-layouts: 2.23 us -> 0.02 us
    pallas_call x1, Pallas kernels: 0.2 us -> 0.95 us  [per_device(): pl.pallas_call(pack_kernel, out_shape=(jax.ShapeDtypeStruct((size + 2 * t...]
    pallas_call x1, Pallas kernels: 4.49 us -> 3.77 us  [per_device(): pl.pallas_call(functools.partial(product_kernel, lo, hi), out_shape=jax.S...]
    pallas_call x1 -> x3, Pallas kernels: 0.78 us -> 0.79 us  [the longest x1 0.78 us: per_device(): pl.pallas_call(update_kernel, out_shape=(jax.ShapeDtypeStruct((cands, siz...]
  transfers between devices with their start and end apart: 12 -> 10, of which waited for: 7 -> 7; matrix products, arithmetic and copies ran while one was open for 0% -> 0% of each run, Pallas kernels for 0% -> 0%
where the time goes in v5:
time: 33.5 us; the launch traced here: 33.3 us
  waiting for transfers between devices  15.5 us (46%)
  starting transfers between devices  11 us (33%)
  Pallas kernels  6.07 us (18%)
  between operations  0.71 us (2%)
    ppermute x5, waiting for transfers between devices, from_col(): return lax.ppermute(x, 'blk', pairs)  12.3 us
    ppermute x5, starting transfers between devices, from_col(): return lax.ppermute(x, 'blk', pairs)  7.38 us
    pallas_call x1, Pallas kernels, per_device(): pl.pallas_call(functools.partial(product_kernel, lo, hi), out_shape=jax.S...  3.77 us
    ppermute x5, starting transfers between devices, from_row(): return lax.ppermute(x, 'blk', pairs)  3.63 us
    ppermute x5, waiting for transfers between devices, from_row(): return lax.ppermute(x, 'blk', pairs)  3.22 us
    pallas_call x1, Pallas kernels, per_device(): pl.pallas_call(pack_kernel, out_shape=(jax.ShapeDtypeStruct((size + 2 * t...  0.95 us
    pallas_call x1, Pallas kernels, per_device(): pl.pallas_call(update_kernel, out_shape=(jax.ShapeDtypeStruct((cands, siz...  0.78 us
  transfers between devices with their start and end apart: 10, of which 7 were waited for; matrix products, arithmetic and copies ran while one was open for 0% of the time, Pallas kernels for 0%

profile of v5, /device:TPU:0, one launch (start us, length us, event | category | flops | bytes accessed | tf_op | source)
XLA Modules:
  0.0 33.3 jit_solution(2668866000124621415)
XLA Ops:
  0.6 1.0 %pack.1 = (bf16[272,128]{1,0:T(8,128)(2,1)S(1)}, bf16[304,128]{1,0:T(8,128)(2,1)S(1)}) custom-call(bf16[256,128]{1,0:T(8,128)(2,1)} %points.1, f32[4,256]{1,0:T(4,128)} %refs_5_.1, f32[4,256]{1,0:T(4,128)} %refs_4_.1), custom_call_target="tpu_custom_call" | custom-call | tf_op jit(solution)/shard_map/pack/pallas_call | solution.py:220
  1.6 0.0 copy-start.4
  1.6 5.1 %collective-permute-start.5 = (bf16[272,128]{1,0:T(8,128)(2,1)S(1)}, bf16[272,128]{1,0:T(8,128)(2,1)S(1)}, u32[]{:S(2)}, u32[]{:S(2)}) collective-permute-start(bf16[272,128]{1,0:T(8,128)(2,1)S(1)} %get-tuple-element.8.refs_4_), channel_id=1, source_target_pairs={{0,12},{1,13},{2,14},{3,15},{4,8},{5,9},{6,10},{7,11},{8,4},{9,5},... | collective-permute-start | bytes 208904 | tf_op jit(solution)/shard_map/ppermute | solution.py:200
  6.7 0.7 %collective-permute-start.2 = (bf16[304,128]{1,0:T(8,128)(2,1)S(1)}, bf16[304,128]{1,0:T(8,128)(2,1)S(1)}, u32[]{:S(2)}, u32[]{:S(2)}) collective-permute-start(bf16[304,128]{1,0:T(8,128)(2,1)S(1)} %get-tuple-element.7.refs_0_.refs_2_), channel_id=1, source_target_pairs={{0,3},{1,2},{2,1},{3,0},{4,7},{5,6},{6,5},{7,4},{8,11},{9,10},{10,... | collective-permute-start | bytes 233480 | tf_op jit(solution)/shard_map/ppermute | solution.py:194
  7.4 0.9 %collective-permute-start.1 = (bf16[304,128]{1,0:T(8,128)(2,1)S(1)}, bf16[304,128]{1,0:T(8,128)(2,1)S(1)}, u32[]{:S(2)}, u32[]{:S(2)}) collective-permute-start(bf16[304,128]{1,0:T(8,128)(2,1)S(1)} %get-tuple-element.7.refs_0_.refs_2_), channel_id=1, source_target_pairs={{0,2},{1,3},{2,0},{3,1},{4,6},{5,7},{6,4},{7,5},{8,10},{9,11},{10,... | collective-permute-start | bytes 233480 | tf_op jit(solution)/shard_map/ppermute | solution.py:194
  8.3 0.3 collective-permute-start
  8.6 0.0 collective-permute-start.4
  8.6 0.5 %collective-permute-done.5.refs_7_ = bf16[272,128]{1,0:T(8,128)(2,1)S(1)} collective-permute-done((bf16[272,128]{1,0:T(8,128)(2,1)S(1)}, bf16[272,128]{1,0:T(8,128)(2,1)S(1)}, u32[]{:S(2)}, u32[]{:S(2)}) %collective-permute-start.5) | collective-permute-done | bytes 69664 | tf_op jit(solution)/shard_map/ppermute | solution.py:200
  9.1 1.1 %collective-permute-start.3 = (bf16[272,128]{1,0:T(8,128)(2,1)S(1)}, bf16[272,128]{1,0:T(8,128)(2,1)S(1)}, u32[]{:S(2)}, u32[]{:S(2)}) collective-permute-start(bf16[272,128]{1,0:T(8,128)(2,1)S(1)} %get-tuple-element.8.refs_4_), channel_id=1, source_target_pairs={{0,4},{1,5},{2,6},{3,7},{4,0},{5,1},{6,2},{7,3},{8,12},{9,13},{10,... | collective-permute-start | bytes 208904 | tf_op jit(solution)/shard_map/ppermute | solution.py:200
  10.2 4.2 %collective-permute-done.4.refs_6_ = bf16[272,128]{1,0:T(8,128)(2,1)S(1)} collective-permute-done((bf16[272,128]{1,0:T(8,128)(2,1)S(1)}, bf16[272,128]{1,0:T(8,128)(2,1)S(1)}, u32[]{:S(2)}, u32[]{:S(2)}) %collective-permute-start.4) | collective-permute-done | bytes 69664 | tf_op jit(solution)/shard_map/ppermute | solution.py:200
  14.4 0.5 %collective-permute-done.3.refs_5_ = bf16[272,128]{1,0:T(8,128)(2,1)S(1)} collective-permute-done((bf16[272,128]{1,0:T(8,128)(2,1)S(1)}, bf16[272,128]{1,0:T(8,128)(2,1)S(1)}, u32[]{:S(2)}, u32[]{:S(2)}) %collective-permute-start.3) | collective-permute-done | bytes 69664 | tf_op jit(solution)/shard_map/ppermute | solution.py:200
  14.8 0.0 collective-permute-done.2.refs_3_.refs_5_
  14.9 3.8 %product.1.mine = f32[32,128]{1,0:T(8,128)S(1)} custom-call(bf16[304,128]{1,0:T(8,128)(2,1)S(1)} %get-tuple-element.7.refs_0_.refs_2_, bf16[304,128]{1,0:T(8,128)(2,1)S(1)} %collective-permute-done.refs_1_.refs_3_, bf16[304,128]{1,0:T(8,128)(2,1)S(1)} %collective-permute-done.1.refs_2_.refs_4_, bf16[304,128]{1,0:T(8,128)(2,1)S(1)} %collective-permute-done.2.refs_3_.refs_5_, ...), custom_call_target="tpu_custom_call" | custom-call | tf_op jit(solution)/shard_map/product/pallas_call | solution.py:239
  18.6 0.0 copy-start.3
  18.6 0.1 collective-permute-start.6
  18.7 1.2 %collective-permute-done.6.other = f32[32,128]{1,0:T(8,128)S(1)} collective-permute-done((f32[32,128]{1,0:T(8,128)S(1)}, f32[32,128]{1,0:T(8,128)S(1)}, u32[]{:S(2)}, u32[]{:S(2)}) %collective-permute-start.6) | collective-permute-done | bytes 16416 | tf_op jit(solution)/shard_map/ppermute | solution.py:194
  19.9 1.7 %collective-permute-start.7 = (f32[32,128]{1,0:T(8,128)S(1)}, f32[32,128]{1,0:T(8,128)S(1)}, u32[]{:S(2)}, u32[]{:S(2)}) collective-permute-start(f32[32,128]{1,0:T(8,128)S(1)} %add.2.refs_0_), channel_id=1, source_target_pairs={{0,2},{1,3},{2,0},{3,1},{4,6},{5,7},{6,4},{7,5},{8,10},{9,11},{10,... | collective-permute-start | bytes 49160 | tf_op jit(solution)/shard_map/ppermute | solution.py:194
  21.6 2.0 %collective-permute-done.7.refs_1_ = f32[32,128]{1,0:T(8,128)S(1)} collective-permute-done((f32[32,128]{1,0:T(8,128)S(1)}, f32[32,128]{1,0:T(8,128)S(1)}, u32[]{:S(2)}, u32[]{:S(2)}) %collective-permute-start.7) | collective-permute-done | bytes 16416 | tf_op jit(solution)/shard_map/ppermute | solution.py:194
  23.6 0.6 %sums.1 = (f32[8,128]{1,0:T(8,128)S(1)}, f32[16,128]{1,0:T(8,128)S(1)}) custom-call(f32[32,128]{1,0:T(8,128)S(1)} %add.2.refs_0_, f32[32,128]{1,0:T(8,128)S(1)} %collective-permute-done.7.refs_1_, bf16[304,128]{1,0:T(8,128)(2,1)S(1)} %get-tuple-element.7.refs_0_.refs_2_, bf16[304,128]{1,0:T(8,128)(2,1)S(1)} %collective-permute-done.refs_1_.refs_3_, ...), custom_call_target="tpu_custom_call" | custom-call | tf_op jit(solution)/shard_map/sums/pallas_call | solution.py:253
  24.2 0.1 collective-permute-start.8
  24.3 3.6 %collective-permute-done.8.other = f32[16,128]{1,0:T(8,128)S(1)} collective-permute-done((f32[16,128]{1,0:T(8,128)S(1)}, f32[16,128]{1,0:T(8,128)S(1)}, u32[]{:S(2)}, u32[]{:S(2)}) %collective-permute-start.8) | collective-permute-done | bytes 8224 | tf_op jit(solution)/shard_map/ppermute | solution.py:200
  27.9 1.1 %collective-permute-start.9 = (f32[16,128]{1,0:T(8,128)S(1)}, f32[16,128]{1,0:T(8,128)S(1)}, u32[]{:S(2)}, u32[]{:S(2)}) collective-permute-start(f32[16,128]{1,0:T(8,128)S(1)} %add.3.refs_0_), channel_id=1, source_target_pairs={{0,8},{1,9},{2,10},{3,11},{4,12},{5,13},{6,14},{7,15},{8,0},{9,1},... | collective-permute-start | bytes 24584 | tf_op jit(solution)/shard_map/ppermute | solution.py:200
  29.0 3.6 %collective-permute-done.9.refs_1_ = f32[16,128]{1,0:T(8,128)S(1)} collective-permute-done((f32[16,128]{1,0:T(8,128)S(1)}, f32[16,128]{1,0:T(8,128)S(1)}, u32[]{:S(2)}, u32[]{:S(2)}) %collective-permute-start.9) | collective-permute-done | bytes 8224 | tf_op jit(solution)/shard_map/ppermute | solution.py:200
  32.6 0.8 %update.1 = (f32[4,256]{1,0:T(4,128)}, f32[4,256]{1,0:T(4,128)}, f32[4,256]{1,0:T(4,128)}) custom-call(f32[16,128]{1,0:T(8,128)S(1)} %add.3.refs_0_, f32[16,128]{1,0:T(8,128)S(1)} %collective-permute-done.9.refs_1_, f32[8,128]{1,0:T(8,128)S(1)} %get-tuple-element.10.refs_2_, f32[4,256]{1,0:T(4,128)S(1)} %copy-done.2, f32[4,256]{1,0:T(4,128)S(1)} %copy-done.1, ...), custom_call_target="tpu_custom_call" | custom-call | tf_op jit(solution)/shard_map/update/pallas_call | solution.py:265
  (12 shorter events, 0.0 us)
Async XLA Ops:
  1.6 13.3 %copy-start.4 = (f32[4]{0:T(128)S(1)}, f32[4]{0:T(128)}, u32[]{:S(2)}) copy-start(f32[4]{0:T(128)} %refs_8_.1) | copy-start | bytes 52
  1.6 7.5 %collective-permute-start.5 = (bf16[272,128]{1,0:T(8,128)(2,1)S(1)}, bf16[272,128]{1,0:T(8,128)(2,1)S(1)}, u32[]{:S(2)}, u32[]{:S(2)}) collective-permute-start(bf16[272,128]{1,0:T(8,128)(2,1)S(1)} %get-tuple-element.8.refs_4_), channel_id=1, source_target_pairs={{0,12},{1,13},{2,14},{3,15},{4,8},{5,9},{6,10},{7,11},{8,4},{9,5},... | collective-permute-start | bytes 208904 | tf_op jit(solution)/shard_map/ppermute | solution.py:200
  6.7 8.1 %collective-permute-start.2 = (bf16[304,128]{1,0:T(8,128)(2,1)S(1)}, bf16[304,128]{1,0:T(8,128)(2,1)S(1)}, u32[]{:S(2)}, u32[]{:S(2)}) collective-permute-start(bf16[304,128]{1,0:T(8,128)(2,1)S(1)} %get-tuple-element.7.refs_0_.refs_2_), channel_id=1, source_target_pairs={{0,3},{1,2},{2,1},{3,0},{4,7},{5,6},{6,5},{7,4},{8,11},{9,10},{10,... | collective-permute-start | bytes 233480 | tf_op jit(solution)/shard_map/ppermute | solution.py:194
  7.4 7.4 %collective-permute-start.1 = (bf16[304,128]{1,0:T(8,128)(2,1)S(1)}, bf16[304,128]{1,0:T(8,128)(2,1)S(1)}, u32[]{:S(2)}, u32[]{:S(2)}) collective-permute-start(bf16[304,128]{1,0:T(8,128)(2,1)S(1)} %get-tuple-element.7.refs_0_.refs_2_), channel_id=1, source_target_pairs={{0,2},{1,3},{2,0},{3,1},{4,6},{5,7},{6,4},{7,5},{8,10},{9,11},{10,... | collective-permute-start | bytes 233480 | tf_op jit(solution)/shard_map/ppermute | solution.py:194
  8.3 6.6 %collective-permute-start = (bf16[304,128]{1,0:T(8,128)(2,1)S(1)}, bf16[304,128]{1,0:T(8,128)(2,1)S(1)}, u32[]{:S(2)}, u32[]{:S(2)}) collective-permute-start(bf16[304,128]{1,0:T(8,128)(2,1)S(1)} %get-tuple-element.7.refs_0_.refs_2_), channel_id=1, source_target_pairs={{0,1},{1,0},{2,3},{3,2},{4,5},{5,4},{6,7},{7,6},{8,9},{9,8},{10,11... | collective-permute-start | bytes 233480 | tf_op jit(solution)/shard_map/ppermute | solution.py:194
  8.6 5.8 %collective-permute-start.4 = (bf16[272,128]{1,0:T(8,128)(2,1)S(1)}, bf16[272,128]{1,0:T(8,128)(2,1)S(1)}, u32[]{:S(2)}, u32[]{:S(2)}) collective-permute-start(bf16[272,128]{1,0:T(8,128)(2,1)S(1)} %get-tuple-element.8.refs_4_), channel_id=1, source_target_pairs={{0,8},{1,9},{2,10},{3,11},{4,12},{5,13},{6,14},{7,15},{8,0},{9,1},... | collective-permute-start | bytes 208904 | tf_op jit(solution)/shard_map/ppermute | solution.py:200
  9.1 5.8 %collective-permute-start.3 = (bf16[272,128]{1,0:T(8,128)(2,1)S(1)}, bf16[272,128]{1,0:T(8,128)(2,1)S(1)}, u32[]{:S(2)}, u32[]{:S(2)}) collective-permute-start(bf16[272,128]{1,0:T(8,128)(2,1)S(1)} %get-tuple-element.8.refs_4_), channel_id=1, source_target_pairs={{0,4},{1,5},{2,6},{3,7},{4,0},{5,1},{6,2},{7,3},{8,12},{9,13},{10,... | collective-permute-start | bytes 208904 | tf_op jit(solution)/shard_map/ppermute | solution.py:200
  18.6 5.0 %copy-start.3 = (f32[4]{0:T(128)S(1)}, f32[4]{0:T(128)}, u32[]{:S(2)}) copy-start(f32[4]{0:T(128)} %refs_6_.1) | copy-start | bytes 52
  18.6 1.2 %collective-permute-start.6 = (f32[32,128]{1,0:T(8,128)S(1)}, f32[32,128]{1,0:T(8,128)S(1)}, u32[]{:S(2)}, u32[]{:S(2)}) collective-permute-start(f32[32,128]{1,0:T(8,128)S(1)} %product.1.mine), channel_id=1, source_target_pairs={{0,1},{1,0},{2,3},{3,2},{4,5},{5,4},{6,7},{7,6},{8,9},{9,8},{10,11... | collective-permute-start | bytes 49160 | tf_op jit(solution)/shard_map/ppermute | solution.py:194
  19.9 3.7 %collective-permute-start.7 = (f32[32,128]{1,0:T(8,128)S(1)}, f32[32,128]{1,0:T(8,128)S(1)}, u32[]{:S(2)}, u32[]{:S(2)}) collective-permute-start(f32[32,128]{1,0:T(8,128)S(1)} %add.2.refs_0_), channel_id=1, source_target_pairs={{0,2},{1,3},{2,0},{3,1},{4,6},{5,7},{6,4},{7,5},{8,10},{9,11},{10,... | collective-permute-start | bytes 49160 | tf_op jit(solution)/shard_map/ppermute | solution.py:194
  24.2 3.7 %collective-permute-start.8 = (f32[16,128]{1,0:T(8,128)S(1)}, f32[16,128]{1,0:T(8,128)S(1)}, u32[]{:S(2)}, u32[]{:S(2)}) collective-permute-start(f32[16,128]{1,0:T(8,128)S(1)} %get-tuple-element.9.mine), channel_id=1, source_target_pairs={{0,4},{1,5},{2,6},{3,7},{4,0},{5,1},{6,2},{7,3},{8,12},{9,13},{10,... | collective-permute-start | bytes 24584 | tf_op jit(solution)/shard_map/ppermute | solution.py:200
  27.9 4.6 %copy-start = (f32[4,256]{1,0:T(4,128)S(1)}, f32[4,256]{1,0:T(4,128)}, u32[]{:S(2)}) copy-start(f32[4,256]{1,0:T(4,128)} %refs_5_.1) | copy-start | bytes 12292
  27.9 4.6 %copy-start.1 = (f32[4,256]{1,0:T(4,128)S(1)}, f32[4,256]{1,0:T(4,128)}, u32[]{:S(2)}) copy-start(f32[4,256]{1,0:T(4,128)} %refs_4_.1) | copy-start | bytes 12292
  27.9 4.6 %copy-start.2 = (f32[4,256]{1,0:T(4,128)S(1)}, f32[4,256]{1,0:T(4,128)}, u32[]{:S(2)}) copy-start(f32[4,256]{1,0:T(4,128)} %refs_3_.1) | copy-start | bytes 12292
  27.9 4.6 %collective-permute-start.9 = (f32[16,128]{1,0:T(8,128)S(1)}, f32[16,128]{1,0:T(8,128)S(1)}, u32[]{:S(2)}, u32[]{:S(2)}) collective-permute-start(f32[16,128]{1,0:T(8,128)S(1)} %add.3.refs_0_), channel_id=1, source_target_pairs={{0,8},{1,9},{2,10},{3,11},{4,12},{5,13},{6,14},{7,15},{8,0},{9,1},... | collective-permute-start | bytes 24584 | tf_op jit(solution)/shard_map/ppermute | solution.py:200

commit v6 on v4

v6 whole, which is shorter than its diff:
```python
import functools
import math

import jax
import jax.numpy as jnp
from jax import lax
from jax.experimental import pallas as pl
from jax.experimental.pallas import tpu as pltpu
from jax.sharding import PartitionSpec as P

LOG2E = 1.4426950408889634
CHUNK = 32


def split_sizes(devices):
    lo = max(d for d in range(1, math.isqrt(devices) + 1) if devices % d == 0)
    hi = devices // lo
    assert hi & (hi - 1) == lo & (lo - 1) == 0
    return hi, lo


def pieces_of(wide):
    high = wide.astype(jnp.bfloat16).astype(jnp.float32)
    middle = (wide - high).astype(jnp.bfloat16).astype(jnp.float32)
    return [high, middle, wide - high - middle]


def fold(wide, dims):
    return jnp.concatenate(
        [wide[:, p : p + dims] for p in range(0, wide.shape[1], dims)], axis=0
    )


def unfold(tall, n):
    return jnp.concatenate(
        [tall[p : p + n] for p in range(0, tall.shape[0], n)], axis=1
    )


def squares(points):
    wide = points.astype(jnp.float32)
    wide = wide * wide
    high = wide.astype(jnp.bfloat16)
    low = (wide - high.astype(jnp.float32)).astype(jnp.bfloat16)
    ones = jnp.ones((8, points.shape[1]), jnp.bfloat16)
    sums = [
        lax.dot_general(
            ones, half, (((1,), (1,)), ((), ())), preferred_element_type=jnp.float32
        )
        for half in (high, low)
    ]
    return (sums[0] + sums[1])[:1]


def pack_kernel(points, direction, residual, length, noise, packed, own, rates, *scratch):
    step_in, rest_in, length_in, noise_in, sems = scratch
    size, dims = points.shape
    cands = direction.shape[0]
    lines = (packed.shape[0] - size) * dims // size
    copies = [
        pltpu.make_async_copy(source, target, sems.at[i])
        for i, (source, target) in enumerate(
            (
                (points, packed.at[pl.ds(0, size), :]),
                (direction, step_in),
                (residual, rest_in),
                (length, length_in),
                (noise, noise_in),
            )
        )
    ]
    for copy in copies:
        copy.start()
    for copy in copies[1:]:
        copy.wait()
    step = step_in[...]
    which = lax.broadcasted_iota(jnp.int32, (cands, 1), 0)
    sigma = jnp.zeros((cands, 1), jnp.float32)
    for c in range(cands):
        sigma = jnp.where(which == c, noise_in[c], sigma)
        rate = (-0.5 * LOG2E) / (length_in[c] * length_in[c])
        rates[pl.ds(8 * c, 8), :] = jnp.full((8, size), rate, jnp.float32)
    tall = own.shape[0] // 3
    for i, wide in enumerate((step, rest_in[...], sigma * step)):
        own[pl.ds(i * tall, tall), :] = fold(wide, dims)
    copies[0].wait()
    sq = squares(packed[:size, :])
    top = [*pieces_of(sq), jnp.ones((3, size), jnp.float32), jnp.zeros((2, size), jnp.float32)]
    top += [step, jnp.zeros((lines - 8 - cands, size), jnp.float32)]
    top = jnp.concatenate([t for t in top if t.shape[0]], axis=0)
    packed[size:, :] = fold(top, dims).astype(jnp.bfloat16)


def product_kernel(lo, hi, cands, *refs):
    cols, refs = refs[:hi], refs[hi:]
    rows, refs = refs[: lo - 1], refs[lo - 1 :]
    own, rates, out, row_wide, weights, dist = refs
    rows = (cols[0], *rows)
    tall = own.shape[0] // 3
    dims = own.shape[1]
    size = rates.shape[1]
    lines = (cols[0].shape[0] - size) * dims // size

    def extra(top):
        top = jnp.concatenate(
            [top, jnp.zeros((dims - top.shape[0], size), jnp.float32)], axis=0
        )
        return top.T

    for k in range(lo):
        top = unfold(rows[k][size:, :].astype(jnp.float32), lines)
        top = jnp.concatenate([top[3:6], top[:3], jnp.zeros((2, size), jnp.float32)])
        row_wide[pl.ds(k * size, size), :] = jnp.concatenate(
            [rows[k][:size, :], extra(top).astype(jnp.bfloat16)], axis=1
        )
    for h in range(hi):
        top = extra(unfold(cols[h][size:, :].astype(jnp.float32), lines))
        for c in range(cands):
            weights[c, pl.ds(h * size, size), :] = jnp.broadcast_to(
                top[:, 8 + c : 9 + c], (size, dims)
            )
        scaled = (cols[h][:size, :].astype(jnp.float32) * -2.0).astype(jnp.bfloat16)
        dist[pl.ds(h * size, size), :] = lax.dot_general(
            jnp.concatenate([scaled, top.astype(jnp.bfloat16)], axis=1),
            row_wide[...],
            (((1,), (1,)), ((), ())),
            preferred_element_type=jnp.float32,
        )

    def body(step, total):
        total = list(total)
        for j in range(0, CHUNK, 8):
            at = pl.ds(pl.multiple_of(step * CHUNK + j, 8), 8)
            for k in range(lo):
                here = dist[at, pl.ds(k * size, size)]
                for c in range(cands):
                    weight = jnp.concatenate(
                        [weights[c, at, :]] * (size // dims), axis=1
                    )
                    kern = jnp.exp2(here * rates[pl.ds(8 * c, 8), :])
                    total[k * cands + c] += kern * weight
        return tuple(total)

    total = lax.fori_loop(
        0,
        hi * size // CHUNK,
        body,
        (jnp.zeros((8, size), jnp.float32),) * (lo * cands),
    )
    for k in range(lo):
        part = [
            jnp.sum(total[k * cands + c], axis=0, keepdims=True) for c in range(cands)
        ]
        part = fold(jnp.concatenate(part, axis=0), dims)
        if k == 0:
            part += own[pl.ds(2 * tall, tall), :]
        out[pl.ds(k * tall, tall), :] = part
    out[pl.ds(lo * tall, 2 * tall), :] = own[pl.ds(0, 2 * tall), :]


def sums_kernel(cands, *refs):
    *parts, image_out, sums_out = refs
    lo = len(parts)
    tall, dims = image_out.shape
    sums = [jnp.zeros((tall, dims), jnp.float32)] * 4
    for k in range(lo):
        step = parts[k][pl.ds(lo * tall, tall), :]
        rest = parts[k][pl.ds((lo + 1) * tall, tall), :]
        image = parts[0][pl.ds(k * tall, tall), :]
        for m in range(1, lo):
            image = image + parts[m][pl.ds((k ^ m) * tall, tall), :]
        if k == 0:
            image_out[...] = image
        terms = (rest * rest, step * image, rest * image, image * image)
        sums = [s + t for s, t in zip(sums, terms)]
    for i, s in enumerate(sums):
        sums_out[pl.ds(i * cands, cands), :] = sum(
            s[p : p + cands] for p in range(0, tall, cands)
        )


def update_kernel(hi, *refs):
    sums, refs = refs[:hi], refs[hi:]
    image, solution, residual, direction, out_s, out_r, out_d = refs
    cands = solution.shape[0]
    total = sums[0][...]
    for h in range(1, hi):
        total = total + sums[h][...]
    total = jnp.sum(total, axis=1, keepdims=True)
    norm, curve, cross, square = (
        total[i * cands : (i + 1) * cands] for i in range(4)
    )
    alpha = norm / curve
    norm_next = norm - 2.0 * alpha * cross + alpha * (alpha * square)
    beta = norm_next / norm
    step = direction[...]
    fresh = residual[...] - alpha * unfold(image[...], cands)
    out_s[...] = solution[...] + alpha * step
    out_r[...] = fresh
    out_d[...] = fresh + beta * step


def per_device(devices, points, lengthscale, noise, solution, residual, direction):
    hi, lo = split_sizes(devices)
    size, dims = points.shape
    cands = direction.shape[0]
    tall = cands * size // dims
    extra = -(-(8 + cands) // 16) * 16 * size // dims

    def meet(x, mask):
        return lax.ppermute(x, "blk", [(d, d ^ mask) for d in range(devices)])

    vmem = pl.BlockSpec(memory_space=pltpu.VMEM)
    hbm = pl.BlockSpec(memory_space=pltpu.HBM)
    params = pltpu.CompilerParams(vmem_limit_bytes=50 * 1024 * 1024)

    packed, own, rates = pl.pallas_call(
        pack_kernel,
        out_shape=(
            jax.ShapeDtypeStruct((size + extra, dims), jnp.bfloat16),
            jax.ShapeDtypeStruct((3 * tall, dims), jnp.float32),
            jax.ShapeDtypeStruct((8 * cands, size), jnp.float32),
        ),
        in_specs=[hbm] * 5,
        out_specs=(vmem,) * 3,
        scratch_shapes=[
            pltpu.VMEM((cands, size), jnp.float32),
            pltpu.VMEM((cands, size), jnp.float32),
            pltpu.SMEM((cands,), jnp.float32),
            pltpu.SMEM((cands,), jnp.float32),
            pltpu.SemaphoreType.DMA((5,)),
        ],
        compiler_params=params,
        name="pack",
    )(
        *(
            pltpu.with_memory_space_constraint(x, pltpu.HBM)
            for x in (points, direction, residual, lengthscale, noise)
        )
    )

    cols = [packed] + [meet(packed, k * lo) for k in range(1, hi)]
    rows = [packed] + [meet(packed, k) for k in range(1, lo) if k == 1 or k % 2 == 0]
    if lo > 2:
        rows = [packed, rows[1]] + [
            block
            for k in range(2, lo, 2)
            for block in (rows[k // 2 + 1], meet(rows[k // 2 + 1], 1))
        ]

    partial = pl.pallas_call(
        functools.partial(product_kernel, lo, hi, cands),
        out_shape=jax.ShapeDtypeStruct(((lo + 2) * tall, dims), jnp.float32),
        in_specs=[vmem] * (hi + lo + 1),
        out_specs=vmem,
        scratch_shapes=[
            pltpu.VMEM((lo * size, 2 * dims), jnp.bfloat16),
            pltpu.VMEM((cands, hi * size, dims), jnp.float32),
            pltpu.VMEM((hi * size, lo * size), jnp.float32),
        ],
        compiler_params=params,
        name="product",
    )(*cols, *rows[1:], own, rates)

    image, sums = pl.pallas_call(
        functools.partial(sums_kernel, cands),
        out_shape=(
            jax.ShapeDtypeStruct((tall, dims), jnp.float32),
            jax.ShapeDtypeStruct((4 * cands, dims), jnp.float32),
        ),
        in_specs=[vmem] * lo,
        out_specs=(vmem, vmem),
        compiler_params=params,
        name="sums",
    )(partial, *(meet(partial, k) for k in range(1, lo)))

    return pl.pallas_call(
        functools.partial(update_kernel, hi),
        out_shape=(jax.ShapeDtypeStruct((cands, size), jnp.float32),) * 3,
        in_specs=[vmem] * (hi + 4),
        out_specs=(vmem,) * 3,
        compiler_params=params,
        name="update",
    )(sums, *(meet(sums, k * lo) for k in range(1, hi)), image, solution, residual, direction)


def solution(mesh):
    split = P(None, ("groups", "blk"))
    return jax.shard_map(
        functools.partial(per_device, mesh.shape["blk"]),
        mesh=mesh,
        in_specs=(P(("groups", "blk"), None), P("groups"), P("groups"), split, split, split),
        out_specs=(split, split, split),
        check_vma=False,
    )
```

time: 33.2 us -> 31 us (0.934)
  local copies, waits for them, and re-layouts: 2.23 us -> 0.01 us
  waiting for transfers between devices: 9.51 us -> 10.8 us
  starting transfers between devices: 14.5 us -> 13.8 us
  Pallas kernels: 6.03 us -> 5.62 us
    unnamed x14 -> x6, local copies, waits for them, and re-layouts: 2.23 us -> 0.01 us
    ppermute x12, waiting for transfers between devices: 9.51 us -> 10.8 us  [meet(): return lax.ppermute(x, 'blk', [(d, d ^ mask) for d in range(devices)])]
    ppermute x12, starting transfers between devices: 14.5 us -> 13.8 us  [meet(): return lax.ppermute(x, 'blk', [(d, d ^ mask) for d in range(devices)])]
    pallas_call x3, Pallas kernels: 5.25 us -> 4.84 us  [the longest x1 3.76 us: per_device(): pl.pallas_call(functools.partial(product_kernel, lo, hi, cands), out_shap...]
  transfers between devices with their start and end apart: 12 -> 12, of which waited for: 7 -> 6; matrix products, arithmetic and copies ran while one was open for 0% -> 0% of each run, Pallas kernels for 0% -> 0%
where the time goes in v6:
time: 31 us; the launch traced here: 30.9 us
  starting transfers between devices  13.8 us (45%)
  waiting for transfers between devices  10.8 us (35%)
  Pallas kernels  5.62 us (18%)
  between operations  0.69 us (2%)
    ppermute x12, starting transfers between devices, meet(): return lax.ppermute(x, 'blk', [(d, d ^ mask) for d in range(devices)])  13.8 us
    ppermute x12, waiting for transfers between devices, meet(): return lax.ppermute(x, 'blk', [(d, d ^ mask) for d in range(devices)])  10.8 us
    pallas_call x1, Pallas kernels, per_device(): pl.pallas_call(functools.partial(product_kernel, lo, hi, cands), out_shap...  3.76 us
    pallas_call x1, Pallas kernels, per_device(): pl.pallas_call(pack_kernel, out_shape=(jax.ShapeDtypeStruct((size + extra...  1.07 us
    pallas_call x1, Pallas kernels, per_device(): pl.pallas_call(functools.partial(update_kernel, hi), out_shape=(jax.Shape...  0.78 us
  transfers between devices with their start and end apart: 12, of which 6 were waited for; matrix products, arithmetic and copies ran while one was open for 0% of the time, Pallas kernels for 0%

profile of v6, /device:TPU:0, one launch (start us, length us, event | category | flops | bytes accessed | tf_op | source)
XLA Modules:
  0.0 30.9 jit_solution(6899504744978134652)
XLA Ops:
  0.6 1.1 %pack.1 = (bf16[288,128]{1,0:T(8,128)(2,1)S(1)}, f32[24,128]{1,0:T(8,128)S(1)}, f32[32,256]{1,0:T(8,128)S(1)}) custom-call(bf16[256,128]{1,0:T(8,128)(2,1)} %points.1, f32[4,256]{1,0:T(4,128)} %refs_7_.1, f32[4,256]{1,0:T(4,128)} %refs_6_.1, f32[4]{0:T(128)} %length.1, f32[4]{0:T(128)} %noise.1), custom_call_target="tpu_custom_call" | custom-call | tf_op jit(solution)/shard_map/pack/pallas_call | solution.py:217
  1.7 3.0 %collective-permute-start.4 = (bf16[288,128]{1,0:T(8,128)(2,1)S(1)}, bf16[288,128]{1,0:T(8,128)(2,1)S(1)}, u32[]{:S(2)}, u32[]{:S(2)}) collective-permute-start(bf16[288,128]{1,0:T(8,128)(2,1)S(1)} %get-tuple-element.8.refs_0_), channel_id=1, source_target_pairs={{0,2},{1,3},{2,0},{3,1},{4,6},{5,7},{6,4},{7,5},{8,10},{9,11},{10,... | collective-permute-start | bytes 221192 | tf_op jit(solution)/shard_map/ppermute | solution.py:211
  4.7 0.0 collective-permute-start.3
  4.7 3.6 %collective-permute-start.2 = (bf16[288,128]{1,0:T(8,128)(2,1)S(1)}, bf16[288,128]{1,0:T(8,128)(2,1)S(1)}, u32[]{:S(2)}, u32[]{:S(2)}) collective-permute-start(bf16[288,128]{1,0:T(8,128)(2,1)S(1)} %get-tuple-element.8.refs_0_), channel_id=1, source_target_pairs={{0,12},{1,13},{2,14},{3,15},{4,8},{5,9},{6,10},{7,11},{8,4},{9,5},... | collective-permute-start | bytes 221192 | tf_op jit(solution)/shard_map/ppermute | solution.py:211
  8.3 0.0 collective-permute-start.1
  8.3 0.8 %collective-permute-start = (bf16[288,128]{1,0:T(8,128)(2,1)S(1)}, bf16[288,128]{1,0:T(8,128)(2,1)S(1)}, u32[]{:S(2)}, u32[]{:S(2)}) collective-permute-start(bf16[288,128]{1,0:T(8,128)(2,1)S(1)} %get-tuple-element.8.refs_0_), channel_id=1, source_target_pairs={{0,4},{1,5},{2,6},{3,7},{4,0},{5,1},{6,2},{7,3},{8,12},{9,13},{10,... | collective-permute-start | bytes 221192 | tf_op jit(solution)/shard_map/ppermute | solution.py:211
  9.1 0.0 collective-permute-done.4.refs_5_
  9.1 0.0 collective-permute-start.5
  9.1 0.0 collective-permute-done.3.refs_4_
  9.1 2.5 %collective-permute-done.2.refs_3_ = bf16[288,128]{1,0:T(8,128)(2,1)S(1)} collective-permute-done((bf16[288,128]{1,0:T(8,128)(2,1)S(1)}, bf16[288,128]{1,0:T(8,128)(2,1)S(1)}, u32[]{:S(2)}, u32[]{:S(2)}) %collective-permute-start.2) | collective-permute-done | bytes 73760 | tf_op jit(solution)/shard_map/ppermute | solution.py:211
  11.7 3.5 %collective-permute-done.1.refs_2_ = bf16[288,128]{1,0:T(8,128)(2,1)S(1)} collective-permute-done((bf16[288,128]{1,0:T(8,128)(2,1)S(1)}, bf16[288,128]{1,0:T(8,128)(2,1)S(1)}, u32[]{:S(2)}, u32[]{:S(2)}) %collective-permute-start.1) | collective-permute-done | bytes 73760 | tf_op jit(solution)/shard_map/ppermute | solution.py:211
  15.2 0.0 collective-permute-done.refs_1_
  15.2 3.8 %product.1.refs_0_ = f32[48,128]{1,0:T(8,128)S(1)} custom-call(bf16[288,128]{1,0:T(8,128)(2,1)S(1)} %get-tuple-element.8.refs_0_, bf16[288,128]{1,0:T(8,128)(2,1)S(1)} %collective-permute-done.refs_1_, bf16[288,128]{1,0:T(8,128)(2,1)S(1)} %collective-permute-done.1.refs_2_, bf16[288,128]{1,0:T(8,128)(2,1)S(1)} %collective-permute-done.2.refs_3_, ...), custom_call_target="tpu_custom_call" | custom-call | tf_op jit(solution)/shard_map/product/pallas_call | solution.py:251
  18.9 0.1 collective-permute-start.8
  19.0 1.3 %collective-permute-start.7 = (f32[48,128]{1,0:T(8,128)S(1)}, f32[48,128]{1,0:T(8,128)S(1)}, u32[]{:S(2)}, u32[]{:S(2)}) collective-permute-start(f32[48,128]{1,0:T(8,128)S(1)} %product.1.refs_0_), channel_id=1, source_target_pairs={{0,2},{1,3},{2,0},{3,1},{4,6},{5,7},{6,4},{7,5},{8,10},{9,11},{10,... | collective-permute-start | bytes 73736 | tf_op jit(solution)/shard_map/ppermute | solution.py:211
  20.4 0.5 %collective-permute-start.6 = (f32[48,128]{1,0:T(8,128)S(1)}, f32[48,128]{1,0:T(8,128)S(1)}, u32[]{:S(2)}, u32[]{:S(2)}) collective-permute-start(f32[48,128]{1,0:T(8,128)S(1)} %product.1.refs_0_), channel_id=1, source_target_pairs={{0,1},{1,0},{2,3},{3,2},{4,5},{5,4},{6,7},{7,6},{8,9},{9,8},{10,11... | collective-permute-start | bytes 73736 | tf_op jit(solution)/shard_map/ppermute | solution.py:211
  20.9 1.6 %collective-permute-done.8.refs_3_ = f32[48,128]{1,0:T(8,128)S(1)} collective-permute-done((f32[48,128]{1,0:T(8,128)S(1)}, f32[48,128]{1,0:T(8,128)S(1)}, u32[]{:S(2)}, u32[]{:S(2)}) %collective-permute-start.8) | collective-permute-done | bytes 24608 | tf_op jit(solution)/shard_map/ppermute | solution.py:211
  22.4 0.5 %collective-permute-done.7.refs_2_ = f32[48,128]{1,0:T(8,128)S(1)} collective-permute-done((f32[48,128]{1,0:T(8,128)S(1)}, f32[48,128]{1,0:T(8,128)S(1)}, u32[]{:S(2)}, u32[]{:S(2)}) %collective-permute-start.7) | collective-permute-done | bytes 24608 | tf_op jit(solution)/shard_map/ppermute | solution.py:211
  23.0 2.5 %collective-permute-start.11 = (f32[16,128]{1,0:T(8,128)S(1)}, f32[16,128]{1,0:T(8,128)S(1)}, u32[]{:S(2)}, u32[]{:S(2)}) collective-permute-start(f32[16,128]{1,0:T(8,128)S(1)} %get-tuple-element.11.refs_0_), channel_id=1, source_target_pairs={{0,12},{1,13},{2,14},{3,15},{4,8},{5,9},{6,10},{7,11},{8,4},{9,5},... | collective-permute-start | bytes 24584 | tf_op jit(solution)/shard_map/ppermute | solution.py:211
  25.5 0.0 collective-permute-start.10
  25.6 1.9 %collective-permute-start.9 = (f32[16,128]{1,0:T(8,128)S(1)}, f32[16,128]{1,0:T(8,128)S(1)}, u32[]{:S(2)}, u32[]{:S(2)}) collective-permute-start(f32[16,128]{1,0:T(8,128)S(1)} %get-tuple-element.11.refs_0_), channel_id=1, source_target_pairs={{0,4},{1,5},{2,6},{3,7},{4,0},{5,1},{6,2},{7,3},{8,12},{9,13},{10,... | collective-permute-start | bytes 24584 | tf_op jit(solution)/shard_map/ppermute | solution.py:211
  27.5 1.1 %collective-permute-done.11.refs_3_ = f32[16,128]{1,0:T(8,128)S(1)} collective-permute-done((f32[16,128]{1,0:T(8,128)S(1)}, f32[16,128]{1,0:T(8,128)S(1)}, u32[]{:S(2)}, u32[]{:S(2)}) %collective-permute-start.11) | collective-permute-done | bytes 8224 | tf_op jit(solution)/shard_map/ppermute | solution.py:211
  28.5 1.6 %collective-permute-done.10.refs_2_ = f32[16,128]{1,0:T(8,128)S(1)} collective-permute-done((f32[16,128]{1,0:T(8,128)S(1)}, f32[16,128]{1,0:T(8,128)S(1)}, u32[]{:S(2)}, u32[]{:S(2)}) %collective-permute-start.10) | collective-permute-done | bytes 8224 | tf_op jit(solution)/shard_map/ppermute | solution.py:211
  30.1 0.8 %update.1 = (f32[4,256]{1,0:T(4,128)}, f32[4,256]{1,0:T(4,128)}, f32[4,256]{1,0:T(4,128)}) custom-call(f32[16,128]{1,0:T(8,128)S(1)} %get-tuple-element.11.refs_0_, f32[16,128]{1,0:T(8,128)S(1)} %collective-permute-done.9.refs_1_, f32[16,128]{1,0:T(8,128)S(1)} %collective-permute-done.10.refs_2_, f32[16,128]{1,0:T(8,128)S(1)} %collective-permute-done.11.refs_3_, ...), custom_call_target="tpu_custom_call" | custom-call | tf_op jit(solution)/shard_map/update/pallas_call | solution.py:277
  (10 shorter events, 0.0 us)
Async XLA Ops:
  1.7 7.4 %collective-permute-start.4 = (bf16[288,128]{1,0:T(8,128)(2,1)S(1)}, bf16[288,128]{1,0:T(8,128)(2,1)S(1)}, u32[]{:S(2)}, u32[]{:S(2)}) collective-permute-start(bf16[288,128]{1,0:T(8,128)(2,1)S(1)} %get-tuple-element.8.refs_0_), channel_id=1, source_target_pairs={{0,2},{1,3},{2,0},{3,1},{4,6},{5,7},{6,4},{7,5},{8,10},{9,11},{10,... | collective-permute-start | bytes 221192 | tf_op jit(solution)/shard_map/ppermute | solution.py:211
  4.7 4.4 %collective-permute-start.3 = (bf16[288,128]{1,0:T(8,128)(2,1)S(1)}, bf16[288,128]{1,0:T(8,128)(2,1)S(1)}, u32[]{:S(2)}, u32[]{:S(2)}) collective-permute-start(bf16[288,128]{1,0:T(8,128)(2,1)S(1)} %get-tuple-element.8.refs_0_), channel_id=1, source_target_pairs={{0,1},{1,0},{2,3},{3,2},{4,5},{5,4},{6,7},{7,6},{8,9},{9,8},{10,11... | collective-permute-start | bytes 221192 | tf_op jit(solution)/shard_map/ppermute | solution.py:211
  4.7 6.9 %collective-permute-start.2 = (bf16[288,128]{1,0:T(8,128)(2,1)S(1)}, bf16[288,128]{1,0:T(8,128)(2,1)S(1)}, u32[]{:S(2)}, u32[]{:S(2)}) collective-permute-start(bf16[288,128]{1,0:T(8,128)(2,1)S(1)} %get-tuple-element.8.refs_0_), channel_id=1, source_target_pairs={{0,12},{1,13},{2,14},{3,15},{4,8},{5,9},{6,10},{7,11},{8,4},{9,5},... | collective-permute-start | bytes 221192 | tf_op jit(solution)/shard_map/ppermute | solution.py:211
  8.3 6.8 %collective-permute-start.1 = (bf16[288,128]{1,0:T(8,128)(2,1)S(1)}, bf16[288,128]{1,0:T(8,128)(2,1)S(1)}, u32[]{:S(2)}, u32[]{:S(2)}) collective-permute-start(bf16[288,128]{1,0:T(8,128)(2,1)S(1)} %get-tuple-element.8.refs_0_), channel_id=1, source_target_pairs={{0,8},{1,9},{2,10},{3,11},{4,12},{5,13},{6,14},{7,15},{8,0},{9,1},... | collective-permute-start | bytes 221192 | tf_op jit(solution)/shard_map/ppermute | solution.py:211
  8.3 6.8 %collective-permute-start = (bf16[288,128]{1,0:T(8,128)(2,1)S(1)}, bf16[288,128]{1,0:T(8,128)(2,1)S(1)}, u32[]{:S(2)}, u32[]{:S(2)}) collective-permute-start(bf16[288,128]{1,0:T(8,128)(2,1)S(1)} %get-tuple-element.8.refs_0_), channel_id=1, source_target_pairs={{0,4},{1,5},{2,6},{3,7},{4,0},{5,1},{6,2},{7,3},{8,12},{9,13},{10,... | collective-permute-start | bytes 221192 | tf_op jit(solution)/shard_map/ppermute | solution.py:211
  9.1 6.0 %collective-permute-start.5 = (bf16[288,128]{1,0:T(8,128)(2,1)S(1)}, bf16[288,128]{1,0:T(8,128)(2,1)S(1)}, u32[]{:S(2)}, u32[]{:S(2)}) collective-permute-start(bf16[288,128]{1,0:T(8,128)(2,1)S(1)} %collective-permute-done.4.refs_5_), channel_id=1, source_target_pairs={{0,1},{1,0},{2,3},{3,2},{4,5},{5,4},{6,7},{7,6},{8,9},{9,8},{10,11... | collective-permute-start | bytes 221192 | tf_op jit(solution)/shard_map/ppermute | solution.py:211
  18.9 3.5 %collective-permute-start.8 = (f32[48,128]{1,0:T(8,128)S(1)}, f32[48,128]{1,0:T(8,128)S(1)}, u32[]{:S(2)}, u32[]{:S(2)}) collective-permute-start(f32[48,128]{1,0:T(8,128)S(1)} %product.1.refs_0_), channel_id=1, source_target_pairs={{0,3},{1,2},{2,1},{3,0},{4,7},{5,6},{6,5},{7,4},{8,11},{9,10},{10,... | collective-permute-start | bytes 73736 | tf_op jit(solution)/shard_map/ppermute | solution.py:211
  19.0 3.9 %collective-permute-start.7 = (f32[48,128]{1,0:T(8,128)S(1)}, f32[48,128]{1,0:T(8,128)S(1)}, u32[]{:S(2)}, u32[]{:S(2)}) collective-permute-start(f32[48,128]{1,0:T(8,128)S(1)} %product.1.refs_0_), channel_id=1, source_target_pairs={{0,2},{1,3},{2,0},{3,1},{4,6},{5,7},{6,4},{7,5},{8,10},{9,11},{10,... | collective-permute-start | bytes 73736 | tf_op jit(solution)/shard_map/ppermute | solution.py:211
  20.4 2.6 %collective-permute-start.6 = (f32[48,128]{1,0:T(8,128)S(1)}, f32[48,128]{1,0:T(8,128)S(1)}, u32[]{:S(2)}, u32[]{:S(2)}) collective-permute-start(f32[48,128]{1,0:T(8,128)S(1)} %product.1.refs_0_), channel_id=1, source_target_pairs={{0,1},{1,0},{2,3},{3,2},{4,5},{5,4},{6,7},{7,6},{8,9},{9,8},{10,11... | collective-permute-start | bytes 73736 | tf_op jit(solution)/shard_map/ppermute | solution.py:211
  23.0 7.1 %copy-start = (f32[4,256]{1,0:T(4,128)S(1)}, f32[4,256]{1,0:T(4,128)}, u32[]{:S(2)}) copy-start(f32[4,256]{1,0:T(4,128)} %refs_7_.1) | copy-start | bytes 12292
  23.0 7.1 %copy-start.1 = (f32[4,256]{1,0:T(4,128)S(1)}, f32[4,256]{1,0:T(4,128)}, u32[]{:S(2)}) copy-start(f32[4,256]{1,0:T(4,128)} %refs_6_.1) | copy-start | bytes 12292
  23.0 7.1 %copy-start.2 = (f32[4,256]{1,0:T(4,128)S(1)}, f32[4,256]{1,0:T(4,128)}, u32[]{:S(2)}) copy-start(f32[4,256]{1,0:T(4,128)} %refs_5_.1) | copy-start | bytes 12292
  23.0 5.5 %collective-permute-start.11 = (f32[16,128]{1,0:T(8,128)S(1)}, f32[16,128]{1,0:T(8,128)S(1)}, u32[]{:S(2)}, u32[]{:S(2)}) collective-permute-start(f32[16,128]{1,0:T(8,128)S(1)} %get-tuple-element.11.refs_0_), channel_id=1, source_target_pairs={{0,12},{1,13},{2,14},{3,15},{4,8},{5,9},{6,10},{7,11},{8,4},{9,5},... | collective-permute-start | bytes 24584 | tf_op jit(solution)/shard_map/ppermute | solution.py:211
  25.5 4.5 %collective-permute-start.10 = (f32[16,128]{1,0:T(8,128)S(1)}, f32[16,128]{1,0:T(8,128)S(1)}, u32[]{:S(2)}, u32[]{:S(2)}) collective-permute-start(f32[16,128]{1,0:T(8,128)S(1)} %get-tuple-element.11.refs_0_), channel_id=1, source_target_pairs={{0,8},{1,9},{2,10},{3,11},{4,12},{5,13},{6,14},{7,15},{8,0},{9,1},... | collective-permute-start | bytes 24584 | tf_op jit(solution)/shard_map/ppermute | solution.py:211
  25.6 4.5 %collective-permute-start.9 = (f32[16,128]{1,0:T(8,128)S(1)}, f32[16,128]{1,0:T(8,128)S(1)}, u32[]{:S(2)}, u32[]{:S(2)}) collective-permute-start(f32[16,128]{1,0:T(8,128)S(1)} %get-tuple-element.11.refs_0_), channel_id=1, source_target_pairs={{0,4},{1,5},{2,6},{3,7},{4,0},{5,1},{6,2},{7,3},{8,12},{9,13},{10,... | collective-permute-start | bytes 24584 | tf_op jit(solution)/shard_map/ppermute | solution.py:211

commit v7 on v6

--- a/solution.py
+++ b/solution.py
@@ -8,7 +8,6 @@
 from jax.experimental.pallas import tpu as pltpu
 from jax.sharding import PartitionSpec as P
 
-LOG2E = 1.4426950408889634
 CHUNK = 32
 
 
@@ -78,8 +77,8 @@
     sigma = jnp.zeros((cands, 1), jnp.float32)
     for c in range(cands):
         sigma = jnp.where(which == c, noise_in[c], sigma)
-        rate = (-0.5 * LOG2E) / (length_in[c] * length_in[c])
-        rates[pl.ds(8 * c, 8), :] = jnp.full((8, size), rate, jnp.float32)
+        rate = -0.5 / (length_in[c] * length_in[c])
+        rates[pl.ds(8 * c, 8), :] = jnp.full((8, dims), rate, jnp.float32)
     tall = own.shape[0] // 3
     for i, wide in enumerate((step, rest_in[...], sigma * step)):
         own[pl.ds(i * tall, tall), :] = fold(wide, dims)
@@ -91,71 +90,106 @@
     packed[size:, :] = fold(top, dims).astype(jnp.bfloat16)
 
 
-def product_kernel(lo, hi, cands, *refs):
-    cols, refs = refs[:hi], refs[hi:]
-    rows, refs = refs[: lo - 1], refs[lo - 1 :]
-    own, rates, out, row_wide, weights, dist = refs
-    rows = (cols[0], *rows)
-    tall = own.shape[0] // 3
-    dims = own.shape[1]
-    size = rates.shape[1]
-    lines = (cols[0].shape[0] - size) * dims // size
-
-    def extra(top):
-        top = jnp.concatenate(
-            [top, jnp.zeros((dims - top.shape[0], size), jnp.float32)], axis=0
-        )
-        return top.T
-
-    for k in range(lo):
-        top = unfold(rows[k][size:, :].astype(jnp.float32), lines)
-        top = jnp.concatenate([top[3:6], top[:3], jnp.zeros((2, size), jnp.float32)])
+def turned(tops, size):
+    row = lax.broadcasted_iota(jnp.int32, (size, size), 0)
+    lane = lax.broadcasted_iota(jnp.int32, (size, size), 1)
+    return lax.dot_general(
+        (row == lane).astype(jnp.bfloat16),
+        jnp.concatenate(tops, axis=0).astype(jnp.bfloat16),
+        (((1,), (1,)), ((), ())),
+        preferred_element_type=jnp.float32,
+    )
+
+
+def top_of(block, size):
+    lines = (block.shape[0] - size) * block.shape[1] // size
+    return unfold(block[size:, :].astype(jnp.float32), lines)
+
+
+def padded(top, dims):
+    return jnp.concatenate(
+        [top, jnp.zeros((dims - top.shape[0], top.shape[1]), jnp.float32)], axis=0
+    )
+
+
+def widen_rows(rows, row_wide, size):
+    dims = rows[0].shape[1]
+    for k, block in enumerate(rows):
+        top = top_of(block, size)
+        top = jnp.concatenate([top[3:6], top[:3]], axis=0)
         row_wide[pl.ds(k * size, size), :] = jnp.concatenate(
-            [rows[k][:size, :], extra(top).astype(jnp.bfloat16)], axis=1
-        )
-    for h in range(hi):
-        top = extra(unfold(cols[h][size:, :].astype(jnp.float32), lines))
-        for c in range(cands):
-            weights[c, pl.ds(h * size, size), :] = jnp.broadcast_to(
-                top[:, 8 + c : 9 + c], (size, dims)
-            )
-        scaled = (cols[h][:size, :].astype(jnp.float32) * -2.0).astype(jnp.bfloat16)
-        dist[pl.ds(h * size, size), :] = lax.dot_general(
-            jnp.concatenate([scaled, top.astype(jnp.bfloat16)], axis=1),
-            row_wide[...],
-            (((1,), (1,)), ((), ())),
-            preferred_element_type=jnp.float32,
-        )
+            [block[:size, :], turned([padded(top, dims)], size).astype(jnp.bfloat16)],
+            axis=1,
+        )
+
+
+def add_column(col, row_wide, rates, weights, dist, size):
+    dims = col.shape[1]
+    cands = rates.shape[0] // 8
+    lo = row_wide.shape[0] // size
+    top = top_of(col, size)
+    steps = top[8 : 8 + cands]
+    tops = [padded(top, dims)]
+    tops += [jnp.broadcast_to(steps[c : c + 1], (dims, size)) for c in range(cands)]
+    columns = turned(tops, size)
+    for c in range(cands):
+        weights[c] = columns[:, (c + 1) * dims : (c + 2) * dims]
+    scaled = (col[:size, :].astype(jnp.float32) * -2.0).astype(jnp.bfloat16)
+    dist[...] = lax.dot_general(
+        jnp.concatenate([scaled, columns[:, :dims].astype(jnp.bfloat16)], axis=1),
+        row_wide[...],
+        (((1,), (1,)), ((), ())),
+        preferred_element_type=jnp.float32,
+    )
+    wide = size // dims
+    rate = [jnp.concatenate([rates[pl.ds(8 * c, 8), :]] * wide, axis=1) for c in range(cands)]
 
     def body(step, total):
         total = list(total)
         for j in range(0, CHUNK, 8):
             at = pl.ds(pl.multiple_of(step * CHUNK + j, 8), 8)
+            weight = [jnp.concatenate([weights[c, at, :]] * wide, axis=1) for c in range(cands)]
             for k in range(lo):
                 here = dist[at, pl.ds(k * size, size)]
                 for c in range(cands):
-                    weight = jnp.concatenate(
-                        [weights[c, at, :]] * (size // dims), axis=1
-                    )
-                    kern = jnp.exp2(here * rates[pl.ds(8 * c, 8), :])
-                    total[k * cands + c] += kern * weight
+                    total[k * cands + c] += jnp.exp(here * rate[c]) * weight[c]
         return tuple(total)
 
     total = lax.fori_loop(
         0,
-        hi * size // CHUNK,
+        size // CHUNK,
         body,
         (jnp.zeros((8, size), jnp.float32),) * (lo * cands),
     )
+    total = [jnp.sum(t, axis=0, keepdims=True) for t in total]
+    return [
+        fold(jnp.concatenate(total[k * cands : (k + 1) * cands], axis=0), dims)
+        for k in range(lo)
+    ]
+
+
+def first_kernel(lo, *refs):
+    rows, refs = refs[:lo], refs[lo:]
+    own, rates, out, row_wide, weights, dist = refs
+    tall, dims = own.shape[0] // 3, own.shape[1]
+    size = row_wide.shape[0] // lo
+    widen_rows(rows, row_wide, size)
+    parts = add_column(rows[0], row_wide, rates, weights, dist, size)
+    parts[0] += own[pl.ds(2 * tall, tall), :]
     for k in range(lo):
-        part = [
-            jnp.sum(total[k * cands + c], axis=0, keepdims=True) for c in range(cands)
-        ]
-        part = fold(jnp.concatenate(part, axis=0), dims)
-        if k == 0:
-            part += own[pl.ds(2 * tall, tall), :]
-        out[pl.ds(k * tall, tall), :] = part
+        out[pl.ds(k * tall, tall), :] = parts[k]
     out[pl.ds(lo * tall, 2 * tall), :] = own[pl.ds(0, 2 * tall), :]
+
+
+def next_kernel(lo, col, row_wide, rates, before, out, weights, dist):
+    size = row_wide.shape[0] // lo
+    tall = before.shape[0] // (lo + 2)
+    parts = add_column(col, row_wide, rates, weights, dist, size)
+    for k in range(lo):
+        at = pl.ds(k * tall, tall)
+        out[at, :] = before[at, :] + parts[k]
+    at = pl.ds(lo * tall, 2 * tall)
+    out[at, :] = before[at, :]
 
 
 def sums_kernel(cands, *refs):
@@ -219,7 +253,7 @@
         out_shape=(
             jax.ShapeDtypeStruct((size + extra, dims), jnp.bfloat16),
             jax.ShapeDtypeStruct((3 * tall, dims), jnp.float32),
-            jax.ShapeDtypeStruct((8 * cands, size), jnp.float32),
+            jax.ShapeDtypeStruct((8 * cands, dims), jnp.float32),
         ),
         in_specs=[hbm] * 5,
         out_specs=(vmem,) * 3,
@@ -239,28 +273,40 @@
         )
     )
 
-    cols = [packed] + [meet(packed, k * lo) for k in range(1, hi)]
-    rows = [packed] + [meet(packed, k) for k in range(1, lo) if k == 1 or k % 2 == 0]
-    if lo > 2:
-        rows = [packed, rows[1]] + [
-            block
-            for k in range(2, lo, 2)
-            for block in (rows[k // 2 + 1], meet(rows[k // 2 + 1], 1))
-        ]
-
-    partial = pl.pallas_call(
-        functools.partial(product_kernel, lo, hi, cands),
-        out_shape=jax.ShapeDtypeStruct(((lo + 2) * tall, dims), jnp.float32),
-        in_specs=[vmem] * (hi + lo + 1),
-        out_specs=vmem,
-        scratch_shapes=[
-            pltpu.VMEM((lo * size, 2 * dims), jnp.bfloat16),
-            pltpu.VMEM((cands, hi * size, dims), jnp.float32),
-            pltpu.VMEM((hi * size, lo * size), jnp.float32),
-        ],
+    rows = [packed] + [meet(packed, k) for k in range(1, lo)]
+
+    terms = size * lo * size
+    cost = pl.CostEstimate(
+        flops=4 * dims * terms + 4 * cands * terms,
+        bytes_accessed=4 * terms,
+        transcendentals=cands * terms,
+    )
+    spare = [
+        pltpu.VMEM((cands, size, dims), jnp.float32),
+        pltpu.VMEM((size, lo * size), jnp.float32),
+    ]
+    result = jax.ShapeDtypeStruct(((lo + 2) * tall, dims), jnp.float32)
+    partial, row_wide = pl.pallas_call(
+        functools.partial(first_kernel, lo),
+        out_shape=(result, jax.ShapeDtypeStruct((lo * size, 2 * dims), jnp.bfloat16)),
+        in_specs=[vmem] * (lo + 2),
+        out_specs=(vmem, vmem),
+        scratch_shapes=spare,
         compiler_params=params,
-        name="product",
-    )(*cols, *rows[1:], own, rates)
+        cost_estimate=cost,
+        name="product_own",
+    )(*rows, own, rates)
+    for k in range(hi - 1, 0, -1):
+        partial = pl.pallas_call(
+            functools.partial(next_kernel, lo),
+            out_shape=result,
+            in_specs=[vmem] * 4,
+            out_specs=vmem,
+            scratch_shapes=spare,
+            compiler_params=params,
+            cost_estimate=cost,
+            name="product_%d" % k,
+        )(meet(packed, k * lo), row_wide, rates, partial)
 
     image, sums = pl.pallas_call(
         functools.partial(sums_kernel, cands),

time: 31 us -> 30.8 us (level)
  Pallas kernels: 5.62 us -> 6.96 us
  waiting for transfers between devices: 10.8 us -> 9.94 us
  starting transfers between devices: 13.8 us -> 13.1 us
    pallas_call x1 -> x4, Pallas kernels: 3.76 us -> 5.1 us  [the longest x3 3.81 us: per_device(): pl.pallas_call(functools.partial(next_kernel, lo), out_shape=result, in_s...]
    ppermute x12, waiting for transfers between devices: 10.8 us -> 9.94 us  [meet(): return lax.ppermute(x, 'blk', [(d, d ^ mask) for d in range(devices)])]
    ppermute x12, starting transfers between devices: 13.8 us -> 13.1 us  [meet(): return lax.ppermute(x, 'blk', [(d, d ^ mask) for d in range(devices)])]
  transfers between devices with their start and end apart: 12 -> 12, of which waited for: 6 -> 6; matrix products, arithmetic and copies ran while one was open for 0% -> 0% of each run, Pallas kernels for 0% -> 12%
where the time goes in v7:
time: 30.8 us; the launch traced here: 30.7 us
  starting transfers between devices  13.1 us (43%)
  waiting for transfers between devices  9.94 us (32%)
  Pallas kernels  6.96 us (23%)
  between operations  0.7 us (2%)
    ppermute x12, starting transfers between devices, meet(): return lax.ppermute(x, 'blk', [(d, d ^ mask) for d in range(devices)])  13.1 us
    ppermute x12, waiting for transfers between devices, meet(): return lax.ppermute(x, 'blk', [(d, d ^ mask) for d in range(devices)])  9.94 us
    pallas_call x3, Pallas kernels, per_device(): pl.pallas_call(functools.partial(next_kernel, lo), out_shape=result, in_s...  3.81 us
    pallas_call x1, Pallas kernels, per_device(): pl.pallas_call(functools.partial(first_kernel, lo), out_shape=(result, ja...  1.29 us
    pallas_call x1, Pallas kernels, per_device(): pl.pallas_call(pack_kernel, out_shape=(jax.ShapeDtypeStruct((size + extra...  1.07 us
    pallas_call x1, Pallas kernels, per_device(): pl.pallas_call(functools.partial(update_kernel, hi), out_shape=(jax.Shape...  0.78 us
  transfers between devices with their start and end apart: 12, of which 6 were waited for; matrix products, arithmetic and copies ran while one was open for 0% of the time, Pallas kernels for 12%

profile of v7, /device:TPU:0, one launch (start us, length us, event | category | flops | bytes accessed | tf_op | source)
XLA Modules:
  0.0 30.7 jit_solution(8019577711055501749)
XLA Ops:
  0.6 1.1 %pack.1 = (bf16[288,128]{1,0:T(8,128)(2,1)S(1)}, f32[24,128]{1,0:T(8,128)S(1)}, f32[32,128]{1,0:T(8,128)S(1)}) custom-call(bf16[256,128]{1,0:T(8,128)(2,1)} %points.1, f32[4,256]{1,0:T(4,128)} %refs_7_.1, f32[4,256]{1,0:T(4,128)} %refs_6_.1, f32[4]{0:T(128)} %length.1, f32[4]{0:T(128)} %noise.1), custom_call_target="tpu_custom_call" | custom-call | tf_op jit(solution)/shard_map/pack/pallas_call | solution.py:251
  1.7 0.5 %collective-permute-start.1 = (bf16[288,128]{1,0:T(8,128)(2,1)S(1)}, bf16[288,128]{1,0:T(8,128)(2,1)S(1)}, u32[]{:S(2)}, u32[]{:S(2)}) collective-permute-start(bf16[288,128]{1,0:T(8,128)(2,1)S(1)} %get-tuple-element.10.refs_0_), channel_id=1, source_target_pairs={{0,1},{1,0},{2,3},{3,2},{4,5},{5,4},{6,7},{7,6},{8,9},{9,8},{10,11... | collective-permute-start | bytes 221192 | tf_op jit(solution)/shard_map/ppermute | solution.py:245
  2.2 2.6 %collective-permute-start.2 = (bf16[288,128]{1,0:T(8,128)(2,1)S(1)}, bf16[288,128]{1,0:T(8,128)(2,1)S(1)}, u32[]{:S(2)}, u32[]{:S(2)}) collective-permute-start(bf16[288,128]{1,0:T(8,128)(2,1)S(1)} %get-tuple-element.10.refs_0_), channel_id=1, source_target_pairs={{0,2},{1,3},{2,0},{3,1},{4,6},{5,7},{6,4},{7,5},{8,10},{9,11},{10,... | collective-permute-start | bytes 221192 | tf_op jit(solution)/shard_map/ppermute | solution.py:245
  4.8 0.1 collective-permute-start.3
  4.9 3.8 %collective-permute-start.5 = (bf16[288,128]{1,0:T(8,128)(2,1)S(1)}, bf16[288,128]{1,0:T(8,128)(2,1)S(1)}, u32[]{:S(2)}, u32[]{:S(2)}) collective-permute-start(bf16[288,128]{1,0:T(8,128)(2,1)S(1)} %get-tuple-element.10.refs_0_), channel_id=1, source_target_pairs={{0,12},{1,13},{2,14},{3,15},{4,8},{5,9},{6,10},{7,11},{8,4},{9,5},... | collective-permute-start | bytes 221192 | tf_op jit(solution)/shard_map/ppermute | solution.py:245
  8.7 0.0 collective-permute-start.4
  8.7 0.6 %collective-permute-start = (bf16[288,128]{1,0:T(8,128)(2,1)S(1)}, bf16[288,128]{1,0:T(8,128)(2,1)S(1)}, u32[]{:S(2)}, u32[]{:S(2)}) collective-permute-start(bf16[288,128]{1,0:T(8,128)(2,1)S(1)} %get-tuple-element.10.refs_0_), channel_id=1, source_target_pairs={{0,4},{1,5},{2,6},{3,7},{4,0},{5,1},{6,2},{7,3},{8,12},{9,13},{10,... | collective-permute-start | bytes 221192 | tf_op jit(solution)/shard_map/ppermute | solution.py:245
  9.3 1.3 %product_own.1 = (f32[48,128]{1,0:T(8,128)S(1)}, bf16[1024,256]{1,0:T(8,128)(2,1)S(1)}) custom-call(bf16[288,128]{1,0:T(8,128)(2,1)S(1)} %get-tuple-element.10.refs_0_, bf16[288,128]{1,0:T(8,128)(2,1)S(1)} %collective-permute-done.1.refs_1_, bf16[288,128]{1,0:T(8,128)(2,1)S(1)} %collective-permute-done.2.refs_2_, ...), custom_call_target="tpu_custom_call" | custom-call | flops 138412032 | bytes 1048576 | tf_op jit(solution)/shard_map/product_own/pallas_call | solution.py:289
  10.6 1.3 %collective-permute-done.5.col = bf16[288,128]{1,0:T(8,128)(2,1)S(1)} collective-permute-done((bf16[288,128]{1,0:T(8,128)(2,1)S(1)}, bf16[288,128]{1,0:T(8,128)(2,1)S(1)}, u32[]{:S(2)}, u32[]{:S(2)}) %collective-permute-start.5) | collective-permute-done | bytes 73760 | tf_op jit(solution)/shard_map/ppermute | solution.py:245
  11.8 1.3 %product_3.1.before = f32[48,128]{1,0:T(8,128)S(1)} custom-call(bf16[288,128]{1,0:T(8,128)(2,1)S(1)} %collective-permute-done.5.col, bf16[1024,256]{1,0:T(8,128)(2,1)S(1)} %get-tuple-element.13.row_wide, f32[32,128]{1,0:T(8,128)S(1)} %get-tuple-element.12.refs_5_.rates, f32[48,128]{1,0:T(8,128)S(1)} %get-tuple-element.14.before), custom_call_target="tpu_custom_call" | custom-call | flops 138412032 | bytes 1048576 | tf_op jit(solution)/shard_map/product_3/pallas_call | solution.py:300
  13.1 2.3 %collective-permute-done.4.col = bf16[288,128]{1,0:T(8,128)(2,1)S(1)} collective-permute-done((bf16[288,128]{1,0:T(8,128)(2,1)S(1)}, bf16[288,128]{1,0:T(8,128)(2,1)S(1)}, u32[]{:S(2)}, u32[]{:S(2)}) %collective-permute-start.4) | collective-permute-done | bytes 73760 | tf_op jit(solution)/shard_map/ppermute | solution.py:245
  15.4 1.3 %product_2.1.before = f32[48,128]{1,0:T(8,128)S(1)} custom-call(bf16[288,128]{1,0:T(8,128)(2,1)S(1)} %collective-permute-done.4.col, bf16[1024,256]{1,0:T(8,128)(2,1)S(1)} %get-tuple-element.13.row_wide, f32[32,128]{1,0:T(8,128)S(1)} %get-tuple-element.12.refs_5_.rates, f32[48,128]{1,0:T(8,128)S(1)} %product_3.1.before), custom_call_target="tpu_custom_call" | custom-call | flops 138412032 | bytes 1048576 | tf_op jit(solution)/shard_map/product_2/pallas_call | solution.py:300
  16.6 1.3 %product_1.1.refs_0_ = f32[48,128]{1,0:T(8,128)S(1)} custom-call(bf16[288,128]{1,0:T(8,128)(2,1)S(1)} %collective-permute-done.col, bf16[1024,256]{1,0:T(8,128)(2,1)S(1)} %get-tuple-element.13.row_wide, f32[32,128]{1,0:T(8,128)S(1)} %get-tuple-element.12.refs_5_.rates, f32[48,128]{1,0:T(8,128)S(1)} %product_2.1.before), custom_call_target="tpu_custom_call" | custom-call | flops 138412032 | bytes 1048576 | tf_op jit(solution)/shard_map/product_1/pallas_call | solution.py:300
  17.9 0.1 collective-permute-start.6
  18.0 1.6 %collective-permute-start.7 = (f32[48,128]{1,0:T(8,128)S(1)}, f32[48,128]{1,0:T(8,128)S(1)}, u32[]{:S(2)}, u32[]{:S(2)}) collective-permute-start(f32[48,128]{1,0:T(8,128)S(1)} %product_1.1.refs_0_), channel_id=1, source_target_pairs={{0,2},{1,3},{2,0},{3,1},{4,6},{5,7},{6,4},{7,5},{8,10},{9,11},{10,... | collective-permute-start | bytes 73736 | tf_op jit(solution)/shard_map/ppermute | solution.py:245
  19.6 0.3 collective-permute-start.8
  19.9 2.0 %collective-permute-done.7.refs_2_ = f32[48,128]{1,0:T(8,128)S(1)} collective-permute-done((f32[48,128]{1,0:T(8,128)S(1)}, f32[48,128]{1,0:T(8,128)S(1)}, u32[]{:S(2)}, u32[]{:S(2)}) %collective-permute-start.7) | collective-permute-done | bytes 24608 | tf_op jit(solution)/shard_map/ppermute | solution.py:245
  21.9 0.9 %collective-permute-done.8.refs_3_ = f32[48,128]{1,0:T(8,128)S(1)} collective-permute-done((f32[48,128]{1,0:T(8,128)S(1)}, f32[48,128]{1,0:T(8,128)S(1)}, u32[]{:S(2)}, u32[]{:S(2)}) %collective-permute-start.8) | collective-permute-done | bytes 24608 | tf_op jit(solution)/shard_map/ppermute | solution.py:245
  22.9 1.5 %collective-permute-start.10 = (f32[16,128]{1,0:T(8,128)S(1)}, f32[16,128]{1,0:T(8,128)S(1)}, u32[]{:S(2)}, u32[]{:S(2)}) collective-permute-start(f32[16,128]{1,0:T(8,128)S(1)} %get-tuple-element.15.refs_0_), channel_id=1, source_target_pairs={{0,8},{1,9},{2,10},{3,11},{4,12},{5,13},{6,14},{7,15},{8,0},{9,1},... | collective-permute-start | bytes 24584 | tf_op jit(solution)/shard_map/ppermute | solution.py:245
  24.4 1.7 %collective-permute-start.11 = (f32[16,128]{1,0:T(8,128)S(1)}, f32[16,128]{1,0:T(8,128)S(1)}, u32[]{:S(2)}, u32[]{:S(2)}) collective-permute-start(f32[16,128]{1,0:T(8,128)S(1)} %get-tuple-element.15.refs_0_), channel_id=1, source_target_pairs={{0,12},{1,13},{2,14},{3,15},{4,8},{5,9},{6,10},{7,11},{8,4},{9,5},... | collective-permute-start | bytes 24584 | tf_op jit(solution)/shard_map/ppermute | solution.py:245
  26.1 0.3 collective-permute-start.9
  26.4 1.1 %collective-permute-done.10.refs_2_ = f32[16,128]{1,0:T(8,128)S(1)} collective-permute-done((f32[16,128]{1,0:T(8,128)S(1)}, f32[16,128]{1,0:T(8,128)S(1)}, u32[]{:S(2)}, u32[]{:S(2)}) %collective-permute-start.10) | collective-permute-done | bytes 8224 | tf_op jit(solution)/shard_map/ppermute | solution.py:245
  27.5 2.4 %collective-permute-done.11.refs_3_ = f32[16,128]{1,0:T(8,128)S(1)} collective-permute-done((f32[16,128]{1,0:T(8,128)S(1)}, f32[16,128]{1,0:T(8,128)S(1)}, u32[]{:S(2)}, u32[]{:S(2)}) %collective-permute-start.11) | collective-permute-done | bytes 8224 | tf_op jit(solution)/shard_map/ppermute | solution.py:245
  29.9 0.8 %update.1 = (f32[4,256]{1,0:T(4,128)}, f32[4,256]{1,0:T(4,128)}, f32[4,256]{1,0:T(4,128)}) custom-call(f32[16,128]{1,0:T(8,128)S(1)} %get-tuple-element.15.refs_0_, f32[16,128]{1,0:T(8,128)S(1)} %collective-permute-done.9.refs_1_, f32[16,128]{1,0:T(8,128)S(1)} %collective-permute-done.10.refs_2_, f32[16,128]{1,0:T(8,128)S(1)} %collective-permute-done.11.refs_3_, ...), custom_call_target="tpu_custom_call" | custom-call | tf_op jit(solution)/shard_map/update/pallas_call | solution.py:323
  (13 shorter events, 0.0 us)
Async XLA Ops:
  1.7 7.0 %collective-permute-start.1 = (bf16[288,128]{1,0:T(8,128)(2,1)S(1)}, bf16[288,128]{1,0:T(8,128)(2,1)S(1)}, u32[]{:S(2)}, u32[]{:S(2)}) collective-permute-start(bf16[288,128]{1,0:T(8,128)(2,1)S(1)} %get-tuple-element.10.refs_0_), channel_id=1, source_target_pairs={{0,1},{1,0},{2,3},{3,2},{4,5},{5,4},{6,7},{7,6},{8,9},{9,8},{10,11... | collective-permute-start | bytes 221192 | tf_op jit(solution)/shard_map/ppermute | solution.py:245
  2.2 7.1 %collective-permute-start.2 = (bf16[288,128]{1,0:T(8,128)(2,1)S(1)}, bf16[288,128]{1,0:T(8,128)(2,1)S(1)}, u32[]{:S(2)}, u32[]{:S(2)}) collective-permute-start(bf16[288,128]{1,0:T(8,128)(2,1)S(1)} %get-tuple-element.10.refs_0_), channel_id=1, source_target_pairs={{0,2},{1,3},{2,0},{3,1},{4,6},{5,7},{6,4},{7,5},{8,10},{9,11},{10,... | collective-permute-start | bytes 221192 | tf_op jit(solution)/shard_map/ppermute | solution.py:245
  4.8 4.5 %collective-permute-start.3 = (bf16[288,128]{1,0:T(8,128)(2,1)S(1)}, bf16[288,128]{1,0:T(8,128)(2,1)S(1)}, u32[]{:S(2)}, u32[]{:S(2)}) collective-permute-start(bf16[288,128]{1,0:T(8,128)(2,1)S(1)} %get-tuple-element.10.refs_0_), channel_id=1, source_target_pairs={{0,3},{1,2},{2,1},{3,0},{4,7},{5,6},{6,5},{7,4},{8,11},{9,10},{10,... | collective-permute-start | bytes 221192 | tf_op jit(solution)/shard_map/ppermute | solution.py:245
  4.9 7.0 %collective-permute-start.5 = (bf16[288,128]{1,0:T(8,128)(2,1)S(1)}, bf16[288,128]{1,0:T(8,128)(2,1)S(1)}, u32[]{:S(2)}, u32[]{:S(2)}) collective-permute-start(bf16[288,128]{1,0:T(8,128)(2,1)S(1)} %get-tuple-element.10.refs_0_), channel_id=1, source_target_pairs={{0,12},{1,13},{2,14},{3,15},{4,8},{5,9},{6,10},{7,11},{8,4},{9,5},... | collective-permute-start | bytes 221192 | tf_op jit(solution)/shard_map/ppermute | solution.py:245
  8.7 6.7 %collective-permute-start.4 = (bf16[288,128]{1,0:T(8,128)(2,1)S(1)}, bf16[288,128]{1,0:T(8,128)(2,1)S(1)}, u32[]{:S(2)}, u32[]{:S(2)}) collective-permute-start(bf16[288,128]{1,0:T(8,128)(2,1)S(1)} %get-tuple-element.10.refs_0_), channel_id=1, source_target_pairs={{0,8},{1,9},{2,10},{3,11},{4,12},{5,13},{6,14},{7,15},{8,0},{9,1},... | collective-permute-start | bytes 221192 | tf_op jit(solution)/shard_map/ppermute | solution.py:245
  8.7 7.9 %collective-permute-start = (bf16[288,128]{1,0:T(8,128)(2,1)S(1)}, bf16[288,128]{1,0:T(8,128)(2,1)S(1)}, u32[]{:S(2)}, u32[]{:S(2)}) collective-permute-start(bf16[288,128]{1,0:T(8,128)(2,1)S(1)} %get-tuple-element.10.refs_0_), channel_id=1, source_target_pairs={{0,4},{1,5},{2,6},{3,7},{4,0},{5,1},{6,2},{7,3},{8,12},{9,13},{10,... | collective-permute-start | bytes 221192 | tf_op jit(solution)/shard_map/ppermute | solution.py:245
  17.9 1.9 %collective-permute-start.6 = (f32[48,128]{1,0:T(8,128)S(1)}, f32[48,128]{1,0:T(8,128)S(1)}, u32[]{:S(2)}, u32[]{:S(2)}) collective-permute-start(f32[48,128]{1,0:T(8,128)S(1)} %product_1.1.refs_0_), channel_id=1, source_target_pairs={{0,1},{1,0},{2,3},{3,2},{4,5},{5,4},{6,7},{7,6},{8,9},{9,8},{10,11... | collective-permute-start | bytes 73736 | tf_op jit(solution)/shard_map/ppermute | solution.py:245
  18.0 3.9 %collective-permute-start.7 = (f32[48,128]{1,0:T(8,128)S(1)}, f32[48,128]{1,0:T(8,128)S(1)}, u32[]{:S(2)}, u32[]{:S(2)}) collective-permute-start(f32[48,128]{1,0:T(8,128)S(1)} %product_1.1.refs_0_), channel_id=1, source_target_pairs={{0,2},{1,3},{2,0},{3,1},{4,6},{5,7},{6,4},{7,5},{8,10},{9,11},{10,... | collective-permute-start | bytes 73736 | tf_op jit(solution)/shard_map/ppermute | solution.py:245
  19.6 3.3 %collective-permute-start.8 = (f32[48,128]{1,0:T(8,128)S(1)}, f32[48,128]{1,0:T(8,128)S(1)}, u32[]{:S(2)}, u32[]{:S(2)}) collective-permute-start(f32[48,128]{1,0:T(8,128)S(1)} %product_1.1.refs_0_), channel_id=1, source_target_pairs={{0,3},{1,2},{2,1},{3,0},{4,7},{5,6},{6,5},{7,4},{8,11},{9,10},{10,... | collective-permute-start | bytes 73736 | tf_op jit(solution)/shard_map/ppermute | solution.py:245
  22.8 7.0 %copy-start = (f32[4,256]{1,0:T(4,128)S(1)}, f32[4,256]{1,0:T(4,128)}, u32[]{:S(2)}) copy-start(f32[4,256]{1,0:T(4,128)} %refs_7_.1) | copy-start | bytes 12292
  22.8 7.0 %copy-start.1 = (f32[4,256]{1,0:T(4,128)S(1)}, f32[4,256]{1,0:T(4,128)}, u32[]{:S(2)}) copy-start(f32[4,256]{1,0:T(4,128)} %refs_6_.1) | copy-start | bytes 12292
  22.8 7.0 %copy-start.2 = (f32[4,256]{1,0:T(4,128)S(1)}, f32[4,256]{1,0:T(4,128)}, u32[]{:S(2)}) copy-start(f32[4,256]{1,0:T(4,128)} %refs_5_.1) | copy-start | bytes 12292
  22.9 4.6 %collective-permute-start.10 = (f32[16,128]{1,0:T(8,128)S(1)}, f32[16,128]{1,0:T(8,128)S(1)}, u32[]{:S(2)}, u32[]{:S(2)}) collective-permute-start(f32[16,128]{1,0:T(8,128)S(1)} %get-tuple-element.15.refs_0_), channel_id=1, source_target_pairs={{0,8},{1,9},{2,10},{3,11},{4,12},{5,13},{6,14},{7,15},{8,0},{9,1},... | collective-permute-start | bytes 24584 | tf_op jit(solution)/shard_map/ppermute | solution.py:245
  24.4 5.5 %collective-permute-start.11 = (f32[16,128]{1,0:T(8,128)S(1)}, f32[16,128]{1,0:T(8,128)S(1)}, u32[]{:S(2)}, u32[]{:S(2)}) collective-permute-start(f32[16,128]{1,0:T(8,128)S(1)} %get-tuple-element.15.refs_0_), channel_id=1, source_target_pairs={{0,12},{1,13},{2,14},{3,15},{4,8},{5,9},{6,10},{7,11},{8,4},{9,5},... | collective-permute-start | bytes 24584 | tf_op jit(solution)/shard_map/ppermute | solution.py:245
  26.1 3.7 %collective-permute-start.9 = (f32[16,128]{1,0:T(8,128)S(1)}, f32[16,128]{1,0:T(8,128)S(1)}, u32[]{:S(2)}, u32[]{:S(2)}) collective-permute-start(f32[16,128]{1,0:T(8,128)S(1)} %get-tuple-element.15.refs_0_), channel_id=1, source_target_pairs={{0,4},{1,5},{2,6},{3,7},{4,0},{5,1},{6,2},{7,3},{8,12},{9,13},{10,... | collective-permute-start | bytes 24584 | tf_op jit(solution)/shard_map/ppermute | solution.py:245

commit v8 on v7

--- a/solution.py
+++ b/solution.py
@@ -7,8 +7,6 @@
 from jax.experimental import pallas as pl
 from jax.experimental.pallas import tpu as pltpu
 from jax.sharding import PartitionSpec as P
-
-CHUNK = 32
 
 
 def split_sizes(devices):
@@ -114,77 +112,67 @@
 
 def widen_rows(rows, row_wide, size):
     dims = rows[0].shape[1]
+    ones = jnp.ones((3, size), jnp.float32)
     for k, block in enumerate(rows):
-        top = top_of(block, size)
-        top = jnp.concatenate([top[3:6], top[:3]], axis=0)
-        row_wide[pl.ds(k * size, size), :] = jnp.concatenate(
-            [block[:size, :], turned([padded(top, dims)], size).astype(jnp.bfloat16)],
-            axis=1,
-        )
-
-
-def add_column(col, row_wide, rates, weights, dist, size):
+        top = jnp.concatenate([ones, *pieces_of(squares(block[:size, :]))], axis=0)
+        scaled = (block[:size, :].astype(jnp.float32) * -2.0).astype(jnp.bfloat16)
+        extra = turned([padded(top, dims)], size).astype(jnp.bfloat16)
+        row_wide[pl.ds(k * size, size), :] = jnp.concatenate([scaled, extra], axis=1)
+
+
+def add_column(col, row_wide, rates, size):
     dims = col.shape[1]
     cands = rates.shape[0] // 8
-    lo = row_wide.shape[0] // size
     top = top_of(col, size)
     steps = top[8 : 8 + cands]
-    tops = [padded(top, dims)]
-    tops += [jnp.broadcast_to(steps[c : c + 1], (dims, size)) for c in range(cands)]
-    columns = turned(tops, size)
-    for c in range(cands):
-        weights[c] = columns[:, (c + 1) * dims : (c + 2) * dims]
-    scaled = (col[:size, :].astype(jnp.float32) * -2.0).astype(jnp.bfloat16)
-    dist[...] = lax.dot_general(
-        jnp.concatenate([scaled, columns[:, :dims].astype(jnp.bfloat16)], axis=1),
-        row_wide[...],
-        (((1,), (1,)), ((), ())),
-        preferred_element_type=jnp.float32,
-    )
-    wide = size // dims
-    rate = [jnp.concatenate([rates[pl.ds(8 * c, 8), :]] * wide, axis=1) for c in range(cands)]
-
-    def body(step, total):
-        total = list(total)
-        for j in range(0, CHUNK, 8):
-            at = pl.ds(pl.multiple_of(step * CHUNK + j, 8), 8)
-            weight = [jnp.concatenate([weights[c, at, :]] * wide, axis=1) for c in range(cands)]
-            for k in range(lo):
-                here = dist[at, pl.ds(k * size, size)]
-                for c in range(cands):
-                    total[k * cands + c] += jnp.exp(here * rate[c]) * weight[c]
-        return tuple(total)
-
-    total = lax.fori_loop(
-        0,
-        size // CHUNK,
-        body,
-        (jnp.zeros((8, size), jnp.float32),) * (lo * cands),
-    )
-    total = [jnp.sum(t, axis=0, keepdims=True) for t in total]
-    return [
-        fold(jnp.concatenate(total[k * cands : (k + 1) * cands], axis=0), dims)
-        for k in range(lo)
+    top = padded(top, dims).astype(jnp.bfloat16)
+    which = lax.broadcasted_iota(jnp.int32, (cands, 1), 0)
+    only = [jnp.where(which == c, steps, 0.0).astype(jnp.bfloat16) for c in range(cands)]
+    rate = [
+        jnp.concatenate([rates[pl.ds(8 * c, 8), :]] * (size // dims), axis=1)
+        for c in range(cands)
     ]
+    parts = []
+    for k in range(row_wide.shape[0] // size):
+        at = pl.ds(k * size, size)
+        dist = lax.dot_general(
+            row_wide[at, :dims],
+            col[:size, :],
+            (((1,), (1,)), ((), ())),
+            preferred_element_type=jnp.float32,
+        )
+        dist += jnp.dot(row_wide[at, dims:], top, preferred_element_type=jnp.float32)
+        dist = dist.reshape(size // 8, 8, size)
+        part = jnp.zeros((cands, size), jnp.float32)
+        for c in range(cands):
+            kern = jnp.exp(dist * rate[c][None]).reshape(size, size)
+            part += lax.dot_general(
+                only[c],
+                kern.astype(jnp.bfloat16),
+                (((1,), (1,)), ((), ())),
+                preferred_element_type=jnp.float32,
+            )
+        parts.append(fold(part, dims))
+    return parts
 
 
 def first_kernel(lo, *refs):
     rows, refs = refs[:lo], refs[lo:]
-    own, rates, out, row_wide, weights, dist = refs
-    tall, dims = own.shape[0] // 3, own.shape[1]
+    own, rates, out, row_wide = refs
+    tall = own.shape[0] // 3
     size = row_wide.shape[0] // lo
     widen_rows(rows, row_wide, size)
-    parts = add_column(rows[0], row_wide, rates, weights, dist, size)
+    parts = add_column(rows[0], row_wide, rates, size)
     parts[0] += own[pl.ds(2 * tall, tall), :]
     for k in range(lo):
         out[pl.ds(k * tall, tall), :] = parts[k]
     out[pl.ds(lo * tall, 2 * tall), :] = own[pl.ds(0, 2 * tall), :]
 
 
-def next_kernel(lo, col, row_wide, rates, before, out, weights, dist):
+def next_kernel(lo, col, row_wide, rates, before, out):
     size = row_wide.shape[0] // lo
     tall = before.shape[0] // (lo + 2)
-    parts = add_column(col, row_wide, rates, weights, dist, size)
+    parts = add_column(col, row_wide, rates, size)
     for k in range(lo):
         at = pl.ds(k * tall, tall)
         out[at, :] = before[at, :] + parts[k]
@@ -273,38 +261,24 @@
         )
     )
 
-    rows = [packed] + [meet(packed, k) for k in range(1, lo)]
-
-    terms = size * lo * size
-    cost = pl.CostEstimate(
-        flops=4 * dims * terms + 4 * cands * terms,
-        bytes_accessed=4 * terms,
-        transcendentals=cands * terms,
-    )
-    spare = [
-        pltpu.VMEM((cands, size, dims), jnp.float32),
-        pltpu.VMEM((size, lo * size), jnp.float32),
-    ]
+    rows = [meet(points, k) for k in range(1, lo)]
+
     result = jax.ShapeDtypeStruct(((lo + 2) * tall, dims), jnp.float32)
     partial, row_wide = pl.pallas_call(
         functools.partial(first_kernel, lo),
         out_shape=(result, jax.ShapeDtypeStruct((lo * size, 2 * dims), jnp.bfloat16)),
         in_specs=[vmem] * (lo + 2),
         out_specs=(vmem, vmem),
-        scratch_shapes=spare,
         compiler_params=params,
-        cost_estimate=cost,
         name="product_own",
-    )(*rows, own, rates)
+    )(packed, *rows, own, rates)
     for k in range(hi - 1, 0, -1):
         partial = pl.pallas_call(
             functools.partial(next_kernel, lo),
             out_shape=result,
             in_specs=[vmem] * 4,
             out_specs=vmem,
-            scratch_shapes=spare,
             compiler_params=params,
-            cost_estimate=cost,
             name="product_%d" % k,
         )(meet(packed, k * lo), row_wide, rates, partial)
 

time: 30.8 us -> 33.5 us (1.088)
  Pallas kernels: 6.96 us -> 8.48 us
  waiting for transfers between devices: 9.94 us -> 10.7 us
  starting transfers between devices: 13.1 us -> 13.5 us
    pallas_call x1, Pallas kernels: 1.29 us -> 2.12 us  [per_device(): pl.pallas_call(functools.partial(first_kernel, lo), out_shape=(result, ja...]
    ppermute x12, waiting for transfers between devices: 9.94 us -> 10.7 us  [meet(): return lax.ppermute(x, 'blk', [(d, d ^ mask) for d in range(devices)])]
    pallas_call x3, Pallas kernels: 3.81 us -> 4.5 us  [per_device(): pl.pallas_call(functools.partial(next_kernel, lo), out_shape=result, in_s...]
    ppermute x12, starting transfers between devices: 13.1 us -> 13.5 us  [meet(): return lax.ppermute(x, 'blk', [(d, d ^ mask) for d in range(devices)])]
  transfers between devices with their start and end apart: 12 -> 12, of which waited for: 6 -> 6; matrix products, arithmetic and copies ran while one was open for 0% -> 0% of each run, Pallas kernels for 12% -> 19%
where the time goes in v8:
time: 33.5 us; the launch traced here: 33.3 us
  starting transfers between devices  13.5 us (40%)
  waiting for transfers between devices  10.7 us (32%)
  Pallas kernels  8.48 us (25%)
  between operations  0.68 us (2%)
    ppermute x12, starting transfers between devices, meet(): return lax.ppermute(x, 'blk', [(d, d ^ mask) for d in range(devices)])  13.5 us
    ppermute x12, waiting for transfers between devices, meet(): return lax.ppermute(x, 'blk', [(d, d ^ mask) for d in range(devices)])  10.7 us
    pallas_call x3, Pallas kernels, per_device(): pl.pallas_call(functools.partial(next_kernel, lo), out_shape=result, in_s...  4.5 us
    pallas_call x1, Pallas kernels, per_device(): pl.pallas_call(functools.partial(first_kernel, lo), out_shape=(result, ja...  2.12 us
    pallas_call x1, Pallas kernels, per_device(): pl.pallas_call(pack_kernel, out_shape=(jax.ShapeDtypeStruct((size + extra...  1.06 us
    pallas_call x1, Pallas kernels, per_device(): pl.pallas_call(functools.partial(update_kernel, hi), out_shape=(jax.Shape...  0.78 us
  transfers between devices with their start and end apart: 12, of which 6 were waited for; matrix products, arithmetic and copies ran while one was open for 0% of the time, Pallas kernels for 19%

profile of v8, /device:TPU:0, one launch (start us, length us, event | category | flops | bytes accessed | tf_op | source)
XLA Modules:
  0.0 33.3 jit_solution(11292788002698138211)
XLA Ops:
  0.6 0.5 %collective-permute-start.1 = (bf16[256,128]{1,0:T(8,128)(2,1)}, bf16[256,128]{1,0:T(8,128)(2,1)S(1)}, u32[]{:S(2)}, u32[]{:S(2)}) collective-permute-start(bf16[256,128]{1,0:T(8,128)(2,1)} %points.1), channel_id=1, source_target_pairs={{0,1},{1,0},{2,3},{3,2},{4,5},{5,4},{6,7},{7,6},{8,9},{9,8},{10,11... | collective-permute-start | bytes 196616 | tf_op jit(solution)/shard_map/ppermute | solution.py:233
  1.2 1.1 %pack.1 = (bf16[288,128]{1,0:T(8,128)(2,1)S(1)}, f32[24,128]{1,0:T(8,128)S(1)}, f32[32,128]{1,0:T(8,128)S(1)}) custom-call(bf16[256,128]{1,0:T(8,128)(2,1)} %points.1, f32[4,256]{1,0:T(4,128)} %refs_7_.1, f32[4,256]{1,0:T(4,128)} %refs_6_.1, f32[4]{0:T(128)} %length.1, f32[4]{0:T(128)} %noise.1), custom_call_target="tpu_custom_call" | custom-call | tf_op jit(solution)/shard_map/pack/pallas_call | solution.py:239
  2.2 4.7 %collective-permute-start.5 = (bf16[288,128]{1,0:T(8,128)(2,1)S(1)}, bf16[288,128]{1,0:T(8,128)(2,1)S(1)}, u32[]{:S(2)}, u32[]{:S(2)}) collective-permute-start(bf16[288,128]{1,0:T(8,128)(2,1)S(1)} %get-tuple-element.10.refs_0_), channel_id=1, source_target_pairs={{0,12},{1,13},{2,14},{3,15},{4,8},{5,9},{6,10},{7,11},{8,4},{9,5},... | collective-permute-start | bytes 221192 | tf_op jit(solution)/shard_map/ppermute | solution.py:233
  6.9 0.6 %collective-permute-start = (bf16[288,128]{1,0:T(8,128)(2,1)S(1)}, bf16[288,128]{1,0:T(8,128)(2,1)S(1)}, u32[]{:S(2)}, u32[]{:S(2)}) collective-permute-start(bf16[288,128]{1,0:T(8,128)(2,1)S(1)} %get-tuple-element.10.refs_0_), channel_id=1, source_target_pairs={{0,4},{1,5},{2,6},{3,7},{4,0},{5,1},{6,2},{7,3},{8,12},{9,13},{10,... | collective-permute-start | bytes 221192 | tf_op jit(solution)/shard_map/ppermute | solution.py:233
  7.6 1.7 %collective-permute-start.2 = (bf16[256,128]{1,0:T(8,128)(2,1)S(1)}, bf16[256,128]{1,0:T(8,128)(2,1)S(1)}, u32[]{:S(2)}, u32[]{:S(2)}) collective-permute-start(bf16[256,128]{1,0:T(8,128)(2,1)S(1)} %copy-done.3), channel_id=1, source_target_pairs={{0,2},{1,3},{2,0},{3,1},{4,6},{5,7},{6,4},{7,5},{8,10},{9,11},{10,... | collective-permute-start | bytes 196616 | tf_op jit(solution)/shard_map/ppermute | solution.py:233
  9.2 0.0 collective-permute-done.1.refs_1_
  9.2 0.0 collective-permute-start.3
  9.2 2.6 %collective-permute-done.2.refs_2_ = bf16[256,128]{1,0:T(8,128)(2,1)S(1)} collective-permute-done((bf16[256,128]{1,0:T(8,128)(2,1)S(1)}, bf16[256,128]{1,0:T(8,128)(2,1)S(1)}, u32[]{:S(2)}, u32[]{:S(2)}) %collective-permute-start.2) | collective-permute-done | bytes 65568 | tf_op jit(solution)/shard_map/ppermute | solution.py:233
  11.8 1.5 %collective-permute-done.3.refs_3_ = bf16[256,128]{1,0:T(8,128)(2,1)S(1)} collective-permute-done((bf16[256,128]{1,0:T(8,128)(2,1)S(1)}, bf16[256,128]{1,0:T(8,128)(2,1)S(1)}, u32[]{:S(2)}, u32[]{:S(2)}) %collective-permute-start.3) | collective-permute-done | bytes 65568 | tf_op jit(solution)/shard_map/ppermute | solution.py:233
  13.3 2.1 %product_own.1 = (f32[48,128]{1,0:T(8,128)S(1)}, bf16[1024,256]{1,0:T(8,128)(2,1)S(1)}) custom-call(bf16[288,128]{1,0:T(8,128)(2,1)S(1)} %get-tuple-element.10.refs_0_, bf16[256,128]{1,0:T(8,128)(2,1)S(1)} %collective-permute-done.1.refs_1_, bf16[256,128]{1,0:T(8,128)(2,1)S(1)} %collective-permute-done.2.refs_2_, ...), custom_call_target="tpu_custom_call" | custom-call | tf_op jit(solution)/shard_map/product_own/pallas_call | solution.py:267
  15.4 1.5 %product_3.1.before = f32[48,128]{1,0:T(8,128)S(1)} custom-call(bf16[288,128]{1,0:T(8,128)(2,1)S(1)} %collective-permute-done.5.col, bf16[1024,256]{1,0:T(8,128)(2,1)S(1)} %get-tuple-element.13.row_wide, f32[32,128]{1,0:T(8,128)S(1)} %get-tuple-element.12.refs_5_.rates, f32[48,128]{1,0:T(8,128)S(1)} %get-tuple-element.14.before), custom_call_target="tpu_custom_call" | custom-call | tf_op jit(solution)/shard_map/product_3/pallas_call | solution.py:276
  16.9 0.0 collective-permute-done.4.col
  16.9 1.5 %product_2.1.before = f32[48,128]{1,0:T(8,128)S(1)} custom-call(bf16[288,128]{1,0:T(8,128)(2,1)S(1)} %collective-permute-done.4.col, bf16[1024,256]{1,0:T(8,128)(2,1)S(1)} %get-tuple-element.13.row_wide, f32[32,128]{1,0:T(8,128)S(1)} %get-tuple-element.12.refs_5_.rates, f32[48,128]{1,0:T(8,128)S(1)} %product_3.1.before), custom_call_target="tpu_custom_call" | custom-call | tf_op jit(solution)/shard_map/product_2/pallas_call | solution.py:276
  18.4 1.5 %product_1.1.refs_0_ = f32[48,128]{1,0:T(8,128)S(1)} custom-call(bf16[288,128]{1,0:T(8,128)(2,1)S(1)} %collective-permute-done.col, bf16[1024,256]{1,0:T(8,128)(2,1)S(1)} %get-tuple-element.13.row_wide, f32[32,128]{1,0:T(8,128)S(1)} %get-tuple-element.12.refs_5_.rates, f32[48,128]{1,0:T(8,128)S(1)} %product_2.1.before), custom_call_target="tpu_custom_call" | custom-call | tf_op jit(solution)/shard_map/product_1/pallas_call | solution.py:276
  19.9 1.5 %collective-permute-start.7 = (f32[48,128]{1,0:T(8,128)S(1)}, f32[48,128]{1,0:T(8,128)S(1)}, u32[]{:S(2)}, u32[]{:S(2)}) collective-permute-start(f32[48,128]{1,0:T(8,128)S(1)} %product_1.1.refs_0_), channel_id=1, source_target_pairs={{0,2},{1,3},{2,0},{3,1},{4,6},{5,7},{6,4},{7,5},{8,10},{9,11},{10,... | collective-permute-start | bytes 73736 | tf_op jit(solution)/shard_map/ppermute | solution.py:233
  21.5 0.4 %collective-permute-start.8 = (f32[48,128]{1,0:T(8,128)S(1)}, f32[48,128]{1,0:T(8,128)S(1)}, u32[]{:S(2)}, u32[]{:S(2)}) collective-permute-start(f32[48,128]{1,0:T(8,128)S(1)} %product_1.1.refs_0_), channel_id=1, source_target_pairs={{0,3},{1,2},{2,1},{3,0},{4,7},{5,6},{6,5},{7,4},{8,11},{9,10},{10,... | collective-permute-start | bytes 73736 | tf_op jit(solution)/shard_map/ppermute | solution.py:233
  21.8 2.0 %collective-permute-done.7.refs_2_ = f32[48,128]{1,0:T(8,128)S(1)} collective-permute-done((f32[48,128]{1,0:T(8,128)S(1)}, f32[48,128]{1,0:T(8,128)S(1)}, u32[]{:S(2)}, u32[]{:S(2)}) %collective-permute-start.7) | collective-permute-done | bytes 24608 | tf_op jit(solution)/shard_map/ppermute | solution.py:233
  23.8 1.1 %collective-permute-done.8.refs_3_ = f32[48,128]{1,0:T(8,128)S(1)} collective-permute-done((f32[48,128]{1,0:T(8,128)S(1)}, f32[48,128]{1,0:T(8,128)S(1)}, u32[]{:S(2)}, u32[]{:S(2)}) %collective-permute-start.8) | collective-permute-done | bytes 24608 | tf_op jit(solution)/shard_map/ppermute | solution.py:233
  25.0 2.0 %collective-permute-start.10 = (f32[16,128]{1,0:T(8,128)S(1)}, f32[16,128]{1,0:T(8,128)S(1)}, u32[]{:S(2)}, u32[]{:S(2)}) collective-permute-start(f32[16,128]{1,0:T(8,128)S(1)} %get-tuple-element.15.refs_0_), channel_id=1, source_target_pairs={{0,8},{1,9},{2,10},{3,11},{4,12},{5,13},{6,14},{7,15},{8,0},{9,1},... | collective-permute-start | bytes 24584 | tf_op jit(solution)/shard_map/ppermute | solution.py:233
  27.0 1.8 %collective-permute-start.11 = (f32[16,128]{1,0:T(8,128)S(1)}, f32[16,128]{1,0:T(8,128)S(1)}, u32[]{:S(2)}, u32[]{:S(2)}) collective-permute-start(f32[16,128]{1,0:T(8,128)S(1)} %get-tuple-element.15.refs_0_), channel_id=1, source_target_pairs={{0,12},{1,13},{2,14},{3,15},{4,8},{5,9},{6,10},{7,11},{8,4},{9,5},... | collective-permute-start | bytes 24584 | tf_op jit(solution)/shard_map/ppermute | solution.py:233
  28.8 0.3 collective-permute-start.9
  29.0 0.5 %collective-permute-done.10.refs_2_ = f32[16,128]{1,0:T(8,128)S(1)} collective-permute-done((f32[16,128]{1,0:T(8,128)S(1)}, f32[16,128]{1,0:T(8,128)S(1)}, u32[]{:S(2)}, u32[]{:S(2)}) %collective-permute-start.10) | collective-permute-done | bytes 8224 | tf_op jit(solution)/shard_map/ppermute | solution.py:233
  29.6 2.9 %collective-permute-done.11.refs_3_ = f32[16,128]{1,0:T(8,128)S(1)} collective-permute-done((f32[16,128]{1,0:T(8,128)S(1)}, f32[16,128]{1,0:T(8,128)S(1)}, u32[]{:S(2)}, u32[]{:S(2)}) %collective-permute-start.11) | collective-permute-done | bytes 8224 | tf_op jit(solution)/shard_map/ppermute | solution.py:233
  32.5 0.8 %update.1 = (f32[4,256]{1,0:T(4,128)}, f32[4,256]{1,0:T(4,128)}, f32[4,256]{1,0:T(4,128)}) custom-call(f32[16,128]{1,0:T(8,128)S(1)} %get-tuple-element.15.refs_0_, f32[16,128]{1,0:T(8,128)S(1)} %collective-permute-done.9.refs_1_, f32[16,128]{1,0:T(8,128)S(1)} %collective-permute-done.10.refs_2_, f32[16,128]{1,0:T(8,128)S(1)} %collective-permute-done.11.refs_3_, ...), custom_call_target="tpu_custom_call" | custom-call | tf_op jit(solution)/shard_map/update/pallas_call | solution.py:297
  (15 shorter events, 0.0 us)
Async XLA Ops:
  0.6 6.9 %copy-start.3 = (bf16[256,128]{1,0:T(8,128)(2,1)S(1)}, bf16[256,128]{1,0:T(8,128)(2,1)}, u32[]{:S(2)}) copy-start(bf16[256,128]{1,0:T(8,128)(2,1)} %points.1) | copy-start | bytes 196612
  0.6 8.6 %collective-permute-start.1 = (bf16[256,128]{1,0:T(8,128)(2,1)}, bf16[256,128]{1,0:T(8,128)(2,1)S(1)}, u32[]{:S(2)}, u32[]{:S(2)}) collective-permute-start(bf16[256,128]{1,0:T(8,128)(2,1)} %points.1), channel_id=1, source_target_pairs={{0,1},{1,0},{2,3},{3,2},{4,5},{5,4},{6,7},{7,6},{8,9},{9,8},{10,11... | collective-permute-start | bytes 196616 | tf_op jit(solution)/shard_map/ppermute | solution.py:233
  2.2 13.2 %collective-permute-start.5 = (bf16[288,128]{1,0:T(8,128)(2,1)S(1)}, bf16[288,128]{1,0:T(8,128)(2,1)S(1)}, u32[]{:S(2)}, u32[]{:S(2)}) collective-permute-start(bf16[288,128]{1,0:T(8,128)(2,1)S(1)} %get-tuple-element.10.refs_0_), channel_id=1, source_target_pairs={{0,12},{1,13},{2,14},{3,15},{4,8},{5,9},{6,10},{7,11},{8,4},{9,5},... | collective-permute-start | bytes 221192 | tf_op jit(solution)/shard_map/ppermute | solution.py:233
  6.9 10.0 %collective-permute-start.4 = (bf16[288,128]{1,0:T(8,128)(2,1)S(1)}, bf16[288,128]{1,0:T(8,128)(2,1)S(1)}, u32[]{:S(2)}, u32[]{:S(2)}) collective-permute-start(bf16[288,128]{1,0:T(8,128)(2,1)S(1)} %get-tuple-element.10.refs_0_), channel_id=1, source_target_pairs={{0,8},{1,9},{2,10},{3,11},{4,12},{5,13},{6,14},{7,15},{8,0},{9,1},... | collective-permute-start | bytes 221192 | tf_op jit(solution)/shard_map/ppermute | solution.py:233
  6.9 11.5 %collective-permute-start = (bf16[288,128]{1,0:T(8,128)(2,1)S(1)}, bf16[288,128]{1,0:T(8,128)(2,1)S(1)}, u32[]{:S(2)}, u32[]{:S(2)}) collective-permute-start(bf16[288,128]{1,0:T(8,128)(2,1)S(1)} %get-tuple-element.10.refs_0_), channel_id=1, source_target_pairs={{0,4},{1,5},{2,6},{3,7},{4,0},{5,1},{6,2},{7,3},{8,12},{9,13},{10,... | collective-permute-start | bytes 221192 | tf_op jit(solution)/shard_map/ppermute | solution.py:233
  7.6 4.3 %collective-permute-start.2 = (bf16[256,128]{1,0:T(8,128)(2,1)S(1)}, bf16[256,128]{1,0:T(8,128)(2,1)S(1)}, u32[]{:S(2)}, u32[]{:S(2)}) collective-permute-start(bf16[256,128]{1,0:T(8,128)(2,1)S(1)} %copy-done.3), channel_id=1, source_target_pairs={{0,2},{1,3},{2,0},{3,1},{4,6},{5,7},{6,4},{7,5},{8,10},{9,11},{10,... | collective-permute-start | bytes 196616 | tf_op jit(solution)/shard_map/ppermute | solution.py:233
  9.2 4.1 %collective-permute-start.3 = (bf16[256,128]{1,0:T(8,128)(2,1)S(1)}, bf16[256,128]{1,0:T(8,128)(2,1)S(1)}, u32[]{:S(2)}, u32[]{:S(2)}) collective-permute-start(bf16[256,128]{1,0:T(8,128)(2,1)S(1)} %copy-done.3), channel_id=1, source_target_pairs={{0,3},{1,2},{2,1},{3,0},{4,7},{5,6},{6,5},{7,4},{8,11},{9,10},{10,... | collective-permute-start | bytes 196616 | tf_op jit(solution)/shard_map/ppermute | solution.py:233
  19.9 1.9 %collective-permute-start.6 = (f32[48,128]{1,0:T(8,128)S(1)}, f32[48,128]{1,0:T(8,128)S(1)}, u32[]{:S(2)}, u32[]{:S(2)}) collective-permute-start(f32[48,128]{1,0:T(8,128)S(1)} %product_1.1.refs_0_), channel_id=1, source_target_pairs={{0,1},{1,0},{2,3},{3,2},{4,5},{5,4},{6,7},{7,6},{8,9},{9,8},{10,11... | collective-permute-start | bytes 73736 | tf_op jit(solution)/shard_map/ppermute | solution.py:233
  19.9 3.9 %collective-permute-start.7 = (f32[48,128]{1,0:T(8,128)S(1)}, f32[48,128]{1,0:T(8,128)S(1)}, u32[]{:S(2)}, u32[]{:S(2)}) collective-permute-start(f32[48,128]{1,0:T(8,128)S(1)} %product_1.1.refs_0_), channel_id=1, source_target_pairs={{0,2},{1,3},{2,0},{3,1},{4,6},{5,7},{6,4},{7,5},{8,10},{9,11},{10,... | collective-permute-start | bytes 73736 | tf_op jit(solution)/shard_map/ppermute | solution.py:233
  21.5 3.5 %collective-permute-start.8 = (f32[48,128]{1,0:T(8,128)S(1)}, f32[48,128]{1,0:T(8,128)S(1)}, u32[]{:S(2)}, u32[]{:S(2)}) collective-permute-start(f32[48,128]{1,0:T(8,128)S(1)} %product_1.1.refs_0_), channel_id=1, source_target_pairs={{0,3},{1,2},{2,1},{3,0},{4,7},{5,6},{6,5},{7,4},{8,11},{9,10},{10,... | collective-permute-start | bytes 73736 | tf_op jit(solution)/shard_map/ppermute | solution.py:233
  24.9 7.6 %copy-start = (f32[4,256]{1,0:T(4,128)S(1)}, f32[4,256]{1,0:T(4,128)}, u32[]{:S(2)}) copy-start(f32[4,256]{1,0:T(4,128)} %refs_7_.1) | copy-start | bytes 12292
  24.9 7.6 %copy-start.1 = (f32[4,256]{1,0:T(4,128)S(1)}, f32[4,256]{1,0:T(4,128)}, u32[]{:S(2)}) copy-start(f32[4,256]{1,0:T(4,128)} %refs_6_.1) | copy-start | bytes 12292
  24.9 7.6 %copy-start.2 = (f32[4,256]{1,0:T(4,128)S(1)}, f32[4,256]{1,0:T(4,128)}, u32[]{:S(2)}) copy-start(f32[4,256]{1,0:T(4,128)} %refs_5_.1) | copy-start | bytes 12292
  25.0 4.6 %collective-permute-start.10 = (f32[16,128]{1,0:T(8,128)S(1)}, f32[16,128]{1,0:T(8,128)S(1)}, u32[]{:S(2)}, u32[]{:S(2)}) collective-permute-start(f32[16,128]{1,0:T(8,128)S(1)} %get-tuple-element.15.refs_0_), channel_id=1, source_target_pairs={{0,8},{1,9},{2,10},{3,11},{4,12},{5,13},{6,14},{7,15},{8,0},{9,1},... | collective-permute-start | bytes 24584 | tf_op jit(solution)/shard_map/ppermute | solution.py:233
  27.0 5.5 %collective-permute-start.11 = (f32[16,128]{1,0:T(8,128)S(1)}, f32[16,128]{1,0:T(8,128)S(1)}, u32[]{:S(2)}, u32[]{:S(2)}) collective-permute-start(f32[16,128]{1,0:T(8,128)S(1)} %get-tuple-element.15.refs_0_), channel_id=1, source_target_pairs={{0,12},{1,13},{2,14},{3,15},{4,8},{5,9},{6,10},{7,11},{8,4},{9,5},... | collective-permute-start | bytes 24584 | tf_op jit(solution)/shard_map/ppermute | solution.py:233
  28.8 3.7 %collective-permute-start.9 = (f32[16,128]{1,0:T(8,128)S(1)}, f32[16,128]{1,0:T(8,128)S(1)}, u32[]{:S(2)}, u32[]{:S(2)}) collective-permute-start(f32[16,128]{1,0:T(8,128)S(1)} %get-tuple-element.15.refs_0_), channel_id=1, source_target_pairs={{0,4},{1,5},{2,6},{3,7},{4,0},{5,1},{6,2},{7,3},{8,12},{9,13},{10,... | collective-permute-start | bytes 24584 | tf_op jit(solution)/shard_map/ppermute | solution.py:233

commit v9 on v6

--- a/solution.py
+++ b/solution.py
@@ -8,14 +8,14 @@
 from jax.experimental.pallas import tpu as pltpu
 from jax.sharding import PartitionSpec as P
 
-LOG2E = 1.4426950408889634
+
 CHUNK = 32
 
 
 def split_sizes(devices):
     lo = max(d for d in range(1, math.isqrt(devices) + 1) if devices % d == 0)
     hi = devices // lo
-    assert hi & (hi - 1) == lo & (lo - 1) == 0
+    assert lo > 1 and hi & (hi - 1) == lo & (lo - 1) == 0
     return hi, lo
 
 
@@ -78,8 +78,8 @@
     sigma = jnp.zeros((cands, 1), jnp.float32)
     for c in range(cands):
         sigma = jnp.where(which == c, noise_in[c], sigma)
-        rate = (-0.5 * LOG2E) / (length_in[c] * length_in[c])
-        rates[pl.ds(8 * c, 8), :] = jnp.full((8, size), rate, jnp.float32)
+        rate = -0.5 / (length_in[c] * length_in[c])
+        rates[pl.ds(8 * c, 8), :] = jnp.full((8, dims), rate, jnp.float32)
     tall = own.shape[0] // 3
     for i, wide in enumerate((step, rest_in[...], sigma * step)):
         own[pl.ds(i * tall, tall), :] = fold(wide, dims)
@@ -91,54 +91,78 @@
     packed[size:, :] = fold(top, dims).astype(jnp.bfloat16)
 
 
+def turned(tops, size):
+    row = lax.broadcasted_iota(jnp.int32, (size, size), 0)
+    lane = lax.broadcasted_iota(jnp.int32, (size, size), 1)
+    return lax.dot_general(
+        (row == lane).astype(jnp.bfloat16),
+        jnp.concatenate(tops, axis=0).astype(jnp.bfloat16),
+        (((1,), (1,)), ((), ())),
+        preferred_element_type=jnp.float32,
+    )
+
+
+def top_of(block, size):
+    lines = (block.shape[0] - size) * block.shape[1] // size
+    return unfold(block[size:, :].astype(jnp.float32), lines)
+
+
+def padded(top, dims):
+    return jnp.concatenate(
+        [top, jnp.zeros((dims - top.shape[0], top.shape[1]), jnp.float32)], axis=0
+    )
+
+
+def widen_rows(rows, row_wide, size):
+    dims = rows[0].shape[1]
+    ones = jnp.ones((3, size), jnp.float32)
+    for k, block in enumerate(rows):
+        top = jnp.concatenate([ones, *pieces_of(squares(block[:size, :]))], axis=0)
+        scaled = (block[:size, :].astype(jnp.float32) * -2.0).astype(jnp.bfloat16)
+        extra = turned([padded(top, dims)], size).astype(jnp.bfloat16)
+        row_wide[pl.ds(k * size, size), :] = jnp.concatenate([scaled, extra], axis=1)
+
+
 def product_kernel(lo, hi, cands, *refs):
     cols, refs = refs[:hi], refs[hi:]
     rows, refs = refs[: lo - 1], refs[lo - 1 :]
     own, rates, out, row_wide, weights, dist = refs
-    rows = (cols[0], *rows)
-    tall = own.shape[0] // 3
-    dims = own.shape[1]
-    size = rates.shape[1]
-    lines = (cols[0].shape[0] - size) * dims // size
-
-    def extra(top):
-        top = jnp.concatenate(
-            [top, jnp.zeros((dims - top.shape[0], size), jnp.float32)], axis=0
-        )
-        return top.T
-
-    for k in range(lo):
-        top = unfold(rows[k][size:, :].astype(jnp.float32), lines)
-        top = jnp.concatenate([top[3:6], top[:3], jnp.zeros((2, size), jnp.float32)])
-        row_wide[pl.ds(k * size, size), :] = jnp.concatenate(
-            [rows[k][:size, :], extra(top).astype(jnp.bfloat16)], axis=1
-        )
+    tall, dims = own.shape[0] // 3, own.shape[1]
+    size = row_wide.shape[0] // lo
+    wide = size // dims
+    widen_rows((cols[0], *rows), row_wide, size)
     for h in range(hi):
-        top = extra(unfold(cols[h][size:, :].astype(jnp.float32), lines))
+        top = top_of(cols[h], size)
+        steps = top[8 : 8 + cands]
+        tops = [padded(top, dims)]
+        tops += [jnp.broadcast_to(steps[c : c + 1], (dims, size)) for c in range(cands)]
+        columns = turned(tops, size)
+        at = pl.ds(h * size, size)
         for c in range(cands):
-            weights[c, pl.ds(h * size, size), :] = jnp.broadcast_to(
-                top[:, 8 + c : 9 + c], (size, dims)
-            )
-        scaled = (cols[h][:size, :].astype(jnp.float32) * -2.0).astype(jnp.bfloat16)
-        dist[pl.ds(h * size, size), :] = lax.dot_general(
-            jnp.concatenate([scaled, top.astype(jnp.bfloat16)], axis=1),
+            weights[c, at, :] = columns[:, (c + 1) * dims : (c + 2) * dims]
+        dist[at, :] = lax.dot_general(
+            jnp.concatenate(
+                [cols[h][:size, :], columns[:, :dims].astype(jnp.bfloat16)], axis=1
+            ),
             row_wide[...],
             (((1,), (1,)), ((), ())),
             preferred_element_type=jnp.float32,
         )
+    rate = [
+        jnp.concatenate([rates[pl.ds(8 * c, 8), :]] * wide, axis=1) for c in range(cands)
+    ]
 
     def body(step, total):
         total = list(total)
         for j in range(0, CHUNK, 8):
             at = pl.ds(pl.multiple_of(step * CHUNK + j, 8), 8)
+            weight = [
+                jnp.concatenate([weights[c, at, :]] * wide, axis=1) for c in range(cands)
+            ]
             for k in range(lo):
                 here = dist[at, pl.ds(k * size, size)]
                 for c in range(cands):
-                    weight = jnp.concatenate(
-                        [weights[c, at, :]] * (size // dims), axis=1
-                    )
-                    kern = jnp.exp2(here * rates[pl.ds(8 * c, 8), :])
-                    total[k * cands + c] += kern * weight
+                    total[k * cands + c] += jnp.exp(here * rate[c]) * weight[c]
         return tuple(total)
 
     total = lax.fori_loop(
@@ -147,15 +171,21 @@
         body,
         (jnp.zeros((8, size), jnp.float32),) * (lo * cands),
     )
+    total = [jnp.sum(t, axis=0, keepdims=True) for t in total]
     for k in range(lo):
-        part = [
-            jnp.sum(total[k * cands + c], axis=0, keepdims=True) for c in range(cands)
-        ]
-        part = fold(jnp.concatenate(part, axis=0), dims)
+        part = fold(jnp.concatenate(total[k * cands : (k + 1) * cands], axis=0), dims)
         if k == 0:
             part += own[pl.ds(2 * tall, tall), :]
         out[pl.ds(k * tall, tall), :] = part
     out[pl.ds(lo * tall, 2 * tall), :] = own[pl.ds(0, 2 * tall), :]
+
+
+def add_kernel(*refs):
+    *parts, out = refs
+    total = parts[0][...]
+    for part in parts[1:]:
+        total = total + part[...]
+    out[...] = total
 
 
 def sums_kernel(cands, *refs):
@@ -179,13 +209,11 @@
         )
 
 
-def update_kernel(hi, *refs):
-    sums, refs = refs[:hi], refs[hi:]
+def update_kernel(*refs):
+    sums, refs = refs[:3], refs[3:]
     image, solution, residual, direction, out_s, out_r, out_d = refs
     cands = solution.shape[0]
-    total = sums[0][...]
-    for h in range(1, hi):
-        total = total + sums[h][...]
+    total = sums[0][...] + (sums[1][...] + sums[2][...])
     total = jnp.sum(total, axis=1, keepdims=True)
     norm, curve, cross, square = (
         total[i * cands : (i + 1) * cands] for i in range(4)
@@ -207,8 +235,9 @@
     tall = cands * size // dims
     extra = -(-(8 + cands) // 16) * 16 * size // dims
 
-    def meet(x, mask):
-        return lax.ppermute(x, "blk", [(d, d ^ mask) for d in range(devices)])
+    def meet(x, mask, core=None):
+        pairs = [(d, d ^ mask) for d in range(devices) if core in (None, d % 2)]
+        return lax.ppermute(x, "blk", pairs)
 
     vmem = pl.BlockSpec(memory_space=pltpu.VMEM)
     hbm = pl.BlockSpec(memory_space=pltpu.HBM)
@@ -219,7 +248,7 @@
         out_shape=(
             jax.ShapeDtypeStruct((size + extra, dims), jnp.bfloat16),
             jax.ShapeDtypeStruct((3 * tall, dims), jnp.float32),
-            jax.ShapeDtypeStruct((8 * cands, size), jnp.float32),
+            jax.ShapeDtypeStruct((8 * cands, dims), jnp.float32),
         ),
         in_specs=[hbm] * 5,
         out_specs=(vmem,) * 3,
@@ -239,15 +268,9 @@
         )
     )
 
+    rows = [meet(points, k) for k in range(1, lo)]
+
     cols = [packed] + [meet(packed, k * lo) for k in range(1, hi)]
-    rows = [packed] + [meet(packed, k) for k in range(1, lo) if k == 1 or k % 2 == 0]
-    if lo > 2:
-        rows = [packed, rows[1]] + [
-            block
-            for k in range(2, lo, 2)
-            for block in (rows[k // 2 + 1], meet(rows[k // 2 + 1], 1))
-        ]
-
     partial = pl.pallas_call(
         functools.partial(product_kernel, lo, hi, cands),
         out_shape=jax.ShapeDtypeStruct(((lo + 2) * tall, dims), jnp.float32),
@@ -260,7 +283,7 @@
         ],
         compiler_params=params,
         name="product",
-    )(*cols, *rows[1:], own, rates)
+    )(*cols, *rows, own, rates)
 
     image, sums = pl.pallas_call(
         functools.partial(sums_kernel, cands),
@@ -274,14 +297,23 @@
         name="sums",
     )(partial, *(meet(partial, k) for k in range(1, lo)))
 
+    others = pl.pallas_call(
+        add_kernel,
+        out_shape=jax.ShapeDtypeStruct(sums.shape, jnp.float32),
+        in_specs=[vmem] * (hi - 1),
+        out_specs=vmem,
+        compiler_params=params,
+        name="others",
+    )(*(meet(sums, k * lo, int(2 * k >= hi)) for k in range(1, hi)))
+
     return pl.pallas_call(
-        functools.partial(update_kernel, hi),
+        update_kernel,
         out_shape=(jax.ShapeDtypeStruct((cands, size), jnp.float32),) * 3,
-        in_specs=[vmem] * (hi + 4),
+        in_specs=[vmem] * 7,
         out_specs=(vmem,) * 3,
         compiler_params=params,
         name="update",
-    )(sums, *(meet(sums, k * lo) for k in range(1, hi)), image, solution, residual, direction)
+    )(sums, others, meet(others, 1), image, solution, residual, direction)
 
 
 def solution(mesh):

time: 31 us -> 35.2 us (1.14)
  starting transfers between devices: 13.8 us -> 16.6 us
  Pallas kernels: 5.62 us -> 7.01 us
    ppermute x12 -> x13, starting transfers between devices: 13.8 us -> 16.6 us  [meet(): return lax.ppermute(x, 'blk', pairs)]
    pallas_call x1, Pallas kernels: 3.76 us -> 5.15 us  [per_device(): pl.pallas_call(functools.partial(product_kernel, lo, hi, cands), out_shap...]
    ppermute x12 -> x13, waiting for transfers between devices: 10.8 us -> 10.7 us  [meet(): return lax.ppermute(x, 'blk', pairs)]
    pallas_call x1 -> x2, Pallas kernels: 0.78 us -> 0.78 us  [the longest x1 0.77 us: per_device(): pl.pallas_call(update_kernel, out_shape=(jax.ShapeDtypeStruct((cands, siz...]
  transfers between devices with their start and end apart: 12 -> 13, of which waited for: 6 -> 7; matrix products, arithmetic and copies ran while one was open for 0% -> 0% of each run, Pallas kernels for 0% -> 3%
where the time goes in v9:
time: 35.2 us; the launch traced here: 35 us
  starting transfers between devices  16.6 us (47%)
  waiting for transfers between devices  10.7 us (30%)
  Pallas kernels  7.01 us (20%)
  between operations  0.71 us (2%)
    ppermute x13, starting transfers between devices, meet(): return lax.ppermute(x, 'blk', pairs)  16.6 us
    ppermute x13, waiting for transfers between devices, meet(): return lax.ppermute(x, 'blk', pairs)  10.7 us
    pallas_call x1, Pallas kernels, per_device(): pl.pallas_call(functools.partial(product_kernel, lo, hi, cands), out_shap...  5.15 us
    pallas_call x1, Pallas kernels, per_device(): pl.pallas_call(pack_kernel, out_shape=(jax.ShapeDtypeStruct((size + extra...  1.06 us
    pallas_call x1, Pallas kernels, per_device(): pl.pallas_call(update_kernel, out_shape=(jax.ShapeDtypeStruct((cands, siz...  0.77 us
  transfers between devices with their start and end apart: 13, of which 7 were waited for; matrix products, arithmetic and copies ran while one was open for 0% of the time, Pallas kernels for 3%

profile of v9, /device:TPU:0, one launch (start us, length us, event | category | flops | bytes accessed | tf_op | source)
XLA Modules:
  0.0 35.0 jit_solution(3009362193638389167)
XLA Ops:
  0.6 0.5 %collective-permute-start.3 = (bf16[256,128]{1,0:T(8,128)(2,1)}, bf16[256,128]{1,0:T(8,128)(2,1)S(1)}, u32[]{:S(2)}, u32[]{:S(2)}) collective-permute-start(bf16[256,128]{1,0:T(8,128)(2,1)} %points.1), channel_id=1, source_target_pairs={{0,1},{1,0},{2,3},{3,2},{4,5},{5,4},{6,7},{7,6},{8,9},{9,8},{10,11... | collective-permute-start | bytes 196616 | tf_op jit(solution)/shard_map/ppermute | solution.py:240
  1.2 1.1 %pack.1 = (bf16[288,128]{1,0:T(8,128)(2,1)S(1)}, f32[24,128]{1,0:T(8,128)S(1)}, f32[32,128]{1,0:T(8,128)S(1)}) custom-call(bf16[256,128]{1,0:T(8,128)(2,1)} %points.1, f32[4,256]{1,0:T(4,128)} %refs_6_.1, f32[4,256]{1,0:T(4,128)} %refs_5_.1, f32[4]{0:T(128)} %length.1, f32[4]{0:T(128)} %noise.1), custom_call_target="tpu_custom_call" | custom-call | tf_op jit(solution)/shard_map/pack/pallas_call | solution.py:246
  2.2 4.7 %collective-permute-start.2 = (bf16[288,128]{1,0:T(8,128)(2,1)S(1)}, bf16[288,128]{1,0:T(8,128)(2,1)S(1)}, u32[]{:S(2)}, u32[]{:S(2)}) collective-permute-start(bf16[288,128]{1,0:T(8,128)(2,1)S(1)} %get-tuple-element.8.refs_0_), channel_id=1, source_target_pairs={{0,12},{1,13},{2,14},{3,15},{4,8},{5,9},{6,10},{7,11},{8,4},{9,5},... | collective-permute-start | bytes 221192 | tf_op jit(solution)/shard_map/ppermute | solution.py:240
  6.9 0.0 collective-permute-start.1
  6.9 0.6 %collective-permute-start = (bf16[288,128]{1,0:T(8,128)(2,1)S(1)}, bf16[288,128]{1,0:T(8,128)(2,1)S(1)}, u32[]{:S(2)}, u32[]{:S(2)}) collective-permute-start(bf16[288,128]{1,0:T(8,128)(2,1)S(1)} %get-tuple-element.8.refs_0_), channel_id=1, source_target_pairs={{0,4},{1,5},{2,6},{3,7},{4,0},{5,1},{6,2},{7,3},{8,12},{9,13},{10,... | collective-permute-start | bytes 221192 | tf_op jit(solution)/shard_map/ppermute | solution.py:240
  7.6 1.1 %collective-permute-start.5 = (bf16[256,128]{1,0:T(8,128)(2,1)S(1)}, bf16[256,128]{1,0:T(8,128)(2,1)S(1)}, u32[]{:S(2)}, u32[]{:S(2)}) collective-permute-start(bf16[256,128]{1,0:T(8,128)(2,1)S(1)} %copy-done.3), channel_id=1, source_target_pairs={{0,3},{1,2},{2,1},{3,0},{4,7},{5,6},{6,5},{7,4},{8,11},{9,10},{10,... | collective-permute-start | bytes 196616 | tf_op jit(solution)/shard_map/ppermute | solution.py:240
  8.6 0.7 %collective-permute-start.4 = (bf16[256,128]{1,0:T(8,128)(2,1)S(1)}, bf16[256,128]{1,0:T(8,128)(2,1)S(1)}, u32[]{:S(2)}, u32[]{:S(2)}) collective-permute-start(bf16[256,128]{1,0:T(8,128)(2,1)S(1)} %copy-done.3), channel_id=1, source_target_pairs={{0,2},{1,3},{2,0},{3,1},{4,6},{5,7},{6,4},{7,5},{8,10},{9,11},{10,... | collective-permute-start | bytes 196616 | tf_op jit(solution)/shard_map/ppermute | solution.py:240
  9.3 2.4 %collective-permute-done.5.refs_6_ = bf16[256,128]{1,0:T(8,128)(2,1)S(1)} collective-permute-done((bf16[256,128]{1,0:T(8,128)(2,1)S(1)}, bf16[256,128]{1,0:T(8,128)(2,1)S(1)}, u32[]{:S(2)}, u32[]{:S(2)}) %collective-permute-start.5) | collective-permute-done | bytes 65568 | tf_op jit(solution)/shard_map/ppermute | solution.py:240
  11.7 1.6 %collective-permute-done.4.refs_5_ = bf16[256,128]{1,0:T(8,128)(2,1)S(1)} collective-permute-done((bf16[256,128]{1,0:T(8,128)(2,1)S(1)}, bf16[256,128]{1,0:T(8,128)(2,1)S(1)}, u32[]{:S(2)}, u32[]{:S(2)}) %collective-permute-start.4) | collective-permute-done | bytes 65568 | tf_op jit(solution)/shard_map/ppermute | solution.py:240
  13.4 0.0 collective-permute-done.2.refs_3_
  13.4 0.4 %collective-permute-done.1.refs_2_ = bf16[288,128]{1,0:T(8,128)(2,1)S(1)} collective-permute-done((bf16[288,128]{1,0:T(8,128)(2,1)S(1)}, bf16[288,128]{1,0:T(8,128)(2,1)S(1)}, u32[]{:S(2)}, u32[]{:S(2)}) %collective-permute-start.1) | collective-permute-done | bytes 73760 | tf_op jit(solution)/shard_map/ppermute | solution.py:240
  13.7 5.2 %product.1.refs_0_ = f32[48,128]{1,0:T(8,128)S(1)} custom-call(bf16[288,128]{1,0:T(8,128)(2,1)S(1)} %get-tuple-element.8.refs_0_, bf16[288,128]{1,0:T(8,128)(2,1)S(1)} %collective-permute-done.refs_1_, bf16[288,128]{1,0:T(8,128)(2,1)S(1)} %collective-permute-done.1.refs_2_, bf16[288,128]{1,0:T(8,128)(2,1)S(1)} %collective-permute-done.2.refs_3_, ...), custom_call_target="tpu_custom_call" | custom-call | tf_op jit(solution)/shard_map/product/pallas_call | solution.py:274
  18.9 1.1 %collective-permute-start.8 = (f32[48,128]{1,0:T(8,128)S(1)}, f32[48,128]{1,0:T(8,128)S(1)}, u32[]{:S(2)}, u32[]{:S(2)}) collective-permute-start(f32[48,128]{1,0:T(8,128)S(1)} %product.1.refs_0_), channel_id=1, source_target_pairs={{0,3},{1,2},{2,1},{3,0},{4,7},{5,6},{6,5},{7,4},{8,11},{9,10},{10,... | collective-permute-start | bytes 73736 | tf_op jit(solution)/shard_map/ppermute | solution.py:240
  19.9 0.6 %collective-permute-start.7 = (f32[48,128]{1,0:T(8,128)S(1)}, f32[48,128]{1,0:T(8,128)S(1)}, u32[]{:S(2)}, u32[]{:S(2)}) collective-permute-start(f32[48,128]{1,0:T(8,128)S(1)} %product.1.refs_0_), channel_id=1, source_target_pairs={{0,2},{1,3},{2,0},{3,1},{4,6},{5,7},{6,4},{7,5},{8,10},{9,11},{10,... | collective-permute-start | bytes 73736 | tf_op jit(solution)/shard_map/ppermute | solution.py:240
  20.6 0.3 collective-permute-start.6
  20.8 1.6 %collective-permute-done.8.refs_3_ = f32[48,128]{1,0:T(8,128)S(1)} collective-permute-done((f32[48,128]{1,0:T(8,128)S(1)}, f32[48,128]{1,0:T(8,128)S(1)}, u32[]{:S(2)}, u32[]{:S(2)}) %collective-permute-start.8) | collective-permute-done | bytes 24608 | tf_op jit(solution)/shard_map/ppermute | solution.py:240
  22.4 1.4 %collective-permute-done.7.refs_2_ = f32[48,128]{1,0:T(8,128)S(1)} collective-permute-done((f32[48,128]{1,0:T(8,128)S(1)}, f32[48,128]{1,0:T(8,128)S(1)}, u32[]{:S(2)}, u32[]{:S(2)}) %collective-permute-start.7) | collective-permute-done | bytes 24608 | tf_op jit(solution)/shard_map/ppermute | solution.py:240
  23.8 0.7 %collective-permute-start.11 = (f32[16,128]{1,0:T(8,128)S(1)}, f32[16,128]{1,0:T(8,128)S(1)}, u32[]{:S(2)}, u32[]{:S(2)}) collective-permute-start(f32[16,128]{1,0:T(8,128)S(1)} %get-tuple-element.11.refs_0_), channel_id=1, source_target_pairs={{1,13},{3,15},{5,9},{7,11},{9,5},{11,7},{13,1},{15,3},{17,29},{19,... | collective-permute-start | bytes 24584 | tf_op jit(solution)/shard_map/ppermute | solution.py:240
  24.5 0.7 %collective-permute-start.10 = (f32[16,128]{1,0:T(8,128)S(1)}, f32[16,128]{1,0:T(8,128)S(1)}, u32[]{:S(2)}, u32[]{:S(2)}) collective-permute-start(f32[16,128]{1,0:T(8,128)S(1)} %get-tuple-element.11.refs_0_), channel_id=1, source_target_pairs={{1,9},{3,11},{5,13},{7,15},{9,1},{11,3},{13,5},{15,7},{17,25},{19,... | collective-permute-start | bytes 24584 | tf_op jit(solution)/shard_map/ppermute | solution.py:240
  25.1 3.1 %collective-permute-start.9 = (f32[16,128]{1,0:T(8,128)S(1)}, f32[16,128]{1,0:T(8,128)S(1)}, u32[]{:S(2)}, u32[]{:S(2)}) collective-permute-start(f32[16,128]{1,0:T(8,128)S(1)} %get-tuple-element.11.refs_0_), channel_id=1, source_target_pairs={{0,4},{2,6},{4,0},{6,2},{8,12},{10,14},{12,8},{14,10},{16,20},{18,... | collective-permute-start | bytes 24584 | tf_op jit(solution)/shard_map/ppermute | solution.py:240
  28.2 2.4 %collective-permute-done.9.refs_0_ = f32[16,128]{1,0:T(8,128)S(1)} collective-permute-done((f32[16,128]{1,0:T(8,128)S(1)}, f32[16,128]{1,0:T(8,128)S(1)}, u32[]{:S(2)}, u32[]{:S(2)}) %collective-permute-start.9) | collective-permute-done | bytes 8224 | tf_op jit(solution)/shard_map/ppermute | solution.py:240
  30.7 2.7 %collective-permute-start.12 = (f32[16,128]{1,0:T(8,128)S(1)}, f32[16,128]{1,0:T(8,128)S(1)}, u32[]{:S(2)}, u32[]{:S(2)}) collective-permute-start(f32[16,128]{1,0:T(8,128)S(1)} %others.1.refs_1_), channel_id=1, source_target_pairs={{0,1},{1,0},{2,3},{3,2},{4,5},{5,4},{6,7},{7,6},{8,9},{9,8},{10,11... | collective-permute-start | bytes 24584 | tf_op jit(solution)/shard_map/ppermute | solution.py:240
  33.4 0.8 %collective-permute-done.12.refs_2_ = f32[16,128]{1,0:T(8,128)S(1)} collective-permute-done((f32[16,128]{1,0:T(8,128)S(1)}, f32[16,128]{1,0:T(8,128)S(1)}, u32[]{:S(2)}, u32[]{:S(2)}) %collective-permute-start.12) | collective-permute-done | bytes 8224 | tf_op jit(solution)/shard_map/ppermute | solution.py:240
  34.2 0.8 %update.1 = (f32[4,256]{1,0:T(4,128)}, f32[4,256]{1,0:T(4,128)}, f32[4,256]{1,0:T(4,128)}) custom-call(f32[16,128]{1,0:T(8,128)S(1)} %get-tuple-element.11.refs_0_, f32[16,128]{1,0:T(8,128)S(1)} %others.1.refs_1_, f32[16,128]{1,0:T(8,128)S(1)} %collective-permute-done.12.refs_2_, f32[8,128]{1,0:T(8,128)S(1)} %get-tuple-element.12.refs_3_, ...), custom_call_target="tpu_custom_call" | custom-call | tf_op jit(solution)/shard_map/update/pallas_call | solution.py:309
  (15 shorter events, 0.1 us)
Async XLA Ops:
  0.6 6.9 %copy-start.3 = (bf16[256,128]{1,0:T(8,128)(2,1)S(1)}, bf16[256,128]{1,0:T(8,128)(2,1)}, u32[]{:S(2)}) copy-start(bf16[256,128]{1,0:T(8,128)(2,1)} %points.1) | copy-start | bytes 196612
  0.6 8.0 %collective-permute-start.3 = (bf16[256,128]{1,0:T(8,128)(2,1)}, bf16[256,128]{1,0:T(8,128)(2,1)S(1)}, u32[]{:S(2)}, u32[]{:S(2)}) collective-permute-start(bf16[256,128]{1,0:T(8,128)(2,1)} %points.1), channel_id=1, source_target_pairs={{0,1},{1,0},{2,3},{3,2},{4,5},{5,4},{6,7},{7,6},{8,9},{9,8},{10,11... | collective-permute-start | bytes 196616 | tf_op jit(solution)/shard_map/ppermute | solution.py:240
  2.2 11.1 %collective-permute-start.2 = (bf16[288,128]{1,0:T(8,128)(2,1)S(1)}, bf16[288,128]{1,0:T(8,128)(2,1)S(1)}, u32[]{:S(2)}, u32[]{:S(2)}) collective-permute-start(bf16[288,128]{1,0:T(8,128)(2,1)S(1)} %get-tuple-element.8.refs_0_), channel_id=1, source_target_pairs={{0,12},{1,13},{2,14},{3,15},{4,8},{5,9},{6,10},{7,11},{8,4},{9,5},... | collective-permute-start | bytes 221192 | tf_op jit(solution)/shard_map/ppermute | solution.py:240
  6.9 6.8 %collective-permute-start.1 = (bf16[288,128]{1,0:T(8,128)(2,1)S(1)}, bf16[288,128]{1,0:T(8,128)(2,1)S(1)}, u32[]{:S(2)}, u32[]{:S(2)}) collective-permute-start(bf16[288,128]{1,0:T(8,128)(2,1)S(1)} %get-tuple-element.8.refs_0_), channel_id=1, source_target_pairs={{0,8},{1,9},{2,10},{3,11},{4,12},{5,13},{6,14},{7,15},{8,0},{9,1},... | collective-permute-start | bytes 221192 | tf_op jit(solution)/shard_map/ppermute | solution.py:240
  6.9 6.8 %collective-permute-start = (bf16[288,128]{1,0:T(8,128)(2,1)S(1)}, bf16[288,128]{1,0:T(8,128)(2,1)S(1)}, u32[]{:S(2)}, u32[]{:S(2)}) collective-permute-start(bf16[288,128]{1,0:T(8,128)(2,1)S(1)} %get-tuple-element.8.refs_0_), channel_id=1, source_target_pairs={{0,4},{1,5},{2,6},{3,7},{4,0},{5,1},{6,2},{7,3},{8,12},{9,13},{10,... | collective-permute-start | bytes 221192 | tf_op jit(solution)/shard_map/ppermute | solution.py:240
  7.6 4.2 %collective-permute-start.5 = (bf16[256,128]{1,0:T(8,128)(2,1)S(1)}, bf16[256,128]{1,0:T(8,128)(2,1)S(1)}, u32[]{:S(2)}, u32[]{:S(2)}) collective-permute-start(bf16[256,128]{1,0:T(8,128)(2,1)S(1)} %copy-done.3), channel_id=1, source_target_pairs={{0,3},{1,2},{2,1},{3,0},{4,7},{5,6},{6,5},{7,4},{8,11},{9,10},{10,... | collective-permute-start | bytes 196616 | tf_op jit(solution)/shard_map/ppermute | solution.py:240
  8.6 4.7 %collective-permute-start.4 = (bf16[256,128]{1,0:T(8,128)(2,1)S(1)}, bf16[256,128]{1,0:T(8,128)(2,1)S(1)}, u32[]{:S(2)}, u32[]{:S(2)}) collective-permute-start(bf16[256,128]{1,0:T(8,128)(2,1)S(1)} %copy-done.3), channel_id=1, source_target_pairs={{0,2},{1,3},{2,0},{3,1},{4,6},{5,7},{6,4},{7,5},{8,10},{9,11},{10,... | collective-permute-start | bytes 196616 | tf_op jit(solution)/shard_map/ppermute | solution.py:240
  18.9 3.5 %collective-permute-start.8 = (f32[48,128]{1,0:T(8,128)S(1)}, f32[48,128]{1,0:T(8,128)S(1)}, u32[]{:S(2)}, u32[]{:S(2)}) collective-permute-start(f32[48,128]{1,0:T(8,128)S(1)} %product.1.refs_0_), channel_id=1, source_target_pairs={{0,3},{1,2},{2,1},{3,0},{4,7},{5,6},{6,5},{7,4},{8,11},{9,10},{10,... | collective-permute-start | bytes 73736 | tf_op jit(solution)/shard_map/ppermute | solution.py:240
  19.9 3.8 %collective-permute-start.7 = (f32[48,128]{1,0:T(8,128)S(1)}, f32[48,128]{1,0:T(8,128)S(1)}, u32[]{:S(2)}, u32[]{:S(2)}) collective-permute-start(f32[48,128]{1,0:T(8,128)S(1)} %product.1.refs_0_), channel_id=1, source_target_pairs={{0,2},{1,3},{2,0},{3,1},{4,6},{5,7},{6,4},{7,5},{8,10},{9,11},{10,... | collective-permute-start | bytes 73736 | tf_op jit(solution)/shard_map/ppermute | solution.py:240
  20.6 3.2 %collective-permute-start.6 = (f32[48,128]{1,0:T(8,128)S(1)}, f32[48,128]{1,0:T(8,128)S(1)}, u32[]{:S(2)}, u32[]{:S(2)}) collective-permute-start(f32[48,128]{1,0:T(8,128)S(1)} %product.1.refs_0_), channel_id=1, source_target_pairs={{0,1},{1,0},{2,3},{3,2},{4,5},{5,4},{6,7},{7,6},{8,9},{9,8},{10,11... | collective-permute-start | bytes 73736 | tf_op jit(solution)/shard_map/ppermute | solution.py:240
  23.8 4.4 %collective-permute-start.11 = (f32[16,128]{1,0:T(8,128)S(1)}, f32[16,128]{1,0:T(8,128)S(1)}, u32[]{:S(2)}, u32[]{:S(2)}) collective-permute-start(f32[16,128]{1,0:T(8,128)S(1)} %get-tuple-element.11.refs_0_), channel_id=1, source_target_pairs={{1,13},{3,15},{5,9},{7,11},{9,5},{11,7},{13,1},{15,3},{17,29},{19,... | collective-permute-start | bytes 24584 | tf_op jit(solution)/shard_map/ppermute | solution.py:240
  24.5 3.8 %collective-permute-start.10 = (f32[16,128]{1,0:T(8,128)S(1)}, f32[16,128]{1,0:T(8,128)S(1)}, u32[]{:S(2)}, u32[]{:S(2)}) collective-permute-start(f32[16,128]{1,0:T(8,128)S(1)} %get-tuple-element.11.refs_0_), channel_id=1, source_target_pairs={{1,9},{3,11},{5,13},{7,15},{9,1},{11,3},{13,5},{15,7},{17,25},{19,... | collective-permute-start | bytes 24584 | tf_op jit(solution)/shard_map/ppermute | solution.py:240
  25.1 5.5 %collective-permute-start.9 = (f32[16,128]{1,0:T(8,128)S(1)}, f32[16,128]{1,0:T(8,128)S(1)}, u32[]{:S(2)}, u32[]{:S(2)}) collective-permute-start(f32[16,128]{1,0:T(8,128)S(1)} %get-tuple-element.11.refs_0_), channel_id=1, source_target_pairs={{0,4},{2,6},{4,0},{6,2},{8,12},{10,14},{12,8},{14,10},{16,20},{18,... | collective-permute-start | bytes 24584 | tf_op jit(solution)/shard_map/ppermute | solution.py:240
  30.7 3.5 %copy-start = (f32[4,256]{1,0:T(4,128)S(1)}, f32[4,256]{1,0:T(4,128)}, u32[]{:S(2)}) copy-start(f32[4,256]{1,0:T(4,128)} %refs_6_.1) | copy-start | bytes 12292
  30.7 3.5 %copy-start.1 = (f32[4,256]{1,0:T(4,128)S(1)}, f32[4,256]{1,0:T(4,128)}, u32[]{:S(2)}) copy-start(f32[4,256]{1,0:T(4,128)} %refs_5_.1) | copy-start | bytes 12292
  30.7 3.5 %copy-start.2 = (f32[4,256]{1,0:T(4,128)S(1)}, f32[4,256]{1,0:T(4,128)}, u32[]{:S(2)}) copy-start(f32[4,256]{1,0:T(4,128)} %refs_4_.1) | copy-start | bytes 12292
  30.7 3.5 %collective-permute-start.12 = (f32[16,128]{1,0:T(8,128)S(1)}, f32[16,128]{1,0:T(8,128)S(1)}, u32[]{:S(2)}, u32[]{:S(2)}) collective-permute-start(f32[16,128]{1,0:T(8,128)S(1)} %others.1.refs_1_), channel_id=1, source_target_pairs={{0,1},{1,0},{2,3},{3,2},{4,5},{5,4},{6,7},{7,6},{8,9},{9,8},{10,11... | collective-permute-start | bytes 24584 | tf_op jit(solution)/shard_map/ppermute | solution.py:240

commit v10 on v6

--- a/solution.py
+++ b/solution.py
@@ -1,5 +1,4 @@
 import functools
-import math
 
 import jax
 import jax.numpy as jnp
@@ -8,15 +7,16 @@
 from jax.experimental.pallas import tpu as pltpu
 from jax.sharding import PartitionSpec as P
 
-LOG2E = 1.4426950408889634
 CHUNK = 32
 
 
-def split_sizes(devices):
-    lo = max(d for d in range(1, math.isqrt(devices) + 1) if devices % d == 0)
-    hi = devices // lo
-    assert hi & (hi - 1) == lo & (lo - 1) == 0
-    return hi, lo
+def split_masks(devices):
+    bits = devices.bit_length() - 1
+    assert devices == 1 << bits and bits > 1
+    far = bits // 2 - 1
+    row = [m << (bits - far) for m in range(1 << far)]
+    col = [m << 1 for m in range(1 << (bits - 1 - far))]
+    return col, [m + core for m in row for core in (0, 1)]
 
 
 def pieces_of(wide):
@@ -78,8 +78,8 @@
     sigma = jnp.zeros((cands, 1), jnp.float32)
     for c in range(cands):
         sigma = jnp.where(which == c, noise_in[c], sigma)
-        rate = (-0.5 * LOG2E) / (length_in[c] * length_in[c])
-        rates[pl.ds(8 * c, 8), :] = jnp.full((8, size), rate, jnp.float32)
+        rate = -0.5 / (length_in[c] * length_in[c])
+        rates[pl.ds(8 * c, 8), :] = jnp.full((8, dims), rate, jnp.float32)
     tall = own.shape[0] // 3
     for i, wide in enumerate((step, rest_in[...], sigma * step)):
         own[pl.ds(i * tall, tall), :] = fold(wide, dims)
@@ -91,54 +91,60 @@
     packed[size:, :] = fold(top, dims).astype(jnp.bfloat16)
 
 
+def widen_row(points):
+    wide = points.astype(jnp.float32)
+    sq = pieces_of(jnp.sum(wide * wide, axis=1, keepdims=True))
+    lane = lax.broadcasted_iota(jnp.int32, wide.shape, 1)
+    extra = jnp.where(lane < 3, 1.0, 0.0)
+    for i, piece in enumerate(sq):
+        extra = jnp.where(lane == 3 + i, piece, extra)
+    return jnp.concatenate(
+        [(wide * -2.0).astype(jnp.bfloat16), extra.astype(jnp.bfloat16)], axis=1
+    )
+
+
 def product_kernel(lo, hi, cands, *refs):
     cols, refs = refs[:hi], refs[hi:]
     rows, refs = refs[: lo - 1], refs[lo - 1 :]
     own, rates, out, row_wide, weights, dist = refs
     rows = (cols[0], *rows)
-    tall = own.shape[0] // 3
-    dims = own.shape[1]
-    size = rates.shape[1]
-    lines = (cols[0].shape[0] - size) * dims // size
-
-    def extra(top):
+    tall, dims = own.shape[0] // 3, own.shape[1]
+    size = row_wide.shape[0] // lo
+    wide = size // dims
+    lines = (cols[0].shape[0] - size) // wide
+    for k in range(lo):
+        row_wide[pl.ds(k * size, size), :] = widen_row(rows[k][:size, :])
+    for h in range(hi):
+        top = unfold(cols[h][size:, :], lines)
         top = jnp.concatenate(
-            [top, jnp.zeros((dims - top.shape[0], size), jnp.float32)], axis=0
-        )
-        return top.T
-
-    for k in range(lo):
-        top = unfold(rows[k][size:, :].astype(jnp.float32), lines)
-        top = jnp.concatenate([top[3:6], top[:3], jnp.zeros((2, size), jnp.float32)])
-        row_wide[pl.ds(k * size, size), :] = jnp.concatenate(
-            [rows[k][:size, :], extra(top).astype(jnp.bfloat16)], axis=1
-        )
-    for h in range(hi):
-        top = extra(unfold(cols[h][size:, :].astype(jnp.float32), lines))
+            [top, jnp.zeros((dims - lines, size), top.dtype)], axis=0
+        ).T
+        steps = top.astype(jnp.float32)
         for c in range(cands):
             weights[c, pl.ds(h * size, size), :] = jnp.broadcast_to(
-                top[:, 8 + c : 9 + c], (size, dims)
+                steps[:, 8 + c : 9 + c], (size, dims)
             )
-        scaled = (cols[h][:size, :].astype(jnp.float32) * -2.0).astype(jnp.bfloat16)
         dist[pl.ds(h * size, size), :] = lax.dot_general(
-            jnp.concatenate([scaled, top.astype(jnp.bfloat16)], axis=1),
+            jnp.concatenate([cols[h][:size, :], top], axis=1),
             row_wide[...],
             (((1,), (1,)), ((), ())),
             preferred_element_type=jnp.float32,
         )
+    rate = [
+        jnp.concatenate([rates[pl.ds(8 * c, 8), :]] * wide, axis=1) for c in range(cands)
+    ]
 
     def body(step, total):
         total = list(total)
         for j in range(0, CHUNK, 8):
             at = pl.ds(pl.multiple_of(step * CHUNK + j, 8), 8)
+            weight = [
+                jnp.concatenate([weights[c, at, :]] * wide, axis=1) for c in range(cands)
+            ]
             for k in range(lo):
                 here = dist[at, pl.ds(k * size, size)]
                 for c in range(cands):
-                    weight = jnp.concatenate(
-                        [weights[c, at, :]] * (size // dims), axis=1
-                    )
-                    kern = jnp.exp2(here * rates[pl.ds(8 * c, 8), :])
-                    total[k * cands + c] += kern * weight
+                    total[k * cands + c] += jnp.exp(here * rate[c]) * weight[c]
         return tuple(total)
 
     total = lax.fori_loop(
@@ -147,11 +153,9 @@
         body,
         (jnp.zeros((8, size), jnp.float32),) * (lo * cands),
     )
+    total = [jnp.sum(t, axis=0, keepdims=True) for t in total]
     for k in range(lo):
-        part = [
-            jnp.sum(total[k * cands + c], axis=0, keepdims=True) for c in range(cands)
-        ]
-        part = fold(jnp.concatenate(part, axis=0), dims)
+        part = fold(jnp.concatenate(total[k * cands : (k + 1) * cands], axis=0), dims)
         if k == 0:
             part += own[pl.ds(2 * tall, tall), :]
         out[pl.ds(k * tall, tall), :] = part
@@ -201,7 +205,8 @@
 
 
 def per_device(devices, points, lengthscale, noise, solution, residual, direction):
-    hi, lo = split_sizes(devices)
+    col_masks, row_masks = split_masks(devices)
+    hi, lo = len(col_masks), len(row_masks)
     size, dims = points.shape
     cands = direction.shape[0]
     tall = cands * size // dims
@@ -219,7 +224,7 @@
         out_shape=(
             jax.ShapeDtypeStruct((size + extra, dims), jnp.bfloat16),
             jax.ShapeDtypeStruct((3 * tall, dims), jnp.float32),
-            jax.ShapeDtypeStruct((8 * cands, size), jnp.float32),
+            jax.ShapeDtypeStruct((8 * cands, dims), jnp.float32),
         ),
         in_specs=[hbm] * 5,
         out_specs=(vmem,) * 3,
@@ -239,14 +244,10 @@
         )
     )
 
-    cols = [packed] + [meet(packed, k * lo) for k in range(1, hi)]
-    rows = [packed] + [meet(packed, k) for k in range(1, lo) if k == 1 or k % 2 == 0]
-    if lo > 2:
-        rows = [packed, rows[1]] + [
-            block
-            for k in range(2, lo, 2)
-            for block in (rows[k // 2 + 1], meet(rows[k // 2 + 1], 1))
-        ]
+    rows = [points]
+    for mask in row_masks[1:]:
+        rows.append(meet(rows[-1], 1) if mask % 2 else meet(points, mask))
+    cols = [packed] + [meet(packed, mask) for mask in col_masks[1:]]
 
     partial = pl.pallas_call(
         functools.partial(product_kernel, lo, hi, cands),
@@ -272,7 +273,7 @@
         out_specs=(vmem, vmem),
         compiler_params=params,
         name="sums",
-    )(partial, *(meet(partial, k) for k in range(1, lo)))
+    )(partial, *(meet(partial, mask) for mask in row_masks[1:]))
 
     return pl.pallas_call(
         functools.partial(update_kernel, hi),
@@ -281,7 +282,7 @@
         out_specs=(vmem,) * 3,
         compiler_params=params,
         name="update",
-    )(sums, *(meet(sums, k * lo) for k in range(1, hi)), image, solution, residual, direction)
+    )(sums, *(meet(sums, mask) for mask in col_masks[1:]), image, solution, residual, direction)
 
 
 def solution(mesh):

time: 31 us -> 29.3 us (0.945)
  waiting for transfers between devices: 10.8 us -> 8.03 us
  starting transfers between devices: 13.8 us -> 14.5 us
    ppermute x12, waiting for transfers between devices: 10.8 us -> 8.03 us  [meet(): return lax.ppermute(x, 'blk', [(d, d ^ mask) for d in range(devices)])]
    ppermute x12, starting transfers between devices: 13.8 us -> 14.5 us  [meet(): return lax.ppermute(x, 'blk', [(d, d ^ mask) for d in range(devices)])]
  transfers between devices with their start and end apart: 12 -> 12, of which waited for: 6 -> 9; matrix products, arithmetic and copies ran while one was open for 0% -> 0% of each run, Pallas kernels for 0% -> 4%
where the time goes in v10:
time: 29.3 us; the launch traced here: 29.1 us
  starting transfers between devices  14.5 us (49%)
  waiting for transfers between devices  8.03 us (27%)
  Pallas kernels  5.87 us (20%)
  between operations  0.69 us (2%)
    ppermute x12, starting transfers between devices, meet(): return lax.ppermute(x, 'blk', [(d, d ^ mask) for d in range(devices)])  14.5 us
    ppermute x12, waiting for transfers between devices, meet(): return lax.ppermute(x, 'blk', [(d, d ^ mask) for d in range(devices)])  8.03 us
    pallas_call x1, Pallas kernels, per_device(): pl.pallas_call(functools.partial(product_kernel, lo, hi, cands), out_shap...  3.99 us
    pallas_call x1, Pallas kernels, per_device(): pl.pallas_call(pack_kernel, out_shape=(jax.ShapeDtypeStruct((size + extra...  1.08 us
    pallas_call x1, Pallas kernels, per_device(): pl.pallas_call(functools.partial(update_kernel, hi), out_shape=(jax.Shape...  0.78 us
  transfers between devices with their start and end apart: 12, of which 9 were waited for; matrix products, arithmetic and copies ran while one was open for 0% of the time, Pallas kernels for 4%

profile of v10, /device:TPU:0, one launch (start us, length us, event | category | flops | bytes accessed | tf_op | source)
XLA Modules:
  0.0 29.1 jit_solution(1646884890446701597)
XLA Ops:
  0.6 4.1 %collective-permute-start.4 = (bf16[256,128]{1,0:T(8,128)(2,1)}, bf16[256,128]{1,0:T(8,128)(2,1)S(1)}, u32[]{:S(2)}, u32[]{:S(2)}) collective-permute-start(bf16[256,128]{1,0:T(8,128)(2,1)} %points.1), channel_id=1, source_target_pairs={{0,8},{1,9},{2,10},{3,11},{4,12},{5,13},{6,14},{7,15},{8,0},{9,1},... | collective-permute-start | bytes 196616 | tf_op jit(solution)/shard_map/ppermute | solution.py:216
  4.7 1.1 %pack.1 = (bf16[288,128]{1,0:T(8,128)(2,1)S(1)}, f32[24,128]{1,0:T(8,128)S(1)}, f32[32,128]{1,0:T(8,128)S(1)}) custom-call(bf16[256,128]{1,0:T(8,128)(2,1)} %points.1, f32[4,256]{1,0:T(4,128)} %refs_7_.1, f32[4,256]{1,0:T(4,128)} %refs_6_.1, f32[4]{0:T(128)} %length.1, f32[4]{0:T(128)} %noise.1), custom_call_target="tpu_custom_call" | custom-call | tf_op jit(solution)/shard_map/pack/pallas_call | solution.py:222
  5.8 2.6 %collective-permute-start.2 = (bf16[288,128]{1,0:T(8,128)(2,1)S(1)}, bf16[288,128]{1,0:T(8,128)(2,1)S(1)}, u32[]{:S(2)}, u32[]{:S(2)}) collective-permute-start(bf16[288,128]{1,0:T(8,128)(2,1)S(1)} %get-tuple-element.8.refs_0_), channel_id=1, source_target_pairs={{0,6},{1,7},{2,4},{3,5},{4,2},{5,3},{6,0},{7,1},{8,14},{9,15},{10,... | collective-permute-start | bytes 221192 | tf_op jit(solution)/shard_map/ppermute | solution.py:216
  8.4 0.4 %collective-permute-start.1 = (bf16[288,128]{1,0:T(8,128)(2,1)S(1)}, bf16[288,128]{1,0:T(8,128)(2,1)S(1)}, u32[]{:S(2)}, u32[]{:S(2)}) collective-permute-start(bf16[288,128]{1,0:T(8,128)(2,1)S(1)} %get-tuple-element.8.refs_0_), channel_id=1, source_target_pairs={{0,4},{1,5},{2,6},{3,7},{4,0},{5,1},{6,2},{7,3},{8,12},{9,13},{10,... | collective-permute-start | bytes 221192 | tf_op jit(solution)/shard_map/ppermute | solution.py:216
  8.9 0.5 %collective-permute-start = (bf16[288,128]{1,0:T(8,128)(2,1)S(1)}, bf16[288,128]{1,0:T(8,128)(2,1)S(1)}, u32[]{:S(2)}, u32[]{:S(2)}) collective-permute-start(bf16[288,128]{1,0:T(8,128)(2,1)S(1)} %get-tuple-element.8.refs_0_), channel_id=1, source_target_pairs={{0,2},{1,3},{2,0},{3,1},{4,6},{5,7},{6,4},{7,5},{8,10},{9,11},{10,... | collective-permute-start | bytes 221192 | tf_op jit(solution)/shard_map/ppermute | solution.py:216
  9.4 0.5 %collective-permute-start.5 = (bf16[256,128]{1,0:T(8,128)(2,1)S(1)}, bf16[256,128]{1,0:T(8,128)(2,1)S(1)}, u32[]{:S(2)}, u32[]{:S(2)}) collective-permute-start(bf16[256,128]{1,0:T(8,128)(2,1)S(1)} %collective-permute-done.4.refs_5_), channel_id=1, source_target_pairs={{0,1},{1,0},{2,3},{3,2},{4,5},{5,4},{6,7},{7,6},{8,9},{9,8},{10,11... | collective-permute-start | bytes 196616 | tf_op jit(solution)/shard_map/ppermute | solution.py:216
  9.9 0.7 %collective-permute-done.3.refs_4_ = bf16[256,128]{1,0:T(8,128)(2,1)S(1)} collective-permute-done((bf16[256,128]{1,0:T(8,128)(2,1)S(1)}, bf16[256,128]{1,0:T(8,128)(2,1)S(1)}, u32[]{:S(2)}, u32[]{:S(2)}) %collective-permute-start.3) | collective-permute-done | bytes 65568 | tf_op jit(solution)/shard_map/ppermute | solution.py:216
  10.6 1.3 %collective-permute-done.2.refs_3_ = bf16[288,128]{1,0:T(8,128)(2,1)S(1)} collective-permute-done((bf16[288,128]{1,0:T(8,128)(2,1)S(1)}, bf16[288,128]{1,0:T(8,128)(2,1)S(1)}, u32[]{:S(2)}, u32[]{:S(2)}) %collective-permute-start.2) | collective-permute-done | bytes 73760 | tf_op jit(solution)/shard_map/ppermute | solution.py:216
  11.9 0.9 %collective-permute-done.1.refs_2_ = bf16[288,128]{1,0:T(8,128)(2,1)S(1)} collective-permute-done((bf16[288,128]{1,0:T(8,128)(2,1)S(1)}, bf16[288,128]{1,0:T(8,128)(2,1)S(1)}, u32[]{:S(2)}, u32[]{:S(2)}) %collective-permute-start.1) | collective-permute-done | bytes 73760 | tf_op jit(solution)/shard_map/ppermute | solution.py:216
  12.8 0.4 %collective-permute-done.refs_1_ = bf16[288,128]{1,0:T(8,128)(2,1)S(1)} collective-permute-done((bf16[288,128]{1,0:T(8,128)(2,1)S(1)}, bf16[288,128]{1,0:T(8,128)(2,1)S(1)}, u32[]{:S(2)}, u32[]{:S(2)}) %collective-permute-start) | collective-permute-done | bytes 73760 | tf_op jit(solution)/shard_map/ppermute | solution.py:216
  13.2 0.0 collective-permute-done.5.refs_6_
  13.2 4.0 %product.1.refs_0_ = f32[48,128]{1,0:T(8,128)S(1)} custom-call(bf16[288,128]{1,0:T(8,128)(2,1)S(1)} %get-tuple-element.8.refs_0_, bf16[288,128]{1,0:T(8,128)(2,1)S(1)} %collective-permute-done.refs_1_, bf16[288,128]{1,0:T(8,128)(2,1)S(1)} %collective-permute-done.1.refs_2_, bf16[288,128]{1,0:T(8,128)(2,1)S(1)} %collective-permute-done.2.refs_3_, ...), custom_call_target="tpu_custom_call" | custom-call | tf_op jit(solution)/shard_map/product/pallas_call | solution.py:252
  17.2 0.1 collective-permute-start.8
  17.3 1.2 %collective-permute-start.7 = (f32[48,128]{1,0:T(8,128)S(1)}, f32[48,128]{1,0:T(8,128)S(1)}, u32[]{:S(2)}, u32[]{:S(2)}) collective-permute-start(f32[48,128]{1,0:T(8,128)S(1)} %product.1.refs_0_), channel_id=1, source_target_pairs={{0,8},{1,9},{2,10},{3,11},{4,12},{5,13},{6,14},{7,15},{8,0},{9,1},... | collective-permute-start | bytes 73736 | tf_op jit(solution)/shard_map/ppermute | solution.py:216
  18.5 1.5 %collective-permute-start.6 = (f32[48,128]{1,0:T(8,128)S(1)}, f32[48,128]{1,0:T(8,128)S(1)}, u32[]{:S(2)}, u32[]{:S(2)}) collective-permute-start(f32[48,128]{1,0:T(8,128)S(1)} %product.1.refs_0_), channel_id=1, source_target_pairs={{0,1},{1,0},{2,3},{3,2},{4,5},{5,4},{6,7},{7,6},{8,9},{9,8},{10,11... | collective-permute-start | bytes 73736 | tf_op jit(solution)/shard_map/ppermute | solution.py:216
  20.1 1.7 %collective-permute-done.8.refs_3_ = f32[48,128]{1,0:T(8,128)S(1)} collective-permute-done((f32[48,128]{1,0:T(8,128)S(1)}, f32[48,128]{1,0:T(8,128)S(1)}, u32[]{:S(2)}, u32[]{:S(2)}) %collective-permute-start.8) | collective-permute-done | bytes 24608 | tf_op jit(solution)/shard_map/ppermute | solution.py:216
  21.7 0.5 %collective-permute-done.7.refs_2_ = f32[48,128]{1,0:T(8,128)S(1)} collective-permute-done((f32[48,128]{1,0:T(8,128)S(1)}, f32[48,128]{1,0:T(8,128)S(1)}, u32[]{:S(2)}, u32[]{:S(2)}) %collective-permute-start.7) | collective-permute-done | bytes 24608 | tf_op jit(solution)/shard_map/ppermute | solution.py:216
  22.3 1.5 %collective-permute-start.11 = (f32[16,128]{1,0:T(8,128)S(1)}, f32[16,128]{1,0:T(8,128)S(1)}, u32[]{:S(2)}, u32[]{:S(2)}) collective-permute-start(f32[16,128]{1,0:T(8,128)S(1)} %get-tuple-element.11.refs_0_), channel_id=1, source_target_pairs={{0,6},{1,7},{2,4},{3,5},{4,2},{5,3},{6,0},{7,1},{8,14},{9,15},{10,... | collective-permute-start | bytes 24584 | tf_op jit(solution)/shard_map/ppermute | solution.py:216
  23.8 0.9 %collective-permute-start.10 = (f32[16,128]{1,0:T(8,128)S(1)}, f32[16,128]{1,0:T(8,128)S(1)}, u32[]{:S(2)}, u32[]{:S(2)}) collective-permute-start(f32[16,128]{1,0:T(8,128)S(1)} %get-tuple-element.11.refs_0_), channel_id=1, source_target_pairs={{0,4},{1,5},{2,6},{3,7},{4,0},{5,1},{6,2},{7,3},{8,12},{9,13},{10,... | collective-permute-start | bytes 24584 | tf_op jit(solution)/shard_map/ppermute | solution.py:216
  24.7 1.1 %collective-permute-start.9 = (f32[16,128]{1,0:T(8,128)S(1)}, f32[16,128]{1,0:T(8,128)S(1)}, u32[]{:S(2)}, u32[]{:S(2)}) collective-permute-start(f32[16,128]{1,0:T(8,128)S(1)} %get-tuple-element.11.refs_0_), channel_id=1, source_target_pairs={{0,2},{1,3},{2,0},{3,1},{4,6},{5,7},{6,4},{7,5},{8,10},{9,11},{10,... | collective-permute-start | bytes 24584 | tf_op jit(solution)/shard_map/ppermute | solution.py:216
  25.8 1.1 %collective-permute-done.11.refs_3_ = f32[16,128]{1,0:T(8,128)S(1)} collective-permute-done((f32[16,128]{1,0:T(8,128)S(1)}, f32[16,128]{1,0:T(8,128)S(1)}, u32[]{:S(2)}, u32[]{:S(2)}) %collective-permute-start.11) | collective-permute-done | bytes 8224 | tf_op jit(solution)/shard_map/ppermute | solution.py:216
  26.9 0.6 %collective-permute-done.10.refs_2_ = f32[16,128]{1,0:T(8,128)S(1)} collective-permute-done((f32[16,128]{1,0:T(8,128)S(1)}, f32[16,128]{1,0:T(8,128)S(1)}, u32[]{:S(2)}, u32[]{:S(2)}) %collective-permute-start.10) | collective-permute-done | bytes 8224 | tf_op jit(solution)/shard_map/ppermute | solution.py:216
  27.5 0.9 %collective-permute-done.9.refs_1_ = f32[16,128]{1,0:T(8,128)S(1)} collective-permute-done((f32[16,128]{1,0:T(8,128)S(1)}, f32[16,128]{1,0:T(8,128)S(1)}, u32[]{:S(2)}, u32[]{:S(2)}) %collective-permute-start.9) | collective-permute-done | bytes 8224 | tf_op jit(solution)/shard_map/ppermute | solution.py:216
  28.4 0.8 %update.1 = (f32[4,256]{1,0:T(4,128)}, f32[4,256]{1,0:T(4,128)}, f32[4,256]{1,0:T(4,128)}) custom-call(f32[16,128]{1,0:T(8,128)S(1)} %get-tuple-element.11.refs_0_, f32[16,128]{1,0:T(8,128)S(1)} %collective-permute-done.9.refs_1_, f32[16,128]{1,0:T(8,128)S(1)} %collective-permute-done.10.refs_2_, f32[16,128]{1,0:T(8,128)S(1)} %collective-permute-done.11.refs_3_, ...), custom_call_target="tpu_custom_call" | custom-call | tf_op jit(solution)/shard_map/update/pallas_call | solution.py:278
  (12 shorter events, 0.0 us)
Async XLA Ops:
  0.6 8.8 %copy-start.3 = (bf16[256,128]{1,0:T(8,128)(2,1)S(1)}, bf16[256,128]{1,0:T(8,128)(2,1)}, u32[]{:S(2)}) copy-start(bf16[256,128]{1,0:T(8,128)(2,1)} %points.1) | copy-start | bytes 196612
  0.6 8.8 %collective-permute-start.4 = (bf16[256,128]{1,0:T(8,128)(2,1)}, bf16[256,128]{1,0:T(8,128)(2,1)S(1)}, u32[]{:S(2)}, u32[]{:S(2)}) collective-permute-start(bf16[256,128]{1,0:T(8,128)(2,1)} %points.1), channel_id=1, source_target_pairs={{0,8},{1,9},{2,10},{3,11},{4,12},{5,13},{6,14},{7,15},{8,0},{9,1},... | collective-permute-start | bytes 196616 | tf_op jit(solution)/shard_map/ppermute | solution.py:216
  5.8 6.1 %collective-permute-start.2 = (bf16[288,128]{1,0:T(8,128)(2,1)S(1)}, bf16[288,128]{1,0:T(8,128)(2,1)S(1)}, u32[]{:S(2)}, u32[]{:S(2)}) collective-permute-start(bf16[288,128]{1,0:T(8,128)(2,1)S(1)} %get-tuple-element.8.refs_0_), channel_id=1, source_target_pairs={{0,6},{1,7},{2,4},{3,5},{4,2},{5,3},{6,0},{7,1},{8,14},{9,15},{10,... | collective-permute-start | bytes 221192 | tf_op jit(solution)/shard_map/ppermute | solution.py:216
  8.4 4.4 %collective-permute-start.1 = (bf16[288,128]{1,0:T(8,128)(2,1)S(1)}, bf16[288,128]{1,0:T(8,128)(2,1)S(1)}, u32[]{:S(2)}, u32[]{:S(2)}) collective-permute-start(bf16[288,128]{1,0:T(8,128)(2,1)S(1)} %get-tuple-element.8.refs_0_), channel_id=1, source_target_pairs={{0,4},{1,5},{2,6},{3,7},{4,0},{5,1},{6,2},{7,3},{8,12},{9,13},{10,... | collective-permute-start | bytes 221192 | tf_op jit(solution)/shard_map/ppermute | solution.py:216
  8.9 4.4 %collective-permute-start = (bf16[288,128]{1,0:T(8,128)(2,1)S(1)}, bf16[288,128]{1,0:T(8,128)(2,1)S(1)}, u32[]{:S(2)}, u32[]{:S(2)}) collective-permute-start(bf16[288,128]{1,0:T(8,128)(2,1)S(1)} %get-tuple-element.8.refs_0_), channel_id=1, source_target_pairs={{0,2},{1,3},{2,0},{3,1},{4,6},{5,7},{6,4},{7,5},{8,10},{9,11},{10,... | collective-permute-start | bytes 221192 | tf_op jit(solution)/shard_map/ppermute | solution.py:216
  9.4 1.3 %collective-permute-start.3 = (bf16[256,128]{1,0:T(8,128)(2,1)S(1)}, bf16[256,128]{1,0:T(8,128)(2,1)S(1)}, u32[]{:S(2)}, u32[]{:S(2)}) collective-permute-start(bf16[256,128]{1,0:T(8,128)(2,1)S(1)} %copy-done.3), channel_id=1, source_target_pairs={{0,1},{1,0},{2,3},{3,2},{4,5},{5,4},{6,7},{7,6},{8,9},{9,8},{10,11... | collective-permute-start | bytes 196616 | tf_op jit(solution)/shard_map/ppermute | solution.py:216
  9.4 3.8 %collective-permute-start.5 = (bf16[256,128]{1,0:T(8,128)(2,1)S(1)}, bf16[256,128]{1,0:T(8,128)(2,1)S(1)}, u32[]{:S(2)}, u32[]{:S(2)}) collective-permute-start(bf16[256,128]{1,0:T(8,128)(2,1)S(1)} %collective-permute-done.4.refs_5_), channel_id=1, source_target_pairs={{0,1},{1,0},{2,3},{3,2},{4,5},{5,4},{6,7},{7,6},{8,9},{9,8},{10,11... | collective-permute-start | bytes 196616 | tf_op jit(solution)/shard_map/ppermute | solution.py:216
  17.2 4.5 %collective-permute-start.8 = (f32[48,128]{1,0:T(8,128)S(1)}, f32[48,128]{1,0:T(8,128)S(1)}, u32[]{:S(2)}, u32[]{:S(2)}) collective-permute-start(f32[48,128]{1,0:T(8,128)S(1)} %product.1.refs_0_), channel_id=1, source_target_pairs={{0,9},{1,8},{2,11},{3,10},{4,13},{5,12},{6,15},{7,14},{8,1},{9,0},... | collective-permute-start | bytes 73736 | tf_op jit(solution)/shard_map/ppermute | solution.py:216
  17.3 4.9 %collective-permute-start.7 = (f32[48,128]{1,0:T(8,128)S(1)}, f32[48,128]{1,0:T(8,128)S(1)}, u32[]{:S(2)}, u32[]{:S(2)}) collective-permute-start(f32[48,128]{1,0:T(8,128)S(1)} %product.1.refs_0_), channel_id=1, source_target_pairs={{0,8},{1,9},{2,10},{3,11},{4,12},{5,13},{6,14},{7,15},{8,0},{9,1},... | collective-permute-start | bytes 73736 | tf_op jit(solution)/shard_map/ppermute | solution.py:216
  18.5 3.7 %collective-permute-start.6 = (f32[48,128]{1,0:T(8,128)S(1)}, f32[48,128]{1,0:T(8,128)S(1)}, u32[]{:S(2)}, u32[]{:S(2)}) collective-permute-start(f32[48,128]{1,0:T(8,128)S(1)} %product.1.refs_0_), channel_id=1, source_target_pairs={{0,1},{1,0},{2,3},{3,2},{4,5},{5,4},{6,7},{7,6},{8,9},{9,8},{10,11... | collective-permute-start | bytes 73736 | tf_op jit(solution)/shard_map/ppermute | solution.py:216
  22.3 6.1 %copy-start = (f32[4,256]{1,0:T(4,128)S(1)}, f32[4,256]{1,0:T(4,128)}, u32[]{:S(2)}) copy-start(f32[4,256]{1,0:T(4,128)} %refs_7_.1) | copy-start | bytes 12292
  22.3 6.1 %copy-start.1 = (f32[4,256]{1,0:T(4,128)S(1)}, f32[4,256]{1,0:T(4,128)}, u32[]{:S(2)}) copy-start(f32[4,256]{1,0:T(4,128)} %refs_6_.1) | copy-start | bytes 12292
  22.3 6.1 %copy-start.2 = (f32[4,256]{1,0:T(4,128)S(1)}, f32[4,256]{1,0:T(4,128)}, u32[]{:S(2)}) copy-start(f32[4,256]{1,0:T(4,128)} %refs_5_.1) | copy-start | bytes 12292
  22.3 4.6 %collective-permute-start.11 = (f32[16,128]{1,0:T(8,128)S(1)}, f32[16,128]{1,0:T(8,128)S(1)}, u32[]{:S(2)}, u32[]{:S(2)}) collective-permute-start(f32[16,128]{1,0:T(8,128)S(1)} %get-tuple-element.11.refs_0_), channel_id=1, source_target_pairs={{0,6},{1,7},{2,4},{3,5},{4,2},{5,3},{6,0},{7,1},{8,14},{9,15},{10,... | collective-permute-start | bytes 24584 | tf_op jit(solution)/shard_map/ppermute | solution.py:216
  23.8 3.7 %collective-permute-start.10 = (f32[16,128]{1,0:T(8,128)S(1)}, f32[16,128]{1,0:T(8,128)S(1)}, u32[]{:S(2)}, u32[]{:S(2)}) collective-permute-start(f32[16,128]{1,0:T(8,128)S(1)} %get-tuple-element.11.refs_0_), channel_id=1, source_target_pairs={{0,4},{1,5},{2,6},{3,7},{4,0},{5,1},{6,2},{7,3},{8,12},{9,13},{10,... | collective-permute-start | bytes 24584 | tf_op jit(solution)/shard_map/ppermute | solution.py:216
  24.7 3.7 %collective-permute-start.9 = (f32[16,128]{1,0:T(8,128)S(1)}, f32[16,128]{1,0:T(8,128)S(1)}, u32[]{:S(2)}, u32[]{:S(2)}) collective-permute-start(f32[16,128]{1,0:T(8,128)S(1)} %get-tuple-element.11.refs_0_), channel_id=1, source_target_pairs={{0,2},{1,3},{2,0},{3,1},{4,6},{5,7},{6,4},{7,5},{8,10},{9,11},{10,... | collective-permute-start | bytes 24584 | tf_op jit(solution)/shard_map/ppermute | solution.py:216

commit v11 on v10

--- a/solution.py
+++ b/solution.py
@@ -7,7 +7,7 @@
 from jax.experimental.pallas import tpu as pltpu
 from jax.sharding import PartitionSpec as P
 
-CHUNK = 32
+CHUNK = 128
 
 
 def split_masks(devices):
@@ -103,33 +103,23 @@
     )
 
 
-def product_kernel(lo, hi, cands, *refs):
-    cols, refs = refs[:hi], refs[hi:]
-    rows, refs = refs[: lo - 1], refs[lo - 1 :]
-    own, rates, out, row_wide, weights, dist = refs
-    rows = (cols[0], *rows)
-    tall, dims = own.shape[0] // 3, own.shape[1]
+def add_column(col, row_wide, rates, weights, dist, lo):
+    dims = col.shape[1]
+    cands = rates.shape[0] // 8
     size = row_wide.shape[0] // lo
     wide = size // dims
-    lines = (cols[0].shape[0] - size) // wide
-    for k in range(lo):
-        row_wide[pl.ds(k * size, size), :] = widen_row(rows[k][:size, :])
-    for h in range(hi):
-        top = unfold(cols[h][size:, :], lines)
-        top = jnp.concatenate(
-            [top, jnp.zeros((dims - lines, size), top.dtype)], axis=0
-        ).T
-        steps = top.astype(jnp.float32)
-        for c in range(cands):
-            weights[c, pl.ds(h * size, size), :] = jnp.broadcast_to(
-                steps[:, 8 + c : 9 + c], (size, dims)
-            )
-        dist[pl.ds(h * size, size), :] = lax.dot_general(
-            jnp.concatenate([cols[h][:size, :], top], axis=1),
-            row_wide[...],
-            (((1,), (1,)), ((), ())),
-            preferred_element_type=jnp.float32,
-        )
+    lines = (col.shape[0] - size) // wide
+    top = unfold(col[size:, :], lines)
+    top = jnp.concatenate([top, jnp.zeros((dims - lines, size), top.dtype)], axis=0).T
+    steps = top.astype(jnp.float32)
+    for c in range(cands):
+        weights[c] = jnp.broadcast_to(steps[:, 8 + c : 9 + c], (size, dims))
+    dist[...] = lax.dot_general(
+        jnp.concatenate([col[:size, :], top], axis=1),
+        row_wide[...],
+        (((1,), (1,)), ((), ())),
+        preferred_element_type=jnp.float32,
+    )
     rate = [
         jnp.concatenate([rates[pl.ds(8 * c, 8), :]] * wide, axis=1) for c in range(cands)
     ]
@@ -149,17 +139,39 @@
 
     total = lax.fori_loop(
         0,
-        hi * size // CHUNK,
+        size // CHUNK,
         body,
         (jnp.zeros((8, size), jnp.float32),) * (lo * cands),
     )
     total = [jnp.sum(t, axis=0, keepdims=True) for t in total]
+    return [
+        fold(jnp.concatenate(total[k * cands : (k + 1) * cands], axis=0), dims)
+        for k in range(lo)
+    ]
+
+
+def first_kernel(lo, col, *refs):
+    rows, refs = refs[: lo - 1], refs[lo - 1 :]
+    own, rates, out, row_wide, weights, dist = refs
+    tall = own.shape[0] // 3
+    size = row_wide.shape[0] // lo
+    for k, block in enumerate((col, *rows)):
+        row_wide[pl.ds(k * size, size), :] = widen_row(block[:size, :])
+    parts = add_column(col, row_wide, rates, weights, dist, lo)
+    parts[0] += own[pl.ds(2 * tall, tall), :]
     for k in range(lo):
-        part = fold(jnp.concatenate(total[k * cands : (k + 1) * cands], axis=0), dims)
-        if k == 0:
-            part += own[pl.ds(2 * tall, tall), :]
-        out[pl.ds(k * tall, tall), :] = part
+        out[pl.ds(k * tall, tall), :] = parts[k]
     out[pl.ds(lo * tall, 2 * tall), :] = own[pl.ds(0, 2 * tall), :]
+
+
+def next_kernel(lo, col, row_wide, rates, before, out, weights, dist):
+    tall = before.shape[0] // (lo + 2)
+    parts = add_column(col, row_wide, rates, weights, dist, lo)
+    for k in range(lo):
+        at = pl.ds(k * tall, tall)
+        out[at, :] = before[at, :] + parts[k]
+    at = pl.ds(lo * tall, 2 * tall)
+    out[at, :] = before[at, :]
 
 
 def sums_kernel(cands, *refs):
@@ -247,21 +259,30 @@
     rows = [points]
     for mask in row_masks[1:]:
         rows.append(meet(rows[-1], 1) if mask % 2 else meet(points, mask))
-    cols = [packed] + [meet(packed, mask) for mask in col_masks[1:]]
-
-    partial = pl.pallas_call(
-        functools.partial(product_kernel, lo, hi, cands),
-        out_shape=jax.ShapeDtypeStruct(((lo + 2) * tall, dims), jnp.float32),
-        in_specs=[vmem] * (hi + lo + 1),
-        out_specs=vmem,
-        scratch_shapes=[
-            pltpu.VMEM((lo * size, 2 * dims), jnp.bfloat16),
-            pltpu.VMEM((cands, hi * size, dims), jnp.float32),
-            pltpu.VMEM((hi * size, lo * size), jnp.float32),
-        ],
+    spare = [
+        pltpu.VMEM((cands, size, dims), jnp.float32),
+        pltpu.VMEM((size, lo * size), jnp.float32),
+    ]
+    result = jax.ShapeDtypeStruct(((lo + 2) * tall, dims), jnp.float32)
+    partial, row_wide = pl.pallas_call(
+        functools.partial(first_kernel, lo),
+        out_shape=(result, jax.ShapeDtypeStruct((lo * size, 2 * dims), jnp.bfloat16)),
+        in_specs=[vmem] * (lo + 2),
+        out_specs=(vmem, vmem),
+        scratch_shapes=spare,
         compiler_params=params,
-        name="product",
-    )(*cols, *rows[1:], own, rates)
+        name="product_0",
+    )(packed, *rows[1:], own, rates)
+    for mask in reversed(col_masks[1:]):
+        partial = pl.pallas_call(
+            functools.partial(next_kernel, lo),
+            out_shape=result,
+            in_specs=[vmem] * 4,
+            out_specs=vmem,
+            scratch_shapes=spare,
+            compiler_params=params,
+            name="product_%d" % mask,
+        )(meet(packed, mask), row_wide, rates, partial)
 
     image, sums = pl.pallas_call(
         functools.partial(sums_kernel, cands),

time: 29.3 us -> 28.6 us (0.976)
  waiting for transfers between devices: 8.03 us -> 6.71 us
  Pallas kernels: 5.87 us -> 6.41 us
    ppermute x12, waiting for transfers between devices: 8.03 us -> 6.71 us  [meet(): return lax.ppermute(x, 'blk', [(d, d ^ mask) for d in range(devices)])]
    pallas_call x1 -> x4, Pallas kernels: 3.99 us -> 4.54 us  [the longest x3 3.28 us: per_device(): pl.pallas_call(functools.partial(next_kernel, lo), out_shape=result, in_s...]
  transfers between devices with their start and end apart: 12 -> 12, of which waited for: 9 -> 6; matrix products, arithmetic and copies ran while one was open for 0% -> 0% of each run, Pallas kernels for 4% -> 16%
where the time goes in v11:
time: 28.6 us; the launch traced here: 28.5 us
  starting transfers between devices  14.6 us (51%)
  waiting for transfers between devices  6.71 us (23%)
  Pallas kernels  6.41 us (22%)
  between operations  0.72 us (3%)
    ppermute x12, starting transfers between devices, meet(): return lax.ppermute(x, 'blk', [(d, d ^ mask) for d in range(devices)])  14.6 us
    ppermute x12, waiting for transfers between devices, meet(): return lax.ppermute(x, 'blk', [(d, d ^ mask) for d in range(devices)])  6.71 us
    pallas_call x3, Pallas kernels, per_device(): pl.pallas_call(functools.partial(next_kernel, lo), out_shape=result, in_s...  3.28 us
    pallas_call x1, Pallas kernels, per_device(): pl.pallas_call(functools.partial(first_kernel, lo), out_shape=(result, ja...  1.26 us
    pallas_call x1, Pallas kernels, per_device(): pl.pallas_call(pack_kernel, out_shape=(jax.ShapeDtypeStruct((size + extra...  1.08 us
    pallas_call x1, Pallas kernels, per_device(): pl.pallas_call(functools.partial(update_kernel, hi), out_shape=(jax.Shape...  0.78 us
  transfers between devices with their start and end apart: 12, of which 6 were waited for; matrix products, arithmetic and copies ran while one was open for 0% of the time, Pallas kernels for 16%

profile of v11, /device:TPU:0, one launch (start us, length us, event | category | flops | bytes accessed | tf_op | source)
XLA Modules:
  0.0 28.5 jit_solution(12285763496517956482)
XLA Ops:
  0.6 4.1 %collective-permute-start.2 = (bf16[256,128]{1,0:T(8,128)(2,1)}, bf16[256,128]{1,0:T(8,128)(2,1)S(1)}, u32[]{:S(2)}, u32[]{:S(2)}) collective-permute-start(bf16[256,128]{1,0:T(8,128)(2,1)} %points.1), channel_id=1, source_target_pairs={{0,8},{1,9},{2,10},{3,11},{4,12},{5,13},{6,14},{7,15},{8,0},{9,1},... | collective-permute-start | bytes 196616 | tf_op jit(solution)/shard_map/ppermute | solution.py:228
  4.7 1.1 %pack.1 = (bf16[288,128]{1,0:T(8,128)(2,1)S(1)}, f32[24,128]{1,0:T(8,128)S(1)}, f32[32,128]{1,0:T(8,128)S(1)}) custom-call(bf16[256,128]{1,0:T(8,128)(2,1)} %points.1, f32[4,256]{1,0:T(4,128)} %refs_7_.1, f32[4,256]{1,0:T(4,128)} %refs_6_.1, f32[4]{0:T(128)} %length.1, f32[4]{0:T(128)} %noise.1), custom_call_target="tpu_custom_call" | custom-call | tf_op jit(solution)/shard_map/pack/pallas_call | solution.py:234
  5.8 2.6 %collective-permute-start.5 = (bf16[288,128]{1,0:T(8,128)(2,1)S(1)}, bf16[288,128]{1,0:T(8,128)(2,1)S(1)}, u32[]{:S(2)}, u32[]{:S(2)}) collective-permute-start(bf16[288,128]{1,0:T(8,128)(2,1)S(1)} %get-tuple-element.10.col), channel_id=1, source_target_pairs={{0,6},{1,7},{2,4},{3,5},{4,2},{5,3},{6,0},{7,1},{8,14},{9,15},{10,... | collective-permute-start | bytes 221192 | tf_op jit(solution)/shard_map/ppermute | solution.py:228
  8.4 0.4 %collective-permute-start.4 = (bf16[288,128]{1,0:T(8,128)(2,1)S(1)}, bf16[288,128]{1,0:T(8,128)(2,1)S(1)}, u32[]{:S(2)}, u32[]{:S(2)}) collective-permute-start(bf16[288,128]{1,0:T(8,128)(2,1)S(1)} %get-tuple-element.10.col), channel_id=1, source_target_pairs={{0,4},{1,5},{2,6},{3,7},{4,0},{5,1},{6,2},{7,3},{8,12},{9,13},{10,... | collective-permute-start | bytes 221192 | tf_op jit(solution)/shard_map/ppermute | solution.py:228
  8.9 0.5 %collective-permute-start = (bf16[288,128]{1,0:T(8,128)(2,1)S(1)}, bf16[288,128]{1,0:T(8,128)(2,1)S(1)}, u32[]{:S(2)}, u32[]{:S(2)}) collective-permute-start(bf16[288,128]{1,0:T(8,128)(2,1)S(1)} %get-tuple-element.10.col), channel_id=1, source_target_pairs={{0,2},{1,3},{2,0},{3,1},{4,6},{5,7},{6,4},{7,5},{8,10},{9,11},{10,... | collective-permute-start | bytes 221192 | tf_op jit(solution)/shard_map/ppermute | solution.py:228
  9.4 0.5 %collective-permute-start.3 = (bf16[256,128]{1,0:T(8,128)(2,1)S(1)}, bf16[256,128]{1,0:T(8,128)(2,1)S(1)}, u32[]{:S(2)}, u32[]{:S(2)}) collective-permute-start(bf16[256,128]{1,0:T(8,128)(2,1)S(1)} %collective-permute-done.2.refs_1_), channel_id=1, source_target_pairs={{0,1},{1,0},{2,3},{3,2},{4,5},{5,4},{6,7},{7,6},{8,9},{9,8},{10,11... | collective-permute-start | bytes 196616 | tf_op jit(solution)/shard_map/ppermute | solution.py:228
  9.9 0.7 %collective-permute-done.1.refs_0_ = bf16[256,128]{1,0:T(8,128)(2,1)S(1)} collective-permute-done((bf16[256,128]{1,0:T(8,128)(2,1)S(1)}, bf16[256,128]{1,0:T(8,128)(2,1)S(1)}, u32[]{:S(2)}, u32[]{:S(2)}) %collective-permute-start.1) | collective-permute-done | bytes 65568 | tf_op jit(solution)/shard_map/ppermute | solution.py:228
  10.6 0.2 collective-permute-done.3.refs_2_
  10.8 1.3 %product_0.1 = (f32[48,128]{1,0:T(8,128)S(1)}, bf16[1024,256]{1,0:T(8,128)(2,1)S(1)}) custom-call(bf16[288,128]{1,0:T(8,128)(2,1)S(1)} %get-tuple-element.10.col, bf16[256,128]{1,0:T(8,128)(2,1)S(1)} %collective-permute-done.1.refs_0_, bf16[256,128]{1,0:T(8,128)(2,1)S(1)} %collective-permute-done.2.refs_1_, ...), custom_call_target="tpu_custom_call" | custom-call | tf_op jit(solution)/shard_map/product_0/pallas_call | solution.py:267
  12.1 1.1 %product_6.1.before = f32[48,128]{1,0:T(8,128)S(1)} custom-call(bf16[288,128]{1,0:T(8,128)(2,1)S(1)} %collective-permute-done.5.col, bf16[1024,256]{1,0:T(8,128)(2,1)S(1)} %get-tuple-element.13.row_wide, f32[32,128]{1,0:T(8,128)S(1)} %get-tuple-element.12.refs_4_.rates, f32[48,128]{1,0:T(8,128)S(1)} %get-tuple-element.14.before), custom_call_target="tpu_custom_call" | custom-call | tf_op jit(solution)/shard_map/product_6/pallas_call | solution.py:277
  13.2 1.1 %product_4.1.before = f32[48,128]{1,0:T(8,128)S(1)} custom-call(bf16[288,128]{1,0:T(8,128)(2,1)S(1)} %collective-permute-done.4.col, bf16[1024,256]{1,0:T(8,128)(2,1)S(1)} %get-tuple-element.13.row_wide, f32[32,128]{1,0:T(8,128)S(1)} %get-tuple-element.12.refs_4_.rates, f32[48,128]{1,0:T(8,128)S(1)} %product_6.1.before), custom_call_target="tpu_custom_call" | custom-call | tf_op jit(solution)/shard_map/product_4/pallas_call | solution.py:277
  14.3 0.0 collective-permute-done.col
  14.3 1.1 %product_2.1.refs_0_ = f32[48,128]{1,0:T(8,128)S(1)} custom-call(bf16[288,128]{1,0:T(8,128)(2,1)S(1)} %collective-permute-done.col, bf16[1024,256]{1,0:T(8,128)(2,1)S(1)} %get-tuple-element.13.row_wide, f32[32,128]{1,0:T(8,128)S(1)} %get-tuple-element.12.refs_4_.rates, f32[48,128]{1,0:T(8,128)S(1)} %product_4.1.before), custom_call_target="tpu_custom_call" | custom-call | tf_op jit(solution)/shard_map/product_2/pallas_call | solution.py:277
  15.4 0.4 %collective-permute-start.6 = (f32[48,128]{1,0:T(8,128)S(1)}, f32[48,128]{1,0:T(8,128)S(1)}, u32[]{:S(2)}, u32[]{:S(2)}) collective-permute-start(f32[48,128]{1,0:T(8,128)S(1)} %product_2.1.refs_0_), channel_id=1, source_target_pairs={{0,1},{1,0},{2,3},{3,2},{4,5},{5,4},{6,7},{7,6},{8,9},{9,8},{10,11... | collective-permute-start | bytes 73736 | tf_op jit(solution)/shard_map/ppermute | solution.py:228
  15.8 0.4 %collective-permute-start.7 = (f32[48,128]{1,0:T(8,128)S(1)}, f32[48,128]{1,0:T(8,128)S(1)}, u32[]{:S(2)}, u32[]{:S(2)}) collective-permute-start(f32[48,128]{1,0:T(8,128)S(1)} %product_2.1.refs_0_), channel_id=1, source_target_pairs={{0,8},{1,9},{2,10},{3,11},{4,12},{5,13},{6,14},{7,15},{8,0},{9,1},... | collective-permute-start | bytes 73736 | tf_op jit(solution)/shard_map/ppermute | solution.py:228
  16.2 2.0 %collective-permute-start.8 = (f32[48,128]{1,0:T(8,128)S(1)}, f32[48,128]{1,0:T(8,128)S(1)}, u32[]{:S(2)}, u32[]{:S(2)}) collective-permute-start(f32[48,128]{1,0:T(8,128)S(1)} %product_2.1.refs_0_), channel_id=1, source_target_pairs={{0,9},{1,8},{2,11},{3,10},{4,13},{5,12},{6,15},{7,14},{8,1},{9,0},... | collective-permute-start | bytes 73736 | tf_op jit(solution)/shard_map/ppermute | solution.py:228
  18.2 2.6 %collective-permute-done.7.refs_2_ = f32[48,128]{1,0:T(8,128)S(1)} collective-permute-done((f32[48,128]{1,0:T(8,128)S(1)}, f32[48,128]{1,0:T(8,128)S(1)}, u32[]{:S(2)}, u32[]{:S(2)}) %collective-permute-start.7) | collective-permute-done | bytes 24608 | tf_op jit(solution)/shard_map/ppermute | solution.py:228
  20.9 2.1 %collective-permute-start.10 = (f32[16,128]{1,0:T(8,128)S(1)}, f32[16,128]{1,0:T(8,128)S(1)}, u32[]{:S(2)}, u32[]{:S(2)}) collective-permute-start(f32[16,128]{1,0:T(8,128)S(1)} %get-tuple-element.15.refs_0_), channel_id=1, source_target_pairs={{0,4},{1,5},{2,6},{3,7},{4,0},{5,1},{6,2},{7,3},{8,12},{9,13},{10,... | collective-permute-start | bytes 24584 | tf_op jit(solution)/shard_map/ppermute | solution.py:228
  23.0 1.1 %collective-permute-start.11 = (f32[16,128]{1,0:T(8,128)S(1)}, f32[16,128]{1,0:T(8,128)S(1)}, u32[]{:S(2)}, u32[]{:S(2)}) collective-permute-start(f32[16,128]{1,0:T(8,128)S(1)} %get-tuple-element.15.refs_0_), channel_id=1, source_target_pairs={{0,6},{1,7},{2,4},{3,5},{4,2},{5,3},{6,0},{7,1},{8,14},{9,15},{10,... | collective-permute-start | bytes 24584 | tf_op jit(solution)/shard_map/ppermute | solution.py:228
  24.0 0.5 %collective-permute-start.9 = (f32[16,128]{1,0:T(8,128)S(1)}, f32[16,128]{1,0:T(8,128)S(1)}, u32[]{:S(2)}, u32[]{:S(2)}) collective-permute-start(f32[16,128]{1,0:T(8,128)S(1)} %get-tuple-element.15.refs_0_), channel_id=1, source_target_pairs={{0,2},{1,3},{2,0},{3,1},{4,6},{5,7},{6,4},{7,5},{8,10},{9,11},{10,... | collective-permute-start | bytes 24584 | tf_op jit(solution)/shard_map/ppermute | solution.py:228
  24.5 0.1 collective-permute-done.10.refs_2_
  24.6 2.9 %collective-permute-done.11.refs_3_ = f32[16,128]{1,0:T(8,128)S(1)} collective-permute-done((f32[16,128]{1,0:T(8,128)S(1)}, f32[16,128]{1,0:T(8,128)S(1)}, u32[]{:S(2)}, u32[]{:S(2)}) %collective-permute-start.11) | collective-permute-done | bytes 8224 | tf_op jit(solution)/shard_map/ppermute | solution.py:228
  27.5 0.2 collective-permute-done.9.refs_1_
  27.7 0.8 %update.1 = (f32[4,256]{1,0:T(4,128)}, f32[4,256]{1,0:T(4,128)}, f32[4,256]{1,0:T(4,128)}) custom-call(f32[16,128]{1,0:T(8,128)S(1)} %get-tuple-element.15.refs_0_, f32[16,128]{1,0:T(8,128)S(1)} %collective-permute-done.9.refs_1_, f32[16,128]{1,0:T(8,128)S(1)} %collective-permute-done.10.refs_2_, f32[16,128]{1,0:T(8,128)S(1)} %collective-permute-done.11.refs_3_, ...), custom_call_target="tpu_custom_call" | custom-call | tf_op jit(solution)/shard_map/update/pallas_call | solution.py:299
  (15 shorter events, 0.0 us)
Async XLA Ops:
  0.6 8.8 %copy-start.3 = (bf16[256,128]{1,0:T(8,128)(2,1)S(1)}, bf16[256,128]{1,0:T(8,128)(2,1)}, u32[]{:S(2)}) copy-start(bf16[256,128]{1,0:T(8,128)(2,1)} %points.1) | copy-start | bytes 196612
  0.6 8.8 %collective-permute-start.2 = (bf16[256,128]{1,0:T(8,128)(2,1)}, bf16[256,128]{1,0:T(8,128)(2,1)S(1)}, u32[]{:S(2)}, u32[]{:S(2)}) collective-permute-start(bf16[256,128]{1,0:T(8,128)(2,1)} %points.1), channel_id=1, source_target_pairs={{0,8},{1,9},{2,10},{3,11},{4,12},{5,13},{6,14},{7,15},{8,0},{9,1},... | collective-permute-start | bytes 196616 | tf_op jit(solution)/shard_map/ppermute | solution.py:228
  5.8 6.2 %collective-permute-start.5 = (bf16[288,128]{1,0:T(8,128)(2,1)S(1)}, bf16[288,128]{1,0:T(8,128)(2,1)S(1)}, u32[]{:S(2)}, u32[]{:S(2)}) collective-permute-start(bf16[288,128]{1,0:T(8,128)(2,1)S(1)} %get-tuple-element.10.col), channel_id=1, source_target_pairs={{0,6},{1,7},{2,4},{3,5},{4,2},{5,3},{6,0},{7,1},{8,14},{9,15},{10,... | collective-permute-start | bytes 221192 | tf_op jit(solution)/shard_map/ppermute | solution.py:228
  8.4 4.8 %collective-permute-start.4 = (bf16[288,128]{1,0:T(8,128)(2,1)S(1)}, bf16[288,128]{1,0:T(8,128)(2,1)S(1)}, u32[]{:S(2)}, u32[]{:S(2)}) collective-permute-start(bf16[288,128]{1,0:T(8,128)(2,1)S(1)} %get-tuple-element.10.col), channel_id=1, source_target_pairs={{0,4},{1,5},{2,6},{3,7},{4,0},{5,1},{6,2},{7,3},{8,12},{9,13},{10,... | collective-permute-start | bytes 221192 | tf_op jit(solution)/shard_map/ppermute | solution.py:228
  8.9 5.4 %collective-permute-start = (bf16[288,128]{1,0:T(8,128)(2,1)S(1)}, bf16[288,128]{1,0:T(8,128)(2,1)S(1)}, u32[]{:S(2)}, u32[]{:S(2)}) collective-permute-start(bf16[288,128]{1,0:T(8,128)(2,1)S(1)} %get-tuple-element.10.col), channel_id=1, source_target_pairs={{0,2},{1,3},{2,0},{3,1},{4,6},{5,7},{6,4},{7,5},{8,10},{9,11},{10,... | collective-permute-start | bytes 221192 | tf_op jit(solution)/shard_map/ppermute | solution.py:228
  9.4 1.3 %collective-permute-start.1 = (bf16[256,128]{1,0:T(8,128)(2,1)S(1)}, bf16[256,128]{1,0:T(8,128)(2,1)S(1)}, u32[]{:S(2)}, u32[]{:S(2)}) collective-permute-start(bf16[256,128]{1,0:T(8,128)(2,1)S(1)} %copy-done.3), channel_id=1, source_target_pairs={{0,1},{1,0},{2,3},{3,2},{4,5},{5,4},{6,7},{7,6},{8,9},{9,8},{10,11... | collective-permute-start | bytes 196616 | tf_op jit(solution)/shard_map/ppermute | solution.py:228
  9.4 1.4 %collective-permute-start.3 = (bf16[256,128]{1,0:T(8,128)(2,1)S(1)}, bf16[256,128]{1,0:T(8,128)(2,1)S(1)}, u32[]{:S(2)}, u32[]{:S(2)}) collective-permute-start(bf16[256,128]{1,0:T(8,128)(2,1)S(1)} %collective-permute-done.2.refs_1_), channel_id=1, source_target_pairs={{0,1},{1,0},{2,3},{3,2},{4,5},{5,4},{6,7},{7,6},{8,9},{9,8},{10,11... | collective-permute-start | bytes 196616 | tf_op jit(solution)/shard_map/ppermute | solution.py:228
  15.4 2.8 %collective-permute-start.6 = (f32[48,128]{1,0:T(8,128)S(1)}, f32[48,128]{1,0:T(8,128)S(1)}, u32[]{:S(2)}, u32[]{:S(2)}) collective-permute-start(f32[48,128]{1,0:T(8,128)S(1)} %product_2.1.refs_0_), channel_id=1, source_target_pairs={{0,1},{1,0},{2,3},{3,2},{4,5},{5,4},{6,7},{7,6},{8,9},{9,8},{10,11... | collective-permute-start | bytes 73736 | tf_op jit(solution)/shard_map/ppermute | solution.py:228
  15.8 5.0 %collective-permute-start.7 = (f32[48,128]{1,0:T(8,128)S(1)}, f32[48,128]{1,0:T(8,128)S(1)}, u32[]{:S(2)}, u32[]{:S(2)}) collective-permute-start(f32[48,128]{1,0:T(8,128)S(1)} %product_2.1.refs_0_), channel_id=1, source_target_pairs={{0,8},{1,9},{2,10},{3,11},{4,12},{5,13},{6,14},{7,15},{8,0},{9,1},... | collective-permute-start | bytes 73736 | tf_op jit(solution)/shard_map/ppermute | solution.py:228
  16.2 4.7 %collective-permute-start.8 = (f32[48,128]{1,0:T(8,128)S(1)}, f32[48,128]{1,0:T(8,128)S(1)}, u32[]{:S(2)}, u32[]{:S(2)}) collective-permute-start(f32[48,128]{1,0:T(8,128)S(1)} %product_2.1.refs_0_), channel_id=1, source_target_pairs={{0,9},{1,8},{2,11},{3,10},{4,13},{5,12},{6,15},{7,14},{8,1},{9,0},... | collective-permute-start | bytes 73736 | tf_op jit(solution)/shard_map/ppermute | solution.py:228
  20.9 6.8 %copy-start = (f32[4,256]{1,0:T(4,128)S(1)}, f32[4,256]{1,0:T(4,128)}, u32[]{:S(2)}) copy-start(f32[4,256]{1,0:T(4,128)} %refs_7_.1) | copy-start | bytes 12292
  20.9 6.8 %copy-start.1 = (f32[4,256]{1,0:T(4,128)S(1)}, f32[4,256]{1,0:T(4,128)}, u32[]{:S(2)}) copy-start(f32[4,256]{1,0:T(4,128)} %refs_6_.1) | copy-start | bytes 12292
  20.9 6.8 %copy-start.2 = (f32[4,256]{1,0:T(4,128)S(1)}, f32[4,256]{1,0:T(4,128)}, u32[]{:S(2)}) copy-start(f32[4,256]{1,0:T(4,128)} %refs_5_.1) | copy-start | bytes 12292
  20.9 3.7 %collective-permute-start.10 = (f32[16,128]{1,0:T(8,128)S(1)}, f32[16,128]{1,0:T(8,128)S(1)}, u32[]{:S(2)}, u32[]{:S(2)}) collective-permute-start(f32[16,128]{1,0:T(8,128)S(1)} %get-tuple-element.15.refs_0_), channel_id=1, source_target_pairs={{0,4},{1,5},{2,6},{3,7},{4,0},{5,1},{6,2},{7,3},{8,12},{9,13},{10,... | collective-permute-start | bytes 24584 | tf_op jit(solution)/shard_map/ppermute | solution.py:228
  23.0 4.5 %collective-permute-start.11 = (f32[16,128]{1,0:T(8,128)S(1)}, f32[16,128]{1,0:T(8,128)S(1)}, u32[]{:S(2)}, u32[]{:S(2)}) collective-permute-start(f32[16,128]{1,0:T(8,128)S(1)} %get-tuple-element.15.refs_0_), channel_id=1, source_target_pairs={{0,6},{1,7},{2,4},{3,5},{4,2},{5,3},{6,0},{7,1},{8,14},{9,15},{10,... | collective-permute-start | bytes 24584 | tf_op jit(solution)/shard_map/ppermute | solution.py:228
  24.0 3.7 %collective-permute-start.9 = (f32[16,128]{1,0:T(8,128)S(1)}, f32[16,128]{1,0:T(8,128)S(1)}, u32[]{:S(2)}, u32[]{:S(2)}) collective-permute-start(f32[16,128]{1,0:T(8,128)S(1)} %get-tuple-element.15.refs_0_), channel_id=1, source_target_pairs={{0,2},{1,3},{2,0},{3,1},{4,6},{5,7},{6,4},{7,5},{8,10},{9,11},{10,... | collective-permute-start | bytes 24584 | tf_op jit(solution)/shard_map/ppermute | solution.py:228

commit v12 on v11

--- a/solution.py
+++ b/solution.py
@@ -103,23 +103,27 @@
     )
 
 
-def add_column(col, row_wide, rates, weights, dist, lo):
-    dims = col.shape[1]
+def add_columns(cols, row_wide, rates, weights, dist, lo):
+    dims = cols[0].shape[1]
     cands = rates.shape[0] // 8
     size = row_wide.shape[0] // lo
     wide = size // dims
-    lines = (col.shape[0] - size) // wide
-    top = unfold(col[size:, :], lines)
-    top = jnp.concatenate([top, jnp.zeros((dims - lines, size), top.dtype)], axis=0).T
-    steps = top.astype(jnp.float32)
-    for c in range(cands):
-        weights[c] = jnp.broadcast_to(steps[:, 8 + c : 9 + c], (size, dims))
-    dist[...] = lax.dot_general(
-        jnp.concatenate([col[:size, :], top], axis=1),
-        row_wide[...],
-        (((1,), (1,)), ((), ())),
-        preferred_element_type=jnp.float32,
-    )
+    lines = (cols[0].shape[0] - size) // wide
+    for h, col in enumerate(cols):
+        at = pl.ds(h * size, size)
+        top = unfold(col[size:, :], lines)
+        top = jnp.concatenate(
+            [top, jnp.zeros((dims - lines, size), top.dtype)], axis=0
+        ).T
+        steps = top.astype(jnp.float32)
+        for c in range(cands):
+            weights[c, at, :] = jnp.broadcast_to(steps[:, 8 + c : 9 + c], (size, dims))
+        dist[at, :] = lax.dot_general(
+            jnp.concatenate([col[:size, :], top], axis=1),
+            row_wide[...],
+            (((1,), (1,)), ((), ())),
+            preferred_element_type=jnp.float32,
+        )
     rate = [
         jnp.concatenate([rates[pl.ds(8 * c, 8), :]] * wide, axis=1) for c in range(cands)
     ]
@@ -139,7 +143,7 @@
 
     total = lax.fori_loop(
         0,
-        size // CHUNK,
+        len(cols) * size // CHUNK,
         body,
         (jnp.zeros((8, size), jnp.float32),) * (lo * cands),
     )
@@ -157,16 +161,17 @@
     size = row_wide.shape[0] // lo
     for k, block in enumerate((col, *rows)):
         row_wide[pl.ds(k * size, size), :] = widen_row(block[:size, :])
-    parts = add_column(col, row_wide, rates, weights, dist, lo)
+    parts = add_columns([col], row_wide, rates, weights, dist, lo)
     parts[0] += own[pl.ds(2 * tall, tall), :]
     for k in range(lo):
         out[pl.ds(k * tall, tall), :] = parts[k]
     out[pl.ds(lo * tall, 2 * tall), :] = own[pl.ds(0, 2 * tall), :]
 
 
-def next_kernel(lo, col, row_wide, rates, before, out, weights, dist):
+def rest_kernel(lo, *refs):
+    *cols, row_wide, rates, before, out, weights, dist = refs
     tall = before.shape[0] // (lo + 2)
-    parts = add_column(col, row_wide, rates, weights, dist, lo)
+    parts = add_columns(cols, row_wide, rates, weights, dist, lo)
     for k in range(lo):
         at = pl.ds(k * tall, tall)
         out[at, :] = before[at, :] + parts[k]
@@ -174,17 +179,27 @@
     out[at, :] = before[at, :]
 
 
-def sums_kernel(cands, *refs):
-    *parts, image_out, sums_out = refs
-    lo = len(parts)
+def merge_kernel(lo, *refs):
+    *parts, out = refs
+    tall = parts[0].shape[0] // (lo + 2)
+    for k in range(lo):
+        total = parts[0][pl.ds(k * tall, tall), :]
+        for m in range(1, len(parts)):
+            total = total + parts[m][pl.ds((k ^ (2 * m)) * tall, tall), :]
+        out[pl.ds(k * tall, tall), :] = total
+    for m, part in enumerate(parts):
+        out[pl.ds((lo + 2 * m) * tall, 2 * tall), :] = part[pl.ds(lo * tall, 2 * tall), :]
+
+
+def sums_kernel(lo, cands, mine, other, image_out, sums_out):
     tall, dims = image_out.shape
     sums = [jnp.zeros((tall, dims), jnp.float32)] * 4
     for k in range(lo):
-        step = parts[k][pl.ds(lo * tall, tall), :]
-        rest = parts[k][pl.ds((lo + 1) * tall, tall), :]
-        image = parts[0][pl.ds(k * tall, tall), :]
-        for m in range(1, lo):
-            image = image + parts[m][pl.ds((k ^ m) * tall, tall), :]
+        holder = other if k % 2 else mine
+        base = lo + 2 * (k // 2)
+        step = holder[pl.ds(base * tall, tall), :]
+        rest = holder[pl.ds((base + 1) * tall, tall), :]
+        image = mine[pl.ds(k * tall, tall), :] + other[pl.ds((k ^ 1) * tall, tall), :]
         if k == 0:
             image_out[...] = image
         terms = (rest * rest, step * image, rest * image, image * image)
@@ -195,13 +210,12 @@
         )
 
 
-def update_kernel(hi, *refs):
-    sums, refs = refs[:hi], refs[hi:]
-    image, solution, residual, direction, out_s, out_r, out_d = refs
+def update_kernel(*refs):
+    *sums, image, solution, residual, direction, out_s, out_r, out_d = refs
     cands = solution.shape[0]
     total = sums[0][...]
-    for h in range(1, hi):
-        total = total + sums[h][...]
+    for part in sums[1:]:
+        total = total + part[...]
     total = jnp.sum(total, axis=1, keepdims=True)
     norm, curve, cross, square = (
         total[i * cands : (i + 1) * cands] for i in range(4)
@@ -224,8 +238,9 @@
     tall = cands * size // dims
     extra = -(-(8 + cands) // 16) * 16 * size // dims
 
-    def meet(x, mask):
-        return lax.ppermute(x, "blk", [(d, d ^ mask) for d in range(devices)])
+    def meet(x, mask, odd_mask=None):
+        masks = (mask, mask if odd_mask is None else odd_mask)
+        return lax.ppermute(x, "blk", [(d, d ^ masks[d % 2]) for d in range(devices)])
 
     vmem = pl.BlockSpec(memory_space=pltpu.VMEM)
     hbm = pl.BlockSpec(memory_space=pltpu.HBM)
@@ -259,51 +274,67 @@
     rows = [points]
     for mask in row_masks[1:]:
         rows.append(meet(rows[-1], 1) if mask % 2 else meet(points, mask))
-    spare = [
-        pltpu.VMEM((cands, size, dims), jnp.float32),
-        pltpu.VMEM((size, lo * size), jnp.float32),
-    ]
+    def spare(count):
+        return [
+            pltpu.VMEM((cands, count * size, dims), jnp.float32),
+            pltpu.VMEM((count * size, lo * size), jnp.float32),
+        ]
+
     result = jax.ShapeDtypeStruct(((lo + 2) * tall, dims), jnp.float32)
     partial, row_wide = pl.pallas_call(
         functools.partial(first_kernel, lo),
         out_shape=(result, jax.ShapeDtypeStruct((lo * size, 2 * dims), jnp.bfloat16)),
         in_specs=[vmem] * (lo + 2),
         out_specs=(vmem, vmem),
-        scratch_shapes=spare,
-        compiler_params=params,
-        name="product_0",
+        scratch_shapes=spare(1),
+        compiler_params=params,
+        name="product_own",
     )(packed, *rows[1:], own, rates)
-    for mask in reversed(col_masks[1:]):
-        partial = pl.pallas_call(
-            functools.partial(next_kernel, lo),
-            out_shape=result,
-            in_specs=[vmem] * 4,
-            out_specs=vmem,
-            scratch_shapes=spare,
-            compiler_params=params,
-            name="product_%d" % mask,
-        )(meet(packed, mask), row_wide, rates, partial)
+    partial = pl.pallas_call(
+        functools.partial(rest_kernel, lo),
+        out_shape=result,
+        in_specs=[vmem] * (hi + 2),
+        out_specs=vmem,
+        scratch_shapes=spare(hi - 1),
+        compiler_params=params,
+        name="product_rest",
+    )(*(meet(packed, mask) for mask in col_masks[1:]), row_wide, rates, partial)
+
+    merged = pl.pallas_call(
+        functools.partial(merge_kernel, lo),
+        out_shape=jax.ShapeDtypeStruct((2 * lo * tall, dims), jnp.float32),
+        in_specs=[vmem] * (lo // 2),
+        out_specs=vmem,
+        compiler_params=params,
+        name="merge",
+    )(partial, *(meet(partial, mask) for mask in row_masks[2::2]))
 
     image, sums = pl.pallas_call(
-        functools.partial(sums_kernel, cands),
+        functools.partial(sums_kernel, lo, cands),
         out_shape=(
             jax.ShapeDtypeStruct((tall, dims), jnp.float32),
             jax.ShapeDtypeStruct((4 * cands, dims), jnp.float32),
         ),
-        in_specs=[vmem] * lo,
+        in_specs=[vmem] * 2,
         out_specs=(vmem, vmem),
         compiler_params=params,
         name="sums",
-    )(partial, *(meet(partial, mask) for mask in row_masks[1:]))
+    )(merged, meet(merged, 1))
+
+    shared = [
+        meet(sums, even, odd) for even, odd in zip(col_masks[1:-1:2], col_masks[2:-1:2])
+    ]
+    shared += [meet(x, 1) for x in shared]
+    parts = [sums, meet(sums, col_masks[-1]), *shared]
 
     return pl.pallas_call(
-        functools.partial(update_kernel, hi),
+        update_kernel,
         out_shape=(jax.ShapeDtypeStruct((cands, size), jnp.float32),) * 3,
-        in_specs=[vmem] * (hi + 4),
+        in_specs=[vmem] * (len(parts) + 4),
         out_specs=(vmem,) * 3,
         compiler_params=params,
         name="update",
-    )(sums, *(meet(sums, mask) for mask in col_masks[1:]), image, solution, residual, direction)
+    )(*parts, image, solution, residual, direction)
 
 
 def solution(mesh):

time: 28.6 us -> 29.1 us (1.017)
  waiting for transfers between devices: 6.71 us -> 11.9 us
  starting transfers between devices: 14.6 us -> 10.4 us
  Pallas kernels: 6.41 us -> 5.93 us
    ppermute x12 -> x11, waiting for transfers between devices: 6.71 us -> 11.9 us  [meet(): lax.ppermute(x, 'blk', [(d, d ^ masks[d % 2]) for d in range(devices)])]
    ppermute x12 -> x11, starting transfers between devices: 14.6 us -> 10.4 us  [meet(): lax.ppermute(x, 'blk', [(d, d ^ masks[d % 2]) for d in range(devices)])]
    pallas_call x5 -> x4, Pallas kernels: 4.07 us -> 3.58 us  [the longest x1 2.78 us: per_device(): pl.pallas_call(functools.partial(rest_kernel, lo), out_shape=result, in_s...]
  transfers between devices with their start and end apart: 12 -> 11, of which waited for: 6 -> 7; matrix products, arithmetic and copies ran while one was open for 0% -> 0% of each run, Pallas kernels for 16% -> 8%
where the time goes in v12:
time: 29.1 us; the launch traced here: 29 us
  waiting for transfers between devices  11.9 us (41%)
  starting transfers between devices  10.4 us (36%)
  Pallas kernels  5.93 us (20%)
  between operations  0.7 us (2%)
    ppermute x11, waiting for transfers between devices, meet(): lax.ppermute(x, 'blk', [(d, d ^ masks[d % 2]) for d in range(devices)])  11.9 us
    ppermute x11, starting transfers between devices, meet(): lax.ppermute(x, 'blk', [(d, d ^ masks[d % 2]) for d in range(devices)])  10.4 us
    pallas_call x1, Pallas kernels, per_device(): pl.pallas_call(functools.partial(rest_kernel, lo), out_shape=result, in_s...  2.78 us
    pallas_call x1, Pallas kernels, per_device(): pl.pallas_call(functools.partial(first_kernel, lo), out_shape=(result, ja...  1.27 us
    pallas_call x1, Pallas kernels, per_device(): pl.pallas_call(pack_kernel, out_shape=(jax.ShapeDtypeStruct((size + extra...  1.08 us
    pallas_call x1, Pallas kernels, per_device(): pl.pallas_call(update_kernel, out_shape=(jax.ShapeDtypeStruct((cands, siz...  0.78 us
  transfers between devices with their start and end apart: 11, of which 7 were waited for; matrix products, arithmetic and copies ran while one was open for 0% of the time, Pallas kernels for 8%

profile of v12, /device:TPU:0, one launch (start us, length us, event | category | flops | bytes accessed | tf_op | source)
XLA Modules:
  0.0 29.0 jit_solution(16170815020243382283)
XLA Ops:
  0.6 4.1 %collective-permute-start.4 = (bf16[256,128]{1,0:T(8,128)(2,1)}, bf16[256,128]{1,0:T(8,128)(2,1)S(1)}, u32[]{:S(2)}, u32[]{:S(2)}) collective-permute-start(bf16[256,128]{1,0:T(8,128)(2,1)} %points.1), channel_id=1, source_target_pairs={{0,8},{1,9},{2,10},{3,11},{4,12},{5,13},{6,14},{7,15},{8,0},{9,1},... | collective-permute-start | bytes 196616 | tf_op jit(solution)/shard_map/ppermute | solution.py:243
  4.7 1.1 %pack.1 = (bf16[288,128]{1,0:T(8,128)(2,1)S(1)}, f32[24,128]{1,0:T(8,128)S(1)}, f32[32,128]{1,0:T(8,128)S(1)}) custom-call(bf16[256,128]{1,0:T(8,128)(2,1)} %points.1, f32[4,256]{1,0:T(4,128)} %refs_7_.1, f32[4,256]{1,0:T(4,128)} %refs_6_.1, f32[4]{0:T(128)} %length.1, f32[4]{0:T(128)} %noise.1), custom_call_target="tpu_custom_call" | custom-call | tf_op jit(solution)/shard_map/pack/pallas_call | solution.py:249
  5.8 1.6 %collective-permute-start = (bf16[288,128]{1,0:T(8,128)(2,1)S(1)}, bf16[288,128]{1,0:T(8,128)(2,1)S(1)}, u32[]{:S(2)}, u32[]{:S(2)}) collective-permute-start(bf16[288,128]{1,0:T(8,128)(2,1)S(1)} %get-tuple-element.10.col), channel_id=1, source_target_pairs={{0,2},{1,3},{2,0},{3,1},{4,6},{5,7},{6,4},{7,5},{8,10},{9,11},{10,... | collective-permute-start | bytes 221192 | tf_op jit(solution)/shard_map/ppermute | solution.py:243
  7.4 1.6 %collective-permute-start.1 = (bf16[288,128]{1,0:T(8,128)(2,1)S(1)}, bf16[288,128]{1,0:T(8,128)(2,1)S(1)}, u32[]{:S(2)}, u32[]{:S(2)}) collective-permute-start(bf16[288,128]{1,0:T(8,128)(2,1)S(1)} %get-tuple-element.10.col), channel_id=1, source_target_pairs={{0,4},{1,5},{2,6},{3,7},{4,0},{5,1},{6,2},{7,3},{8,12},{9,13},{10,... | collective-permute-start | bytes 221192 | tf_op jit(solution)/shard_map/ppermute | solution.py:243
  9.0 0.4 %collective-permute-start.2 = (bf16[288,128]{1,0:T(8,128)(2,1)S(1)}, bf16[288,128]{1,0:T(8,128)(2,1)S(1)}, u32[]{:S(2)}, u32[]{:S(2)}) collective-permute-start(bf16[288,128]{1,0:T(8,128)(2,1)S(1)} %get-tuple-element.10.col), channel_id=1, source_target_pairs={{0,6},{1,7},{2,4},{3,5},{4,2},{5,3},{6,0},{7,1},{8,14},{9,15},{10,... | collective-permute-start | bytes 221192 | tf_op jit(solution)/shard_map/ppermute | solution.py:243
  9.4 0.0 collective-permute-start.3
  9.4 0.0 collective-permute-done.4.refs_1_
  9.4 0.5 %collective-permute-start.5 = (bf16[256,128]{1,0:T(8,128)(2,1)S(1)}, bf16[256,128]{1,0:T(8,128)(2,1)S(1)}, u32[]{:S(2)}, u32[]{:S(2)}) collective-permute-start(bf16[256,128]{1,0:T(8,128)(2,1)S(1)} %collective-permute-done.4.refs_1_), channel_id=1, source_target_pairs={{0,1},{1,0},{2,3},{3,2},{4,5},{5,4},{6,7},{7,6},{8,9},{9,8},{10,11... | collective-permute-start | bytes 196616 | tf_op jit(solution)/shard_map/ppermute | solution.py:243
  9.9 0.7 %collective-permute-done.3.refs_0_ = bf16[256,128]{1,0:T(8,128)(2,1)S(1)} collective-permute-done((bf16[256,128]{1,0:T(8,128)(2,1)S(1)}, bf16[256,128]{1,0:T(8,128)(2,1)S(1)}, u32[]{:S(2)}, u32[]{:S(2)}) %collective-permute-start.3) | collective-permute-done | bytes 65568 | tf_op jit(solution)/shard_map/ppermute | solution.py:243
  10.6 0.2 collective-permute-done.5.refs_2_
  10.8 1.3 %product_own.1 = (f32[48,128]{1,0:T(8,128)S(1)}, bf16[1024,256]{1,0:T(8,128)(2,1)S(1)}) custom-call(bf16[288,128]{1,0:T(8,128)(2,1)S(1)} %get-tuple-element.10.col, bf16[256,128]{1,0:T(8,128)(2,1)S(1)} %collective-permute-done.3.refs_0_, bf16[256,128]{1,0:T(8,128)(2,1)S(1)} %collective-permute-done.4.refs_1_, ...), custom_call_target="tpu_custom_call" | custom-call | tf_op jit(solution)/shard_map/product_own/pallas_call | solution.py:284
  12.1 0.0 collective-permute-done.refs_0_
  12.1 0.0 collective-permute-done.1.refs_1_
  12.1 2.1 %collective-permute-done.2.refs_2_ = bf16[288,128]{1,0:T(8,128)(2,1)S(1)} collective-permute-done((bf16[288,128]{1,0:T(8,128)(2,1)S(1)}, bf16[288,128]{1,0:T(8,128)(2,1)S(1)}, u32[]{:S(2)}, u32[]{:S(2)}) %collective-permute-start.2) | collective-permute-done | bytes 73760 | tf_op jit(solution)/shard_map/ppermute | solution.py:243
  14.2 2.8 %product_rest.1.refs_0_ = f32[48,128]{1,0:T(8,128)S(1)} custom-call(bf16[288,128]{1,0:T(8,128)(2,1)S(1)} %collective-permute-done.refs_0_, bf16[288,128]{1,0:T(8,128)(2,1)S(1)} %collective-permute-done.1.refs_1_, bf16[288,128]{1,0:T(8,128)(2,1)S(1)} %collective-permute-done.2.refs_2_, bf16[1024,256]{1,0:T(8,128)(2,1)S(1)} %get-tuple-element.13.refs_3_, ...), custom_call_target="tpu_custom_call" | custom-call | tf_op jit(solution)/shard_map/product_rest/pallas_call | solution.py:293
  17.0 0.4 %collective-permute-start.6 = (f32[48,128]{1,0:T(8,128)S(1)}, f32[48,128]{1,0:T(8,128)S(1)}, u32[]{:S(2)}, u32[]{:S(2)}) collective-permute-start(f32[48,128]{1,0:T(8,128)S(1)} %product_rest.1.refs_0_), channel_id=1, source_target_pairs={{0,8},{1,9},{2,10},{3,11},{4,12},{5,13},{6,14},{7,15},{8,0},{9,1},... | collective-permute-start | bytes 73736 | tf_op jit(solution)/shard_map/ppermute | solution.py:243
  17.4 4.5 %collective-permute-done.6.refs_1_ = f32[48,128]{1,0:T(8,128)S(1)} collective-permute-done((f32[48,128]{1,0:T(8,128)S(1)}, f32[48,128]{1,0:T(8,128)S(1)}, u32[]{:S(2)}, u32[]{:S(2)}) %collective-permute-start.6) | collective-permute-done | bytes 24608 | tf_op jit(solution)/shard_map/ppermute | solution.py:243
  22.0 1.2 %collective-permute-done.7.other = f32[64,128]{1,0:T(8,128)S(1)} collective-permute-done((f32[64,128]{1,0:T(8,128)S(1)}, f32[64,128]{1,0:T(8,128)S(1)}, u32[]{:S(2)}, u32[]{:S(2)}) %collective-permute-start.7) | collective-permute-done | bytes 32800 | tf_op jit(solution)/shard_map/ppermute | solution.py:243
  23.2 0.4 %collective-permute-start.9 = (f32[16,128]{1,0:T(8,128)S(1)}, f32[16,128]{1,0:T(8,128)S(1)}, u32[]{:S(2)}, u32[]{:S(2)}) collective-permute-start(f32[16,128]{1,0:T(8,128)S(1)} %get-tuple-element.15.refs_0_), channel_id=1, source_target_pairs={{0,2},{1,5},{2,0},{3,7},{4,6},{5,1},{6,4},{7,3},{8,10},{9,13},{10,... | collective-permute-start | bytes 24584 | tf_op jit(solution)/shard_map/ppermute | solution.py:243
  23.6 1.4 %collective-permute-start.8 = (f32[16,128]{1,0:T(8,128)S(1)}, f32[16,128]{1,0:T(8,128)S(1)}, u32[]{:S(2)}, u32[]{:S(2)}) collective-permute-start(f32[16,128]{1,0:T(8,128)S(1)} %get-tuple-element.15.refs_0_), channel_id=1, source_target_pairs={{0,6},{1,7},{2,4},{3,5},{4,2},{5,3},{6,0},{7,1},{8,14},{9,15},{10,... | collective-permute-start | bytes 24584 | tf_op jit(solution)/shard_map/ppermute | solution.py:243
  25.0 1.9 %collective-permute-done.9.refs_2_ = f32[16,128]{1,0:T(8,128)S(1)} collective-permute-done((f32[16,128]{1,0:T(8,128)S(1)}, f32[16,128]{1,0:T(8,128)S(1)}, u32[]{:S(2)}, u32[]{:S(2)}) %collective-permute-start.9) | collective-permute-done | bytes 8224 | tf_op jit(solution)/shard_map/ppermute | solution.py:243
  26.9 1.3 %collective-permute-done.8.refs_1_ = f32[16,128]{1,0:T(8,128)S(1)} collective-permute-done((f32[16,128]{1,0:T(8,128)S(1)}, f32[16,128]{1,0:T(8,128)S(1)}, u32[]{:S(2)}, u32[]{:S(2)}) %collective-permute-start.8) | collective-permute-done | bytes 8224 | tf_op jit(solution)/shard_map/ppermute | solution.py:243
  28.2 0.0 collective-permute-done.10.refs_3_
  28.2 0.8 %update.1 = (f32[4,256]{1,0:T(4,128)}, f32[4,256]{1,0:T(4,128)}, f32[4,256]{1,0:T(4,128)}) custom-call(f32[16,128]{1,0:T(8,128)S(1)} %get-tuple-element.15.refs_0_, f32[16,128]{1,0:T(8,128)S(1)} %collective-permute-done.8.refs_1_, f32[16,128]{1,0:T(8,128)S(1)} %collective-permute-done.9.refs_2_, f32[16,128]{1,0:T(8,128)S(1)} %collective-permute-done.10.refs_3_, ...), custom_call_target="tpu_custom_call" | custom-call | tf_op jit(solution)/shard_map/update/pallas_call | solution.py:330
  (12 shorter events, 0.0 us)
Async XLA Ops:
  0.6 8.8 %copy-start.3 = (bf16[256,128]{1,0:T(8,128)(2,1)S(1)}, bf16[256,128]{1,0:T(8,128)(2,1)}, u32[]{:S(2)}) copy-start(bf16[256,128]{1,0:T(8,128)(2,1)} %points.1) | copy-start | bytes 196612
  0.6 8.8 %collective-permute-start.4 = (bf16[256,128]{1,0:T(8,128)(2,1)}, bf16[256,128]{1,0:T(8,128)(2,1)S(1)}, u32[]{:S(2)}, u32[]{:S(2)}) collective-permute-start(bf16[256,128]{1,0:T(8,128)(2,1)} %points.1), channel_id=1, source_target_pairs={{0,8},{1,9},{2,10},{3,11},{4,12},{5,13},{6,14},{7,15},{8,0},{9,1},... | collective-permute-start | bytes 196616 | tf_op jit(solution)/shard_map/ppermute | solution.py:243
  5.8 6.3 %collective-permute-start = (bf16[288,128]{1,0:T(8,128)(2,1)S(1)}, bf16[288,128]{1,0:T(8,128)(2,1)S(1)}, u32[]{:S(2)}, u32[]{:S(2)}) collective-permute-start(bf16[288,128]{1,0:T(8,128)(2,1)S(1)} %get-tuple-element.10.col), channel_id=1, source_target_pairs={{0,2},{1,3},{2,0},{3,1},{4,6},{5,7},{6,4},{7,5},{8,10},{9,11},{10,... | collective-permute-start | bytes 221192 | tf_op jit(solution)/shard_map/ppermute | solution.py:243
  7.4 4.7 %collective-permute-start.1 = (bf16[288,128]{1,0:T(8,128)(2,1)S(1)}, bf16[288,128]{1,0:T(8,128)(2,1)S(1)}, u32[]{:S(2)}, u32[]{:S(2)}) collective-permute-start(bf16[288,128]{1,0:T(8,128)(2,1)S(1)} %get-tuple-element.10.col), channel_id=1, source_target_pairs={{0,4},{1,5},{2,6},{3,7},{4,0},{5,1},{6,2},{7,3},{8,12},{9,13},{10,... | collective-permute-start | bytes 221192 | tf_op jit(solution)/shard_map/ppermute | solution.py:243
  9.0 5.3 %collective-permute-start.2 = (bf16[288,128]{1,0:T(8,128)(2,1)S(1)}, bf16[288,128]{1,0:T(8,128)(2,1)S(1)}, u32[]{:S(2)}, u32[]{:S(2)}) collective-permute-start(bf16[288,128]{1,0:T(8,128)(2,1)S(1)} %get-tuple-element.10.col), channel_id=1, source_target_pairs={{0,6},{1,7},{2,4},{3,5},{4,2},{5,3},{6,0},{7,1},{8,14},{9,15},{10,... | collective-permute-start | bytes 221192 | tf_op jit(solution)/shard_map/ppermute | solution.py:243
  9.4 1.3 %collective-permute-start.3 = (bf16[256,128]{1,0:T(8,128)(2,1)S(1)}, bf16[256,128]{1,0:T(8,128)(2,1)S(1)}, u32[]{:S(2)}, u32[]{:S(2)}) collective-permute-start(bf16[256,128]{1,0:T(8,128)(2,1)S(1)} %copy-done.3), channel_id=1, source_target_pairs={{0,1},{1,0},{2,3},{3,2},{4,5},{5,4},{6,7},{7,6},{8,9},{9,8},{10,11... | collective-permute-start | bytes 196616 | tf_op jit(solution)/shard_map/ppermute | solution.py:243
  9.4 1.4 %collective-permute-start.5 = (bf16[256,128]{1,0:T(8,128)(2,1)S(1)}, bf16[256,128]{1,0:T(8,128)(2,1)S(1)}, u32[]{:S(2)}, u32[]{:S(2)}) collective-permute-start(bf16[256,128]{1,0:T(8,128)(2,1)S(1)} %collective-permute-done.4.refs_1_), channel_id=1, source_target_pairs={{0,1},{1,0},{2,3},{3,2},{4,5},{5,4},{6,7},{7,6},{8,9},{9,8},{10,11... | collective-permute-start | bytes 196616 | tf_op jit(solution)/shard_map/ppermute | solution.py:243
  17.0 4.9 %collective-permute-start.6 = (f32[48,128]{1,0:T(8,128)S(1)}, f32[48,128]{1,0:T(8,128)S(1)}, u32[]{:S(2)}, u32[]{:S(2)}) collective-permute-start(f32[48,128]{1,0:T(8,128)S(1)} %product_rest.1.refs_0_), channel_id=1, source_target_pairs={{0,8},{1,9},{2,10},{3,11},{4,12},{5,13},{6,14},{7,15},{8,0},{9,1},... | collective-permute-start | bytes 73736 | tf_op jit(solution)/shard_map/ppermute | solution.py:243
  22.0 1.2 %collective-permute-start.7 = (f32[64,128]{1,0:T(8,128)S(1)}, f32[64,128]{1,0:T(8,128)S(1)}, u32[]{:S(2)}, u32[]{:S(2)}) collective-permute-start(f32[64,128]{1,0:T(8,128)S(1)} %merge.1.mine), channel_id=1, source_target_pairs={{0,1},{1,0},{2,3},{3,2},{4,5},{5,4},{6,7},{7,6},{8,9},{9,8},{10,11... | collective-permute-start | bytes 98312 | tf_op jit(solution)/shard_map/ppermute | solution.py:243
  23.2 5.0 %copy-start = (f32[4,256]{1,0:T(4,128)S(1)}, f32[4,256]{1,0:T(4,128)}, u32[]{:S(2)}) copy-start(f32[4,256]{1,0:T(4,128)} %refs_7_.1) | copy-start | bytes 12292
  23.2 5.0 %copy-start.1 = (f32[4,256]{1,0:T(4,128)S(1)}, f32[4,256]{1,0:T(4,128)}, u32[]{:S(2)}) copy-start(f32[4,256]{1,0:T(4,128)} %refs_6_.1) | copy-start | bytes 12292
  23.2 5.0 %copy-start.2 = (f32[4,256]{1,0:T(4,128)S(1)}, f32[4,256]{1,0:T(4,128)}, u32[]{:S(2)}) copy-start(f32[4,256]{1,0:T(4,128)} %refs_5_.1) | copy-start | bytes 12292
  23.2 3.7 %collective-permute-start.9 = (f32[16,128]{1,0:T(8,128)S(1)}, f32[16,128]{1,0:T(8,128)S(1)}, u32[]{:S(2)}, u32[]{:S(2)}) collective-permute-start(f32[16,128]{1,0:T(8,128)S(1)} %get-tuple-element.15.refs_0_), channel_id=1, source_target_pairs={{0,2},{1,5},{2,0},{3,7},{4,6},{5,1},{6,4},{7,3},{8,10},{9,13},{10,... | collective-permute-start | bytes 24584 | tf_op jit(solution)/shard_map/ppermute | solution.py:243
  23.6 4.5 %collective-permute-start.8 = (f32[16,128]{1,0:T(8,128)S(1)}, f32[16,128]{1,0:T(8,128)S(1)}, u32[]{:S(2)}, u32[]{:S(2)}) collective-permute-start(f32[16,128]{1,0:T(8,128)S(1)} %get-tuple-element.15.refs_0_), channel_id=1, source_target_pairs={{0,6},{1,7},{2,4},{3,5},{4,2},{5,3},{6,0},{7,1},{8,14},{9,15},{10,... | collective-permute-start | bytes 24584 | tf_op jit(solution)/shard_map/ppermute | solution.py:243
  26.9 1.3 %collective-permute-start.10 = (f32[16,128]{1,0:T(8,128)S(1)}, f32[16,128]{1,0:T(8,128)S(1)}, u32[]{:S(2)}, u32[]{:S(2)}) collective-permute-start(f32[16,128]{1,0:T(8,128)S(1)} %collective-permute-done.9.refs_2_), channel_id=1, source_target_pairs={{0,1},{1,0},{2,3},{3,2},{4,5},{5,4},{6,7},{7,6},{8,9},{9,8},{10,11... | collective-permute-start | bytes 24584 | tf_op jit(solution)/shard_map/ppermute | solution.py:243

commit v13 on v11

--- a/solution.py
+++ b/solution.py
@@ -6,9 +6,6 @@
 from jax.experimental import pallas as pl
 from jax.experimental.pallas import tpu as pltpu
 from jax.sharding import PartitionSpec as P
-
-CHUNK = 128
-
 
 def split_masks(devices):
     bits = devices.bit_length() - 1
@@ -103,7 +100,7 @@
     )
 
 
-def add_column(col, row_wide, rates, weights, dist, lo):
+def add_column(col, row_wide, rates, weights, dist, before, out, lo):
     dims = col.shape[1]
     cands = rates.shape[0] // 8
     size = row_wide.shape[0] // lo
@@ -111,67 +108,64 @@
     lines = (col.shape[0] - size) // wide
     top = unfold(col[size:, :], lines)
     top = jnp.concatenate([top, jnp.zeros((dims - lines, size), top.dtype)], axis=0).T
+    both = jnp.concatenate([col[:size, :], top], axis=1)
     steps = top.astype(jnp.float32)
+
+    def distances(k):
+        dist[k] = lax.dot_general(
+            both,
+            row_wide[pl.ds(k * size, size), :],
+            (((1,), (1,)), ((), ())),
+            preferred_element_type=jnp.float32,
+        )
+
+    distances(0)
     for c in range(cands):
         weights[c] = jnp.broadcast_to(steps[:, 8 + c : 9 + c], (size, dims))
-    dist[...] = lax.dot_general(
-        jnp.concatenate([col[:size, :], top], axis=1),
-        row_wide[...],
-        (((1,), (1,)), ((), ())),
-        preferred_element_type=jnp.float32,
-    )
     rate = [
         jnp.concatenate([rates[pl.ds(8 * c, 8), :]] * wide, axis=1) for c in range(cands)
     ]
-
-    def body(step, total):
-        total = list(total)
-        for j in range(0, CHUNK, 8):
-            at = pl.ds(pl.multiple_of(step * CHUNK + j, 8), 8)
-            weight = [
-                jnp.concatenate([weights[c, at, :]] * wide, axis=1) for c in range(cands)
-            ]
-            for k in range(lo):
-                here = dist[at, pl.ds(k * size, size)]
-                for c in range(cands):
-                    total[k * cands + c] += jnp.exp(here * rate[c]) * weight[c]
-        return tuple(total)
-
-    total = lax.fori_loop(
-        0,
-        size // CHUNK,
-        body,
-        (jnp.zeros((8, size), jnp.float32),) * (lo * cands),
-    )
-    total = [jnp.sum(t, axis=0, keepdims=True) for t in total]
-    return [
-        fold(jnp.concatenate(total[k * cands : (k + 1) * cands], axis=0), dims)
-        for k in range(lo)
-    ]
+    for k in range(lo):
+        if k + 1 < lo:
+            distances(k + 1)
+        places = [pl.ds((k * cands + c) * 8, 8) for c in range(cands)]
+        total = [0.0 if before is None else before[at, :] for at in places]
+        for j in range(0, size, 8):
+            here = dist[k, pl.ds(j, 8), :]
+            for c in range(cands):
+                weight = jnp.concatenate([weights[c, pl.ds(j, 8), :]] * wide, axis=1)
+                total[c] = total[c] + jnp.exp(here * rate[c]) * weight
+        for c in range(cands):
+            out[places[c], :] = total[c]
 
 
 def first_kernel(lo, col, *refs):
     rows, refs = refs[: lo - 1], refs[lo - 1 :]
-    own, rates, out, row_wide, weights, dist = refs
-    tall = own.shape[0] // 3
+    rates, out, row_wide, weights, dist = refs
     size = row_wide.shape[0] // lo
     for k, block in enumerate((col, *rows)):
         row_wide[pl.ds(k * size, size), :] = widen_row(block[:size, :])
-    parts = add_column(col, row_wide, rates, weights, dist, lo)
-    parts[0] += own[pl.ds(2 * tall, tall), :]
+    add_column(col, row_wide, rates, weights, dist, None, out, lo)
+
+
+def next_kernel(lo, col, row_wide, rates, before, out, weights, dist):
+    add_column(col, row_wide, rates, weights, dist, before, out, lo)
+
+
+def last_kernel(lo, col, row_wide, rates, before, own, out, weights, dist, spread):
+    add_column(col, row_wide, rates, weights, dist, before, spread, lo)
+    tall, dims = own.shape[0] // 3, own.shape[1]
+    cands = rates.shape[0] // 8
     for k in range(lo):
-        out[pl.ds(k * tall, tall), :] = parts[k]
+        part = [
+            jnp.sum(spread[pl.ds((k * cands + c) * 8, 8), :], axis=0, keepdims=True)
+            for c in range(cands)
+        ]
+        part = fold(jnp.concatenate(part, axis=0), dims)
+        if k == 0:
+            part += own[pl.ds(2 * tall, tall), :]
+        out[pl.ds(k * tall, tall), :] = part
     out[pl.ds(lo * tall, 2 * tall), :] = own[pl.ds(0, 2 * tall), :]
-
-
-def next_kernel(lo, col, row_wide, rates, before, out, weights, dist):
-    tall = before.shape[0] // (lo + 2)
-    parts = add_column(col, row_wide, rates, weights, dist, lo)
-    for k in range(lo):
-        at = pl.ds(k * tall, tall)
-        out[at, :] = before[at, :] + parts[k]
-    at = pl.ds(lo * tall, 2 * tall)
-    out[at, :] = before[at, :]
 
 
 def sums_kernel(cands, *refs):
@@ -195,13 +189,12 @@
         )
 
 
-def update_kernel(hi, *refs):
-    sums, refs = refs[:hi], refs[hi:]
-    image, solution, residual, direction, out_s, out_r, out_d = refs
+def update_kernel(*refs):
+    *sums, image, solution, residual, direction, out_s, out_r, out_d = refs
     cands = solution.shape[0]
     total = sums[0][...]
-    for h in range(1, hi):
-        total = total + sums[h][...]
+    for part in sums[1:]:
+        total = total + part[...]
     total = jnp.sum(total, axis=1, keepdims=True)
     norm, curve, cross, square = (
         total[i * cands : (i + 1) * cands] for i in range(4)
@@ -224,8 +217,9 @@
     tall = cands * size // dims
     extra = -(-(8 + cands) // 16) * 16 * size // dims
 
-    def meet(x, mask):
-        return lax.ppermute(x, "blk", [(d, d ^ mask) for d in range(devices)])
+    def meet(x, mask, odd_mask=None):
+        masks = (mask, mask if odd_mask is None else odd_mask)
+        return lax.ppermute(x, "blk", [(d, d ^ masks[d % 2]) for d in range(devices)])
 
     vmem = pl.BlockSpec(memory_space=pltpu.VMEM)
     hbm = pl.BlockSpec(memory_space=pltpu.HBM)
@@ -261,28 +255,37 @@
         rows.append(meet(rows[-1], 1) if mask % 2 else meet(points, mask))
     spare = [
         pltpu.VMEM((cands, size, dims), jnp.float32),
-        pltpu.VMEM((size, lo * size), jnp.float32),
-    ]
-    result = jax.ShapeDtypeStruct(((lo + 2) * tall, dims), jnp.float32)
-    partial, row_wide = pl.pallas_call(
+        pltpu.VMEM((lo, size, size), jnp.float32),
+    ]
+    spread = jax.ShapeDtypeStruct((lo * cands * 8, size), jnp.float32)
+    total, row_wide = pl.pallas_call(
         functools.partial(first_kernel, lo),
-        out_shape=(result, jax.ShapeDtypeStruct((lo * size, 2 * dims), jnp.bfloat16)),
-        in_specs=[vmem] * (lo + 2),
+        out_shape=(spread, jax.ShapeDtypeStruct((lo * size, 2 * dims), jnp.bfloat16)),
+        in_specs=[vmem] * (lo + 1),
         out_specs=(vmem, vmem),
         scratch_shapes=spare,
         compiler_params=params,
         name="product_0",
-    )(packed, *rows[1:], own, rates)
-    for mask in reversed(col_masks[1:]):
-        partial = pl.pallas_call(
+    )(packed, *rows[1:], rates)
+    for mask in reversed(col_masks[2:]):
+        total = pl.pallas_call(
             functools.partial(next_kernel, lo),
-            out_shape=result,
+            out_shape=spread,
             in_specs=[vmem] * 4,
             out_specs=vmem,
             scratch_shapes=spare,
             compiler_params=params,
             name="product_%d" % mask,
-        )(meet(packed, mask), row_wide, rates, partial)
+        )(meet(packed, mask), row_wide, rates, total)
+    partial = pl.pallas_call(
+        functools.partial(last_kernel, lo),
+        out_shape=jax.ShapeDtypeStruct(((lo + 2) * tall, dims), jnp.float32),
+        in_specs=[vmem] * 5,
+        out_specs=vmem,
+        scratch_shapes=[*spare, pltpu.VMEM(spread.shape, jnp.float32)],
+        compiler_params=params,
+        name="product_last",
+    )(meet(packed, col_masks[1]), row_wide, rates, total, own)
 
     image, sums = pl.pallas_call(
         functools.partial(sums_kernel, cands),
@@ -296,14 +299,20 @@
         name="sums",
     )(partial, *(meet(partial, mask) for mask in row_masks[1:]))
 
+    shared = [
+        meet(sums, even, odd) for even, odd in zip(col_masks[1:-1:2], col_masks[2:-1:2])
+    ]
+    shared += [meet(x, 1) for x in shared]
+    parts = [sums, meet(sums, col_masks[-1]), *shared]
+
     return pl.pallas_call(
-        functools.partial(update_kernel, hi),
+        update_kernel,
         out_shape=(jax.ShapeDtypeStruct((cands, size), jnp.float32),) * 3,
-        in_specs=[vmem] * (hi + 4),
+        in_specs=[vmem] * (len(parts) + 4),
         out_specs=(vmem,) * 3,
         compiler_params=params,
         name="update",
-    )(sums, *(meet(sums, mask) for mask in col_masks[1:]), image, solution, residual, direction)
+    )(*parts, image, solution, residual, direction)
 
 
 def solution(mesh):

time: 28.6 us -> 27.3 us (0.955)
  Pallas kernels: 6.41 us -> 5.72 us
  waiting for transfers between devices: 6.71 us -> 6.16 us
    pallas_call x5, Pallas kernels: 5.31 us -> 4.62 us  [the longest x2 1.82 us: per_device(): pl.pallas_call(functools.partial(next_kernel, lo), out_shape=spread, in_s...]
    ppermute x12, waiting for transfers between devices: 6.71 us -> 6.16 us  [meet(): lax.ppermute(x, 'blk', [(d, d ^ masks[d % 2]) for d in range(devices)])]
  transfers between devices with their start and end apart: 12 -> 12, of which waited for: 6 -> 5; matrix products, arithmetic and copies ran while one was open for 0% -> 0% of each run, Pallas kernels for 16% -> 15%
where the time goes in v13:
time: 27.3 us; the launch traced here: 27.2 us
  starting transfers between devices  14.5 us (53%)
  waiting for transfers between devices  6.16 us (23%)
  Pallas kernels  5.72 us (21%)
  between operations  0.73 us (3%)
    ppermute x12, starting transfers between devices, meet(): lax.ppermute(x, 'blk', [(d, d ^ masks[d % 2]) for d in range(devices)])  14.5 us
    ppermute x12, waiting for transfers between devices, meet(): lax.ppermute(x, 'blk', [(d, d ^ masks[d % 2]) for d in range(devices)])  6.16 us
    pallas_call x2, Pallas kernels, per_device(): pl.pallas_call(functools.partial(next_kernel, lo), out_shape=spread, in_s...  1.82 us
    pallas_call x1, Pallas kernels, per_device(): pl.pallas_call(pack_kernel, out_shape=(jax.ShapeDtypeStruct((size + extra...  1.08 us
    pallas_call x1, Pallas kernels, per_device(): pl.pallas_call(functools.partial(first_kernel, lo), out_shape=(spread, ja...  1.08 us
    pallas_call x1, Pallas kernels, per_device(): pl.pallas_call(functools.partial(last_kernel, lo), out_shape=jax.ShapeDty...  0.94 us
    pallas_call x1, Pallas kernels, per_device(): pl.pallas_call(update_kernel, out_shape=(jax.ShapeDtypeStruct((cands, siz...  0.78 us
  transfers between devices with their start and end apart: 12, of which 5 were waited for; matrix products, arithmetic and copies ran while one was open for 0% of the time, Pallas kernels for 15%

profile of v13, /device:TPU:0, one launch (start us, length us, event | category | flops | bytes accessed | tf_op | source)
XLA Modules:
  0.0 27.2 jit_solution(12203883319409967253)
XLA Ops:
  0.6 4.1 %collective-permute-start.2 = (bf16[256,128]{1,0:T(8,128)(2,1)}, bf16[256,128]{1,0:T(8,128)(2,1)S(1)}, u32[]{:S(2)}, u32[]{:S(2)}) collective-permute-start(bf16[256,128]{1,0:T(8,128)(2,1)} %points.1), channel_id=1, source_target_pairs={{0,8},{1,9},{2,10},{3,11},{4,12},{5,13},{6,14},{7,15},{8,0},{9,1},... | collective-permute-start | bytes 196616 | tf_op jit(solution)/shard_map/ppermute | solution.py:222
  4.7 1.1 %pack.1 = (bf16[288,128]{1,0:T(8,128)(2,1)S(1)}, f32[24,128]{1,0:T(8,128)S(1)}, f32[32,128]{1,0:T(8,128)S(1)}) custom-call(bf16[256,128]{1,0:T(8,128)(2,1)} %points.1, f32[4,256]{1,0:T(4,128)} %refs_7_.1, f32[4,256]{1,0:T(4,128)} %refs_6_.1, f32[4]{0:T(128)} %length.1, f32[4]{0:T(128)} %noise.1), custom_call_target="tpu_custom_call" | custom-call | tf_op jit(solution)/shard_map/pack/pallas_call | solution.py:228
  5.8 2.6 %collective-permute-start.5 = (bf16[288,128]{1,0:T(8,128)(2,1)S(1)}, bf16[288,128]{1,0:T(8,128)(2,1)S(1)}, u32[]{:S(2)}, u32[]{:S(2)}) collective-permute-start(bf16[288,128]{1,0:T(8,128)(2,1)S(1)} %get-tuple-element.10.col), channel_id=1, source_target_pairs={{0,6},{1,7},{2,4},{3,5},{4,2},{5,3},{6,0},{7,1},{8,14},{9,15},{10,... | collective-permute-start | bytes 221192 | tf_op jit(solution)/shard_map/ppermute | solution.py:222
  8.4 0.4 %collective-permute-start.4 = (bf16[288,128]{1,0:T(8,128)(2,1)S(1)}, bf16[288,128]{1,0:T(8,128)(2,1)S(1)}, u32[]{:S(2)}, u32[]{:S(2)}) collective-permute-start(bf16[288,128]{1,0:T(8,128)(2,1)S(1)} %get-tuple-element.10.col), channel_id=1, source_target_pairs={{0,4},{1,5},{2,6},{3,7},{4,0},{5,1},{6,2},{7,3},{8,12},{9,13},{10,... | collective-permute-start | bytes 221192 | tf_op jit(solution)/shard_map/ppermute | solution.py:222
  8.9 0.5 %collective-permute-start = (bf16[288,128]{1,0:T(8,128)(2,1)S(1)}, bf16[288,128]{1,0:T(8,128)(2,1)S(1)}, u32[]{:S(2)}, u32[]{:S(2)}) collective-permute-start(bf16[288,128]{1,0:T(8,128)(2,1)S(1)} %get-tuple-element.10.col), channel_id=1, source_target_pairs={{0,2},{1,3},{2,0},{3,1},{4,6},{5,7},{6,4},{7,5},{8,10},{9,11},{10,... | collective-permute-start | bytes 221192 | tf_op jit(solution)/shard_map/ppermute | solution.py:222
  9.4 0.0 collective-permute-start.1
  9.4 0.0 collective-permute-done.2.refs_1_
  9.4 0.5 %collective-permute-start.3 = (bf16[256,128]{1,0:T(8,128)(2,1)S(1)}, bf16[256,128]{1,0:T(8,128)(2,1)S(1)}, u32[]{:S(2)}, u32[]{:S(2)}) collective-permute-start(bf16[256,128]{1,0:T(8,128)(2,1)S(1)} %collective-permute-done.2.refs_1_), channel_id=1, source_target_pairs={{0,1},{1,0},{2,3},{3,2},{4,5},{5,4},{6,7},{7,6},{8,9},{9,8},{10,11... | collective-permute-start | bytes 196616 | tf_op jit(solution)/shard_map/ppermute | solution.py:222
  9.9 0.7 %collective-permute-done.1.refs_0_ = bf16[256,128]{1,0:T(8,128)(2,1)S(1)} collective-permute-done((bf16[256,128]{1,0:T(8,128)(2,1)S(1)}, bf16[256,128]{1,0:T(8,128)(2,1)S(1)}, u32[]{:S(2)}, u32[]{:S(2)}) %collective-permute-start.1) | collective-permute-done | bytes 65568 | tf_op jit(solution)/shard_map/ppermute | solution.py:222
  10.6 0.2 collective-permute-done.3.refs_2_
  10.8 1.1 %product_0.1 = (f32[128,256]{1,0:T(8,128)S(1)}, bf16[1024,256]{1,0:T(8,128)(2,1)S(1)}) custom-call(bf16[288,128]{1,0:T(8,128)(2,1)S(1)} %get-tuple-element.10.col, bf16[256,128]{1,0:T(8,128)(2,1)S(1)} %collective-permute-done.1.refs_0_, bf16[256,128]{1,0:T(8,128)(2,1)S(1)} %collective-permute-done.2.refs_1_, ...), custom_call_target="tpu_custom_call" | custom-call | tf_op jit(solution)/shard_map/product_0/pallas_call | solution.py:261
  11.9 0.0 collective-permute-done.5.col
  11.9 0.9 %product_6.1.before = f32[128,256]{1,0:T(8,128)S(1)} custom-call(bf16[288,128]{1,0:T(8,128)(2,1)S(1)} %collective-permute-done.5.col, bf16[1024,256]{1,0:T(8,128)(2,1)S(1)} %get-tuple-element.12.row_wide, f32[32,128]{1,0:T(8,128)S(1)} %get-tuple-element.11.refs_3_.rates, f32[128,256]{1,0:T(8,128)S(1)} %get-tuple-element.13.before), custom_call_target="tpu_custom_call" | custom-call | tf_op jit(solution)/shard_map/product_6/pallas_call | solution.py:271
  12.9 0.9 %product_4.1.before = f32[128,256]{1,0:T(8,128)S(1)} custom-call(bf16[288,128]{1,0:T(8,128)(2,1)S(1)} %collective-permute-done.4.col, bf16[1024,256]{1,0:T(8,128)(2,1)S(1)} %get-tuple-element.12.row_wide, f32[32,128]{1,0:T(8,128)S(1)} %get-tuple-element.11.refs_3_.rates, f32[128,256]{1,0:T(8,128)S(1)} %product_6.1.before), custom_call_target="tpu_custom_call" | custom-call | tf_op jit(solution)/shard_map/product_4/pallas_call | solution.py:271
  13.8 0.9 %product_last.1.refs_0_ = f32[48,128]{1,0:T(8,128)S(1)} custom-call(bf16[288,128]{1,0:T(8,128)(2,1)S(1)} %collective-permute-done.col, bf16[1024,256]{1,0:T(8,128)(2,1)S(1)} %get-tuple-element.12.row_wide, f32[32,128]{1,0:T(8,128)S(1)} %get-tuple-element.11.refs_3_.rates, f32[128,256]{1,0:T(8,128)S(1)} %product_4.1.before, f32[24,128]{1,0:T(8,128)S(1)} %get-tuple-element.14.own), custom_call_target="tpu_custom_call" | custom-call | tf_op jit(solution)/shard_map/product_last/pallas_call | solution.py:280
  14.7 0.4 %collective-permute-start.6 = (f32[48,128]{1,0:T(8,128)S(1)}, f32[48,128]{1,0:T(8,128)S(1)}, u32[]{:S(2)}, u32[]{:S(2)}) collective-permute-start(f32[48,128]{1,0:T(8,128)S(1)} %product_last.1.refs_0_), channel_id=1, source_target_pairs={{0,1},{1,0},{2,3},{3,2},{4,5},{5,4},{6,7},{7,6},{8,9},{9,8},{10,11... | collective-permute-start | bytes 73736 | tf_op jit(solution)/shard_map/ppermute | solution.py:222
  15.1 0.4 %collective-permute-start.7 = (f32[48,128]{1,0:T(8,128)S(1)}, f32[48,128]{1,0:T(8,128)S(1)}, u32[]{:S(2)}, u32[]{:S(2)}) collective-permute-start(f32[48,128]{1,0:T(8,128)S(1)} %product_last.1.refs_0_), channel_id=1, source_target_pairs={{0,8},{1,9},{2,10},{3,11},{4,12},{5,13},{6,14},{7,15},{8,0},{9,1},... | collective-permute-start | bytes 73736 | tf_op jit(solution)/shard_map/ppermute | solution.py:222
  15.5 2.1 %collective-permute-start.8 = (f32[48,128]{1,0:T(8,128)S(1)}, f32[48,128]{1,0:T(8,128)S(1)}, u32[]{:S(2)}, u32[]{:S(2)}) collective-permute-start(f32[48,128]{1,0:T(8,128)S(1)} %product_last.1.refs_0_), channel_id=1, source_target_pairs={{0,9},{1,8},{2,11},{3,10},{4,13},{5,12},{6,15},{7,14},{8,1},{9,0},... | collective-permute-start | bytes 73736 | tf_op jit(solution)/shard_map/ppermute | solution.py:222
  17.6 2.6 %collective-permute-done.7.refs_2_ = f32[48,128]{1,0:T(8,128)S(1)} collective-permute-done((f32[48,128]{1,0:T(8,128)S(1)}, f32[48,128]{1,0:T(8,128)S(1)}, u32[]{:S(2)}, u32[]{:S(2)}) %collective-permute-start.7) | collective-permute-done | bytes 24608 | tf_op jit(solution)/shard_map/ppermute | solution.py:222
  20.2 1.6 %collective-permute-start.10 = (f32[16,128]{1,0:T(8,128)S(1)}, f32[16,128]{1,0:T(8,128)S(1)}, u32[]{:S(2)}, u32[]{:S(2)}) collective-permute-start(f32[16,128]{1,0:T(8,128)S(1)} %get-tuple-element.15.refs_0_), channel_id=1, source_target_pairs={{0,2},{1,5},{2,0},{3,7},{4,6},{5,1},{6,4},{7,3},{8,10},{9,13},{10,... | collective-permute-start | bytes 24584 | tf_op jit(solution)/shard_map/ppermute | solution.py:222
  21.8 1.9 %collective-permute-start.9 = (f32[16,128]{1,0:T(8,128)S(1)}, f32[16,128]{1,0:T(8,128)S(1)}, u32[]{:S(2)}, u32[]{:S(2)}) collective-permute-start(f32[16,128]{1,0:T(8,128)S(1)} %get-tuple-element.15.refs_0_), channel_id=1, source_target_pairs={{0,6},{1,7},{2,4},{3,5},{4,2},{5,3},{6,0},{7,1},{8,14},{9,15},{10,... | collective-permute-start | bytes 24584 | tf_op jit(solution)/shard_map/ppermute | solution.py:222
  23.8 0.2 collective-permute-done.10.refs_2_
  23.9 2.4 %collective-permute-done.9.refs_1_ = f32[16,128]{1,0:T(8,128)S(1)} collective-permute-done((f32[16,128]{1,0:T(8,128)S(1)}, f32[16,128]{1,0:T(8,128)S(1)}, u32[]{:S(2)}, u32[]{:S(2)}) %collective-permute-start.9) | collective-permute-done | bytes 8224 | tf_op jit(solution)/shard_map/ppermute | solution.py:222
  26.4 0.8 %update.1 = (f32[4,256]{1,0:T(4,128)}, f32[4,256]{1,0:T(4,128)}, f32[4,256]{1,0:T(4,128)}) custom-call(f32[16,128]{1,0:T(8,128)S(1)} %get-tuple-element.15.refs_0_, f32[16,128]{1,0:T(8,128)S(1)} %collective-permute-done.9.refs_1_, f32[16,128]{1,0:T(8,128)S(1)} %collective-permute-done.10.refs_2_, f32[16,128]{1,0:T(8,128)S(1)} %collective-permute-done.11.refs_3_, ...), custom_call_target="tpu_custom_call" | custom-call | tf_op jit(solution)/shard_map/update/pallas_call | solution.py:308
  (15 shorter events, 0.1 us)
Async XLA Ops:
  0.6 8.8 %copy-start.3 = (bf16[256,128]{1,0:T(8,128)(2,1)S(1)}, bf16[256,128]{1,0:T(8,128)(2,1)}, u32[]{:S(2)}) copy-start(bf16[256,128]{1,0:T(8,128)(2,1)} %points.1) | copy-start | bytes 196612
  0.6 8.8 %collective-permute-start.2 = (bf16[256,128]{1,0:T(8,128)(2,1)}, bf16[256,128]{1,0:T(8,128)(2,1)S(1)}, u32[]{:S(2)}, u32[]{:S(2)}) collective-permute-start(bf16[256,128]{1,0:T(8,128)(2,1)} %points.1), channel_id=1, source_target_pairs={{0,8},{1,9},{2,10},{3,11},{4,12},{5,13},{6,14},{7,15},{8,0},{9,1},... | collective-permute-start | bytes 196616 | tf_op jit(solution)/shard_map/ppermute | solution.py:222
  5.8 6.1 %collective-permute-start.5 = (bf16[288,128]{1,0:T(8,128)(2,1)S(1)}, bf16[288,128]{1,0:T(8,128)(2,1)S(1)}, u32[]{:S(2)}, u32[]{:S(2)}) collective-permute-start(bf16[288,128]{1,0:T(8,128)(2,1)S(1)} %get-tuple-element.10.col), channel_id=1, source_target_pairs={{0,6},{1,7},{2,4},{3,5},{4,2},{5,3},{6,0},{7,1},{8,14},{9,15},{10,... | collective-permute-start | bytes 221192 | tf_op jit(solution)/shard_map/ppermute | solution.py:222
  8.4 4.4 %collective-permute-start.4 = (bf16[288,128]{1,0:T(8,128)(2,1)S(1)}, bf16[288,128]{1,0:T(8,128)(2,1)S(1)}, u32[]{:S(2)}, u32[]{:S(2)}) collective-permute-start(bf16[288,128]{1,0:T(8,128)(2,1)S(1)} %get-tuple-element.10.col), channel_id=1, source_target_pairs={{0,4},{1,5},{2,6},{3,7},{4,0},{5,1},{6,2},{7,3},{8,12},{9,13},{10,... | collective-permute-start | bytes 221192 | tf_op jit(solution)/shard_map/ppermute | solution.py:222
  8.9 4.9 %collective-permute-start = (bf16[288,128]{1,0:T(8,128)(2,1)S(1)}, bf16[288,128]{1,0:T(8,128)(2,1)S(1)}, u32[]{:S(2)}, u32[]{:S(2)}) collective-permute-start(bf16[288,128]{1,0:T(8,128)(2,1)S(1)} %get-tuple-element.10.col), channel_id=1, source_target_pairs={{0,2},{1,3},{2,0},{3,1},{4,6},{5,7},{6,4},{7,5},{8,10},{9,11},{10,... | collective-permute-start | bytes 221192 | tf_op jit(solution)/shard_map/ppermute | solution.py:222
  9.4 1.3 %collective-permute-start.1 = (bf16[256,128]{1,0:T(8,128)(2,1)S(1)}, bf16[256,128]{1,0:T(8,128)(2,1)S(1)}, u32[]{:S(2)}, u32[]{:S(2)}) collective-permute-start(bf16[256,128]{1,0:T(8,128)(2,1)S(1)} %copy-done.3), channel_id=1, source_target_pairs={{0,1},{1,0},{2,3},{3,2},{4,5},{5,4},{6,7},{7,6},{8,9},{9,8},{10,11... | collective-permute-start | bytes 196616 | tf_op jit(solution)/shard_map/ppermute | solution.py:222
  9.4 1.4 %collective-permute-start.3 = (bf16[256,128]{1,0:T(8,128)(2,1)S(1)}, bf16[256,128]{1,0:T(8,128)(2,1)S(1)}, u32[]{:S(2)}, u32[]{:S(2)}) collective-permute-start(bf16[256,128]{1,0:T(8,128)(2,1)S(1)} %collective-permute-done.2.refs_1_), channel_id=1, source_target_pairs={{0,1},{1,0},{2,3},{3,2},{4,5},{5,4},{6,7},{7,6},{8,9},{9,8},{10,11... | collective-permute-start | bytes 196616 | tf_op jit(solution)/shard_map/ppermute | solution.py:222
  14.7 2.8 %collective-permute-start.6 = (f32[48,128]{1,0:T(8,128)S(1)}, f32[48,128]{1,0:T(8,128)S(1)}, u32[]{:S(2)}, u32[]{:S(2)}) collective-permute-start(f32[48,128]{1,0:T(8,128)S(1)} %product_last.1.refs_0_), channel_id=1, source_target_pairs={{0,1},{1,0},{2,3},{3,2},{4,5},{5,4},{6,7},{7,6},{8,9},{9,8},{10,11... | collective-permute-start | bytes 73736 | tf_op jit(solution)/shard_map/ppermute | solution.py:222
  15.1 5.0 %collective-permute-start.7 = (f32[48,128]{1,0:T(8,128)S(1)}, f32[48,128]{1,0:T(8,128)S(1)}, u32[]{:S(2)}, u32[]{:S(2)}) collective-permute-start(f32[48,128]{1,0:T(8,128)S(1)} %product_last.1.refs_0_), channel_id=1, source_target_pairs={{0,8},{1,9},{2,10},{3,11},{4,12},{5,13},{6,14},{7,15},{8,0},{9,1},... | collective-permute-start | bytes 73736 | tf_op jit(solution)/shard_map/ppermute | solution.py:222
  15.5 4.7 %collective-permute-start.8 = (f32[48,128]{1,0:T(8,128)S(1)}, f32[48,128]{1,0:T(8,128)S(1)}, u32[]{:S(2)}, u32[]{:S(2)}) collective-permute-start(f32[48,128]{1,0:T(8,128)S(1)} %product_last.1.refs_0_), channel_id=1, source_target_pairs={{0,9},{1,8},{2,11},{3,10},{4,13},{5,12},{6,15},{7,14},{8,1},{9,0},... | collective-permute-start | bytes 73736 | tf_op jit(solution)/shard_map/ppermute | solution.py:222
  20.2 6.2 %copy-start = (f32[4,256]{1,0:T(4,128)S(1)}, f32[4,256]{1,0:T(4,128)}, u32[]{:S(2)}) copy-start(f32[4,256]{1,0:T(4,128)} %refs_7_.1) | copy-start | bytes 12292
  20.2 6.2 %copy-start.1 = (f32[4,256]{1,0:T(4,128)S(1)}, f32[4,256]{1,0:T(4,128)}, u32[]{:S(2)}) copy-start(f32[4,256]{1,0:T(4,128)} %refs_6_.1) | copy-start | bytes 12292
  20.2 6.2 %copy-start.2 = (f32[4,256]{1,0:T(4,128)S(1)}, f32[4,256]{1,0:T(4,128)}, u32[]{:S(2)}) copy-start(f32[4,256]{1,0:T(4,128)} %refs_5_.1) | copy-start | bytes 12292
  20.2 3.7 %collective-permute-start.10 = (f32[16,128]{1,0:T(8,128)S(1)}, f32[16,128]{1,0:T(8,128)S(1)}, u32[]{:S(2)}, u32[]{:S(2)}) collective-permute-start(f32[16,128]{1,0:T(8,128)S(1)} %get-tuple-element.15.refs_0_), channel_id=1, source_target_pairs={{0,2},{1,5},{2,0},{3,7},{4,6},{5,1},{6,4},{7,3},{8,10},{9,13},{10,... | collective-permute-start | bytes 24584 | tf_op jit(solution)/shard_map/ppermute | solution.py:222
  21.8 4.5 %collective-permute-start.9 = (f32[16,128]{1,0:T(8,128)S(1)}, f32[16,128]{1,0:T(8,128)S(1)}, u32[]{:S(2)}, u32[]{:S(2)}) collective-permute-start(f32[16,128]{1,0:T(8,128)S(1)} %get-tuple-element.15.refs_0_), channel_id=1, source_target_pairs={{0,6},{1,7},{2,4},{3,5},{4,2},{5,3},{6,0},{7,1},{8,14},{9,15},{10,... | collective-permute-start | bytes 24584 | tf_op jit(solution)/shard_map/ppermute | solution.py:222
  23.9 2.4 %collective-permute-start.11 = (f32[16,128]{1,0:T(8,128)S(1)}, f32[16,128]{1,0:T(8,128)S(1)}, u32[]{:S(2)}, u32[]{:S(2)}) collective-permute-start(f32[16,128]{1,0:T(8,128)S(1)} %collective-permute-done.10.refs_2_), channel_id=1, source_target_pairs={{0,1},{1,0},{2,3},{3,2},{4,5},{5,4},{6,7},{7,6},{8,9},{9,8},{10,11... | collective-permute-start | bytes 24584 | tf_op jit(solution)/shard_map/ppermute | solution.py:222

commit v14 on v13

--- a/solution.py
+++ b/solution.py
@@ -10,10 +10,8 @@
 def split_masks(devices):
     bits = devices.bit_length() - 1
     assert devices == 1 << bits and bits > 1
-    far = bits // 2 - 1
-    row = [m << (bits - far) for m in range(1 << far)]
-    col = [m << 1 for m in range(1 << (bits - 1 - far))]
-    return col, [m + core for m in row for core in (0, 1)]
+    lo = 1 << (bits // 2)
+    return list(range(0, devices, lo)), list(range(lo))
 
 
 def pieces_of(wide):
@@ -299,11 +297,13 @@
         name="sums",
     )(partial, *(meet(partial, mask) for mask in row_masks[1:]))
 
+    half = hi // 2
     shared = [
-        meet(sums, even, odd) for even, odd in zip(col_masks[1:-1:2], col_masks[2:-1:2])
+        meet(sums, even, odd)
+        for even, odd in zip(col_masks[1:half], reversed(col_masks[half + 1 :]))
     ]
     shared += [meet(x, 1) for x in shared]
-    parts = [sums, meet(sums, col_masks[-1]), *shared]
+    parts = [sums, meet(sums, col_masks[half]), *shared]
 
     return pl.pallas_call(
         update_kernel,

time: 27.3 us -> 27 us (0.989); the launches traced: 27.2 us -> 26.5 us
  starting transfers between devices: 14.5 us -> 14 us
    ppermute x12, starting transfers between devices: 14.5 us -> 14 us  [meet(): lax.ppermute(x, 'blk', [(d, d ^ masks[d % 2]) for d in range(devices)])]
  transfers between devices with their start and end apart: 12 -> 12, of which waited for: 5 -> 8; matrix products, arithmetic and copies ran while one was open for 0% -> 0% of each run, Pallas kernels for 15% -> 15%
where the time goes in v14:
time: 27 us; the launch traced here: 26.5 us
  starting transfers between devices  14 us (52%)
  waiting for transfers between devices  6.07 us (22%)
  Pallas kernels  5.72 us (21%)
  between operations  0.72 us (3%)
    ppermute x12, starting transfers between devices, meet(): lax.ppermute(x, 'blk', [(d, d ^ masks[d % 2]) for d in range(devices)])  14 us
    ppermute x12, waiting for transfers between devices, meet(): lax.ppermute(x, 'blk', [(d, d ^ masks[d % 2]) for d in range(devices)])  6.07 us
    pallas_call x2, Pallas kernels, per_device(): pl.pallas_call(functools.partial(next_kernel, lo), out_shape=spread, in_s...  1.82 us
    pallas_call x1, Pallas kernels, per_device(): pl.pallas_call(pack_kernel, out_shape=(jax.ShapeDtypeStruct((size + extra...  1.08 us
    pallas_call x1, Pallas kernels, per_device(): pl.pallas_call(functools.partial(first_kernel, lo), out_shape=(spread, ja...  1.08 us
    pallas_call x1, Pallas kernels, per_device(): pl.pallas_call(functools.partial(last_kernel, lo), out_shape=jax.ShapeDty...  0.95 us
    pallas_call x1, Pallas kernels, per_device(): pl.pallas_call(update_kernel, out_shape=(jax.ShapeDtypeStruct((cands, siz...  0.77 us
  transfers between devices with their start and end apart: 12, of which 8 were waited for; matrix products, arithmetic and copies ran while one was open for 0% of the time, Pallas kernels for 15%

profile of v14, /device:TPU:0, one launch (start us, length us, event | category | flops | bytes accessed | tf_op | source)
XLA Modules:
  0.0 26.5 jit_solution(8381126677822090408)
XLA Ops:
  0.6 3.0 %collective-permute-start.2 = (bf16[256,128]{1,0:T(8,128)(2,1)}, bf16[256,128]{1,0:T(8,128)(2,1)S(1)}, u32[]{:S(2)}, u32[]{:S(2)}) collective-permute-start(bf16[256,128]{1,0:T(8,128)(2,1)} %points.1), channel_id=1, source_target_pairs={{0,2},{1,3},{2,0},{3,1},{4,6},{5,7},{6,4},{7,5},{8,10},{9,11},{10,... | collective-permute-start | bytes 196616 | tf_op jit(solution)/shard_map/ppermute | solution.py:220
  3.7 1.1 %pack.1 = (bf16[288,128]{1,0:T(8,128)(2,1)S(1)}, f32[24,128]{1,0:T(8,128)S(1)}, f32[32,128]{1,0:T(8,128)S(1)}) custom-call(bf16[256,128]{1,0:T(8,128)(2,1)} %points.1, f32[4,256]{1,0:T(4,128)} %refs_7_.1, f32[4,256]{1,0:T(4,128)} %refs_6_.1, f32[4]{0:T(128)} %length.1, f32[4]{0:T(128)} %noise.1), custom_call_target="tpu_custom_call" | custom-call | tf_op jit(solution)/shard_map/pack/pallas_call | solution.py:226
  4.8 3.7 %collective-permute-start.5 = (bf16[288,128]{1,0:T(8,128)(2,1)S(1)}, bf16[288,128]{1,0:T(8,128)(2,1)S(1)}, u32[]{:S(2)}, u32[]{:S(2)}) collective-permute-start(bf16[288,128]{1,0:T(8,128)(2,1)S(1)} %get-tuple-element.10.col), channel_id=1, source_target_pairs={{0,12},{1,13},{2,14},{3,15},{4,8},{5,9},{6,10},{7,11},{8,4},{9,5},... | collective-permute-start | bytes 221192 | tf_op jit(solution)/shard_map/ppermute | solution.py:220
  8.4 0.8 %collective-permute-start = (bf16[288,128]{1,0:T(8,128)(2,1)S(1)}, bf16[288,128]{1,0:T(8,128)(2,1)S(1)}, u32[]{:S(2)}, u32[]{:S(2)}) collective-permute-start(bf16[288,128]{1,0:T(8,128)(2,1)S(1)} %get-tuple-element.10.col), channel_id=1, source_target_pairs={{0,4},{1,5},{2,6},{3,7},{4,0},{5,1},{6,2},{7,3},{8,12},{9,13},{10,... | collective-permute-start | bytes 221192 | tf_op jit(solution)/shard_map/ppermute | solution.py:220
  9.2 0.5 %collective-permute-start.3 = (bf16[256,128]{1,0:T(8,128)(2,1)S(1)}, bf16[256,128]{1,0:T(8,128)(2,1)S(1)}, u32[]{:S(2)}, u32[]{:S(2)}) collective-permute-start(bf16[256,128]{1,0:T(8,128)(2,1)S(1)} %collective-permute-done.2.refs_1_), channel_id=1, source_target_pairs={{0,1},{1,0},{2,3},{3,2},{4,5},{5,4},{6,7},{7,6},{8,9},{9,8},{10,11... | collective-permute-start | bytes 196616 | tf_op jit(solution)/shard_map/ppermute | solution.py:220
  9.7 0.7 %collective-permute-done.1.refs_0_ = bf16[256,128]{1,0:T(8,128)(2,1)S(1)} collective-permute-done((bf16[256,128]{1,0:T(8,128)(2,1)S(1)}, bf16[256,128]{1,0:T(8,128)(2,1)S(1)}, u32[]{:S(2)}, u32[]{:S(2)}) %collective-permute-start.1) | collective-permute-done | bytes 65568 | tf_op jit(solution)/shard_map/ppermute | solution.py:220
  10.5 0.2 collective-permute-done.3.refs_2_
  10.6 1.1 %product_0.1 = (f32[128,256]{1,0:T(8,128)S(1)}, bf16[1024,256]{1,0:T(8,128)(2,1)S(1)}) custom-call(bf16[288,128]{1,0:T(8,128)(2,1)S(1)} %get-tuple-element.10.col, bf16[256,128]{1,0:T(8,128)(2,1)S(1)} %collective-permute-done.1.refs_0_, bf16[256,128]{1,0:T(8,128)(2,1)S(1)} %collective-permute-done.2.refs_1_, ...), custom_call_target="tpu_custom_call" | custom-call | tf_op jit(solution)/shard_map/product_0/pallas_call | solution.py:259
  11.7 0.1 collective-permute-done.5.col
  11.9 0.9 %product_12.1.before = f32[128,256]{1,0:T(8,128)S(1)} custom-call(bf16[288,128]{1,0:T(8,128)(2,1)S(1)} %collective-permute-done.5.col, bf16[1024,256]{1,0:T(8,128)(2,1)S(1)} %get-tuple-element.12.row_wide, f32[32,128]{1,0:T(8,128)S(1)} %get-tuple-element.11.refs_3_.rates, f32[128,256]{1,0:T(8,128)S(1)} %get-tuple-element.13.before), custom_call_target="tpu_custom_call" | custom-call | tf_op jit(solution)/shard_map/product_12/pallas_call | solution.py:269
  12.8 1.6 %collective-permute-done.4.col = bf16[288,128]{1,0:T(8,128)(2,1)S(1)} collective-permute-done((bf16[288,128]{1,0:T(8,128)(2,1)S(1)}, bf16[288,128]{1,0:T(8,128)(2,1)S(1)}, u32[]{:S(2)}, u32[]{:S(2)}) %collective-permute-start.4) | collective-permute-done | bytes 73760 | tf_op jit(solution)/shard_map/ppermute | solution.py:220
  14.4 0.9 %product_8.1.before = f32[128,256]{1,0:T(8,128)S(1)} custom-call(bf16[288,128]{1,0:T(8,128)(2,1)S(1)} %collective-permute-done.4.col, bf16[1024,256]{1,0:T(8,128)(2,1)S(1)} %get-tuple-element.12.row_wide, f32[32,128]{1,0:T(8,128)S(1)} %get-tuple-element.11.refs_3_.rates, f32[128,256]{1,0:T(8,128)S(1)} %product_12.1.before), custom_call_target="tpu_custom_call" | custom-call | tf_op jit(solution)/shard_map/product_8/pallas_call | solution.py:269
  15.3 0.9 %product_last.1.refs_0_ = f32[48,128]{1,0:T(8,128)S(1)} custom-call(bf16[288,128]{1,0:T(8,128)(2,1)S(1)} %collective-permute-done.col, bf16[1024,256]{1,0:T(8,128)(2,1)S(1)} %get-tuple-element.12.row_wide, f32[32,128]{1,0:T(8,128)S(1)} %get-tuple-element.11.refs_3_.rates, f32[128,256]{1,0:T(8,128)S(1)} %product_8.1.before, f32[24,128]{1,0:T(8,128)S(1)} %get-tuple-element.14.own), custom_call_target="tpu_custom_call" | custom-call | tf_op jit(solution)/shard_map/product_last/pallas_call | solution.py:278
  16.3 0.1 collective-permute-start.6
  16.3 0.6 %collective-permute-start.7 = (f32[48,128]{1,0:T(8,128)S(1)}, f32[48,128]{1,0:T(8,128)S(1)}, u32[]{:S(2)}, u32[]{:S(2)}) collective-permute-start(f32[48,128]{1,0:T(8,128)S(1)} %product_last.1.refs_0_), channel_id=1, source_target_pairs={{0,2},{1,3},{2,0},{3,1},{4,6},{5,7},{6,4},{7,5},{8,10},{9,11},{10,... | collective-permute-start | bytes 73736 | tf_op jit(solution)/shard_map/ppermute | solution.py:220
  16.9 1.3 %collective-permute-start.8 = (f32[48,128]{1,0:T(8,128)S(1)}, f32[48,128]{1,0:T(8,128)S(1)}, u32[]{:S(2)}, u32[]{:S(2)}) collective-permute-start(f32[48,128]{1,0:T(8,128)S(1)} %product_last.1.refs_0_), channel_id=1, source_target_pairs={{0,3},{1,2},{2,1},{3,0},{4,7},{5,6},{6,5},{7,4},{8,11},{9,10},{10,... | collective-permute-start | bytes 73736 | tf_op jit(solution)/shard_map/ppermute | solution.py:220
  18.2 2.2 %collective-permute-done.7.refs_2_ = f32[48,128]{1,0:T(8,128)S(1)} collective-permute-done((f32[48,128]{1,0:T(8,128)S(1)}, f32[48,128]{1,0:T(8,128)S(1)}, u32[]{:S(2)}, u32[]{:S(2)}) %collective-permute-start.7) | collective-permute-done | bytes 24608 | tf_op jit(solution)/shard_map/ppermute | solution.py:220
  20.5 0.3 collective-permute-start.10
  20.7 3.1 %collective-permute-start.9 = (f32[16,128]{1,0:T(8,128)S(1)}, f32[16,128]{1,0:T(8,128)S(1)}, u32[]{:S(2)}, u32[]{:S(2)}) collective-permute-start(f32[16,128]{1,0:T(8,128)S(1)} %get-tuple-element.15.refs_0_), channel_id=1, source_target_pairs={{0,8},{1,9},{2,10},{3,11},{4,12},{5,13},{6,14},{7,15},{8,0},{9,1},... | collective-permute-start | bytes 24584 | tf_op jit(solution)/shard_map/ppermute | solution.py:220
  23.8 0.4 %collective-permute-done.10.refs_2_ = f32[16,128]{1,0:T(8,128)S(1)} collective-permute-done((f32[16,128]{1,0:T(8,128)S(1)}, f32[16,128]{1,0:T(8,128)S(1)}, u32[]{:S(2)}, u32[]{:S(2)}) %collective-permute-start.10) | collective-permute-done | bytes 8224 | tf_op jit(solution)/shard_map/ppermute | solution.py:220
  24.2 0.8 %collective-permute-start.11 = (f32[16,128]{1,0:T(8,128)S(1)}, f32[16,128]{1,0:T(8,128)S(1)}, u32[]{:S(2)}, u32[]{:S(2)}) collective-permute-start(f32[16,128]{1,0:T(8,128)S(1)} %collective-permute-done.10.refs_2_), channel_id=1, source_target_pairs={{0,1},{1,0},{2,3},{3,2},{4,5},{5,4},{6,7},{7,6},{8,9},{9,8},{10,11... | collective-permute-start | bytes 24584 | tf_op jit(solution)/shard_map/ppermute | solution.py:220
  24.9 0.5 %collective-permute-done.9.refs_1_ = f32[16,128]{1,0:T(8,128)S(1)} collective-permute-done((f32[16,128]{1,0:T(8,128)S(1)}, f32[16,128]{1,0:T(8,128)S(1)}, u32[]{:S(2)}, u32[]{:S(2)}) %collective-permute-start.9) | collective-permute-done | bytes 8224 | tf_op jit(solution)/shard_map/ppermute | solution.py:220
  25.4 0.3 %collective-permute-done.11.refs_3_ = f32[16,128]{1,0:T(8,128)S(1)} collective-permute-done((f32[16,128]{1,0:T(8,128)S(1)}, f32[16,128]{1,0:T(8,128)S(1)}, u32[]{:S(2)}, u32[]{:S(2)}) %collective-permute-start.11) | collective-permute-done | bytes 8224 | tf_op jit(solution)/shard_map/ppermute | solution.py:220
  25.8 0.8 %update.1 = (f32[4,256]{1,0:T(4,128)}, f32[4,256]{1,0:T(4,128)}, f32[4,256]{1,0:T(4,128)}) custom-call(f32[16,128]{1,0:T(8,128)S(1)} %get-tuple-element.15.refs_0_, f32[16,128]{1,0:T(8,128)S(1)} %collective-permute-done.9.refs_1_, f32[16,128]{1,0:T(8,128)S(1)} %collective-permute-done.10.refs_2_, f32[16,128]{1,0:T(8,128)S(1)} %collective-permute-done.11.refs_3_, ...), custom_call_target="tpu_custom_call" | custom-call | tf_op jit(solution)/shard_map/update/pallas_call | solution.py:308
  (15 shorter events, 0.1 us)
Async XLA Ops:
  0.6 8.6 %copy-start.3 = (bf16[256,128]{1,0:T(8,128)(2,1)S(1)}, bf16[256,128]{1,0:T(8,128)(2,1)}, u32[]{:S(2)}) copy-start(bf16[256,128]{1,0:T(8,128)(2,1)} %points.1) | copy-start | bytes 196612
  0.6 8.6 %collective-permute-start.2 = (bf16[256,128]{1,0:T(8,128)(2,1)}, bf16[256,128]{1,0:T(8,128)(2,1)S(1)}, u32[]{:S(2)}, u32[]{:S(2)}) collective-permute-start(bf16[256,128]{1,0:T(8,128)(2,1)} %points.1), channel_id=1, source_target_pairs={{0,2},{1,3},{2,0},{3,1},{4,6},{5,7},{6,4},{7,5},{8,10},{9,11},{10,... | collective-permute-start | bytes 196616 | tf_op jit(solution)/shard_map/ppermute | solution.py:220
  4.8 7.1 %collective-permute-start.5 = (bf16[288,128]{1,0:T(8,128)(2,1)S(1)}, bf16[288,128]{1,0:T(8,128)(2,1)S(1)}, u32[]{:S(2)}, u32[]{:S(2)}) collective-permute-start(bf16[288,128]{1,0:T(8,128)(2,1)S(1)} %get-tuple-element.10.col), channel_id=1, source_target_pairs={{0,12},{1,13},{2,14},{3,15},{4,8},{5,9},{6,10},{7,11},{8,4},{9,5},... | collective-permute-start | bytes 221192 | tf_op jit(solution)/shard_map/ppermute | solution.py:220
  8.4 5.9 %collective-permute-start.4 = (bf16[288,128]{1,0:T(8,128)(2,1)S(1)}, bf16[288,128]{1,0:T(8,128)(2,1)S(1)}, u32[]{:S(2)}, u32[]{:S(2)}) collective-permute-start(bf16[288,128]{1,0:T(8,128)(2,1)S(1)} %get-tuple-element.10.col), channel_id=1, source_target_pairs={{0,8},{1,9},{2,10},{3,11},{4,12},{5,13},{6,14},{7,15},{8,0},{9,1},... | collective-permute-start | bytes 221192 | tf_op jit(solution)/shard_map/ppermute | solution.py:220
  8.4 6.9 %collective-permute-start = (bf16[288,128]{1,0:T(8,128)(2,1)S(1)}, bf16[288,128]{1,0:T(8,128)(2,1)S(1)}, u32[]{:S(2)}, u32[]{:S(2)}) collective-permute-start(bf16[288,128]{1,0:T(8,128)(2,1)S(1)} %get-tuple-element.10.col), channel_id=1, source_target_pairs={{0,4},{1,5},{2,6},{3,7},{4,0},{5,1},{6,2},{7,3},{8,12},{9,13},{10,... | collective-permute-start | bytes 221192 | tf_op jit(solution)/shard_map/ppermute | solution.py:220
  9.2 1.3 %collective-permute-start.1 = (bf16[256,128]{1,0:T(8,128)(2,1)S(1)}, bf16[256,128]{1,0:T(8,128)(2,1)S(1)}, u32[]{:S(2)}, u32[]{:S(2)}) collective-permute-start(bf16[256,128]{1,0:T(8,128)(2,1)S(1)} %copy-done.3), channel_id=1, source_target_pairs={{0,1},{1,0},{2,3},{3,2},{4,5},{5,4},{6,7},{7,6},{8,9},{9,8},{10,11... | collective-permute-start | bytes 196616 | tf_op jit(solution)/shard_map/ppermute | solution.py:220
  9.2 1.4 %collective-permute-start.3 = (bf16[256,128]{1,0:T(8,128)(2,1)S(1)}, bf16[256,128]{1,0:T(8,128)(2,1)S(1)}, u32[]{:S(2)}, u32[]{:S(2)}) collective-permute-start(bf16[256,128]{1,0:T(8,128)(2,1)S(1)} %collective-permute-done.2.refs_1_), channel_id=1, source_target_pairs={{0,1},{1,0},{2,3},{3,2},{4,5},{5,4},{6,7},{7,6},{8,9},{9,8},{10,11... | collective-permute-start | bytes 196616 | tf_op jit(solution)/shard_map/ppermute | solution.py:220
  16.3 1.9 %collective-permute-start.6 = (f32[48,128]{1,0:T(8,128)S(1)}, f32[48,128]{1,0:T(8,128)S(1)}, u32[]{:S(2)}, u32[]{:S(2)}) collective-permute-start(f32[48,128]{1,0:T(8,128)S(1)} %product_last.1.refs_0_), channel_id=1, source_target_pairs={{0,1},{1,0},{2,3},{3,2},{4,5},{5,4},{6,7},{7,6},{8,9},{9,8},{10,11... | collective-permute-start | bytes 73736 | tf_op jit(solution)/shard_map/ppermute | solution.py:220
  16.3 4.1 %collective-permute-start.7 = (f32[48,128]{1,0:T(8,128)S(1)}, f32[48,128]{1,0:T(8,128)S(1)}, u32[]{:S(2)}, u32[]{:S(2)}) collective-permute-start(f32[48,128]{1,0:T(8,128)S(1)} %product_last.1.refs_0_), channel_id=1, source_target_pairs={{0,2},{1,3},{2,0},{3,1},{4,6},{5,7},{6,4},{7,5},{8,10},{9,11},{10,... | collective-permute-start | bytes 73736 | tf_op jit(solution)/shard_map/ppermute | solution.py:220
  16.9 3.5 %collective-permute-start.8 = (f32[48,128]{1,0:T(8,128)S(1)}, f32[48,128]{1,0:T(8,128)S(1)}, u32[]{:S(2)}, u32[]{:S(2)}) collective-permute-start(f32[48,128]{1,0:T(8,128)S(1)} %product_last.1.refs_0_), channel_id=1, source_target_pairs={{0,3},{1,2},{2,1},{3,0},{4,7},{5,6},{6,5},{7,4},{8,11},{9,10},{10,... | collective-permute-start | bytes 73736 | tf_op jit(solution)/shard_map/ppermute | solution.py:220
  20.4 5.3 %copy-start = (f32[4,256]{1,0:T(4,128)S(1)}, f32[4,256]{1,0:T(4,128)}, u32[]{:S(2)}) copy-start(f32[4,256]{1,0:T(4,128)} %refs_7_.1) | copy-start | bytes 12292
  20.4 5.3 %copy-start.1 = (f32[4,256]{1,0:T(4,128)S(1)}, f32[4,256]{1,0:T(4,128)}, u32[]{:S(2)}) copy-start(f32[4,256]{1,0:T(4,128)} %refs_6_.1) | copy-start | bytes 12292
  20.4 5.3 %copy-start.2 = (f32[4,256]{1,0:T(4,128)S(1)}, f32[4,256]{1,0:T(4,128)}, u32[]{:S(2)}) copy-start(f32[4,256]{1,0:T(4,128)} %refs_5_.1) | copy-start | bytes 12292
  20.5 3.7 %collective-permute-start.10 = (f32[16,128]{1,0:T(8,128)S(1)}, f32[16,128]{1,0:T(8,128)S(1)}, u32[]{:S(2)}, u32[]{:S(2)}) collective-permute-start(f32[16,128]{1,0:T(8,128)S(1)} %get-tuple-element.15.refs_0_), channel_id=1, source_target_pairs={{0,4},{1,13},{2,6},{3,15},{4,0},{5,9},{6,2},{7,11},{8,12},{9,5},{1... | collective-permute-start | bytes 24584 | tf_op jit(solution)/shard_map/ppermute | solution.py:220
  20.7 4.7 %collective-permute-start.9 = (f32[16,128]{1,0:T(8,128)S(1)}, f32[16,128]{1,0:T(8,128)S(1)}, u32[]{:S(2)}, u32[]{:S(2)}) collective-permute-start(f32[16,128]{1,0:T(8,128)S(1)} %get-tuple-element.15.refs_0_), channel_id=1, source_target_pairs={{0,8},{1,9},{2,10},{3,11},{4,12},{5,13},{6,14},{7,15},{8,0},{9,1},... | collective-permute-start | bytes 24584 | tf_op jit(solution)/shard_map/ppermute | solution.py:220
  24.2 1.6 %collective-permute-start.11 = (f32[16,128]{1,0:T(8,128)S(1)}, f32[16,128]{1,0:T(8,128)S(1)}, u32[]{:S(2)}, u32[]{:S(2)}) collective-permute-start(f32[16,128]{1,0:T(8,128)S(1)} %collective-permute-done.10.refs_2_), channel_id=1, source_target_pairs={{0,1},{1,0},{2,3},{3,2},{4,5},{5,4},{6,7},{7,6},{8,9},{9,8},{10,11... | collective-permute-start | bytes 24584 | tf_op jit(solution)/shard_map/ppermute | solution.py:220

commit v15 on v14

--- a/solution.py
+++ b/solution.py
@@ -47,8 +47,8 @@
     return (sums[0] + sums[1])[:1]
 
 
-def pack_kernel(points, direction, residual, length, noise, packed, own, rates, *scratch):
-    step_in, rest_in, length_in, noise_in, sems = scratch
+def pack_kernel(points, direction, residual, length, noise, packed, own, rates, *refs):
+    *wider, step_in, rest_in, length_in, noise_in, sems = refs
     size, dims = points.shape
     cands = direction.shape[0]
     lines = (packed.shape[0] - size) * dims // size
@@ -80,19 +80,27 @@
         own[pl.ds(i * tall, tall), :] = fold(wide, dims)
     copies[0].wait()
     sq = squares(packed[:size, :])
-    top = [*pieces_of(sq), jnp.ones((3, size), jnp.float32), jnp.zeros((2, size), jnp.float32)]
-    top += [step, jnp.zeros((lines - 8 - cands, size), jnp.float32)]
+    top = [*pieces_of(sq), step, jnp.zeros((lines - 3 - cands, size), jnp.float32)]
     top = jnp.concatenate([t for t in top if t.shape[0]], axis=0)
     packed[size:, :] = fold(top, dims).astype(jnp.bfloat16)
-
-
-def widen_row(points):
+    filled = packed.shape[0]
+    for copy in wider:
+        copy[:filled, :] = packed[...]
+        spare = copy.shape[0] - filled
+        copy[filled:, :] = jnp.zeros((spare, dims), jnp.bfloat16)
+
+
+def lines_of(cands):
+    return -(-(3 + cands) // 8) * 8
+
+
+def widen_row(points, lines):
     wide = points.astype(jnp.float32)
     sq = pieces_of(jnp.sum(wide * wide, axis=1, keepdims=True))
     lane = lax.broadcasted_iota(jnp.int32, wide.shape, 1)
     extra = jnp.where(lane < 3, 1.0, 0.0)
     for i, piece in enumerate(sq):
-        extra = jnp.where(lane == 3 + i, piece, extra)
+        extra = jnp.where(lane == lines + i, piece, extra)
     return jnp.concatenate(
         [(wide * -2.0).astype(jnp.bfloat16), extra.astype(jnp.bfloat16)], axis=1
     )
@@ -103,9 +111,12 @@
     cands = rates.shape[0] // 8
     size = row_wide.shape[0] // lo
     wide = size // dims
-    lines = (col.shape[0] - size) // wide
-    top = unfold(col[size:, :], lines)
-    top = jnp.concatenate([top, jnp.zeros((dims - lines, size), top.dtype)], axis=0).T
+    lines = lines_of(cands)
+    top = unfold(col[size : size + lines * wide, :].astype(jnp.float32), lines)
+    ones = lax.broadcasted_iota(jnp.int32, (8, size), 0) < 3
+    rest = jnp.zeros((dims - lines - 8, size), jnp.float32)
+    top = jnp.concatenate([top, ones.astype(jnp.float32), rest], axis=0)
+    top = top.astype(jnp.bfloat16).T
     both = jnp.concatenate([col[:size, :], top], axis=1)
     steps = top.astype(jnp.float32)
 
@@ -119,7 +130,7 @@
 
     distances(0)
     for c in range(cands):
-        weights[c] = jnp.broadcast_to(steps[:, 8 + c : 9 + c], (size, dims))
+        weights[c] = jnp.broadcast_to(steps[:, 3 + c : 4 + c], (size, dims))
     rate = [
         jnp.concatenate([rates[pl.ds(8 * c, 8), :]] * wide, axis=1) for c in range(cands)
     ]
@@ -137,12 +148,20 @@
             out[places[c], :] = total[c]
 
 
+def stretch_kernel(block, out):
+    size = block.shape[0]
+    out[:size, :] = block[...]
+    out[size:, :] = jnp.zeros((out.shape[0] - size, out.shape[1]), out.dtype)
+
+
 def first_kernel(lo, col, *refs):
     rows, refs = refs[: lo - 1], refs[lo - 1 :]
     rates, out, row_wide, weights, dist = refs
     size = row_wide.shape[0] // lo
     for k, block in enumerate((col, *rows)):
-        row_wide[pl.ds(k * size, size), :] = widen_row(block[:size, :])
+        row_wide[pl.ds(k * size, size), :] = widen_row(
+            block[:size, :], lines_of(rates.shape[0] // 8)
+        )
     add_column(col, row_wide, rates, weights, dist, None, out, lo)
 
 
@@ -213,7 +232,7 @@
     size, dims = points.shape
     cands = direction.shape[0]
     tall = cands * size // dims
-    extra = -(-(8 + cands) // 16) * 16 * size // dims
+    filled = size + lines_of(cands) * size // dims
 
     def meet(x, mask, odd_mask=None):
         masks = (mask, mask if odd_mask is None else odd_mask)
@@ -223,15 +242,18 @@
     hbm = pl.BlockSpec(memory_space=pltpu.HBM)
     params = pltpu.CompilerParams(vmem_limit_bytes=50 * 1024 * 1024)
 
-    packed, own, rates = pl.pallas_call(
+    packed, own, rates, middle, core, far = pl.pallas_call(
         pack_kernel,
         out_shape=(
-            jax.ShapeDtypeStruct((size + extra, dims), jnp.bfloat16),
+            jax.ShapeDtypeStruct((filled, dims), jnp.bfloat16),
             jax.ShapeDtypeStruct((3 * tall, dims), jnp.float32),
             jax.ShapeDtypeStruct((8 * cands, dims), jnp.float32),
+            jax.ShapeDtypeStruct((filled + 16, dims), jnp.bfloat16),
+            jax.ShapeDtypeStruct((filled + 32, dims), jnp.bfloat16),
+            jax.ShapeDtypeStruct((filled + 48, dims), jnp.bfloat16),
         ),
         in_specs=[hbm] * 5,
-        out_specs=(vmem,) * 3,
+        out_specs=(vmem,) * 6,
         scratch_shapes=[
             pltpu.VMEM((cands, size), jnp.float32),
             pltpu.VMEM((cands, size), jnp.float32),
@@ -248,9 +270,23 @@
         )
     )
 
-    rows = [points]
-    for mask in row_masks[1:]:
-        rows.append(meet(rows[-1], 1) if mask % 2 else meet(points, mask))
+    rows = [packed, meet(core, 1)]
+    for mask in row_masks[2::2]:
+        block = meet(points, mask)
+        stretched = pl.pallas_call(
+            stretch_kernel,
+            out_shape=jax.ShapeDtypeStruct(core.shape, core.dtype),
+            in_specs=[vmem],
+            out_specs=vmem,
+            compiler_params=params,
+            name="stretch",
+        )(block)
+        rows += [block, meet(stretched, 1)]
+
+    def column(k):
+        wider = far if k > hi // 2 else middle if k == hi // 2 else packed
+        return meet(wider, col_masks[k])
+
     spare = [
         pltpu.VMEM((cands, size, dims), jnp.float32),
         pltpu.VMEM((lo, size, size), jnp.float32),
@@ -265,7 +301,8 @@
         compiler_params=params,
         name="product_0",
     )(packed, *rows[1:], rates)
-    for mask in reversed(col_masks[2:]):
+    order = [*range(hi - 1, hi // 2, -1), *range(1, hi // 2 + 1)]
+    for k in order[:-1]:
         total = pl.pallas_call(
             functools.partial(next_kernel, lo),
             out_shape=spread,
@@ -273,8 +310,8 @@
             out_specs=vmem,
             scratch_shapes=spare,
             compiler_params=params,
-            name="product_%d" % mask,
-        )(meet(packed, mask), row_wide, rates, total)
+            name="product_%d" % k,
+        )(column(k), row_wide, rates, total)
     partial = pl.pallas_call(
         functools.partial(last_kernel, lo),
         out_shape=jax.ShapeDtypeStruct(((lo + 2) * tall, dims), jnp.float32),
@@ -283,7 +320,7 @@
         scratch_shapes=[*spare, pltpu.VMEM(spread.shape, jnp.float32)],
         compiler_params=params,
         name="product_last",
-    )(meet(packed, col_masks[1]), row_wide, rates, total, own)
+    )(column(order[-1]), row_wide, rates, total, own)
 
     image, sums = pl.pallas_call(
         functools.partial(sums_kernel, cands),

time: 27 us -> 28.1 us (1.041); the launches traced: 26.5 us -> 28 us
  waiting for transfers between devices: 6.07 us -> 7.55 us
    ppermute x12, waiting for transfers between devices: 6.07 us -> 7.55 us  [meet(): lax.ppermute(x, 'blk', [(d, d ^ masks[d % 2]) for d in range(devices)])]
    pallas_call x1 -> x2, Pallas kernels: 1.08 us -> 1.11 us  [the longest x1 1.11 us: per_device(): pl.pallas_call(pack_kernel, out_shape=(jax.ShapeDtypeStruct((filled, dims...]
  transfers between devices with their start and end apart: 12 -> 12, of which waited for: 8 -> 6; matrix products, arithmetic and copies ran while one was open for 0% -> 0% of each run, Pallas kernels for 15% -> 14%
where the time goes in v15:
time: 28.1 us; the launch traced here: 28 us
  starting transfers between devices  14 us (50%)
  waiting for transfers between devices  7.55 us (27%)
  Pallas kernels  5.74 us (20%)
  between operations  0.71 us (3%)
    ppermute x12, starting transfers between devices, meet(): lax.ppermute(x, 'blk', [(d, d ^ masks[d % 2]) for d in range(devices)])  14 us
    ppermute x12, waiting for transfers between devices, meet(): lax.ppermute(x, 'blk', [(d, d ^ masks[d % 2]) for d in range(devices)])  7.55 us
    pallas_call x2, Pallas kernels, per_device(): pl.pallas_call(functools.partial(next_kernel, lo), out_shape=spread, in_s...  1.82 us
    pallas_call x1, Pallas kernels, per_device(): pl.pallas_call(pack_kernel, out_shape=(jax.ShapeDtypeStruct((filled, dims...  1.11 us
    pallas_call x1, Pallas kernels, per_device(): pl.pallas_call(functools.partial(first_kernel, lo), out_shape=(spread, ja...  1.07 us
    pallas_call x1, Pallas kernels, per_device(): pl.pallas_call(functools.partial(last_kernel, lo), out_shape=jax.ShapeDty...  0.94 us
    pallas_call x1, Pallas kernels, per_device(): pl.pallas_call(update_kernel, out_shape=(jax.ShapeDtypeStruct((cands, siz...  0.77 us
  transfers between devices with their start and end apart: 12, of which 6 were waited for; matrix products, arithmetic and copies ran while one was open for 0% of the time, Pallas kernels for 14%

profile of v15, /device:TPU:0, one launch (start us, length us, event | category | flops | bytes accessed | tf_op | source)
XLA Modules:
  0.0 28.0 jit_solution(2432694963267453540)
XLA Ops:
  0.6 3.0 %collective-permute-start.2 = (bf16[256,128]{1,0:T(8,128)(2,1)}, bf16[256,128]{1,0:T(8,128)(2,1)S(1)}, u32[]{:S(2)}, u32[]{:S(2)}) collective-permute-start(bf16[256,128]{1,0:T(8,128)(2,1)} %points.1), channel_id=1, source_target_pairs={{0,2},{1,3},{2,0},{3,1},{4,6},{5,7},{6,4},{7,5},{8,10},{9,11},{10,... | collective-permute-start | bytes 196616 | tf_op jit(solution)/shard_map/ppermute | solution.py:239
  3.7 1.1 %pack.1 = (bf16[272,128]{1,0:T(8,128)(2,1)S(1)}, f32[24,128]{1,0:T(8,128)S(1)}, f32[32,128]{1,0:T(8,128)S(1)}, bf16[288,128]{1,0:T(8,128)(2,1)S(1)}, bf16[304,12...) custom-call(bf16[256,128]{1,0:T(8,128)(2,1)} %points.1, f32[4,256]{1,0:T(4,128)} %refs_7_.1, f32[4,256]{1,0:T(4,128)} %refs_6_.1, ...), custom_call_target="tpu_custom_call" | custom-call | tf_op jit(solution)/shard_map/pack/pallas_call | solution.py:245
  4.8 3.7 %collective-permute-start.5 = (bf16[320,128]{1,0:T(8,128)(2,1)S(1)}, bf16[320,128]{1,0:T(8,128)(2,1)S(1)}, u32[]{:S(2)}, u32[]{:S(2)}) collective-permute-start(bf16[320,128]{1,0:T(8,128)(2,1)S(1)} %get-tuple-element.18), channel_id=1, source_target_pairs={{0,12},{1,13},{2,14},{3,15},{4,8},{5,9},{6,10},{7,11},{8,4},{9,5},... | collective-permute-start | bytes 245768 | tf_op jit(solution)/shard_map/ppermute | solution.py:239
  8.4 0.0 collective-permute-start.1
  8.5 0.6 %collective-permute-start.3 = (bf16[304,128]{1,0:T(8,128)(2,1)S(1)}, bf16[304,128]{1,0:T(8,128)(2,1)S(1)}, u32[]{:S(2)}, u32[]{:S(2)}) collective-permute-start(bf16[304,128]{1,0:T(8,128)(2,1)S(1)} %stretch.1), channel_id=1, source_target_pairs={{0,1},{1,0},{2,3},{3,2},{4,5},{5,4},{6,7},{7,6},{8,9},{9,8},{10,11... | collective-permute-start | bytes 233480 | tf_op jit(solution)/shard_map/ppermute | solution.py:239
  9.0 0.3 %collective-permute-start = (bf16[288,128]{1,0:T(8,128)(2,1)S(1)}, bf16[288,128]{1,0:T(8,128)(2,1)S(1)}, u32[]{:S(2)}, u32[]{:S(2)}) collective-permute-start(bf16[288,128]{1,0:T(8,128)(2,1)S(1)} %get-tuple-element.13), channel_id=1, source_target_pairs={{0,8},{1,9},{2,10},{3,11},{4,12},{5,13},{6,14},{7,15},{8,0},{9,1},... | collective-permute-start | bytes 221192 | tf_op jit(solution)/shard_map/ppermute | solution.py:239
  9.4 1.6 %collective-permute-start.4 = (bf16[272,128]{1,0:T(8,128)(2,1)S(1)}, bf16[272,128]{1,0:T(8,128)(2,1)S(1)}, u32[]{:S(2)}, u32[]{:S(2)}) collective-permute-start(bf16[272,128]{1,0:T(8,128)(2,1)S(1)} %get-tuple-element.14.col), channel_id=1, source_target_pairs={{0,4},{1,5},{2,6},{3,7},{4,0},{5,1},{6,2},{7,3},{8,12},{9,13},{10,... | collective-permute-start | bytes 208904 | tf_op jit(solution)/shard_map/ppermute | solution.py:239
  10.9 1.1 %product_0.1 = (f32[128,256]{1,0:T(8,128)S(1)}, bf16[1024,256]{1,0:T(8,128)(2,1)S(1)}) custom-call(bf16[272,128]{1,0:T(8,128)(2,1)S(1)} %get-tuple-element.14.col, bf16[304,128]{1,0:T(8,128)(2,1)S(1)} %collective-permute-done.1.refs_0_, bf16[256,128]{1,0:T(8,128)(2,1)S(1)} %collective-permute-done.2.block.refs_1_, ...), custom_call_target="tpu_custom_call" | custom-call | tf_op jit(solution)/shard_map/product_0/pallas_call | solution.py:295
  12.0 0.9 %product_3.1.before = f32[128,256]{1,0:T(8,128)S(1)} custom-call(bf16[320,128]{1,0:T(8,128)(2,1)S(1)} %collective-permute-done.5.col, bf16[1024,256]{1,0:T(8,128)(2,1)S(1)} %get-tuple-element.17.row_wide, f32[32,128]{1,0:T(8,128)S(1)} %get-tuple-element.16.refs_3_.rates, f32[128,256]{1,0:T(8,128)S(1)} %get-tuple-element.19.before), custom_call_target="tpu_custom_call" | custom-call | tf_op jit(solution)/shard_map/product_3/pallas_call | solution.py:306
  13.0 2.3 %collective-permute-done.4.col = bf16[272,128]{1,0:T(8,128)(2,1)S(1)} collective-permute-done((bf16[272,128]{1,0:T(8,128)(2,1)S(1)}, bf16[272,128]{1,0:T(8,128)(2,1)S(1)}, u32[]{:S(2)}, u32[]{:S(2)}) %collective-permute-start.4) | collective-permute-done | bytes 69664 | tf_op jit(solution)/shard_map/ppermute | solution.py:239
  15.2 0.9 %product_1.1.before = f32[128,256]{1,0:T(8,128)S(1)} custom-call(bf16[272,128]{1,0:T(8,128)(2,1)S(1)} %collective-permute-done.4.col, bf16[1024,256]{1,0:T(8,128)(2,1)S(1)} %get-tuple-element.17.row_wide, f32[32,128]{1,0:T(8,128)S(1)} %get-tuple-element.16.refs_3_.rates, f32[128,256]{1,0:T(8,128)S(1)} %product_3.1.before), custom_call_target="tpu_custom_call" | custom-call | tf_op jit(solution)/shard_map/product_1/pallas_call | solution.py:306
  16.2 0.9 %product_last.1.refs_0_ = f32[48,128]{1,0:T(8,128)S(1)} custom-call(bf16[288,128]{1,0:T(8,128)(2,1)S(1)} %collective-permute-done.col, bf16[1024,256]{1,0:T(8,128)(2,1)S(1)} %get-tuple-element.17.row_wide, f32[32,128]{1,0:T(8,128)S(1)} %get-tuple-element.16.refs_3_.rates, f32[128,256]{1,0:T(8,128)S(1)} %product_1.1.before, f32[24,128]{1,0:T(8,128)S(1)} %get-tuple-element.20.own), custom_call_target="tpu_custom_call" | custom-call | tf_op jit(solution)/shard_map/product_last/pallas_call | solution.py:315
  17.1 0.1 collective-permute-start.6
  17.2 1.4 %collective-permute-start.7 = (f32[48,128]{1,0:T(8,128)S(1)}, f32[48,128]{1,0:T(8,128)S(1)}, u32[]{:S(2)}, u32[]{:S(2)}) collective-permute-start(f32[48,128]{1,0:T(8,128)S(1)} %product_last.1.refs_0_), channel_id=1, source_target_pairs={{0,2},{1,3},{2,0},{3,1},{4,6},{5,7},{6,4},{7,5},{8,10},{9,11},{10,... | collective-permute-start | bytes 73736 | tf_op jit(solution)/shard_map/ppermute | solution.py:239
  18.6 0.5 %collective-permute-start.8 = (f32[48,128]{1,0:T(8,128)S(1)}, f32[48,128]{1,0:T(8,128)S(1)}, u32[]{:S(2)}, u32[]{:S(2)}) collective-permute-start(f32[48,128]{1,0:T(8,128)S(1)} %product_last.1.refs_0_), channel_id=1, source_target_pairs={{0,3},{1,2},{2,1},{3,0},{4,7},{5,6},{6,5},{7,4},{8,11},{9,10},{10,... | collective-permute-start | bytes 73736 | tf_op jit(solution)/shard_map/ppermute | solution.py:239
  19.0 2.0 %collective-permute-done.7.refs_2_ = f32[48,128]{1,0:T(8,128)S(1)} collective-permute-done((f32[48,128]{1,0:T(8,128)S(1)}, f32[48,128]{1,0:T(8,128)S(1)}, u32[]{:S(2)}, u32[]{:S(2)}) %collective-permute-start.7) | collective-permute-done | bytes 24608 | tf_op jit(solution)/shard_map/ppermute | solution.py:239
  21.1 0.7 %collective-permute-done.8.refs_3_ = f32[48,128]{1,0:T(8,128)S(1)} collective-permute-done((f32[48,128]{1,0:T(8,128)S(1)}, f32[48,128]{1,0:T(8,128)S(1)}, u32[]{:S(2)}, u32[]{:S(2)}) %collective-permute-start.8) | collective-permute-done | bytes 24608 | tf_op jit(solution)/shard_map/ppermute | solution.py:239
  21.8 0.5 %collective-permute-start.10 = (f32[16,128]{1,0:T(8,128)S(1)}, f32[16,128]{1,0:T(8,128)S(1)}, u32[]{:S(2)}, u32[]{:S(2)}) collective-permute-start(f32[16,128]{1,0:T(8,128)S(1)} %get-tuple-element.21.refs_0_), channel_id=1, source_target_pairs={{0,4},{1,13},{2,6},{3,15},{4,0},{5,9},{6,2},{7,11},{8,12},{9,5},{1... | collective-permute-start | bytes 24584 | tf_op jit(solution)/shard_map/ppermute | solution.py:239
  22.4 1.5 %collective-permute-start.9 = (f32[16,128]{1,0:T(8,128)S(1)}, f32[16,128]{1,0:T(8,128)S(1)}, u32[]{:S(2)}, u32[]{:S(2)}) collective-permute-start(f32[16,128]{1,0:T(8,128)S(1)} %get-tuple-element.21.refs_0_), channel_id=1, source_target_pairs={{0,8},{1,9},{2,10},{3,11},{4,12},{5,13},{6,14},{7,15},{8,0},{9,1},... | collective-permute-start | bytes 24584 | tf_op jit(solution)/shard_map/ppermute | solution.py:239
  23.9 1.7 %collective-permute-done.10.refs_2_ = f32[16,128]{1,0:T(8,128)S(1)} collective-permute-done((f32[16,128]{1,0:T(8,128)S(1)}, f32[16,128]{1,0:T(8,128)S(1)}, u32[]{:S(2)}, u32[]{:S(2)}) %collective-permute-start.10) | collective-permute-done | bytes 8224 | tf_op jit(solution)/shard_map/ppermute | solution.py:239
  25.6 0.8 %collective-permute-start.11 = (f32[16,128]{1,0:T(8,128)S(1)}, f32[16,128]{1,0:T(8,128)S(1)}, u32[]{:S(2)}, u32[]{:S(2)}) collective-permute-start(f32[16,128]{1,0:T(8,128)S(1)} %collective-permute-done.10.refs_2_), channel_id=1, source_target_pairs={{0,1},{1,0},{2,3},{3,2},{4,5},{5,4},{6,7},{7,6},{8,9},{9,8},{10,11... | collective-permute-start | bytes 24584 | tf_op jit(solution)/shard_map/ppermute | solution.py:239
  26.4 0.5 %collective-permute-done.9.refs_1_ = f32[16,128]{1,0:T(8,128)S(1)} collective-permute-done((f32[16,128]{1,0:T(8,128)S(1)}, f32[16,128]{1,0:T(8,128)S(1)}, u32[]{:S(2)}, u32[]{:S(2)}) %collective-permute-start.9) | collective-permute-done | bytes 8224 | tf_op jit(solution)/shard_map/ppermute | solution.py:239
  26.9 0.3 %collective-permute-done.11.refs_3_ = f32[16,128]{1,0:T(8,128)S(1)} collective-permute-done((f32[16,128]{1,0:T(8,128)S(1)}, f32[16,128]{1,0:T(8,128)S(1)}, u32[]{:S(2)}, u32[]{:S(2)}) %collective-permute-start.11) | collective-permute-done | bytes 8224 | tf_op jit(solution)/shard_map/ppermute | solution.py:239
  27.2 0.8 %update.1 = (f32[4,256]{1,0:T(4,128)}, f32[4,256]{1,0:T(4,128)}, f32[4,256]{1,0:T(4,128)}) custom-call(f32[16,128]{1,0:T(8,128)S(1)} %get-tuple-element.21.refs_0_, f32[16,128]{1,0:T(8,128)S(1)} %collective-permute-done.9.refs_1_, f32[16,128]{1,0:T(8,128)S(1)} %collective-permute-done.10.refs_2_, f32[16,128]{1,0:T(8,128)S(1)} %collective-permute-done.11.refs_3_, ...), custom_call_target="tpu_custom_call" | custom-call | tf_op jit(solution)/shard_map/update/pallas_call | solution.py:345
  (14 shorter events, 0.1 us)
Async XLA Ops:
  0.6 7.8 %collective-permute-start.2 = (bf16[256,128]{1,0:T(8,128)(2,1)}, bf16[256,128]{1,0:T(8,128)(2,1)S(1)}, u32[]{:S(2)}, u32[]{:S(2)}) collective-permute-start(bf16[256,128]{1,0:T(8,128)(2,1)} %points.1), channel_id=1, source_target_pairs={{0,2},{1,3},{2,0},{3,1},{4,6},{5,7},{6,4},{7,5},{8,10},{9,11},{10,... | collective-permute-start | bytes 196616 | tf_op jit(solution)/shard_map/ppermute | solution.py:239
  4.8 7.3 %collective-permute-start.5 = (bf16[320,128]{1,0:T(8,128)(2,1)S(1)}, bf16[320,128]{1,0:T(8,128)(2,1)S(1)}, u32[]{:S(2)}, u32[]{:S(2)}) collective-permute-start(bf16[320,128]{1,0:T(8,128)(2,1)S(1)} %get-tuple-element.18), channel_id=1, source_target_pairs={{0,12},{1,13},{2,14},{3,15},{4,8},{5,9},{6,10},{7,11},{8,4},{9,5},... | collective-permute-start | bytes 245768 | tf_op jit(solution)/shard_map/ppermute | solution.py:239
  8.4 2.5 %collective-permute-start.1 = (bf16[304,128]{1,0:T(8,128)(2,1)S(1)}, bf16[304,128]{1,0:T(8,128)(2,1)S(1)}, u32[]{:S(2)}, u32[]{:S(2)}) collective-permute-start(bf16[304,128]{1,0:T(8,128)(2,1)S(1)} %get-tuple-element.15), channel_id=1, source_target_pairs={{0,1},{1,0},{2,3},{3,2},{4,5},{5,4},{6,7},{7,6},{8,9},{9,8},{10,11... | collective-permute-start | bytes 233480 | tf_op jit(solution)/shard_map/ppermute | solution.py:239
  8.5 2.5 %collective-permute-start.3 = (bf16[304,128]{1,0:T(8,128)(2,1)S(1)}, bf16[304,128]{1,0:T(8,128)(2,1)S(1)}, u32[]{:S(2)}, u32[]{:S(2)}) collective-permute-start(bf16[304,128]{1,0:T(8,128)(2,1)S(1)} %stretch.1), channel_id=1, source_target_pairs={{0,1},{1,0},{2,3},{3,2},{4,5},{5,4},{6,7},{7,6},{8,9},{9,8},{10,11... | collective-permute-start | bytes 233480 | tf_op jit(solution)/shard_map/ppermute | solution.py:239
  9.0 7.1 %collective-permute-start = (bf16[288,128]{1,0:T(8,128)(2,1)S(1)}, bf16[288,128]{1,0:T(8,128)(2,1)S(1)}, u32[]{:S(2)}, u32[]{:S(2)}) collective-permute-start(bf16[288,128]{1,0:T(8,128)(2,1)S(1)} %get-tuple-element.13), channel_id=1, source_target_pairs={{0,8},{1,9},{2,10},{3,11},{4,12},{5,13},{6,14},{7,15},{8,0},{9,1},... | collective-permute-start | bytes 221192 | tf_op jit(solution)/shard_map/ppermute | solution.py:239
  9.4 5.9 %collective-permute-start.4 = (bf16[272,128]{1,0:T(8,128)(2,1)S(1)}, bf16[272,128]{1,0:T(8,128)(2,1)S(1)}, u32[]{:S(2)}, u32[]{:S(2)}) collective-permute-start(bf16[272,128]{1,0:T(8,128)(2,1)S(1)} %get-tuple-element.14.col), channel_id=1, source_target_pairs={{0,4},{1,5},{2,6},{3,7},{4,0},{5,1},{6,2},{7,3},{8,12},{9,13},{10,... | collective-permute-start | bytes 208904 | tf_op jit(solution)/shard_map/ppermute | solution.py:239
  17.1 1.9 %collective-permute-start.6 = (f32[48,128]{1,0:T(8,128)S(1)}, f32[48,128]{1,0:T(8,128)S(1)}, u32[]{:S(2)}, u32[]{:S(2)}) collective-permute-start(f32[48,128]{1,0:T(8,128)S(1)} %product_last.1.refs_0_), channel_id=1, source_target_pairs={{0,1},{1,0},{2,3},{3,2},{4,5},{5,4},{6,7},{7,6},{8,9},{9,8},{10,11... | collective-permute-start | bytes 73736 | tf_op jit(solution)/shard_map/ppermute | solution.py:239
  17.2 3.9 %collective-permute-start.7 = (f32[48,128]{1,0:T(8,128)S(1)}, f32[48,128]{1,0:T(8,128)S(1)}, u32[]{:S(2)}, u32[]{:S(2)}) collective-permute-start(f32[48,128]{1,0:T(8,128)S(1)} %product_last.1.refs_0_), channel_id=1, source_target_pairs={{0,2},{1,3},{2,0},{3,1},{4,6},{5,7},{6,4},{7,5},{8,10},{9,11},{10,... | collective-permute-start | bytes 73736 | tf_op jit(solution)/shard_map/ppermute | solution.py:239
  18.6 3.3 %collective-permute-start.8 = (f32[48,128]{1,0:T(8,128)S(1)}, f32[48,128]{1,0:T(8,128)S(1)}, u32[]{:S(2)}, u32[]{:S(2)}) collective-permute-start(f32[48,128]{1,0:T(8,128)S(1)} %product_last.1.refs_0_), channel_id=1, source_target_pairs={{0,3},{1,2},{2,1},{3,0},{4,7},{5,6},{6,5},{7,4},{8,11},{9,10},{10,... | collective-permute-start | bytes 73736 | tf_op jit(solution)/shard_map/ppermute | solution.py:239
  21.8 5.4 %copy-start = (f32[4,256]{1,0:T(4,128)S(1)}, f32[4,256]{1,0:T(4,128)}, u32[]{:S(2)}) copy-start(f32[4,256]{1,0:T(4,128)} %refs_7_.1) | copy-start | bytes 12292
  21.8 5.4 %copy-start.1 = (f32[4,256]{1,0:T(4,128)S(1)}, f32[4,256]{1,0:T(4,128)}, u32[]{:S(2)}) copy-start(f32[4,256]{1,0:T(4,128)} %refs_6_.1) | copy-start | bytes 12292
  21.8 5.4 %copy-start.2 = (f32[4,256]{1,0:T(4,128)S(1)}, f32[4,256]{1,0:T(4,128)}, u32[]{:S(2)}) copy-start(f32[4,256]{1,0:T(4,128)} %refs_5_.1) | copy-start | bytes 12292
  21.8 3.7 %collective-permute-start.10 = (f32[16,128]{1,0:T(8,128)S(1)}, f32[16,128]{1,0:T(8,128)S(1)}, u32[]{:S(2)}, u32[]{:S(2)}) collective-permute-start(f32[16,128]{1,0:T(8,128)S(1)} %get-tuple-element.21.refs_0_), channel_id=1, source_target_pairs={{0,4},{1,13},{2,6},{3,15},{4,0},{5,9},{6,2},{7,11},{8,12},{9,5},{1... | collective-permute-start | bytes 24584 | tf_op jit(solution)/shard_map/ppermute | solution.py:239
  22.4 4.5 %collective-permute-start.9 = (f32[16,128]{1,0:T(8,128)S(1)}, f32[16,128]{1,0:T(8,128)S(1)}, u32[]{:S(2)}, u32[]{:S(2)}) collective-permute-start(f32[16,128]{1,0:T(8,128)S(1)} %get-tuple-element.21.refs_0_), channel_id=1, source_target_pairs={{0,8},{1,9},{2,10},{3,11},{4,12},{5,13},{6,14},{7,15},{8,0},{9,1},... | collective-permute-start | bytes 24584 | tf_op jit(solution)/shard_map/ppermute | solution.py:239
  25.6 1.6 %collective-permute-start.11 = (f32[16,128]{1,0:T(8,128)S(1)}, f32[16,128]{1,0:T(8,128)S(1)}, u32[]{:S(2)}, u32[]{:S(2)}) collective-permute-start(f32[16,128]{1,0:T(8,128)S(1)} %collective-permute-done.10.refs_2_), channel_id=1, source_target_pairs={{0,1},{1,0},{2,3},{3,2},{4,5},{5,4},{6,7},{7,6},{8,9},{9,8},{10,11... | collective-permute-start | bytes 24584 | tf_op jit(solution)/shard_map/ppermute | solution.py:239

commit v16 on v15

--- a/solution.py
+++ b/solution.py
@@ -10,8 +10,10 @@
 def split_masks(devices):
     bits = devices.bit_length() - 1
     assert devices == 1 << bits and bits > 1
-    lo = 1 << (bits // 2)
-    return list(range(0, devices, lo)), list(range(lo))
+    far = bits // 2 - 1
+    row = [m << (bits - far) for m in range(1 << far)]
+    col = [m << 1 for m in range(1 << (bits - 1 - far))]
+    return col, [m + core for m in row for core in (0, 1)]
 
 
 def pieces_of(wide):
@@ -242,7 +244,7 @@
     hbm = pl.BlockSpec(memory_space=pltpu.HBM)
     params = pltpu.CompilerParams(vmem_limit_bytes=50 * 1024 * 1024)
 
-    packed, own, rates, middle, core, far = pl.pallas_call(
+    packed, own, rates, core, middle, far = pl.pallas_call(
         pack_kernel,
         out_shape=(
             jax.ShapeDtypeStruct((filled, dims), jnp.bfloat16),
@@ -301,7 +303,7 @@
         compiler_params=params,
         name="product_0",
     )(packed, *rows[1:], rates)
-    order = [*range(hi - 1, hi // 2, -1), *range(1, hi // 2 + 1)]
+    order = list(range(hi - 1, 0, -1))
     for k in order[:-1]:
         total = pl.pallas_call(
             functools.partial(next_kernel, lo),

time: 28.1 us -> 26.8 us (0.954)
  waiting for transfers between devices: 7.55 us -> 5.76 us
  starting transfers between devices: 14 us -> 14.4 us
    ppermute x12, waiting for transfers between devices: 7.55 us -> 5.76 us  [meet(): lax.ppermute(x, 'blk', [(d, d ^ masks[d % 2]) for d in range(devices)])]
    ppermute x12, starting transfers between devices: 14 us -> 14.4 us  [meet(): lax.ppermute(x, 'blk', [(d, d ^ masks[d % 2]) for d in range(devices)])]
  transfers between devices with their start and end apart: 12 -> 12, of which waited for: 6 -> 7; matrix products, arithmetic and copies ran while one was open for 0% -> 0% of each run, Pallas kernels for 14% -> 15%
where the time goes in v16:
time: 26.8 us; the launch traced here: 26.6 us
  starting transfers between devices  14.4 us (54%)
  waiting for transfers between devices  5.76 us (21%)
  Pallas kernels  5.74 us (21%)
  between operations  0.72 us (3%)
    ppermute x12, starting transfers between devices, meet(): lax.ppermute(x, 'blk', [(d, d ^ masks[d % 2]) for d in range(devices)])  14.4 us
    ppermute x12, waiting for transfers between devices, meet(): lax.ppermute(x, 'blk', [(d, d ^ masks[d % 2]) for d in range(devices)])  5.76 us
    pallas_call x2, Pallas kernels, per_device(): pl.pallas_call(functools.partial(next_kernel, lo), out_shape=spread, in_s...  1.81 us
    pallas_call x1, Pallas kernels, per_device(): pl.pallas_call(pack_kernel, out_shape=(jax.ShapeDtypeStruct((filled, dims...  1.11 us
    pallas_call x1, Pallas kernels, per_device(): pl.pallas_call(functools.partial(first_kernel, lo), out_shape=(spread, ja...  1.08 us
    pallas_call x1, Pallas kernels, per_device(): pl.pallas_call(functools.partial(last_kernel, lo), out_shape=jax.ShapeDty...  0.94 us
    pallas_call x1, Pallas kernels, per_device(): pl.pallas_call(update_kernel, out_shape=(jax.ShapeDtypeStruct((cands, siz...  0.78 us
  transfers between devices with their start and end apart: 12, of which 7 were waited for; matrix products, arithmetic and copies ran while one was open for 0% of the time, Pallas kernels for 15%

profile of v16, /device:TPU:0, one launch (start us, length us, event | category | flops | bytes accessed | tf_op | source)
XLA Modules:
  0.0 26.6 jit_solution(10621490917443341469)
XLA Ops:
  0.6 4.1 %collective-permute-start.2 = (bf16[256,128]{1,0:T(8,128)(2,1)}, bf16[256,128]{1,0:T(8,128)(2,1)S(1)}, u32[]{:S(2)}, u32[]{:S(2)}) collective-permute-start(bf16[256,128]{1,0:T(8,128)(2,1)} %points.1), channel_id=1, source_target_pairs={{0,8},{1,9},{2,10},{3,11},{4,12},{5,13},{6,14},{7,15},{8,0},{9,1},... | collective-permute-start | bytes 196616 | tf_op jit(solution)/shard_map/ppermute | solution.py:241
  4.7 1.1 %pack.1 = (bf16[272,128]{1,0:T(8,128)(2,1)S(1)}, f32[24,128]{1,0:T(8,128)S(1)}, f32[32,128]{1,0:T(8,128)S(1)}, bf16[288,128]{1,0:T(8,128)(2,1)S(1)}, bf16[304,12...) custom-call(bf16[256,128]{1,0:T(8,128)(2,1)} %points.1, f32[4,256]{1,0:T(4,128)} %refs_7_.1, f32[4,256]{1,0:T(4,128)} %refs_6_.1, ...), custom_call_target="tpu_custom_call" | custom-call | tf_op jit(solution)/shard_map/pack/pallas_call | solution.py:247
  5.8 2.6 %collective-permute-start.5 = (bf16[320,128]{1,0:T(8,128)(2,1)S(1)}, bf16[320,128]{1,0:T(8,128)(2,1)S(1)}, u32[]{:S(2)}, u32[]{:S(2)}) collective-permute-start(bf16[320,128]{1,0:T(8,128)(2,1)S(1)} %get-tuple-element.18), channel_id=1, source_target_pairs={{0,6},{1,7},{2,4},{3,5},{4,2},{5,3},{6,0},{7,1},{8,14},{9,15},{10,... | collective-permute-start | bytes 245768 | tf_op jit(solution)/shard_map/ppermute | solution.py:241
  8.4 0.4 %collective-permute-start.4 = (bf16[304,128]{1,0:T(8,128)(2,1)S(1)}, bf16[304,128]{1,0:T(8,128)(2,1)S(1)}, u32[]{:S(2)}, u32[]{:S(2)}) collective-permute-start(bf16[304,128]{1,0:T(8,128)(2,1)S(1)} %get-tuple-element.17), channel_id=1, source_target_pairs={{0,4},{1,5},{2,6},{3,7},{4,0},{5,1},{6,2},{7,3},{8,12},{9,13},{10,... | collective-permute-start | bytes 233480 | tf_op jit(solution)/shard_map/ppermute | solution.py:241
  8.9 0.0 collective-permute-done.2.block.refs_1_
  8.9 0.6 %collective-permute-start.3 = (bf16[288,128]{1,0:T(8,128)(2,1)S(1)}, bf16[288,128]{1,0:T(8,128)(2,1)S(1)}, u32[]{:S(2)}, u32[]{:S(2)}) collective-permute-start(bf16[288,128]{1,0:T(8,128)(2,1)S(1)} %stretch.1), channel_id=1, source_target_pairs={{0,1},{1,0},{2,3},{3,2},{4,5},{5,4},{6,7},{7,6},{8,9},{9,8},{10,11... | collective-permute-start | bytes 221192 | tf_op jit(solution)/shard_map/ppermute | solution.py:241
  9.5 0.5 %collective-permute-start = (bf16[272,128]{1,0:T(8,128)(2,1)S(1)}, bf16[272,128]{1,0:T(8,128)(2,1)S(1)}, u32[]{:S(2)}, u32[]{:S(2)}) collective-permute-start(bf16[272,128]{1,0:T(8,128)(2,1)S(1)} %get-tuple-element.13.col), channel_id=1, source_target_pairs={{0,2},{1,3},{2,0},{3,1},{4,6},{5,7},{6,4},{7,5},{8,10},{9,11},{10,... | collective-permute-start | bytes 208904 | tf_op jit(solution)/shard_map/ppermute | solution.py:241
  10.0 0.1 collective-permute-done.1.refs_0_
  10.2 0.2 collective-permute-done.3.refs_2_
  10.4 1.1 %product_0.1 = (f32[128,256]{1,0:T(8,128)S(1)}, bf16[1024,256]{1,0:T(8,128)(2,1)S(1)}) custom-call(bf16[272,128]{1,0:T(8,128)(2,1)S(1)} %get-tuple-element.13.col, bf16[288,128]{1,0:T(8,128)(2,1)S(1)} %collective-permute-done.1.refs_0_, bf16[256,128]{1,0:T(8,128)(2,1)S(1)} %collective-permute-done.2.block.refs_1_, ...), custom_call_target="tpu_custom_call" | custom-call | tf_op jit(solution)/shard_map/product_0/pallas_call | solution.py:297
  11.5 0.5 %collective-permute-done.5.col = bf16[320,128]{1,0:T(8,128)(2,1)S(1)} collective-permute-done((bf16[320,128]{1,0:T(8,128)(2,1)S(1)}, bf16[320,128]{1,0:T(8,128)(2,1)S(1)}, u32[]{:S(2)}, u32[]{:S(2)}) %collective-permute-start.5) | collective-permute-done | bytes 81952 | tf_op jit(solution)/shard_map/ppermute | solution.py:241
  12.0 0.9 %product_3.1.before = f32[128,256]{1,0:T(8,128)S(1)} custom-call(bf16[320,128]{1,0:T(8,128)(2,1)S(1)} %collective-permute-done.5.col, bf16[1024,256]{1,0:T(8,128)(2,1)S(1)} %get-tuple-element.16.row_wide, f32[32,128]{1,0:T(8,128)S(1)} %get-tuple-element.15.refs_3_.rates, f32[128,256]{1,0:T(8,128)S(1)} %get-tuple-element.19.before), custom_call_target="tpu_custom_call" | custom-call | tf_op jit(solution)/shard_map/product_3/pallas_call | solution.py:308
  12.9 0.9 %product_2.1.before = f32[128,256]{1,0:T(8,128)S(1)} custom-call(bf16[304,128]{1,0:T(8,128)(2,1)S(1)} %collective-permute-done.4.col, bf16[1024,256]{1,0:T(8,128)(2,1)S(1)} %get-tuple-element.16.row_wide, f32[32,128]{1,0:T(8,128)S(1)} %get-tuple-element.15.refs_3_.rates, f32[128,256]{1,0:T(8,128)S(1)} %product_3.1.before), custom_call_target="tpu_custom_call" | custom-call | tf_op jit(solution)/shard_map/product_2/pallas_call | solution.py:308
  13.8 0.9 %product_last.1.refs_0_ = f32[48,128]{1,0:T(8,128)S(1)} custom-call(bf16[272,128]{1,0:T(8,128)(2,1)S(1)} %collective-permute-done.col, bf16[1024,256]{1,0:T(8,128)(2,1)S(1)} %get-tuple-element.16.row_wide, f32[32,128]{1,0:T(8,128)S(1)} %get-tuple-element.15.refs_3_.rates, f32[128,256]{1,0:T(8,128)S(1)} %product_2.1.before, f32[24,128]{1,0:T(8,128)S(1)} %get-tuple-element.20.own), custom_call_target="tpu_custom_call" | custom-call | tf_op jit(solution)/shard_map/product_last/pallas_call | solution.py:317
  14.8 0.1 collective-permute-start.6
  14.8 1.1 %collective-permute-start.7 = (f32[48,128]{1,0:T(8,128)S(1)}, f32[48,128]{1,0:T(8,128)S(1)}, u32[]{:S(2)}, u32[]{:S(2)}) collective-permute-start(f32[48,128]{1,0:T(8,128)S(1)} %product_last.1.refs_0_), channel_id=1, source_target_pairs={{0,8},{1,9},{2,10},{3,11},{4,12},{5,13},{6,14},{7,15},{8,0},{9,1},... | collective-permute-start | bytes 73736 | tf_op jit(solution)/shard_map/ppermute | solution.py:241
  15.9 1.7 %collective-permute-start.8 = (f32[48,128]{1,0:T(8,128)S(1)}, f32[48,128]{1,0:T(8,128)S(1)}, u32[]{:S(2)}, u32[]{:S(2)}) collective-permute-start(f32[48,128]{1,0:T(8,128)S(1)} %product_last.1.refs_0_), channel_id=1, source_target_pairs={{0,9},{1,8},{2,11},{3,10},{4,13},{5,12},{6,15},{7,14},{8,1},{9,0},... | collective-permute-start | bytes 73736 | tf_op jit(solution)/shard_map/ppermute | solution.py:241
  17.6 2.0 %collective-permute-done.7.refs_2_ = f32[48,128]{1,0:T(8,128)S(1)} collective-permute-done((f32[48,128]{1,0:T(8,128)S(1)}, f32[48,128]{1,0:T(8,128)S(1)}, u32[]{:S(2)}, u32[]{:S(2)}) %collective-permute-start.7) | collective-permute-done | bytes 24608 | tf_op jit(solution)/shard_map/ppermute | solution.py:241
  19.6 1.2 %collective-permute-done.8.refs_3_ = f32[48,128]{1,0:T(8,128)S(1)} collective-permute-done((f32[48,128]{1,0:T(8,128)S(1)}, f32[48,128]{1,0:T(8,128)S(1)}, u32[]{:S(2)}, u32[]{:S(2)}) %collective-permute-start.8) | collective-permute-done | bytes 24608 | tf_op jit(solution)/shard_map/ppermute | solution.py:241
  20.9 1.3 %collective-permute-start.10 = (f32[16,128]{1,0:T(8,128)S(1)}, f32[16,128]{1,0:T(8,128)S(1)}, u32[]{:S(2)}, u32[]{:S(2)}) collective-permute-start(f32[16,128]{1,0:T(8,128)S(1)} %get-tuple-element.21.refs_0_), channel_id=1, source_target_pairs={{0,2},{1,7},{2,0},{3,5},{4,6},{5,3},{6,4},{7,1},{8,10},{9,15},{10,... | collective-permute-start | bytes 24584 | tf_op jit(solution)/shard_map/ppermute | solution.py:241
  22.2 2.0 %collective-permute-start.9 = (f32[16,128]{1,0:T(8,128)S(1)}, f32[16,128]{1,0:T(8,128)S(1)}, u32[]{:S(2)}, u32[]{:S(2)}) collective-permute-start(f32[16,128]{1,0:T(8,128)S(1)} %get-tuple-element.21.refs_0_), channel_id=1, source_target_pairs={{0,4},{1,5},{2,6},{3,7},{4,0},{5,1},{6,2},{7,3},{8,12},{9,13},{10,... | collective-permute-start | bytes 24584 | tf_op jit(solution)/shard_map/ppermute | solution.py:241
  24.2 0.4 %collective-permute-done.10.refs_2_ = f32[16,128]{1,0:T(8,128)S(1)} collective-permute-done((f32[16,128]{1,0:T(8,128)S(1)}, f32[16,128]{1,0:T(8,128)S(1)}, u32[]{:S(2)}, u32[]{:S(2)}) %collective-permute-start.10) | collective-permute-done | bytes 8224 | tf_op jit(solution)/shard_map/ppermute | solution.py:241
  24.6 1.2 %collective-permute-done.9.refs_1_ = f32[16,128]{1,0:T(8,128)S(1)} collective-permute-done((f32[16,128]{1,0:T(8,128)S(1)}, f32[16,128]{1,0:T(8,128)S(1)}, u32[]{:S(2)}, u32[]{:S(2)}) %collective-permute-start.9) | collective-permute-done | bytes 8224 | tf_op jit(solution)/shard_map/ppermute | solution.py:241
  25.8 0.8 %update.1 = (f32[4,256]{1,0:T(4,128)}, f32[4,256]{1,0:T(4,128)}, f32[4,256]{1,0:T(4,128)}) custom-call(f32[16,128]{1,0:T(8,128)S(1)} %get-tuple-element.21.refs_0_, f32[16,128]{1,0:T(8,128)S(1)} %collective-permute-done.9.refs_1_, f32[16,128]{1,0:T(8,128)S(1)} %collective-permute-done.10.refs_2_, f32[16,128]{1,0:T(8,128)S(1)} %collective-permute-done.11.refs_3_, ...), custom_call_target="tpu_custom_call" | custom-call | tf_op jit(solution)/shard_map/update/pallas_call | solution.py:347
  (14 shorter events, 0.1 us)
Async XLA Ops:
  0.6 8.3 %collective-permute-start.2 = (bf16[256,128]{1,0:T(8,128)(2,1)}, bf16[256,128]{1,0:T(8,128)(2,1)S(1)}, u32[]{:S(2)}, u32[]{:S(2)}) collective-permute-start(bf16[256,128]{1,0:T(8,128)(2,1)} %points.1), channel_id=1, source_target_pairs={{0,8},{1,9},{2,10},{3,11},{4,12},{5,13},{6,14},{7,15},{8,0},{9,1},... | collective-permute-start | bytes 196616 | tf_op jit(solution)/shard_map/ppermute | solution.py:241
  5.8 6.1 %collective-permute-start.5 = (bf16[320,128]{1,0:T(8,128)(2,1)S(1)}, bf16[320,128]{1,0:T(8,128)(2,1)S(1)}, u32[]{:S(2)}, u32[]{:S(2)}) collective-permute-start(bf16[320,128]{1,0:T(8,128)(2,1)S(1)} %get-tuple-element.18), channel_id=1, source_target_pairs={{0,6},{1,7},{2,4},{3,5},{4,2},{5,3},{6,0},{7,1},{8,14},{9,15},{10,... | collective-permute-start | bytes 245768 | tf_op jit(solution)/shard_map/ppermute | solution.py:241
  8.4 4.4 %collective-permute-start.4 = (bf16[304,128]{1,0:T(8,128)(2,1)S(1)}, bf16[304,128]{1,0:T(8,128)(2,1)S(1)}, u32[]{:S(2)}, u32[]{:S(2)}) collective-permute-start(bf16[304,128]{1,0:T(8,128)(2,1)S(1)} %get-tuple-element.17), channel_id=1, source_target_pairs={{0,4},{1,5},{2,6},{3,7},{4,0},{5,1},{6,2},{7,3},{8,12},{9,13},{10,... | collective-permute-start | bytes 233480 | tf_op jit(solution)/shard_map/ppermute | solution.py:241
  8.9 1.3 %collective-permute-start.1 = (bf16[288,128]{1,0:T(8,128)(2,1)S(1)}, bf16[288,128]{1,0:T(8,128)(2,1)S(1)}, u32[]{:S(2)}, u32[]{:S(2)}) collective-permute-start(bf16[288,128]{1,0:T(8,128)(2,1)S(1)} %get-tuple-element.14), channel_id=1, source_target_pairs={{0,1},{1,0},{2,3},{3,2},{4,5},{5,4},{6,7},{7,6},{8,9},{9,8},{10,11... | collective-permute-start | bytes 221192 | tf_op jit(solution)/shard_map/ppermute | solution.py:241
  8.9 1.5 %collective-permute-start.3 = (bf16[288,128]{1,0:T(8,128)(2,1)S(1)}, bf16[288,128]{1,0:T(8,128)(2,1)S(1)}, u32[]{:S(2)}, u32[]{:S(2)}) collective-permute-start(bf16[288,128]{1,0:T(8,128)(2,1)S(1)} %stretch.1), channel_id=1, source_target_pairs={{0,1},{1,0},{2,3},{3,2},{4,5},{5,4},{6,7},{7,6},{8,9},{9,8},{10,11... | collective-permute-start | bytes 221192 | tf_op jit(solution)/shard_map/ppermute | solution.py:241
  9.5 4.3 %collective-permute-start = (bf16[272,128]{1,0:T(8,128)(2,1)S(1)}, bf16[272,128]{1,0:T(8,128)(2,1)S(1)}, u32[]{:S(2)}, u32[]{:S(2)}) collective-permute-start(bf16[272,128]{1,0:T(8,128)(2,1)S(1)} %get-tuple-element.13.col), channel_id=1, source_target_pairs={{0,2},{1,3},{2,0},{3,1},{4,6},{5,7},{6,4},{7,5},{8,10},{9,11},{10,... | collective-permute-start | bytes 208904 | tf_op jit(solution)/shard_map/ppermute | solution.py:241
  14.8 2.8 %collective-permute-start.6 = (f32[48,128]{1,0:T(8,128)S(1)}, f32[48,128]{1,0:T(8,128)S(1)}, u32[]{:S(2)}, u32[]{:S(2)}) collective-permute-start(f32[48,128]{1,0:T(8,128)S(1)} %product_last.1.refs_0_), channel_id=1, source_target_pairs={{0,1},{1,0},{2,3},{3,2},{4,5},{5,4},{6,7},{7,6},{8,9},{9,8},{10,11... | collective-permute-start | bytes 73736 | tf_op jit(solution)/shard_map/ppermute | solution.py:241
  14.8 4.8 %collective-permute-start.7 = (f32[48,128]{1,0:T(8,128)S(1)}, f32[48,128]{1,0:T(8,128)S(1)}, u32[]{:S(2)}, u32[]{:S(2)}) collective-permute-start(f32[48,128]{1,0:T(8,128)S(1)} %product_last.1.refs_0_), channel_id=1, source_target_pairs={{0,8},{1,9},{2,10},{3,11},{4,12},{5,13},{6,14},{7,15},{8,0},{9,1},... | collective-permute-start | bytes 73736 | tf_op jit(solution)/shard_map/ppermute | solution.py:241
  15.9 4.9 %collective-permute-start.8 = (f32[48,128]{1,0:T(8,128)S(1)}, f32[48,128]{1,0:T(8,128)S(1)}, u32[]{:S(2)}, u32[]{:S(2)}) collective-permute-start(f32[48,128]{1,0:T(8,128)S(1)} %product_last.1.refs_0_), channel_id=1, source_target_pairs={{0,9},{1,8},{2,11},{3,10},{4,13},{5,12},{6,15},{7,14},{8,1},{9,0},... | collective-permute-start | bytes 73736 | tf_op jit(solution)/shard_map/ppermute | solution.py:241
  20.9 5.0 %copy-start = (f32[4,256]{1,0:T(4,128)S(1)}, f32[4,256]{1,0:T(4,128)}, u32[]{:S(2)}) copy-start(f32[4,256]{1,0:T(4,128)} %refs_7_.1) | copy-start | bytes 12292
  20.9 5.0 %copy-start.1 = (f32[4,256]{1,0:T(4,128)S(1)}, f32[4,256]{1,0:T(4,128)}, u32[]{:S(2)}) copy-start(f32[4,256]{1,0:T(4,128)} %refs_6_.1) | copy-start | bytes 12292
  20.9 5.0 %copy-start.2 = (f32[4,256]{1,0:T(4,128)S(1)}, f32[4,256]{1,0:T(4,128)}, u32[]{:S(2)}) copy-start(f32[4,256]{1,0:T(4,128)} %refs_5_.1) | copy-start | bytes 12292
  20.9 3.7 %collective-permute-start.10 = (f32[16,128]{1,0:T(8,128)S(1)}, f32[16,128]{1,0:T(8,128)S(1)}, u32[]{:S(2)}, u32[]{:S(2)}) collective-permute-start(f32[16,128]{1,0:T(8,128)S(1)} %get-tuple-element.21.refs_0_), channel_id=1, source_target_pairs={{0,2},{1,7},{2,0},{3,5},{4,6},{5,3},{6,4},{7,1},{8,10},{9,15},{10,... | collective-permute-start | bytes 24584 | tf_op jit(solution)/shard_map/ppermute | solution.py:241
  22.2 3.7 %collective-permute-start.9 = (f32[16,128]{1,0:T(8,128)S(1)}, f32[16,128]{1,0:T(8,128)S(1)}, u32[]{:S(2)}, u32[]{:S(2)}) collective-permute-start(f32[16,128]{1,0:T(8,128)S(1)} %get-tuple-element.21.refs_0_), channel_id=1, source_target_pairs={{0,4},{1,5},{2,6},{3,7},{4,0},{5,1},{6,2},{7,3},{8,12},{9,13},{10,... | collective-permute-start | bytes 24584 | tf_op jit(solution)/shard_map/ppermute | solution.py:241
  24.6 1.2 %collective-permute-start.11 = (f32[16,128]{1,0:T(8,128)S(1)}, f32[16,128]{1,0:T(8,128)S(1)}, u32[]{:S(2)}, u32[]{:S(2)}) collective-permute-start(f32[16,128]{1,0:T(8,128)S(1)} %collective-permute-done.10.refs_2_), channel_id=1, source_target_pairs={{0,1},{1,0},{2,3},{3,2},{4,5},{5,4},{6,7},{7,6},{8,9},{9,8},{10,11... | collective-permute-start | bytes 24584 | tf_op jit(solution)/shard_map/ppermute | solution.py:241

commit v17 on v16

--- a/solution.py
+++ b/solution.py
@@ -6,6 +6,9 @@
 from jax.experimental import pallas as pl
 from jax.experimental.pallas import tpu as pltpu
 from jax.sharding import PartitionSpec as P
+
+LOG2E = 1.4426950408889634
+
 
 def split_masks(devices):
     bits = devices.bit_length() - 1
@@ -75,7 +78,7 @@
     sigma = jnp.zeros((cands, 1), jnp.float32)
     for c in range(cands):
         sigma = jnp.where(which == c, noise_in[c], sigma)
-        rate = -0.5 / (length_in[c] * length_in[c])
+        rate = (-0.5 * LOG2E) / (length_in[c] * length_in[c])
         rates[pl.ds(8 * c, 8), :] = jnp.full((8, dims), rate, jnp.float32)
     tall = own.shape[0] // 3
     for i, wide in enumerate((step, rest_in[...], sigma * step)):
@@ -145,7 +148,7 @@
             here = dist[k, pl.ds(j, 8), :]
             for c in range(cands):
                 weight = jnp.concatenate([weights[c, pl.ds(j, 8), :]] * wide, axis=1)
-                total[c] = total[c] + jnp.exp(here * rate[c]) * weight
+                total[c] = total[c] + jnp.exp2(here * rate[c]) * weight
         for c in range(cands):
             out[places[c], :] = total[c]
 
@@ -189,6 +192,7 @@
 
 def sums_kernel(cands, *refs):
     *parts, image_out, sums_out = refs
+    parts = [*reversed(parts[-2:]), *parts[:-2]]
     lo = len(parts)
     tall, dims = image_out.shape
     sums = [jnp.zeros((tall, dims), jnp.float32)] * 4
@@ -303,7 +307,7 @@
         compiler_params=params,
         name="product_0",
     )(packed, *rows[1:], rates)
-    order = list(range(hi - 1, 0, -1))
+    order = [hi // 2, *range(hi - 1, hi // 2, -1), *range(hi // 2 - 1, 0, -1)]
     for k in order[:-1]:
         total = pl.pallas_call(
             functools.partial(next_kernel, lo),
@@ -334,7 +338,7 @@
         out_specs=(vmem, vmem),
         compiler_params=params,
         name="sums",
-    )(partial, *(meet(partial, mask) for mask in row_masks[1:]))
+    )(*(meet(partial, mask) for mask in (*row_masks[2:], 1)), partial)
 
     half = hi // 2
     shared = [

time: 26.8 us -> 26.6 us (level)
  starting transfers between devices: 14.4 us -> 15.2 us
  waiting for transfers between devices: 5.76 us -> 5.22 us
  Pallas kernels: 5.74 us -> 5.25 us
    ppermute x12, starting transfers between devices: 14.4 us -> 15.2 us  [meet(): lax.ppermute(x, 'blk', [(d, d ^ masks[d % 2]) for d in range(devices)])]
    ppermute x12, waiting for transfers between devices: 5.76 us -> 5.22 us  [meet(): lax.ppermute(x, 'blk', [(d, d ^ masks[d % 2]) for d in range(devices)])]
  transfers between devices with their start and end apart: 12 -> 12, of which waited for: 7 -> 5; matrix products, arithmetic and copies ran while one was open for 0% -> 0% of each run, Pallas kernels for 15% -> 14%
where the time goes in v17:
time: 26.6 us; the launch traced here: 26.4 us
  starting transfers between devices  15.2 us (57%)
  Pallas kernels  5.25 us (20%)
  waiting for transfers between devices  5.22 us (20%)
  between operations  0.74 us (3%)
    ppermute x12, starting transfers between devices, meet(): lax.ppermute(x, 'blk', [(d, d ^ masks[d % 2]) for d in range(devices)])  15.2 us
    ppermute x12, waiting for transfers between devices, meet(): lax.ppermute(x, 'blk', [(d, d ^ masks[d % 2]) for d in range(devices)])  5.22 us
    pallas_call x2, Pallas kernels, per_device(): pl.pallas_call(functools.partial(next_kernel, lo), out_shape=spread, in_s...  1.58 us
    pallas_call x1, Pallas kernels, per_device(): pl.pallas_call(pack_kernel, out_shape=(jax.ShapeDtypeStruct((filled, dims...  1.11 us
    pallas_call x1, Pallas kernels, per_device(): pl.pallas_call(functools.partial(first_kernel, lo), out_shape=(spread, ja...  0.95 us
    pallas_call x1, Pallas kernels, per_device(): pl.pallas_call(functools.partial(last_kernel, lo), out_shape=jax.ShapeDty...  0.81 us
    pallas_call x1, Pallas kernels, per_device(): pl.pallas_call(update_kernel, out_shape=(jax.ShapeDtypeStruct((cands, siz...  0.78 us
  transfers between devices with their start and end apart: 12, of which 5 were waited for; matrix products, arithmetic and copies ran while one was open for 0% of the time, Pallas kernels for 14%

profile of v17, /device:TPU:0, one launch (start us, length us, event | category | flops | bytes accessed | tf_op | source)
XLA Modules:
  0.0 26.4 jit_solution(4722183787009622133)
XLA Ops:
  0.6 4.1 %collective-permute-start.2 = (bf16[256,128]{1,0:T(8,128)(2,1)}, bf16[256,128]{1,0:T(8,128)(2,1)S(1)}, u32[]{:S(2)}, u32[]{:S(2)}) collective-permute-start(bf16[256,128]{1,0:T(8,128)(2,1)} %points.1), channel_id=1, source_target_pairs={{0,8},{1,9},{2,10},{3,11},{4,12},{5,13},{6,14},{7,15},{8,0},{9,1},... | collective-permute-start | bytes 196616 | tf_op jit(solution)/shard_map/ppermute | solution.py:245
  4.7 1.1 %pack.1 = (bf16[272,128]{1,0:T(8,128)(2,1)S(1)}, f32[24,128]{1,0:T(8,128)S(1)}, f32[32,128]{1,0:T(8,128)S(1)}, bf16[288,128]{1,0:T(8,128)(2,1)S(1)}, bf16[304,12...) custom-call(bf16[256,128]{1,0:T(8,128)(2,1)} %points.1, f32[4,256]{1,0:T(4,128)} %refs_7_.1, f32[4,256]{1,0:T(4,128)} %refs_6_.1, ...), custom_call_target="tpu_custom_call" | custom-call | tf_op jit(solution)/shard_map/pack/pallas_call | solution.py:251
  5.8 2.6 %collective-permute-start.4 = (bf16[320,128]{1,0:T(8,128)(2,1)S(1)}, bf16[320,128]{1,0:T(8,128)(2,1)S(1)}, u32[]{:S(2)}, u32[]{:S(2)}) collective-permute-start(bf16[320,128]{1,0:T(8,128)(2,1)S(1)} %get-tuple-element.17), channel_id=1, source_target_pairs={{0,6},{1,7},{2,4},{3,5},{4,2},{5,3},{6,0},{7,1},{8,14},{9,15},{10,... | collective-permute-start | bytes 245768 | tf_op jit(solution)/shard_map/ppermute | solution.py:245
  8.4 0.4 %collective-permute-start.5 = (bf16[304,128]{1,0:T(8,128)(2,1)S(1)}, bf16[304,128]{1,0:T(8,128)(2,1)S(1)}, u32[]{:S(2)}, u32[]{:S(2)}) collective-permute-start(bf16[304,128]{1,0:T(8,128)(2,1)S(1)} %get-tuple-element.18), channel_id=1, source_target_pairs={{0,4},{1,5},{2,6},{3,7},{4,0},{5,1},{6,2},{7,3},{8,12},{9,13},{10,... | collective-permute-start | bytes 233480 | tf_op jit(solution)/shard_map/ppermute | solution.py:245
  8.9 0.0 collective-permute-start.1
  8.9 0.6 %collective-permute-start.3 = (bf16[288,128]{1,0:T(8,128)(2,1)S(1)}, bf16[288,128]{1,0:T(8,128)(2,1)S(1)}, u32[]{:S(2)}, u32[]{:S(2)}) collective-permute-start(bf16[288,128]{1,0:T(8,128)(2,1)S(1)} %stretch.1), channel_id=1, source_target_pairs={{0,1},{1,0},{2,3},{3,2},{4,5},{5,4},{6,7},{7,6},{8,9},{9,8},{10,11... | collective-permute-start | bytes 221192 | tf_op jit(solution)/shard_map/ppermute | solution.py:245
  9.5 0.5 %collective-permute-start = (bf16[272,128]{1,0:T(8,128)(2,1)S(1)}, bf16[272,128]{1,0:T(8,128)(2,1)S(1)}, u32[]{:S(2)}, u32[]{:S(2)}) collective-permute-start(bf16[272,128]{1,0:T(8,128)(2,1)S(1)} %get-tuple-element.13.col), channel_id=1, source_target_pairs={{0,2},{1,3},{2,0},{3,1},{4,6},{5,7},{6,4},{7,5},{8,10},{9,11},{10,... | collective-permute-start | bytes 208904 | tf_op jit(solution)/shard_map/ppermute | solution.py:245
  10.0 0.1 collective-permute-done.1.refs_0_
  10.2 0.2 collective-permute-done.3.refs_2_
  10.4 0.9 %product_0.1 = (f32[128,256]{1,0:T(8,128)S(1)}, bf16[1024,256]{1,0:T(8,128)(2,1)S(1)}) custom-call(bf16[272,128]{1,0:T(8,128)(2,1)S(1)} %get-tuple-element.13.col, bf16[288,128]{1,0:T(8,128)(2,1)S(1)} %collective-permute-done.1.refs_0_, bf16[256,128]{1,0:T(8,128)(2,1)S(1)} %collective-permute-done.2.block.refs_1_, ...), custom_call_target="tpu_custom_call" | custom-call | tf_op jit(solution)/shard_map/product_0/pallas_call | solution.py:301
  11.4 1.5 %collective-permute-done.5.col = bf16[304,128]{1,0:T(8,128)(2,1)S(1)} collective-permute-done((bf16[304,128]{1,0:T(8,128)(2,1)S(1)}, bf16[304,128]{1,0:T(8,128)(2,1)S(1)}, u32[]{:S(2)}, u32[]{:S(2)}) %collective-permute-start.5) | collective-permute-done | bytes 77856 | tf_op jit(solution)/shard_map/ppermute | solution.py:245
  12.9 0.8 %product_2.1.before = f32[128,256]{1,0:T(8,128)S(1)} custom-call(bf16[304,128]{1,0:T(8,128)(2,1)S(1)} %collective-permute-done.5.col, bf16[1024,256]{1,0:T(8,128)(2,1)S(1)} %get-tuple-element.16.row_wide, f32[32,128]{1,0:T(8,128)S(1)} %get-tuple-element.15.refs_3_.rates, f32[128,256]{1,0:T(8,128)S(1)} %get-tuple-element.19.before), custom_call_target="tpu_custom_call" | custom-call | tf_op jit(solution)/shard_map/product_2/pallas_call | solution.py:312
  13.7 0.8 %product_3.1.before = f32[128,256]{1,0:T(8,128)S(1)} custom-call(bf16[320,128]{1,0:T(8,128)(2,1)S(1)} %collective-permute-done.4.col, bf16[1024,256]{1,0:T(8,128)(2,1)S(1)} %get-tuple-element.16.row_wide, f32[32,128]{1,0:T(8,128)S(1)} %get-tuple-element.15.refs_3_.rates, f32[128,256]{1,0:T(8,128)S(1)} %product_2.1.before), custom_call_target="tpu_custom_call" | custom-call | tf_op jit(solution)/shard_map/product_3/pallas_call | solution.py:312
  14.5 0.8 %product_last.1.refs_3_ = f32[48,128]{1,0:T(8,128)S(1)} custom-call(bf16[272,128]{1,0:T(8,128)(2,1)S(1)} %collective-permute-done.col, bf16[1024,256]{1,0:T(8,128)(2,1)S(1)} %get-tuple-element.16.row_wide, f32[32,128]{1,0:T(8,128)S(1)} %get-tuple-element.15.refs_3_.rates, f32[128,256]{1,0:T(8,128)S(1)} %product_3.1.before, f32[24,128]{1,0:T(8,128)S(1)} %get-tuple-element.20.own), custom_call_target="tpu_custom_call" | custom-call | tf_op jit(solution)/shard_map/product_last/pallas_call | solution.py:321
  15.3 0.4 %collective-permute-start.6 = (f32[48,128]{1,0:T(8,128)S(1)}, f32[48,128]{1,0:T(8,128)S(1)}, u32[]{:S(2)}, u32[]{:S(2)}) collective-permute-start(f32[48,128]{1,0:T(8,128)S(1)} %product_last.1.refs_3_), channel_id=1, source_target_pairs={{0,8},{1,9},{2,10},{3,11},{4,12},{5,13},{6,14},{7,15},{8,0},{9,1},... | collective-permute-start | bytes 73736 | tf_op jit(solution)/shard_map/ppermute | solution.py:245
  15.7 1.0 %collective-permute-start.7 = (f32[48,128]{1,0:T(8,128)S(1)}, f32[48,128]{1,0:T(8,128)S(1)}, u32[]{:S(2)}, u32[]{:S(2)}) collective-permute-start(f32[48,128]{1,0:T(8,128)S(1)} %product_last.1.refs_3_), channel_id=1, source_target_pairs={{0,9},{1,8},{2,11},{3,10},{4,13},{5,12},{6,15},{7,14},{8,1},{9,0},... | collective-permute-start | bytes 73736 | tf_op jit(solution)/shard_map/ppermute | solution.py:245
  16.7 1.7 %collective-permute-start.8 = (f32[48,128]{1,0:T(8,128)S(1)}, f32[48,128]{1,0:T(8,128)S(1)}, u32[]{:S(2)}, u32[]{:S(2)}) collective-permute-start(f32[48,128]{1,0:T(8,128)S(1)} %product_last.1.refs_3_), channel_id=1, source_target_pairs={{0,1},{1,0},{2,3},{3,2},{4,5},{5,4},{6,7},{7,6},{8,9},{9,8},{10,11... | collective-permute-start | bytes 73736 | tf_op jit(solution)/shard_map/ppermute | solution.py:245
  18.4 1.7 %collective-permute-done.6.refs_0_ = f32[48,128]{1,0:T(8,128)S(1)} collective-permute-done((f32[48,128]{1,0:T(8,128)S(1)}, f32[48,128]{1,0:T(8,128)S(1)}, u32[]{:S(2)}, u32[]{:S(2)}) %collective-permute-start.6) | collective-permute-done | bytes 24608 | tf_op jit(solution)/shard_map/ppermute | solution.py:245
  20.1 0.0 copy-start.1
  20.1 0.0 copy-start.2
  20.2 1.4 %collective-permute-start.10 = (f32[16,128]{1,0:T(8,128)S(1)}, f32[16,128]{1,0:T(8,128)S(1)}, u32[]{:S(2)}, u32[]{:S(2)}) collective-permute-start(f32[16,128]{1,0:T(8,128)S(1)} %get-tuple-element.21.refs_0_), channel_id=1, source_target_pairs={{0,2},{1,7},{2,0},{3,5},{4,6},{5,3},{6,4},{7,1},{8,10},{9,15},{10,... | collective-permute-start | bytes 24584 | tf_op jit(solution)/shard_map/ppermute | solution.py:245
  21.6 2.4 %collective-permute-start.9 = (f32[16,128]{1,0:T(8,128)S(1)}, f32[16,128]{1,0:T(8,128)S(1)}, u32[]{:S(2)}, u32[]{:S(2)}) collective-permute-start(f32[16,128]{1,0:T(8,128)S(1)} %get-tuple-element.21.refs_0_), channel_id=1, source_target_pairs={{0,4},{1,5},{2,6},{3,7},{4,0},{5,1},{6,2},{7,3},{8,12},{9,13},{10,... | collective-permute-start | bytes 24584 | tf_op jit(solution)/shard_map/ppermute | solution.py:245
  24.0 1.6 %collective-permute-done.9.refs_1_ = f32[16,128]{1,0:T(8,128)S(1)} collective-permute-done((f32[16,128]{1,0:T(8,128)S(1)}, f32[16,128]{1,0:T(8,128)S(1)}, u32[]{:S(2)}, u32[]{:S(2)}) %collective-permute-start.9) | collective-permute-done | bytes 8224 | tf_op jit(solution)/shard_map/ppermute | solution.py:245
  25.6 0.8 %update.1 = (f32[4,256]{1,0:T(4,128)}, f32[4,256]{1,0:T(4,128)}, f32[4,256]{1,0:T(4,128)}) custom-call(f32[16,128]{1,0:T(8,128)S(1)} %get-tuple-element.21.refs_0_, f32[16,128]{1,0:T(8,128)S(1)} %collective-permute-done.9.refs_1_, f32[16,128]{1,0:T(8,128)S(1)} %collective-permute-done.10.refs_2_, f32[16,128]{1,0:T(8,128)S(1)} %collective-permute-done.11.refs_3_, ...), custom_call_target="tpu_custom_call" | custom-call | tf_op jit(solution)/shard_map/update/pallas_call | solution.py:351
  (14 shorter events, 0.1 us)
Async XLA Ops:
  0.6 8.3 %collective-permute-start.2 = (bf16[256,128]{1,0:T(8,128)(2,1)}, bf16[256,128]{1,0:T(8,128)(2,1)S(1)}, u32[]{:S(2)}, u32[]{:S(2)}) collective-permute-start(bf16[256,128]{1,0:T(8,128)(2,1)} %points.1), channel_id=1, source_target_pairs={{0,8},{1,9},{2,10},{3,11},{4,12},{5,13},{6,14},{7,15},{8,0},{9,1},... | collective-permute-start | bytes 196616 | tf_op jit(solution)/shard_map/ppermute | solution.py:245
  5.8 7.8 %collective-permute-start.4 = (bf16[320,128]{1,0:T(8,128)(2,1)S(1)}, bf16[320,128]{1,0:T(8,128)(2,1)S(1)}, u32[]{:S(2)}, u32[]{:S(2)}) collective-permute-start(bf16[320,128]{1,0:T(8,128)(2,1)S(1)} %get-tuple-element.17), channel_id=1, source_target_pairs={{0,6},{1,7},{2,4},{3,5},{4,2},{5,3},{6,0},{7,1},{8,14},{9,15},{10,... | collective-permute-start | bytes 245768 | tf_op jit(solution)/shard_map/ppermute | solution.py:245
  8.4 4.4 %collective-permute-start.5 = (bf16[304,128]{1,0:T(8,128)(2,1)S(1)}, bf16[304,128]{1,0:T(8,128)(2,1)S(1)}, u32[]{:S(2)}, u32[]{:S(2)}) collective-permute-start(bf16[304,128]{1,0:T(8,128)(2,1)S(1)} %get-tuple-element.18), channel_id=1, source_target_pairs={{0,4},{1,5},{2,6},{3,7},{4,0},{5,1},{6,2},{7,3},{8,12},{9,13},{10,... | collective-permute-start | bytes 233480 | tf_op jit(solution)/shard_map/ppermute | solution.py:245
  8.9 1.3 %collective-permute-start.1 = (bf16[288,128]{1,0:T(8,128)(2,1)S(1)}, bf16[288,128]{1,0:T(8,128)(2,1)S(1)}, u32[]{:S(2)}, u32[]{:S(2)}) collective-permute-start(bf16[288,128]{1,0:T(8,128)(2,1)S(1)} %get-tuple-element.14), channel_id=1, source_target_pairs={{0,1},{1,0},{2,3},{3,2},{4,5},{5,4},{6,7},{7,6},{8,9},{9,8},{10,11... | collective-permute-start | bytes 221192 | tf_op jit(solution)/shard_map/ppermute | solution.py:245
  8.9 1.5 %collective-permute-start.3 = (bf16[288,128]{1,0:T(8,128)(2,1)S(1)}, bf16[288,128]{1,0:T(8,128)(2,1)S(1)}, u32[]{:S(2)}, u32[]{:S(2)}) collective-permute-start(bf16[288,128]{1,0:T(8,128)(2,1)S(1)} %stretch.1), channel_id=1, source_target_pairs={{0,1},{1,0},{2,3},{3,2},{4,5},{5,4},{6,7},{7,6},{8,9},{9,8},{10,11... | collective-permute-start | bytes 221192 | tf_op jit(solution)/shard_map/ppermute | solution.py:245
  9.5 5.0 %collective-permute-start = (bf16[272,128]{1,0:T(8,128)(2,1)S(1)}, bf16[272,128]{1,0:T(8,128)(2,1)S(1)}, u32[]{:S(2)}, u32[]{:S(2)}) collective-permute-start(bf16[272,128]{1,0:T(8,128)(2,1)S(1)} %get-tuple-element.13.col), channel_id=1, source_target_pairs={{0,2},{1,3},{2,0},{3,1},{4,6},{5,7},{6,4},{7,5},{8,10},{9,11},{10,... | collective-permute-start | bytes 208904 | tf_op jit(solution)/shard_map/ppermute | solution.py:245
  15.3 4.8 %collective-permute-start.6 = (f32[48,128]{1,0:T(8,128)S(1)}, f32[48,128]{1,0:T(8,128)S(1)}, u32[]{:S(2)}, u32[]{:S(2)}) collective-permute-start(f32[48,128]{1,0:T(8,128)S(1)} %product_last.1.refs_3_), channel_id=1, source_target_pairs={{0,8},{1,9},{2,10},{3,11},{4,12},{5,13},{6,14},{7,15},{8,0},{9,1},... | collective-permute-start | bytes 73736 | tf_op jit(solution)/shard_map/ppermute | solution.py:245
  15.7 4.4 %collective-permute-start.7 = (f32[48,128]{1,0:T(8,128)S(1)}, f32[48,128]{1,0:T(8,128)S(1)}, u32[]{:S(2)}, u32[]{:S(2)}) collective-permute-start(f32[48,128]{1,0:T(8,128)S(1)} %product_last.1.refs_3_), channel_id=1, source_target_pairs={{0,9},{1,8},{2,11},{3,10},{4,13},{5,12},{6,15},{7,14},{8,1},{9,0},... | collective-permute-start | bytes 73736 | tf_op jit(solution)/shard_map/ppermute | solution.py:245
  16.7 3.4 %collective-permute-start.8 = (f32[48,128]{1,0:T(8,128)S(1)}, f32[48,128]{1,0:T(8,128)S(1)}, u32[]{:S(2)}, u32[]{:S(2)}) collective-permute-start(f32[48,128]{1,0:T(8,128)S(1)} %product_last.1.refs_3_), channel_id=1, source_target_pairs={{0,1},{1,0},{2,3},{3,2},{4,5},{5,4},{6,7},{7,6},{8,9},{9,8},{10,11... | collective-permute-start | bytes 73736 | tf_op jit(solution)/shard_map/ppermute | solution.py:245
  20.1 5.5 %copy-start = (f32[4,256]{1,0:T(4,128)S(1)}, f32[4,256]{1,0:T(4,128)}, u32[]{:S(2)}) copy-start(f32[4,256]{1,0:T(4,128)} %refs_7_.1) | copy-start | bytes 12292
  20.1 5.5 %copy-start.1 = (f32[4,256]{1,0:T(4,128)S(1)}, f32[4,256]{1,0:T(4,128)}, u32[]{:S(2)}) copy-start(f32[4,256]{1,0:T(4,128)} %refs_6_.1) | copy-start | bytes 12292
  20.1 5.5 %copy-start.2 = (f32[4,256]{1,0:T(4,128)S(1)}, f32[4,256]{1,0:T(4,128)}, u32[]{:S(2)}) copy-start(f32[4,256]{1,0:T(4,128)} %refs_5_.1) | copy-start | bytes 12292
  20.2 3.8 %collective-permute-start.10 = (f32[16,128]{1,0:T(8,128)S(1)}, f32[16,128]{1,0:T(8,128)S(1)}, u32[]{:S(2)}, u32[]{:S(2)}) collective-permute-start(f32[16,128]{1,0:T(8,128)S(1)} %get-tuple-element.21.refs_0_), channel_id=1, source_target_pairs={{0,2},{1,7},{2,0},{3,5},{4,6},{5,3},{6,4},{7,1},{8,10},{9,15},{10,... | collective-permute-start | bytes 24584 | tf_op jit(solution)/shard_map/ppermute | solution.py:245
  21.6 4.0 %collective-permute-start.9 = (f32[16,128]{1,0:T(8,128)S(1)}, f32[16,128]{1,0:T(8,128)S(1)}, u32[]{:S(2)}, u32[]{:S(2)}) collective-permute-start(f32[16,128]{1,0:T(8,128)S(1)} %get-tuple-element.21.refs_0_), channel_id=1, source_target_pairs={{0,4},{1,5},{2,6},{3,7},{4,0},{5,1},{6,2},{7,3},{8,12},{9,13},{10,... | collective-permute-start | bytes 24584 | tf_op jit(solution)/shard_map/ppermute | solution.py:245
  24.0 1.6 %collective-permute-start.11 = (f32[16,128]{1,0:T(8,128)S(1)}, f32[16,128]{1,0:T(8,128)S(1)}, u32[]{:S(2)}, u32[]{:S(2)}) collective-permute-start(f32[16,128]{1,0:T(8,128)S(1)} %collective-permute-done.10.refs_2_), channel_id=1, source_target_pairs={{0,1},{1,0},{2,3},{3,2},{4,5},{5,4},{6,7},{7,6},{8,9},{9,8},{10,11... | collective-permute-start | bytes 24584 | tf_op jit(solution)/shard_map/ppermute | solution.py:245

commit v18 on v17

--- a/solution.py
+++ b/solution.py
@@ -192,7 +192,7 @@
 
 def sums_kernel(cands, *refs):
     *parts, image_out, sums_out = refs
-    parts = [*reversed(parts[-2:]), *parts[:-2]]
+    parts = parts[::-1]
     lo = len(parts)
     tall, dims = image_out.shape
     sums = [jnp.zeros((tall, dims), jnp.float32)] * 4
@@ -248,7 +248,7 @@
     hbm = pl.BlockSpec(memory_space=pltpu.HBM)
     params = pltpu.CompilerParams(vmem_limit_bytes=50 * 1024 * 1024)
 
-    packed, own, rates, core, middle, far = pl.pallas_call(
+    packed, own, rates, wider, widest = pl.pallas_call(
         pack_kernel,
         out_shape=(
             jax.ShapeDtypeStruct((filled, dims), jnp.bfloat16),
@@ -256,10 +256,9 @@
             jax.ShapeDtypeStruct((8 * cands, dims), jnp.float32),
             jax.ShapeDtypeStruct((filled + 16, dims), jnp.bfloat16),
             jax.ShapeDtypeStruct((filled + 32, dims), jnp.bfloat16),
-            jax.ShapeDtypeStruct((filled + 48, dims), jnp.bfloat16),
         ),
         in_specs=[hbm] * 5,
-        out_specs=(vmem,) * 6,
+        out_specs=(vmem,) * 5,
         scratch_shapes=[
             pltpu.VMEM((cands, size), jnp.float32),
             pltpu.VMEM((cands, size), jnp.float32),
@@ -276,12 +275,12 @@
         )
     )
 
-    rows = [packed, meet(core, 1)]
+    rows = [packed, meet(wider, 1)]
     for mask in row_masks[2::2]:
         block = meet(points, mask)
         stretched = pl.pallas_call(
             stretch_kernel,
-            out_shape=jax.ShapeDtypeStruct(core.shape, core.dtype),
+            out_shape=jax.ShapeDtypeStruct(wider.shape, wider.dtype),
             in_specs=[vmem],
             out_specs=vmem,
             compiler_params=params,
@@ -290,8 +289,7 @@
         rows += [block, meet(stretched, 1)]
 
     def column(k):
-        wider = far if k > hi // 2 else middle if k == hi // 2 else packed
-        return meet(wider, col_masks[k])
+        return meet(packed if k < hi // 2 else widest, col_masks[k])
 
     spare = [
         pltpu.VMEM((cands, size, dims), jnp.float32),
@@ -338,7 +336,7 @@
         out_specs=(vmem, vmem),
         compiler_params=params,
         name="sums",
-    )(*(meet(partial, mask) for mask in (*row_masks[2:], 1)), partial)
+    )(*(meet(partial, mask) for mask in reversed(row_masks[1:])), partial)
 
     half = hi // 2
     shared = [

time: 26.6 us -> 26.6 us (level)
  waiting for transfers between devices: 5.22 us -> 6.02 us
  starting transfers between devices: 15.2 us -> 14.4 us
    ppermute x12, waiting for transfers between devices: 5.22 us -> 6.02 us  [meet(): lax.ppermute(x, 'blk', [(d, d ^ masks[d % 2]) for d in range(devices)])]
    ppermute x12, starting transfers between devices: 15.2 us -> 14.4 us  [meet(): lax.ppermute(x, 'blk', [(d, d ^ masks[d % 2]) for d in range(devices)])]
  transfers between devices with their start and end apart: 12 -> 12, of which waited for: 5 -> 8; matrix products, arithmetic and copies ran while one was open for 0% -> 0% of each run, Pallas kernels for 14% -> 14%
where the time goes in v18:
time: 26.6 us; the launch traced here: 26.4 us
  starting transfers between devices  14.4 us (54%)
  waiting for transfers between devices  6.02 us (23%)
  Pallas kernels  5.24 us (20%)
  between operations  0.72 us (3%)
    ppermute x12, starting transfers between devices, meet(): lax.ppermute(x, 'blk', [(d, d ^ masks[d % 2]) for d in range(devices)])  14.4 us
    ppermute x12, waiting for transfers between devices, meet(): lax.ppermute(x, 'blk', [(d, d ^ masks[d % 2]) for d in range(devices)])  6.02 us
    pallas_call x2, Pallas kernels, per_device(): pl.pallas_call(functools.partial(next_kernel, lo), out_shape=spread, in_s...  1.59 us
    pallas_call x1, Pallas kernels, per_device(): pl.pallas_call(pack_kernel, out_shape=(jax.ShapeDtypeStruct((filled, dims...  1.1 us
    pallas_call x1, Pallas kernels, per_device(): pl.pallas_call(functools.partial(first_kernel, lo), out_shape=(spread, ja...  0.94 us
    pallas_call x1, Pallas kernels, per_device(): pl.pallas_call(functools.partial(last_kernel, lo), out_shape=jax.ShapeDty...  0.81 us
    pallas_call x1, Pallas kernels, per_device(): pl.pallas_call(update_kernel, out_shape=(jax.ShapeDtypeStruct((cands, siz...  0.78 us
  transfers between devices with their start and end apart: 12, of which 8 were waited for; matrix products, arithmetic and copies ran while one was open for 0% of the time, Pallas kernels for 14%

profile of v18, /device:TPU:0, one launch (start us, length us, event | category | flops | bytes accessed | tf_op | source)
XLA Modules:
  0.0 26.4 jit_solution(1847573471125090179)
XLA Ops:
  0.6 4.1 %collective-permute-start.2 = (bf16[256,128]{1,0:T(8,128)(2,1)}, bf16[256,128]{1,0:T(8,128)(2,1)S(1)}, u32[]{:S(2)}, u32[]{:S(2)}) collective-permute-start(bf16[256,128]{1,0:T(8,128)(2,1)} %points.1), channel_id=1, source_target_pairs={{0,8},{1,9},{2,10},{3,11},{4,12},{5,13},{6,14},{7,15},{8,0},{9,1},... | collective-permute-start | bytes 196616 | tf_op jit(solution)/shard_map/ppermute | solution.py:245
  4.7 1.1 %pack.1 = (bf16[272,128]{1,0:T(8,128)(2,1)S(1)}, f32[24,128]{1,0:T(8,128)S(1)}, f32[32,128]{1,0:T(8,128)S(1)}, bf16[288,128]{1,0:T(8,128)(2,1)S(1)}, bf16[304,128]{1,0:T(8,128)(2,1)S(1)}) custom-call(bf16[256,128]{1,0:T(8,128)(2,1)} %points.1, f32[4,256]{1,0:T(4,128)} %refs_7_.1, f32[4,256]{1,0:T(4,128)} %refs_6_.1, f32[4]{0:T(128)} %length.1, f32[4]{0:T(128)} %noise.1), custom_call_target="tpu_custom_call" | custom-call | tf_op jit(solution)/shard_map/pack/pallas_call | solution.py:251
  5.8 1.6 %collective-permute-start.5 = (bf16[304,128]{1,0:T(8,128)(2,1)S(1)}, bf16[304,128]{1,0:T(8,128)(2,1)S(1)}, u32[]{:S(2)}, u32[]{:S(2)}) collective-permute-start(bf16[304,128]{1,0:T(8,128)(2,1)S(1)} %get-tuple-element.16), channel_id=1, source_target_pairs={{0,4},{1,5},{2,6},{3,7},{4,0},{5,1},{6,2},{7,3},{8,12},{9,13},{10,... | collective-permute-start | bytes 233480 | tf_op jit(solution)/shard_map/ppermute | solution.py:245
  7.5 1.4 %collective-permute-start.4 = (bf16[304,128]{1,0:T(8,128)(2,1)S(1)}, bf16[304,128]{1,0:T(8,128)(2,1)S(1)}, u32[]{:S(2)}, u32[]{:S(2)}) collective-permute-start(bf16[304,128]{1,0:T(8,128)(2,1)S(1)} %get-tuple-element.16), channel_id=1, source_target_pairs={{0,6},{1,7},{2,4},{3,5},{4,2},{5,3},{6,0},{7,1},{8,14},{9,15},{10,... | collective-permute-start | bytes 233480 | tf_op jit(solution)/shard_map/ppermute | solution.py:245
  8.9 0.6 %collective-permute-start.3 = (bf16[288,128]{1,0:T(8,128)(2,1)S(1)}, bf16[288,128]{1,0:T(8,128)(2,1)S(1)}, u32[]{:S(2)}, u32[]{:S(2)}) collective-permute-start(bf16[288,128]{1,0:T(8,128)(2,1)S(1)} %stretch.1), channel_id=1, source_target_pairs={{0,1},{1,0},{2,3},{3,2},{4,5},{5,4},{6,7},{7,6},{8,9},{9,8},{10,11... | collective-permute-start | bytes 221192 | tf_op jit(solution)/shard_map/ppermute | solution.py:245
  9.5 0.6 %collective-permute-start = (bf16[272,128]{1,0:T(8,128)(2,1)S(1)}, bf16[272,128]{1,0:T(8,128)(2,1)S(1)}, u32[]{:S(2)}, u32[]{:S(2)}) collective-permute-start(bf16[272,128]{1,0:T(8,128)(2,1)S(1)} %get-tuple-element.12.col), channel_id=1, source_target_pairs={{0,2},{1,3},{2,0},{3,1},{4,6},{5,7},{6,4},{7,5},{8,10},{9,11},{10,... | collective-permute-start | bytes 208904 | tf_op jit(solution)/shard_map/ppermute | solution.py:245
  10.0 0.1 collective-permute-done.1.refs_0_
  10.2 0.2 collective-permute-done.3.refs_2_
  10.4 0.9 %product_0.1 = (f32[128,256]{1,0:T(8,128)S(1)}, bf16[1024,256]{1,0:T(8,128)(2,1)S(1)}) custom-call(bf16[272,128]{1,0:T(8,128)(2,1)S(1)} %get-tuple-element.12.col, bf16[288,128]{1,0:T(8,128)(2,1)S(1)} %collective-permute-done.1.refs_0_, bf16[256,128]{1,0:T(8,128)(2,1)S(1)} %collective-permute-done.2.block.refs_1_, ...), custom_call_target="tpu_custom_call" | custom-call | tf_op jit(solution)/shard_map/product_0/pallas_call | solution.py:299
  11.4 0.8 %product_2.1.before = f32[128,256]{1,0:T(8,128)S(1)} custom-call(bf16[304,128]{1,0:T(8,128)(2,1)S(1)} %collective-permute-done.5.col, bf16[1024,256]{1,0:T(8,128)(2,1)S(1)} %get-tuple-element.15.row_wide, f32[32,128]{1,0:T(8,128)S(1)} %get-tuple-element.14.refs_3_.rates, f32[128,256]{1,0:T(8,128)S(1)} %get-tuple-element.17.before), custom_call_target="tpu_custom_call" | custom-call | tf_op jit(solution)/shard_map/product_2/pallas_call | solution.py:310
  12.2 0.7 %collective-permute-done.4.col = bf16[304,128]{1,0:T(8,128)(2,1)S(1)} collective-permute-done((bf16[304,128]{1,0:T(8,128)(2,1)S(1)}, bf16[304,128]{1,0:T(8,128)(2,1)S(1)}, u32[]{:S(2)}, u32[]{:S(2)}) %collective-permute-start.4) | collective-permute-done | bytes 77856 | tf_op jit(solution)/shard_map/ppermute | solution.py:245
  12.8 0.8 %product_3.1.before = f32[128,256]{1,0:T(8,128)S(1)} custom-call(bf16[304,128]{1,0:T(8,128)(2,1)S(1)} %collective-permute-done.4.col, bf16[1024,256]{1,0:T(8,128)(2,1)S(1)} %get-tuple-element.15.row_wide, f32[32,128]{1,0:T(8,128)S(1)} %get-tuple-element.14.refs_3_.rates, f32[128,256]{1,0:T(8,128)S(1)} %product_2.1.before), custom_call_target="tpu_custom_call" | custom-call | tf_op jit(solution)/shard_map/product_3/pallas_call | solution.py:310
  13.6 0.6 %collective-permute-done.col = bf16[272,128]{1,0:T(8,128)(2,1)S(1)} collective-permute-done((bf16[272,128]{1,0:T(8,128)(2,1)S(1)}, bf16[272,128]{1,0:T(8,128)(2,1)S(1)}, u32[]{:S(2)}, u32[]{:S(2)}) %collective-permute-start) | collective-permute-done | bytes 69664 | tf_op jit(solution)/shard_map/ppermute | solution.py:245
  14.3 0.8 %product_last.1.refs_3_ = f32[48,128]{1,0:T(8,128)S(1)} custom-call(bf16[272,128]{1,0:T(8,128)(2,1)S(1)} %collective-permute-done.col, bf16[1024,256]{1,0:T(8,128)(2,1)S(1)} %get-tuple-element.15.row_wide, f32[32,128]{1,0:T(8,128)S(1)} %get-tuple-element.14.refs_3_.rates, f32[128,256]{1,0:T(8,128)S(1)} %product_3.1.before, f32[24,128]{1,0:T(8,128)S(1)} %get-tuple-element.18.own), custom_call_target="tpu_custom_call" | custom-call | tf_op jit(solution)/shard_map/product_last/pallas_call | solution.py:319
  15.1 0.1 collective-permute-start.6
  15.2 2.4 %collective-permute-start.7 = (f32[48,128]{1,0:T(8,128)S(1)}, f32[48,128]{1,0:T(8,128)S(1)}, u32[]{:S(2)}, u32[]{:S(2)}) collective-permute-start(f32[48,128]{1,0:T(8,128)S(1)} %product_last.1.refs_3_), channel_id=1, source_target_pairs={{0,8},{1,9},{2,10},{3,11},{4,12},{5,13},{6,14},{7,15},{8,0},{9,1},... | collective-permute-start | bytes 73736 | tf_op jit(solution)/shard_map/ppermute | solution.py:245
  17.5 0.4 %collective-permute-start.8 = (f32[48,128]{1,0:T(8,128)S(1)}, f32[48,128]{1,0:T(8,128)S(1)}, u32[]{:S(2)}, u32[]{:S(2)}) collective-permute-start(f32[48,128]{1,0:T(8,128)S(1)} %product_last.1.refs_3_), channel_id=1, source_target_pairs={{0,1},{1,0},{2,3},{3,2},{4,5},{5,4},{6,7},{7,6},{8,9},{9,8},{10,11... | collective-permute-start | bytes 73736 | tf_op jit(solution)/shard_map/ppermute | solution.py:245
  17.9 2.1 %collective-permute-done.6.refs_0_ = f32[48,128]{1,0:T(8,128)S(1)} collective-permute-done((f32[48,128]{1,0:T(8,128)S(1)}, f32[48,128]{1,0:T(8,128)S(1)}, u32[]{:S(2)}, u32[]{:S(2)}) %collective-permute-start.6) | collective-permute-done | bytes 24608 | tf_op jit(solution)/shard_map/ppermute | solution.py:245
  20.1 0.6 %collective-permute-done.7.refs_1_ = f32[48,128]{1,0:T(8,128)S(1)} collective-permute-done((f32[48,128]{1,0:T(8,128)S(1)}, f32[48,128]{1,0:T(8,128)S(1)}, u32[]{:S(2)}, u32[]{:S(2)}) %collective-permute-start.7) | collective-permute-done | bytes 24608 | tf_op jit(solution)/shard_map/ppermute | solution.py:245
  20.7 1.0 %collective-permute-start.10 = (f32[16,128]{1,0:T(8,128)S(1)}, f32[16,128]{1,0:T(8,128)S(1)}, u32[]{:S(2)}, u32[]{:S(2)}) collective-permute-start(f32[16,128]{1,0:T(8,128)S(1)} %get-tuple-element.19.refs_0_), channel_id=1, source_target_pairs={{0,2},{1,7},{2,0},{3,5},{4,6},{5,3},{6,4},{7,1},{8,10},{9,15},{10,... | collective-permute-start | bytes 24584 | tf_op jit(solution)/shard_map/ppermute | solution.py:245
  21.7 2.3 %collective-permute-start.9 = (f32[16,128]{1,0:T(8,128)S(1)}, f32[16,128]{1,0:T(8,128)S(1)}, u32[]{:S(2)}, u32[]{:S(2)}) collective-permute-start(f32[16,128]{1,0:T(8,128)S(1)} %get-tuple-element.19.refs_0_), channel_id=1, source_target_pairs={{0,4},{1,5},{2,6},{3,7},{4,0},{5,1},{6,2},{7,3},{8,12},{9,13},{10,... | collective-permute-start | bytes 24584 | tf_op jit(solution)/shard_map/ppermute | solution.py:245
  24.0 0.4 %collective-permute-done.10.refs_2_ = f32[16,128]{1,0:T(8,128)S(1)} collective-permute-done((f32[16,128]{1,0:T(8,128)S(1)}, f32[16,128]{1,0:T(8,128)S(1)}, u32[]{:S(2)}, u32[]{:S(2)}) %collective-permute-start.10) | collective-permute-done | bytes 8224 | tf_op jit(solution)/shard_map/ppermute | solution.py:245
  24.4 1.2 %collective-permute-done.9.refs_1_ = f32[16,128]{1,0:T(8,128)S(1)} collective-permute-done((f32[16,128]{1,0:T(8,128)S(1)}, f32[16,128]{1,0:T(8,128)S(1)}, u32[]{:S(2)}, u32[]{:S(2)}) %collective-permute-start.9) | collective-permute-done | bytes 8224 | tf_op jit(solution)/shard_map/ppermute | solution.py:245
  25.6 0.8 %update.1 = (f32[4,256]{1,0:T(4,128)}, f32[4,256]{1,0:T(4,128)}, f32[4,256]{1,0:T(4,128)}) custom-call(f32[16,128]{1,0:T(8,128)S(1)} %get-tuple-element.19.refs_0_, f32[16,128]{1,0:T(8,128)S(1)} %collective-permute-done.9.refs_1_, f32[16,128]{1,0:T(8,128)S(1)} %collective-permute-done.10.refs_2_, f32[16,128]{1,0:T(8,128)S(1)} %collective-permute-done.11.refs_3_, ...), custom_call_target="tpu_custom_call" | custom-call | tf_op jit(solution)/shard_map/update/pallas_call | solution.py:349
  (14 shorter events, 0.1 us)
Async XLA Ops:
  0.6 8.3 %collective-permute-start.2 = (bf16[256,128]{1,0:T(8,128)(2,1)}, bf16[256,128]{1,0:T(8,128)(2,1)S(1)}, u32[]{:S(2)}, u32[]{:S(2)}) collective-permute-start(bf16[256,128]{1,0:T(8,128)(2,1)} %points.1), channel_id=1, source_target_pairs={{0,8},{1,9},{2,10},{3,11},{4,12},{5,13},{6,14},{7,15},{8,0},{9,1},... | collective-permute-start | bytes 196616 | tf_op jit(solution)/shard_map/ppermute | solution.py:245
  5.8 5.5 %collective-permute-start.5 = (bf16[304,128]{1,0:T(8,128)(2,1)S(1)}, bf16[304,128]{1,0:T(8,128)(2,1)S(1)}, u32[]{:S(2)}, u32[]{:S(2)}) collective-permute-start(bf16[304,128]{1,0:T(8,128)(2,1)S(1)} %get-tuple-element.16), channel_id=1, source_target_pairs={{0,4},{1,5},{2,6},{3,7},{4,0},{5,1},{6,2},{7,3},{8,12},{9,13},{10,... | collective-permute-start | bytes 233480 | tf_op jit(solution)/shard_map/ppermute | solution.py:245
  7.5 5.4 %collective-permute-start.4 = (bf16[304,128]{1,0:T(8,128)(2,1)S(1)}, bf16[304,128]{1,0:T(8,128)(2,1)S(1)}, u32[]{:S(2)}, u32[]{:S(2)}) collective-permute-start(bf16[304,128]{1,0:T(8,128)(2,1)S(1)} %get-tuple-element.16), channel_id=1, source_target_pairs={{0,6},{1,7},{2,4},{3,5},{4,2},{5,3},{6,0},{7,1},{8,14},{9,15},{10,... | collective-permute-start | bytes 233480 | tf_op jit(solution)/shard_map/ppermute | solution.py:245
  8.9 1.3 %collective-permute-start.1 = (bf16[288,128]{1,0:T(8,128)(2,1)S(1)}, bf16[288,128]{1,0:T(8,128)(2,1)S(1)}, u32[]{:S(2)}, u32[]{:S(2)}) collective-permute-start(bf16[288,128]{1,0:T(8,128)(2,1)S(1)} %get-tuple-element.13), channel_id=1, source_target_pairs={{0,1},{1,0},{2,3},{3,2},{4,5},{5,4},{6,7},{7,6},{8,9},{9,8},{10,11... | collective-permute-start | bytes 221192 | tf_op jit(solution)/shard_map/ppermute | solution.py:245
  8.9 1.5 %collective-permute-start.3 = (bf16[288,128]{1,0:T(8,128)(2,1)S(1)}, bf16[288,128]{1,0:T(8,128)(2,1)S(1)}, u32[]{:S(2)}, u32[]{:S(2)}) collective-permute-start(bf16[288,128]{1,0:T(8,128)(2,1)S(1)} %stretch.1), channel_id=1, source_target_pairs={{0,1},{1,0},{2,3},{3,2},{4,5},{5,4},{6,7},{7,6},{8,9},{9,8},{10,11... | collective-permute-start | bytes 221192 | tf_op jit(solution)/shard_map/ppermute | solution.py:245
  9.5 4.8 %collective-permute-start = (bf16[272,128]{1,0:T(8,128)(2,1)S(1)}, bf16[272,128]{1,0:T(8,128)(2,1)S(1)}, u32[]{:S(2)}, u32[]{:S(2)}) collective-permute-start(bf16[272,128]{1,0:T(8,128)(2,1)S(1)} %get-tuple-element.12.col), channel_id=1, source_target_pairs={{0,2},{1,3},{2,0},{3,1},{4,6},{5,7},{6,4},{7,5},{8,10},{9,11},{10,... | collective-permute-start | bytes 208904 | tf_op jit(solution)/shard_map/ppermute | solution.py:245
  15.1 5.0 %collective-permute-start.6 = (f32[48,128]{1,0:T(8,128)S(1)}, f32[48,128]{1,0:T(8,128)S(1)}, u32[]{:S(2)}, u32[]{:S(2)}) collective-permute-start(f32[48,128]{1,0:T(8,128)S(1)} %product_last.1.refs_3_), channel_id=1, source_target_pairs={{0,9},{1,8},{2,11},{3,10},{4,13},{5,12},{6,15},{7,14},{8,1},{9,0},... | collective-permute-start | bytes 73736 | tf_op jit(solution)/shard_map/ppermute | solution.py:245
  15.2 5.5 %collective-permute-start.7 = (f32[48,128]{1,0:T(8,128)S(1)}, f32[48,128]{1,0:T(8,128)S(1)}, u32[]{:S(2)}, u32[]{:S(2)}) collective-permute-start(f32[48,128]{1,0:T(8,128)S(1)} %product_last.1.refs_3_), channel_id=1, source_target_pairs={{0,8},{1,9},{2,10},{3,11},{4,12},{5,13},{6,14},{7,15},{8,0},{9,1},... | collective-permute-start | bytes 73736 | tf_op jit(solution)/shard_map/ppermute | solution.py:245
  17.5 3.1 %collective-permute-start.8 = (f32[48,128]{1,0:T(8,128)S(1)}, f32[48,128]{1,0:T(8,128)S(1)}, u32[]{:S(2)}, u32[]{:S(2)}) collective-permute-start(f32[48,128]{1,0:T(8,128)S(1)} %product_last.1.refs_3_), channel_id=1, source_target_pairs={{0,1},{1,0},{2,3},{3,2},{4,5},{5,4},{6,7},{7,6},{8,9},{9,8},{10,11... | collective-permute-start | bytes 73736 | tf_op jit(solution)/shard_map/ppermute | solution.py:245
  20.6 5.0 %copy-start = (f32[4,256]{1,0:T(4,128)S(1)}, f32[4,256]{1,0:T(4,128)}, u32[]{:S(2)}) copy-start(f32[4,256]{1,0:T(4,128)} %refs_7_.1) | copy-start | bytes 12292
  20.6 5.0 %copy-start.1 = (f32[4,256]{1,0:T(4,128)S(1)}, f32[4,256]{1,0:T(4,128)}, u32[]{:S(2)}) copy-start(f32[4,256]{1,0:T(4,128)} %refs_6_.1) | copy-start | bytes 12292
  20.6 5.0 %copy-start.2 = (f32[4,256]{1,0:T(4,128)S(1)}, f32[4,256]{1,0:T(4,128)}, u32[]{:S(2)}) copy-start(f32[4,256]{1,0:T(4,128)} %refs_5_.1) | copy-start | bytes 12292
  20.7 3.7 %collective-permute-start.10 = (f32[16,128]{1,0:T(8,128)S(1)}, f32[16,128]{1,0:T(8,128)S(1)}, u32[]{:S(2)}, u32[]{:S(2)}) collective-permute-start(f32[16,128]{1,0:T(8,128)S(1)} %get-tuple-element.19.refs_0_), channel_id=1, source_target_pairs={{0,2},{1,7},{2,0},{3,5},{4,6},{5,3},{6,4},{7,1},{8,10},{9,15},{10,... | collective-permute-start | bytes 24584 | tf_op jit(solution)/shard_map/ppermute | solution.py:245
  21.7 3.9 %collective-permute-start.9 = (f32[16,128]{1,0:T(8,128)S(1)}, f32[16,128]{1,0:T(8,128)S(1)}, u32[]{:S(2)}, u32[]{:S(2)}) collective-permute-start(f32[16,128]{1,0:T(8,128)S(1)} %get-tuple-element.19.refs_0_), channel_id=1, source_target_pairs={{0,4},{1,5},{2,6},{3,7},{4,0},{5,1},{6,2},{7,3},{8,12},{9,13},{10,... | collective-permute-start | bytes 24584 | tf_op jit(solution)/shard_map/ppermute | solution.py:245
  24.4 1.2 %collective-permute-start.11 = (f32[16,128]{1,0:T(8,128)S(1)}, f32[16,128]{1,0:T(8,128)S(1)}, u32[]{:S(2)}, u32[]{:S(2)}) collective-permute-start(f32[16,128]{1,0:T(8,128)S(1)} %collective-permute-done.10.refs_2_), channel_id=1, source_target_pairs={{0,1},{1,0},{2,3},{3,2},{4,5},{5,4},{6,7},{7,6},{8,9},{9,8},{10,11... | collective-permute-start | bytes 24584 | tf_op jit(solution)/shard_map/ppermute | solution.py:245

commit v19 on v18

--- a/solution.py
+++ b/solution.py
@@ -52,8 +52,8 @@
     return (sums[0] + sums[1])[:1]
 
 
-def pack_kernel(points, direction, residual, length, noise, packed, own, rates, *refs):
-    *wider, step_in, rest_in, length_in, noise_in, sems = refs
+def pack_kernel(points, direction, residual, length, noise, packed, own, rates, *scratch):
+    step_in, rest_in, length_in, noise_in, sems = scratch
     size, dims = points.shape
     cands = direction.shape[0]
     lines = (packed.shape[0] - size) * dims // size
@@ -88,11 +88,6 @@
     top = [*pieces_of(sq), step, jnp.zeros((lines - 3 - cands, size), jnp.float32)]
     top = jnp.concatenate([t for t in top if t.shape[0]], axis=0)
     packed[size:, :] = fold(top, dims).astype(jnp.bfloat16)
-    filled = packed.shape[0]
-    for copy in wider:
-        copy[:filled, :] = packed[...]
-        spare = copy.shape[0] - filled
-        copy[filled:, :] = jnp.zeros((spare, dims), jnp.bfloat16)
 
 
 def lines_of(cands):
@@ -151,12 +146,6 @@
                 total[c] = total[c] + jnp.exp2(here * rate[c]) * weight
         for c in range(cands):
             out[places[c], :] = total[c]
-
-
-def stretch_kernel(block, out):
-    size = block.shape[0]
-    out[:size, :] = block[...]
-    out[size:, :] = jnp.zeros((out.shape[0] - size, out.shape[1]), out.dtype)
 
 
 def first_kernel(lo, col, *refs):
@@ -248,17 +237,15 @@
     hbm = pl.BlockSpec(memory_space=pltpu.HBM)
     params = pltpu.CompilerParams(vmem_limit_bytes=50 * 1024 * 1024)
 
-    packed, own, rates, wider, widest = pl.pallas_call(
+    packed, own, rates = pl.pallas_call(
         pack_kernel,
         out_shape=(
             jax.ShapeDtypeStruct((filled, dims), jnp.bfloat16),
             jax.ShapeDtypeStruct((3 * tall, dims), jnp.float32),
             jax.ShapeDtypeStruct((8 * cands, dims), jnp.float32),
-            jax.ShapeDtypeStruct((filled + 16, dims), jnp.bfloat16),
-            jax.ShapeDtypeStruct((filled + 32, dims), jnp.bfloat16),
         ),
         in_specs=[hbm] * 5,
-        out_specs=(vmem,) * 5,
+        out_specs=(vmem,) * 3,
         scratch_shapes=[
             pltpu.VMEM((cands, size), jnp.float32),
             pltpu.VMEM((cands, size), jnp.float32),
@@ -275,21 +262,9 @@
         )
     )
 
-    rows = [packed, meet(wider, 1)]
-    for mask in row_masks[2::2]:
-        block = meet(points, mask)
-        stretched = pl.pallas_call(
-            stretch_kernel,
-            out_shape=jax.ShapeDtypeStruct(wider.shape, wider.dtype),
-            in_specs=[vmem],
-            out_specs=vmem,
-            compiler_params=params,
-            name="stretch",
-        )(block)
-        rows += [block, meet(stretched, 1)]
-
-    def column(k):
-        return meet(packed if k < hi // 2 else widest, col_masks[k])
+    rows = [points]
+    for mask in row_masks[1:]:
+        rows.append(meet(rows[-1], 1) if mask % 2 else meet(points, mask))
 
     spare = [
         pltpu.VMEM((cands, size, dims), jnp.float32),
@@ -315,7 +290,7 @@
             scratch_shapes=spare,
             compiler_params=params,
             name="product_%d" % k,
-        )(column(k), row_wide, rates, total)
+        )(meet(packed, col_masks[k]), row_wide, rates, total)
     partial = pl.pallas_call(
         functools.partial(last_kernel, lo),
         out_shape=jax.ShapeDtypeStruct(((lo + 2) * tall, dims), jnp.float32),
@@ -324,7 +299,7 @@
         scratch_shapes=[*spare, pltpu.VMEM(spread.shape, jnp.float32)],
         compiler_params=params,
         name="product_last",
-    )(column(order[-1]), row_wide, rates, total, own)
+    )(meet(packed, col_masks[order[-1]]), row_wide, rates, total, own)
 
     image, sums = pl.pallas_call(
         functools.partial(sums_kernel, cands),

time: 26.6 us -> 26.1 us (0.981)
  waiting for transfers between devices: 6.02 us -> 5.1 us
  starting transfers between devices: 14.4 us -> 14.9 us
    ppermute x12, waiting for transfers between devices: 6.02 us -> 5.1 us  [meet(): lax.ppermute(x, 'blk', [(d, d ^ masks[d % 2]) for d in range(devices)])]
    ppermute x12, starting transfers between devices: 14.4 us -> 14.9 us  [meet(): lax.ppermute(x, 'blk', [(d, d ^ masks[d % 2]) for d in range(devices)])]
  transfers between devices with their start and end apart: 12 -> 12, of which waited for: 8 -> 6; matrix products, arithmetic and copies ran while one was open for 0% -> 0% of each run, Pallas kernels for 14% -> 14%
where the time goes in v19:
time: 26.1 us; the launch traced here: 25.9 us
  starting transfers between devices  14.9 us (57%)
  Pallas kernels  5.23 us (20%)
  waiting for transfers between devices  5.1 us (20%)
  between operations  0.73 us (3%)
    ppermute x12, starting transfers between devices, meet(): lax.ppermute(x, 'blk', [(d, d ^ masks[d % 2]) for d in range(devices)])  14.9 us
    ppermute x12, waiting for transfers between devices, meet(): lax.ppermute(x, 'blk', [(d, d ^ masks[d % 2]) for d in range(devices)])  5.1 us
    pallas_call x2, Pallas kernels, per_device(): pl.pallas_call(functools.partial(next_kernel, lo), out_shape=spread, in_s...  1.59 us
    pallas_call x1, Pallas kernels, per_device(): pl.pallas_call(pack_kernel, out_shape=(jax.ShapeDtypeStruct((filled, dims...  1.08 us
    pallas_call x1, Pallas kernels, per_device(): pl.pallas_call(functools.partial(first_kernel, lo), out_shape=(spread, ja...  0.95 us
    pallas_call x1, Pallas kernels, per_device(): pl.pallas_call(functools.partial(last_kernel, lo), out_shape=jax.ShapeDty...  0.81 us
    pallas_call x1, Pallas kernels, per_device(): pl.pallas_call(update_kernel, out_shape=(jax.ShapeDtypeStruct((cands, siz...  0.78 us
  transfers between devices with their start and end apart: 12, of which 6 were waited for; matrix products, arithmetic and copies ran while one was open for 0% of the time, Pallas kernels for 14%

profile of v19, /device:TPU:0, one launch (start us, length us, event | category | flops | bytes accessed | tf_op | source)
XLA Modules:
  0.0 25.9 jit_solution(17321008812144906630)
XLA Ops:
  0.6 4.1 %collective-permute-start.2 = (bf16[256,128]{1,0:T(8,128)(2,1)}, bf16[256,128]{1,0:T(8,128)(2,1)S(1)}, u32[]{:S(2)}, u32[]{:S(2)}) collective-permute-start(bf16[256,128]{1,0:T(8,128)(2,1)} %points.1), channel_id=1, source_target_pairs={{0,8},{1,9},{2,10},{3,11},{4,12},{5,13},{6,14},{7,15},{8,0},{9,1},... | collective-permute-start | bytes 196616 | tf_op jit(solution)/shard_map/ppermute | solution.py:234
  4.7 1.1 %pack.1 = (bf16[272,128]{1,0:T(8,128)(2,1)S(1)}, f32[24,128]{1,0:T(8,128)S(1)}, f32[32,128]{1,0:T(8,128)S(1)}) custom-call(bf16[256,128]{1,0:T(8,128)(2,1)} %points.1, f32[4,256]{1,0:T(4,128)} %refs_7_.1, f32[4,256]{1,0:T(4,128)} %refs_6_.1, f32[4]{0:T(128)} %length.1, f32[4]{0:T(128)} %noise.1), custom_call_target="tpu_custom_call" | custom-call | tf_op jit(solution)/shard_map/pack/pallas_call | solution.py:240
  5.8 1.6 %collective-permute-start.5 = (bf16[272,128]{1,0:T(8,128)(2,1)S(1)}, bf16[272,128]{1,0:T(8,128)(2,1)S(1)}, u32[]{:S(2)}, u32[]{:S(2)}) collective-permute-start(bf16[272,128]{1,0:T(8,128)(2,1)S(1)} %get-tuple-element.10.col), channel_id=1, source_target_pairs={{0,4},{1,5},{2,6},{3,7},{4,0},{5,1},{6,2},{7,3},{8,12},{9,13},{10,... | collective-permute-start | bytes 208904 | tf_op jit(solution)/shard_map/ppermute | solution.py:234
  7.5 1.4 %collective-permute-start.4 = (bf16[272,128]{1,0:T(8,128)(2,1)S(1)}, bf16[272,128]{1,0:T(8,128)(2,1)S(1)}, u32[]{:S(2)}, u32[]{:S(2)}) collective-permute-start(bf16[272,128]{1,0:T(8,128)(2,1)S(1)} %get-tuple-element.10.col), channel_id=1, source_target_pairs={{0,6},{1,7},{2,4},{3,5},{4,2},{5,3},{6,0},{7,1},{8,14},{9,15},{10,... | collective-permute-start | bytes 208904 | tf_op jit(solution)/shard_map/ppermute | solution.py:234
  8.9 0.5 %collective-permute-start = (bf16[272,128]{1,0:T(8,128)(2,1)S(1)}, bf16[272,128]{1,0:T(8,128)(2,1)S(1)}, u32[]{:S(2)}, u32[]{:S(2)}) collective-permute-start(bf16[272,128]{1,0:T(8,128)(2,1)S(1)} %get-tuple-element.10.col), channel_id=1, source_target_pairs={{0,2},{1,3},{2,0},{3,1},{4,6},{5,7},{6,4},{7,5},{8,10},{9,11},{10,... | collective-permute-start | bytes 208904 | tf_op jit(solution)/shard_map/ppermute | solution.py:234
  9.4 0.5 %collective-permute-start.3 = (bf16[256,128]{1,0:T(8,128)(2,1)S(1)}, bf16[256,128]{1,0:T(8,128)(2,1)S(1)}, u32[]{:S(2)}, u32[]{:S(2)}) collective-permute-start(bf16[256,128]{1,0:T(8,128)(2,1)S(1)} %collective-permute-done.2.refs_1_), channel_id=1, source_target_pairs={{0,1},{1,0},{2,3},{3,2},{4,5},{5,4},{6,7},{7,6},{8,9},{9,8},{10,11... | collective-permute-start | bytes 196616 | tf_op jit(solution)/shard_map/ppermute | solution.py:234
  9.9 0.7 %collective-permute-done.1.refs_0_ = bf16[256,128]{1,0:T(8,128)(2,1)S(1)} collective-permute-done((bf16[256,128]{1,0:T(8,128)(2,1)S(1)}, bf16[256,128]{1,0:T(8,128)(2,1)S(1)}, u32[]{:S(2)}, u32[]{:S(2)}) %collective-permute-start.1) | collective-permute-done | bytes 65568 | tf_op jit(solution)/shard_map/ppermute | solution.py:234
  10.6 0.2 collective-permute-done.3.refs_2_
  10.8 0.9 %product_0.1 = (f32[128,256]{1,0:T(8,128)S(1)}, bf16[1024,256]{1,0:T(8,128)(2,1)S(1)}) custom-call(bf16[272,128]{1,0:T(8,128)(2,1)S(1)} %get-tuple-element.10.col, bf16[256,128]{1,0:T(8,128)(2,1)S(1)} %collective-permute-done.1.refs_0_, bf16[256,128]{1,0:T(8,128)(2,1)S(1)} %collective-permute-done.2.refs_1_, ...), custom_call_target="tpu_custom_call" | custom-call | tf_op jit(solution)/shard_map/product_0/pallas_call | solution.py:274
  11.8 0.8 %product_2.1.before = f32[128,256]{1,0:T(8,128)S(1)} custom-call(bf16[272,128]{1,0:T(8,128)(2,1)S(1)} %collective-permute-done.5.col, bf16[1024,256]{1,0:T(8,128)(2,1)S(1)} %get-tuple-element.12.row_wide, f32[32,128]{1,0:T(8,128)S(1)} %get-tuple-element.11.refs_3_.rates, f32[128,256]{1,0:T(8,128)S(1)} %get-tuple-element.13.before), custom_call_target="tpu_custom_call" | custom-call | tf_op jit(solution)/shard_map/product_2/pallas_call | solution.py:285
  12.6 0.1 collective-permute-done.4.col
  12.7 0.8 %product_3.1.before = f32[128,256]{1,0:T(8,128)S(1)} custom-call(bf16[272,128]{1,0:T(8,128)(2,1)S(1)} %collective-permute-done.4.col, bf16[1024,256]{1,0:T(8,128)(2,1)S(1)} %get-tuple-element.12.row_wide, f32[32,128]{1,0:T(8,128)S(1)} %get-tuple-element.11.refs_3_.rates, f32[128,256]{1,0:T(8,128)S(1)} %product_2.1.before), custom_call_target="tpu_custom_call" | custom-call | tf_op jit(solution)/shard_map/product_3/pallas_call | solution.py:285
  13.5 0.0 collective-permute-done.col
  13.5 0.8 %product_last.1.refs_3_ = f32[48,128]{1,0:T(8,128)S(1)} custom-call(bf16[272,128]{1,0:T(8,128)(2,1)S(1)} %collective-permute-done.col, bf16[1024,256]{1,0:T(8,128)(2,1)S(1)} %get-tuple-element.12.row_wide, f32[32,128]{1,0:T(8,128)S(1)} %get-tuple-element.11.refs_3_.rates, f32[128,256]{1,0:T(8,128)S(1)} %product_3.1.before, f32[24,128]{1,0:T(8,128)S(1)} %get-tuple-element.14.own), custom_call_target="tpu_custom_call" | custom-call | tf_op jit(solution)/shard_map/product_last/pallas_call | solution.py:294
  14.3 0.3 %collective-permute-start.6 = (f32[48,128]{1,0:T(8,128)S(1)}, f32[48,128]{1,0:T(8,128)S(1)}, u32[]{:S(2)}, u32[]{:S(2)}) collective-permute-start(f32[48,128]{1,0:T(8,128)S(1)} %product_last.1.refs_3_), channel_id=1, source_target_pairs={{0,9},{1,8},{2,11},{3,10},{4,13},{5,12},{6,15},{7,14},{8,1},{9,0},... | collective-permute-start | bytes 73736 | tf_op jit(solution)/shard_map/ppermute | solution.py:234
  14.6 2.6 %collective-permute-start.7 = (f32[48,128]{1,0:T(8,128)S(1)}, f32[48,128]{1,0:T(8,128)S(1)}, u32[]{:S(2)}, u32[]{:S(2)}) collective-permute-start(f32[48,128]{1,0:T(8,128)S(1)} %product_last.1.refs_3_), channel_id=1, source_target_pairs={{0,8},{1,9},{2,10},{3,11},{4,12},{5,13},{6,14},{7,15},{8,0},{9,1},... | collective-permute-start | bytes 73736 | tf_op jit(solution)/shard_map/ppermute | solution.py:234
  17.2 0.0 collective-permute-start.8
  17.2 1.4 %collective-permute-done.6.refs_0_ = f32[48,128]{1,0:T(8,128)S(1)} collective-permute-done((f32[48,128]{1,0:T(8,128)S(1)}, f32[48,128]{1,0:T(8,128)S(1)}, u32[]{:S(2)}, u32[]{:S(2)}) %collective-permute-start.6) | collective-permute-done | bytes 24608 | tf_op jit(solution)/shard_map/ppermute | solution.py:234
  18.6 1.1 %collective-permute-done.7.refs_1_ = f32[48,128]{1,0:T(8,128)S(1)} collective-permute-done((f32[48,128]{1,0:T(8,128)S(1)}, f32[48,128]{1,0:T(8,128)S(1)}, u32[]{:S(2)}, u32[]{:S(2)}) %collective-permute-start.7) | collective-permute-done | bytes 24608 | tf_op jit(solution)/shard_map/ppermute | solution.py:234
  19.6 0.0 collective-permute-done.8.refs_2_
  19.7 1.7 %collective-permute-start.10 = (f32[16,128]{1,0:T(8,128)S(1)}, f32[16,128]{1,0:T(8,128)S(1)}, u32[]{:S(2)}, u32[]{:S(2)}) collective-permute-start(f32[16,128]{1,0:T(8,128)S(1)} %get-tuple-element.15.refs_0_), channel_id=1, source_target_pairs={{0,2},{1,7},{2,0},{3,5},{4,6},{5,3},{6,4},{7,1},{8,10},{9,15},{10,... | collective-permute-start | bytes 24584 | tf_op jit(solution)/shard_map/ppermute | solution.py:234
  21.3 2.2 %collective-permute-start.9 = (f32[16,128]{1,0:T(8,128)S(1)}, f32[16,128]{1,0:T(8,128)S(1)}, u32[]{:S(2)}, u32[]{:S(2)}) collective-permute-start(f32[16,128]{1,0:T(8,128)S(1)} %get-tuple-element.15.refs_0_), channel_id=1, source_target_pairs={{0,4},{1,5},{2,6},{3,7},{4,0},{5,1},{6,2},{7,3},{8,12},{9,13},{10,... | collective-permute-start | bytes 24584 | tf_op jit(solution)/shard_map/ppermute | solution.py:234
  23.5 1.6 %collective-permute-done.9.refs_1_ = f32[16,128]{1,0:T(8,128)S(1)} collective-permute-done((f32[16,128]{1,0:T(8,128)S(1)}, f32[16,128]{1,0:T(8,128)S(1)}, u32[]{:S(2)}, u32[]{:S(2)}) %collective-permute-start.9) | collective-permute-done | bytes 8224 | tf_op jit(solution)/shard_map/ppermute | solution.py:234
  25.2 0.8 %update.1 = (f32[4,256]{1,0:T(4,128)}, f32[4,256]{1,0:T(4,128)}, f32[4,256]{1,0:T(4,128)}) custom-call(f32[16,128]{1,0:T(8,128)S(1)} %get-tuple-element.15.refs_0_, f32[16,128]{1,0:T(8,128)S(1)} %collective-permute-done.9.refs_1_, f32[16,128]{1,0:T(8,128)S(1)} %collective-permute-done.10.refs_2_, f32[16,128]{1,0:T(8,128)S(1)} %collective-permute-done.11.refs_3_, ...), custom_call_target="tpu_custom_call" | custom-call | tf_op jit(solution)/shard_map/update/pallas_call | solution.py:324
  (15 shorter events, 0.0 us)
Async XLA Ops:
  0.6 8.8 %copy-start.3 = (bf16[256,128]{1,0:T(8,128)(2,1)S(1)}, bf16[256,128]{1,0:T(8,128)(2,1)}, u32[]{:S(2)}) copy-start(bf16[256,128]{1,0:T(8,128)(2,1)} %points.1) | copy-start | bytes 196612
  0.6 8.8 %collective-permute-start.2 = (bf16[256,128]{1,0:T(8,128)(2,1)}, bf16[256,128]{1,0:T(8,128)(2,1)S(1)}, u32[]{:S(2)}, u32[]{:S(2)}) collective-permute-start(bf16[256,128]{1,0:T(8,128)(2,1)} %points.1), channel_id=1, source_target_pairs={{0,8},{1,9},{2,10},{3,11},{4,12},{5,13},{6,14},{7,15},{8,0},{9,1},... | collective-permute-start | bytes 196616 | tf_op jit(solution)/shard_map/ppermute | solution.py:234
  5.8 5.9 %collective-permute-start.5 = (bf16[272,128]{1,0:T(8,128)(2,1)S(1)}, bf16[272,128]{1,0:T(8,128)(2,1)S(1)}, u32[]{:S(2)}, u32[]{:S(2)}) collective-permute-start(bf16[272,128]{1,0:T(8,128)(2,1)S(1)} %get-tuple-element.10.col), channel_id=1, source_target_pairs={{0,4},{1,5},{2,6},{3,7},{4,0},{5,1},{6,2},{7,3},{8,12},{9,13},{10,... | collective-permute-start | bytes 208904 | tf_op jit(solution)/shard_map/ppermute | solution.py:234
  7.5 5.2 %collective-permute-start.4 = (bf16[272,128]{1,0:T(8,128)(2,1)S(1)}, bf16[272,128]{1,0:T(8,128)(2,1)S(1)}, u32[]{:S(2)}, u32[]{:S(2)}) collective-permute-start(bf16[272,128]{1,0:T(8,128)(2,1)S(1)} %get-tuple-element.10.col), channel_id=1, source_target_pairs={{0,6},{1,7},{2,4},{3,5},{4,2},{5,3},{6,0},{7,1},{8,14},{9,15},{10,... | collective-permute-start | bytes 208904 | tf_op jit(solution)/shard_map/ppermute | solution.py:234
  8.9 4.6 %collective-permute-start = (bf16[272,128]{1,0:T(8,128)(2,1)S(1)}, bf16[272,128]{1,0:T(8,128)(2,1)S(1)}, u32[]{:S(2)}, u32[]{:S(2)}) collective-permute-start(bf16[272,128]{1,0:T(8,128)(2,1)S(1)} %get-tuple-element.10.col), channel_id=1, source_target_pairs={{0,2},{1,3},{2,0},{3,1},{4,6},{5,7},{6,4},{7,5},{8,10},{9,11},{10,... | collective-permute-start | bytes 208904 | tf_op jit(solution)/shard_map/ppermute | solution.py:234
  9.4 1.3 %collective-permute-start.1 = (bf16[256,128]{1,0:T(8,128)(2,1)S(1)}, bf16[256,128]{1,0:T(8,128)(2,1)S(1)}, u32[]{:S(2)}, u32[]{:S(2)}) collective-permute-start(bf16[256,128]{1,0:T(8,128)(2,1)S(1)} %copy-done.3), channel_id=1, source_target_pairs={{0,1},{1,0},{2,3},{3,2},{4,5},{5,4},{6,7},{7,6},{8,9},{9,8},{10,11... | collective-permute-start | bytes 196616 | tf_op jit(solution)/shard_map/ppermute | solution.py:234
  9.4 1.4 %collective-permute-start.3 = (bf16[256,128]{1,0:T(8,128)(2,1)S(1)}, bf16[256,128]{1,0:T(8,128)(2,1)S(1)}, u32[]{:S(2)}, u32[]{:S(2)}) collective-permute-start(bf16[256,128]{1,0:T(8,128)(2,1)S(1)} %collective-permute-done.2.refs_1_), channel_id=1, source_target_pairs={{0,1},{1,0},{2,3},{3,2},{4,5},{5,4},{6,7},{7,6},{8,9},{9,8},{10,11... | collective-permute-start | bytes 196616 | tf_op jit(solution)/shard_map/ppermute | solution.py:234
  14.3 4.2 %collective-permute-start.6 = (f32[48,128]{1,0:T(8,128)S(1)}, f32[48,128]{1,0:T(8,128)S(1)}, u32[]{:S(2)}, u32[]{:S(2)}) collective-permute-start(f32[48,128]{1,0:T(8,128)S(1)} %product_last.1.refs_3_), channel_id=1, source_target_pairs={{0,9},{1,8},{2,11},{3,10},{4,13},{5,12},{6,15},{7,14},{8,1},{9,0},... | collective-permute-start | bytes 73736 | tf_op jit(solution)/shard_map/ppermute | solution.py:234
  14.6 5.0 %collective-permute-start.7 = (f32[48,128]{1,0:T(8,128)S(1)}, f32[48,128]{1,0:T(8,128)S(1)}, u32[]{:S(2)}, u32[]{:S(2)}) collective-permute-start(f32[48,128]{1,0:T(8,128)S(1)} %product_last.1.refs_3_), channel_id=1, source_target_pairs={{0,8},{1,9},{2,10},{3,11},{4,12},{5,13},{6,14},{7,15},{8,0},{9,1},... | collective-permute-start | bytes 73736 | tf_op jit(solution)/shard_map/ppermute | solution.py:234
  17.2 2.4 %collective-permute-start.8 = (f32[48,128]{1,0:T(8,128)S(1)}, f32[48,128]{1,0:T(8,128)S(1)}, u32[]{:S(2)}, u32[]{:S(2)}) collective-permute-start(f32[48,128]{1,0:T(8,128)S(1)} %product_last.1.refs_3_), channel_id=1, source_target_pairs={{0,1},{1,0},{2,3},{3,2},{4,5},{5,4},{6,7},{7,6},{8,9},{9,8},{10,11... | collective-permute-start | bytes 73736 | tf_op jit(solution)/shard_map/ppermute | solution.py:234
  19.6 5.5 %copy-start = (f32[4,256]{1,0:T(4,128)S(1)}, f32[4,256]{1,0:T(4,128)}, u32[]{:S(2)}) copy-start(f32[4,256]{1,0:T(4,128)} %refs_7_.1) | copy-start | bytes 12292
  19.6 5.5 %copy-start.1 = (f32[4,256]{1,0:T(4,128)S(1)}, f32[4,256]{1,0:T(4,128)}, u32[]{:S(2)}) copy-start(f32[4,256]{1,0:T(4,128)} %refs_6_.1) | copy-start | bytes 12292
  19.6 5.5 %copy-start.2 = (f32[4,256]{1,0:T(4,128)S(1)}, f32[4,256]{1,0:T(4,128)}, u32[]{:S(2)}) copy-start(f32[4,256]{1,0:T(4,128)} %refs_5_.1) | copy-start | bytes 12292
  19.7 3.9 %collective-permute-start.10 = (f32[16,128]{1,0:T(8,128)S(1)}, f32[16,128]{1,0:T(8,128)S(1)}, u32[]{:S(2)}, u32[]{:S(2)}) collective-permute-start(f32[16,128]{1,0:T(8,128)S(1)} %get-tuple-element.15.refs_0_), channel_id=1, source_target_pairs={{0,2},{1,7},{2,0},{3,5},{4,6},{5,3},{6,4},{7,1},{8,10},{9,15},{10,... | collective-permute-start | bytes 24584 | tf_op jit(solution)/shard_map/ppermute | solution.py:234
  21.3 3.8 %collective-permute-start.9 = (f32[16,128]{1,0:T(8,128)S(1)}, f32[16,128]{1,0:T(8,128)S(1)}, u32[]{:S(2)}, u32[]{:S(2)}) collective-permute-start(f32[16,128]{1,0:T(8,128)S(1)} %get-tuple-element.15.refs_0_), channel_id=1, source_target_pairs={{0,4},{1,5},{2,6},{3,7},{4,0},{5,1},{6,2},{7,3},{8,12},{9,13},{10,... | collective-permute-start | bytes 24584 | tf_op jit(solution)/shard_map/ppermute | solution.py:234
  23.5 1.6 %collective-permute-start.11 = (f32[16,128]{1,0:T(8,128)S(1)}, f32[16,128]{1,0:T(8,128)S(1)}, u32[]{:S(2)}, u32[]{:S(2)}) collective-permute-start(f32[16,128]{1,0:T(8,128)S(1)} %collective-permute-done.10.refs_2_), channel_id=1, source_target_pairs={{0,1},{1,0},{2,3},{3,2},{4,5},{5,4},{6,7},{7,6},{8,9},{9,8},{10,11... | collective-permute-start | bytes 24584 | tf_op jit(solution)/shard_map/ppermute | solution.py:234

commit v20 on v19

--- a/solution.py
+++ b/solution.py
@@ -106,11 +106,12 @@
     )
 
 
-def add_column(col, row_wide, rates, weights, dist, before, out, lo):
+def add_column(col, row_wide, rates, weights, dist, before, out, lo, ks=None):
     dims = col.shape[1]
     cands = rates.shape[0] // 8
-    size = row_wide.shape[0] // lo
+    size = dist.shape[1]
     wide = size // dims
+    ks = list(range(lo)) if ks is None else ks
     lines = lines_of(cands)
     top = unfold(col[size : size + lines * wide, :].astype(jnp.float32), lines)
     ones = lax.broadcasted_iota(jnp.int32, (8, size), 0) < 3
@@ -128,15 +129,15 @@
             preferred_element_type=jnp.float32,
         )
 
-    distances(0)
+    distances(ks[0])
     for c in range(cands):
         weights[c] = jnp.broadcast_to(steps[:, 3 + c : 4 + c], (size, dims))
     rate = [
         jnp.concatenate([rates[pl.ds(8 * c, 8), :]] * wide, axis=1) for c in range(cands)
     ]
-    for k in range(lo):
-        if k + 1 < lo:
-            distances(k + 1)
+    for i, k in enumerate(ks):
+        if i + 1 < len(ks):
+            distances(ks[i + 1])
         places = [pl.ds((k * cands + c) * 8, 8) for c in range(cands)]
         total = [0.0 if before is None else before[at, :] for at in places]
         for j in range(0, size, 8):
@@ -149,14 +150,30 @@
 
 
 def first_kernel(lo, col, *refs):
-    rows, refs = refs[: lo - 1], refs[lo - 1 :]
-    rates, out, row_wide, weights, dist = refs
-    size = row_wide.shape[0] // lo
-    for k, block in enumerate((col, *rows)):
-        row_wide[pl.ds(k * size, size), :] = widen_row(
-            block[:size, :], lines_of(rates.shape[0] // 8)
-        )
-    add_column(col, row_wide, rates, weights, dist, None, out, lo)
+    *rows, rates, out, row_wide, weights, dist = refs
+    size = dist.shape[1]
+    for i, block in enumerate(rows):
+        row_wide[pl.ds(2 * i * size, size), :] = widen_row(
+            block[...], lines_of(rates.shape[0] // 8)
+        )
+    ks = range(0, lo, 2)
+    add_column(col, row_wide, rates, weights, dist, None, out, lo, list(ks))
+
+
+def second_kernel(lo, col, *refs):
+    *rows, rates, half, half_wide, out, row_wide, weights, dist = refs
+    size = dist.shape[1]
+    tall = out.shape[0] // lo
+    for i, block in enumerate(rows):
+        row_wide[pl.ds((2 * i + 1) * size, size), :] = widen_row(
+            block[...], lines_of(rates.shape[0] // 8)
+        )
+        at = pl.ds(2 * i * size, size)
+        row_wide[at, :] = half_wide[at, :]
+        at = pl.ds(2 * i * tall, tall)
+        out[at, :] = half[at, :]
+    ks = range(1, lo, 2)
+    add_column(col, row_wide, rates, weights, dist, None, out, lo, list(ks))
 
 
 def next_kernel(lo, col, row_wide, rates, before, out, weights, dist):
@@ -271,15 +288,25 @@
         pltpu.VMEM((lo, size, size), jnp.float32),
     ]
     spread = jax.ShapeDtypeStruct((lo * cands * 8, size), jnp.float32)
-    total, row_wide = pl.pallas_call(
+    wide_shape = jax.ShapeDtypeStruct((lo * size, 2 * dims), jnp.bfloat16)
+    half, half_wide = pl.pallas_call(
         functools.partial(first_kernel, lo),
-        out_shape=(spread, jax.ShapeDtypeStruct((lo * size, 2 * dims), jnp.bfloat16)),
-        in_specs=[vmem] * (lo + 1),
+        out_shape=(spread, wide_shape),
+        in_specs=[vmem] * (lo // 2 + 2),
         out_specs=(vmem, vmem),
         scratch_shapes=spare,
         compiler_params=params,
-        name="product_0",
-    )(packed, *rows[1:], rates)
+        name="product_own",
+    )(packed, *rows[::2], rates)
+    total, row_wide = pl.pallas_call(
+        functools.partial(second_kernel, lo),
+        out_shape=(spread, wide_shape),
+        in_specs=[vmem] * (lo // 2 + 4),
+        out_specs=(vmem, vmem),
+        scratch_shapes=spare,
+        compiler_params=params,
+        name="product_core",
+    )(packed, *rows[1::2], rates, half, half_wide)
     order = [hi // 2, *range(hi - 1, hi // 2, -1), *range(hi // 2 - 1, 0, -1)]
     for k in order[:-1]:
         total = pl.pallas_call(

time: 26.1 us -> 26.2 us (level)
  starting transfers between devices: 14.9 us -> 14.2 us
  waiting for transfers between devices: 5.1 us -> 5.57 us
    ppermute x12, starting transfers between devices: 14.9 us -> 14.2 us  [meet(): lax.ppermute(x, 'blk', [(d, d ^ masks[d % 2]) for d in range(devices)])]
    ppermute x12, waiting for transfers between devices: 5.1 us -> 5.57 us  [meet(): lax.ppermute(x, 'blk', [(d, d ^ masks[d % 2]) for d in range(devices)])]
    pallas_call x1 -> x2, Pallas kernels: 0.95 us -> 1.17 us  [the longest x1 0.59 us: per_device(): pl.pallas_call(functools.partial(second_kernel, lo), out_shape=(spread, w...]
  transfers between devices with their start and end apart: 12 -> 12, of which waited for: 6 -> 7; matrix products, arithmetic and copies ran while one was open for 0% -> 0% of each run, Pallas kernels for 14% -> 15%
where the time goes in v20:
time: 26.2 us; the launch traced here: 26 us
  starting transfers between devices  14.2 us (54%)
  waiting for transfers between devices  5.57 us (21%)
  Pallas kernels  5.45 us (21%)
  between operations  0.74 us (3%)
    ppermute x12, starting transfers between devices, meet(): lax.ppermute(x, 'blk', [(d, d ^ masks[d % 2]) for d in range(devices)])  14.2 us
    ppermute x12, waiting for transfers between devices, meet(): lax.ppermute(x, 'blk', [(d, d ^ masks[d % 2]) for d in range(devices)])  5.57 us
    pallas_call x2, Pallas kernels, per_device(): pl.pallas_call(functools.partial(next_kernel, lo), out_shape=spread, in_s...  1.58 us
    pallas_call x1, Pallas kernels, per_device(): pl.pallas_call(pack_kernel, out_shape=(jax.ShapeDtypeStruct((filled, dims...  1.08 us
    pallas_call x1, Pallas kernels, per_device(): pl.pallas_call(functools.partial(last_kernel, lo), out_shape=jax.ShapeDty...  0.81 us
    pallas_call x1, Pallas kernels, per_device(): pl.pallas_call(update_kernel, out_shape=(jax.ShapeDtypeStruct((cands, siz...  0.78 us
    pallas_call x1, Pallas kernels, per_device(): pl.pallas_call(functools.partial(second_kernel, lo), out_shape=(spread, w...  0.59 us
    pallas_call x1, Pallas kernels, per_device(): pl.pallas_call(functools.partial(first_kernel, lo), out_shape=(spread, wi...  0.59 us
  transfers between devices with their start and end apart: 12, of which 7 were waited for; matrix products, arithmetic and copies ran while one was open for 0% of the time, Pallas kernels for 15%

profile of v20, /device:TPU:0, one launch (start us, length us, event | category | flops | bytes accessed | tf_op | source)
XLA Modules:
  0.0 26.0 jit_solution(7535614291128308744)
XLA Ops:
  0.6 4.1 %collective-permute-start.2 = (bf16[256,128]{1,0:T(8,128)(2,1)}, bf16[256,128]{1,0:T(8,128)(2,1)S(1)}, u32[]{:S(2)}, u32[]{:S(2)}) collective-permute-start(bf16[256,128]{1,0:T(8,128)(2,1)} %refs_0_.1), channel_id=1, source_target_pairs={{0,8},{1,9},{2,10},{3,11},{4,12},{5,13},{6,14},{7,15},{8,0},{9,1},... | collective-permute-start | bytes 196616 | tf_op jit(solution)/shard_map/ppermute | solution.py:251
  4.7 1.1 %pack.1 = (bf16[272,128]{1,0:T(8,128)(2,1)S(1)}, f32[24,128]{1,0:T(8,128)S(1)}, f32[32,128]{1,0:T(8,128)S(1)}) custom-call(bf16[256,128]{1,0:T(8,128)(2,1)} %refs_0_.1, f32[4,256]{1,0:T(4,128)} %refs_7_.1, f32[4,256]{1,0:T(4,128)} %refs_6_.1, f32[4]{0:T(128)} %length.1, f32[4]{0:T(128)} %noise.1), custom_call_target="tpu_custom_call" | custom-call | tf_op jit(solution)/shard_map/pack/pallas_call | solution.py:257
  5.8 1.6 %collective-permute-start.5 = (bf16[272,128]{1,0:T(8,128)(2,1)S(1)}, bf16[272,128]{1,0:T(8,128)(2,1)S(1)}, u32[]{:S(2)}, u32[]{:S(2)}) collective-permute-start(bf16[272,128]{1,0:T(8,128)(2,1)S(1)} %get-tuple-element.12.col), channel_id=1, source_target_pairs={{0,4},{1,5},{2,6},{3,7},{4,0},{5,1},{6,2},{7,3},{8,12},{9,13},{10,... | collective-permute-start | bytes 208904 | tf_op jit(solution)/shard_map/ppermute | solution.py:251
  7.5 1.4 %collective-permute-start.4 = (bf16[272,128]{1,0:T(8,128)(2,1)S(1)}, bf16[272,128]{1,0:T(8,128)(2,1)S(1)}, u32[]{:S(2)}, u32[]{:S(2)}) collective-permute-start(bf16[272,128]{1,0:T(8,128)(2,1)S(1)} %get-tuple-element.12.col), channel_id=1, source_target_pairs={{0,6},{1,7},{2,4},{3,5},{4,2},{5,3},{6,0},{7,1},{8,14},{9,15},{10,... | collective-permute-start | bytes 208904 | tf_op jit(solution)/shard_map/ppermute | solution.py:251
  8.9 0.5 %collective-permute-start = (bf16[272,128]{1,0:T(8,128)(2,1)S(1)}, bf16[272,128]{1,0:T(8,128)(2,1)S(1)}, u32[]{:S(2)}, u32[]{:S(2)}) collective-permute-start(bf16[272,128]{1,0:T(8,128)(2,1)S(1)} %get-tuple-element.12.col), channel_id=1, source_target_pairs={{0,2},{1,3},{2,0},{3,1},{4,6},{5,7},{6,4},{7,5},{8,10},{9,11},{10,... | collective-permute-start | bytes 208904 | tf_op jit(solution)/shard_map/ppermute | solution.py:251
  9.4 0.5 %collective-permute-start.3 = (bf16[256,128]{1,0:T(8,128)(2,1)S(1)}, bf16[256,128]{1,0:T(8,128)(2,1)S(1)}, u32[]{:S(2)}, u32[]{:S(2)}) collective-permute-start(bf16[256,128]{1,0:T(8,128)(2,1)S(1)} %collective-permute-done.2.refs_1_), channel_id=1, source_target_pairs={{0,1},{1,0},{2,3},{3,2},{4,5},{5,4},{6,7},{7,6},{8,9},{9,8},{10,11... | collective-permute-start | bytes 196616 | tf_op jit(solution)/shard_map/ppermute | solution.py:251
  9.9 0.6 %product_own.1 = (f32[128,256]{1,0:T(8,128)S(1)}, bf16[1024,256]{1,0:T(8,128)(2,1)S(1)}) custom-call(bf16[272,128]{1,0:T(8,128)(2,1)S(1)} %get-tuple-element.12.col, bf16[256,128]{1,0:T(8,128)(2,1)S(1)} %copy-done, bf16[256,128]{1,0:T(8,128)(2,1)S(1)} %collective-permute-done.2.refs_1_, f32[32,128]{1,0:T(8,128)S(1)} %get-tuple-element.13.refs_2_.rates), custom_call_target="tpu_custom_call" | custom-call | tf_op jit(solution)/shard_map/product_own/pallas_call | solution.py:292
  10.5 0.1 collective-permute-done.1.refs_0_
  10.6 0.2 collective-permute-done.3.refs_1_
  10.8 0.6 %product_core.1 = (f32[128,256]{1,0:T(8,128)S(1)}, bf16[1024,256]{1,0:T(8,128)(2,1)S(1)}) custom-call(bf16[272,128]{1,0:T(8,128)(2,1)S(1)} %get-tuple-element.12.col, bf16[256,128]{1,0:T(8,128)(2,1)S(1)} %collective-permute-done.1.refs_0_, bf16[256,128]{1,0:T(8,128)(2,1)S(1)} %collective-permute-done.3.refs_1_, ...), custom_call_target="tpu_custom_call" | custom-call | tf_op jit(solution)/shard_map/product_core/pallas_call | solution.py:301
  11.4 0.8 %product_2.1.before = f32[128,256]{1,0:T(8,128)S(1)} custom-call(bf16[272,128]{1,0:T(8,128)(2,1)S(1)} %collective-permute-done.5.col, bf16[1024,256]{1,0:T(8,128)(2,1)S(1)} %get-tuple-element.16.row_wide, f32[32,128]{1,0:T(8,128)S(1)} %get-tuple-element.13.refs_2_.rates, f32[128,256]{1,0:T(8,128)S(1)} %get-tuple-element.17.before), custom_call_target="tpu_custom_call" | custom-call | tf_op jit(solution)/shard_map/product_2/pallas_call | solution.py:312
  12.2 0.5 %collective-permute-done.4.col = bf16[272,128]{1,0:T(8,128)(2,1)S(1)} collective-permute-done((bf16[272,128]{1,0:T(8,128)(2,1)S(1)}, bf16[272,128]{1,0:T(8,128)(2,1)S(1)}, u32[]{:S(2)}, u32[]{:S(2)}) %collective-permute-start.4) | collective-permute-done | bytes 69664 | tf_op jit(solution)/shard_map/ppermute | solution.py:251
  12.7 0.8 %product_3.1.before = f32[128,256]{1,0:T(8,128)S(1)} custom-call(bf16[272,128]{1,0:T(8,128)(2,1)S(1)} %collective-permute-done.4.col, bf16[1024,256]{1,0:T(8,128)(2,1)S(1)} %get-tuple-element.16.row_wide, f32[32,128]{1,0:T(8,128)S(1)} %get-tuple-element.13.refs_2_.rates, f32[128,256]{1,0:T(8,128)S(1)} %product_2.1.before), custom_call_target="tpu_custom_call" | custom-call | tf_op jit(solution)/shard_map/product_3/pallas_call | solution.py:312
  13.5 0.8 %product_last.1.refs_3_ = f32[48,128]{1,0:T(8,128)S(1)} custom-call(bf16[272,128]{1,0:T(8,128)(2,1)S(1)} %collective-permute-done.col, bf16[1024,256]{1,0:T(8,128)(2,1)S(1)} %get-tuple-element.16.row_wide, f32[32,128]{1,0:T(8,128)S(1)} %get-tuple-element.13.refs_2_.rates, f32[128,256]{1,0:T(8,128)S(1)} %product_3.1.before, f32[24,128]{1,0:T(8,128)S(1)} %get-tuple-element.18.own), custom_call_target="tpu_custom_call" | custom-call | tf_op jit(solution)/shard_map/product_last/pallas_call | solution.py:321
  14.3 0.1 collective-permute-start.6
  14.4 2.4 %collective-permute-start.7 = (f32[48,128]{1,0:T(8,128)S(1)}, f32[48,128]{1,0:T(8,128)S(1)}, u32[]{:S(2)}, u32[]{:S(2)}) collective-permute-start(f32[48,128]{1,0:T(8,128)S(1)} %product_last.1.refs_3_), channel_id=1, source_target_pairs={{0,8},{1,9},{2,10},{3,11},{4,12},{5,13},{6,14},{7,15},{8,0},{9,1},... | collective-permute-start | bytes 73736 | tf_op jit(solution)/shard_map/ppermute | solution.py:251
  16.8 0.4 %collective-permute-start.8 = (f32[48,128]{1,0:T(8,128)S(1)}, f32[48,128]{1,0:T(8,128)S(1)}, u32[]{:S(2)}, u32[]{:S(2)}) collective-permute-start(f32[48,128]{1,0:T(8,128)S(1)} %product_last.1.refs_3_), channel_id=1, source_target_pairs={{0,1},{1,0},{2,3},{3,2},{4,5},{5,4},{6,7},{7,6},{8,9},{9,8},{10,11... | collective-permute-start | bytes 73736 | tf_op jit(solution)/shard_map/ppermute | solution.py:251
  17.2 1.6 %collective-permute-done.6.refs_0_ = f32[48,128]{1,0:T(8,128)S(1)} collective-permute-done((f32[48,128]{1,0:T(8,128)S(1)}, f32[48,128]{1,0:T(8,128)S(1)}, u32[]{:S(2)}, u32[]{:S(2)}) %collective-permute-start.6) | collective-permute-done | bytes 24608 | tf_op jit(solution)/shard_map/ppermute | solution.py:251
  18.8 1.1 %collective-permute-done.7.refs_1_ = f32[48,128]{1,0:T(8,128)S(1)} collective-permute-done((f32[48,128]{1,0:T(8,128)S(1)}, f32[48,128]{1,0:T(8,128)S(1)}, u32[]{:S(2)}, u32[]{:S(2)}) %collective-permute-start.7) | collective-permute-done | bytes 24608 | tf_op jit(solution)/shard_map/ppermute | solution.py:251
  19.9 1.6 %collective-permute-start.10 = (f32[16,128]{1,0:T(8,128)S(1)}, f32[16,128]{1,0:T(8,128)S(1)}, u32[]{:S(2)}, u32[]{:S(2)}) collective-permute-start(f32[16,128]{1,0:T(8,128)S(1)} %get-tuple-element.19.refs_0_), channel_id=1, source_target_pairs={{0,2},{1,7},{2,0},{3,5},{4,6},{5,3},{6,4},{7,1},{8,10},{9,15},{10,... | collective-permute-start | bytes 24584 | tf_op jit(solution)/shard_map/ppermute | solution.py:251
  21.5 1.6 %collective-permute-start.9 = (f32[16,128]{1,0:T(8,128)S(1)}, f32[16,128]{1,0:T(8,128)S(1)}, u32[]{:S(2)}, u32[]{:S(2)}) collective-permute-start(f32[16,128]{1,0:T(8,128)S(1)} %get-tuple-element.19.refs_0_), channel_id=1, source_target_pairs={{0,4},{1,5},{2,6},{3,7},{4,0},{5,1},{6,2},{7,3},{8,12},{9,13},{10,... | collective-permute-start | bytes 24584 | tf_op jit(solution)/shard_map/ppermute | solution.py:251
  23.1 0.5 %collective-permute-done.10.refs_2_ = f32[16,128]{1,0:T(8,128)S(1)} collective-permute-done((f32[16,128]{1,0:T(8,128)S(1)}, f32[16,128]{1,0:T(8,128)S(1)}, u32[]{:S(2)}, u32[]{:S(2)}) %collective-permute-start.10) | collective-permute-done | bytes 8224 | tf_op jit(solution)/shard_map/ppermute | solution.py:251
  23.7 1.5 %collective-permute-done.9.refs_1_ = f32[16,128]{1,0:T(8,128)S(1)} collective-permute-done((f32[16,128]{1,0:T(8,128)S(1)}, f32[16,128]{1,0:T(8,128)S(1)}, u32[]{:S(2)}, u32[]{:S(2)}) %collective-permute-start.9) | collective-permute-done | bytes 8224 | tf_op jit(solution)/shard_map/ppermute | solution.py:251
  25.2 0.8 %update.1 = (f32[4,256]{1,0:T(4,128)}, f32[4,256]{1,0:T(4,128)}, f32[4,256]{1,0:T(4,128)}) custom-call(f32[16,128]{1,0:T(8,128)S(1)} %get-tuple-element.19.refs_0_, f32[16,128]{1,0:T(8,128)S(1)} %collective-permute-done.9.refs_1_, f32[16,128]{1,0:T(8,128)S(1)} %collective-permute-done.10.refs_2_, f32[16,128]{1,0:T(8,128)S(1)} %collective-permute-done.11.refs_3_, ...), custom_call_target="tpu_custom_call" | custom-call | tf_op jit(solution)/shard_map/update/pallas_call | solution.py:351
  (16 shorter events, 0.1 us)
Async XLA Ops:
  0.6 8.8 %copy-start = (bf16[256,128]{1,0:T(8,128)(2,1)S(1)}, bf16[256,128]{1,0:T(8,128)(2,1)}, u32[]{:S(2)}) copy-start(bf16[256,128]{1,0:T(8,128)(2,1)} %refs_0_.1) | copy-start | bytes 196612
  0.6 8.8 %collective-permute-start.2 = (bf16[256,128]{1,0:T(8,128)(2,1)}, bf16[256,128]{1,0:T(8,128)(2,1)S(1)}, u32[]{:S(2)}, u32[]{:S(2)}) collective-permute-start(bf16[256,128]{1,0:T(8,128)(2,1)} %refs_0_.1), channel_id=1, source_target_pairs={{0,8},{1,9},{2,10},{3,11},{4,12},{5,13},{6,14},{7,15},{8,0},{9,1},... | collective-permute-start | bytes 196616 | tf_op jit(solution)/shard_map/ppermute | solution.py:251
  5.8 5.6 %collective-permute-start.5 = (bf16[272,128]{1,0:T(8,128)(2,1)S(1)}, bf16[272,128]{1,0:T(8,128)(2,1)S(1)}, u32[]{:S(2)}, u32[]{:S(2)}) collective-permute-start(bf16[272,128]{1,0:T(8,128)(2,1)S(1)} %get-tuple-element.12.col), channel_id=1, source_target_pairs={{0,4},{1,5},{2,6},{3,7},{4,0},{5,1},{6,2},{7,3},{8,12},{9,13},{10,... | collective-permute-start | bytes 208904 | tf_op jit(solution)/shard_map/ppermute | solution.py:251
  7.5 5.2 %collective-permute-start.4 = (bf16[272,128]{1,0:T(8,128)(2,1)S(1)}, bf16[272,128]{1,0:T(8,128)(2,1)S(1)}, u32[]{:S(2)}, u32[]{:S(2)}) collective-permute-start(bf16[272,128]{1,0:T(8,128)(2,1)S(1)} %get-tuple-element.12.col), channel_id=1, source_target_pairs={{0,6},{1,7},{2,4},{3,5},{4,2},{5,3},{6,0},{7,1},{8,14},{9,15},{10,... | collective-permute-start | bytes 208904 | tf_op jit(solution)/shard_map/ppermute | solution.py:251
  8.9 4.6 %collective-permute-start = (bf16[272,128]{1,0:T(8,128)(2,1)S(1)}, bf16[272,128]{1,0:T(8,128)(2,1)S(1)}, u32[]{:S(2)}, u32[]{:S(2)}) collective-permute-start(bf16[272,128]{1,0:T(8,128)(2,1)S(1)} %get-tuple-element.12.col), channel_id=1, source_target_pairs={{0,2},{1,3},{2,0},{3,1},{4,6},{5,7},{6,4},{7,5},{8,10},{9,11},{10,... | collective-permute-start | bytes 208904 | tf_op jit(solution)/shard_map/ppermute | solution.py:251
  9.4 1.3 %collective-permute-start.1 = (bf16[256,128]{1,0:T(8,128)(2,1)S(1)}, bf16[256,128]{1,0:T(8,128)(2,1)S(1)}, u32[]{:S(2)}, u32[]{:S(2)}) collective-permute-start(bf16[256,128]{1,0:T(8,128)(2,1)S(1)} %copy-done), channel_id=1, source_target_pairs={{0,1},{1,0},{2,3},{3,2},{4,5},{5,4},{6,7},{7,6},{8,9},{9,8},{10,11... | collective-permute-start | bytes 196616 | tf_op jit(solution)/shard_map/ppermute | solution.py:251
  9.4 1.4 %collective-permute-start.3 = (bf16[256,128]{1,0:T(8,128)(2,1)S(1)}, bf16[256,128]{1,0:T(8,128)(2,1)S(1)}, u32[]{:S(2)}, u32[]{:S(2)}) collective-permute-start(bf16[256,128]{1,0:T(8,128)(2,1)S(1)} %collective-permute-done.2.refs_1_), channel_id=1, source_target_pairs={{0,1},{1,0},{2,3},{3,2},{4,5},{5,4},{6,7},{7,6},{8,9},{9,8},{10,11... | collective-permute-start | bytes 196616 | tf_op jit(solution)/shard_map/ppermute | solution.py:251
  14.3 4.4 %collective-permute-start.6 = (f32[48,128]{1,0:T(8,128)S(1)}, f32[48,128]{1,0:T(8,128)S(1)}, u32[]{:S(2)}, u32[]{:S(2)}) collective-permute-start(f32[48,128]{1,0:T(8,128)S(1)} %product_last.1.refs_3_), channel_id=1, source_target_pairs={{0,9},{1,8},{2,11},{3,10},{4,13},{5,12},{6,15},{7,14},{8,1},{9,0},... | collective-permute-start | bytes 73736 | tf_op jit(solution)/shard_map/ppermute | solution.py:251
  14.4 5.5 %collective-permute-start.7 = (f32[48,128]{1,0:T(8,128)S(1)}, f32[48,128]{1,0:T(8,128)S(1)}, u32[]{:S(2)}, u32[]{:S(2)}) collective-permute-start(f32[48,128]{1,0:T(8,128)S(1)} %product_last.1.refs_3_), channel_id=1, source_target_pairs={{0,8},{1,9},{2,10},{3,11},{4,12},{5,13},{6,14},{7,15},{8,0},{9,1},... | collective-permute-start | bytes 73736 | tf_op jit(solution)/shard_map/ppermute | solution.py:251
  16.8 3.1 %collective-permute-start.8 = (f32[48,128]{1,0:T(8,128)S(1)}, f32[48,128]{1,0:T(8,128)S(1)}, u32[]{:S(2)}, u32[]{:S(2)}) collective-permute-start(f32[48,128]{1,0:T(8,128)S(1)} %product_last.1.refs_3_), channel_id=1, source_target_pairs={{0,1},{1,0},{2,3},{3,2},{4,5},{5,4},{6,7},{7,6},{8,9},{9,8},{10,11... | collective-permute-start | bytes 73736 | tf_op jit(solution)/shard_map/ppermute | solution.py:251
  19.9 5.3 %copy-start.1 = (f32[4,256]{1,0:T(4,128)S(1)}, f32[4,256]{1,0:T(4,128)}, u32[]{:S(2)}) copy-start(f32[4,256]{1,0:T(4,128)} %refs_7_.1) | copy-start | bytes 12292
  19.9 5.3 %copy-start.2 = (f32[4,256]{1,0:T(4,128)S(1)}, f32[4,256]{1,0:T(4,128)}, u32[]{:S(2)}) copy-start(f32[4,256]{1,0:T(4,128)} %refs_6_.1) | copy-start | bytes 12292
  19.9 5.3 %copy-start.3 = (f32[4,256]{1,0:T(4,128)S(1)}, f32[4,256]{1,0:T(4,128)}, u32[]{:S(2)}) copy-start(f32[4,256]{1,0:T(4,128)} %refs_5_.1) | copy-start | bytes 12292
  19.9 3.8 %collective-permute-start.10 = (f32[16,128]{1,0:T(8,128)S(1)}, f32[16,128]{1,0:T(8,128)S(1)}, u32[]{:S(2)}, u32[]{:S(2)}) collective-permute-start(f32[16,128]{1,0:T(8,128)S(1)} %get-tuple-element.19.refs_0_), channel_id=1, source_target_pairs={{0,2},{1,7},{2,0},{3,5},{4,6},{5,3},{6,4},{7,1},{8,10},{9,15},{10,... | collective-permute-start | bytes 24584 | tf_op jit(solution)/shard_map/ppermute | solution.py:251
  21.5 3.7 %collective-permute-start.9 = (f32[16,128]{1,0:T(8,128)S(1)}, f32[16,128]{1,0:T(8,128)S(1)}, u32[]{:S(2)}, u32[]{:S(2)}) collective-permute-start(f32[16,128]{1,0:T(8,128)S(1)} %get-tuple-element.19.refs_0_), channel_id=1, source_target_pairs={{0,4},{1,5},{2,6},{3,7},{4,0},{5,1},{6,2},{7,3},{8,12},{9,13},{10,... | collective-permute-start | bytes 24584 | tf_op jit(solution)/shard_map/ppermute | solution.py:251
  23.7 1.5 %collective-permute-start.11 = (f32[16,128]{1,0:T(8,128)S(1)}, f32[16,128]{1,0:T(8,128)S(1)}, u32[]{:S(2)}, u32[]{:S(2)}) collective-permute-start(f32[16,128]{1,0:T(8,128)S(1)} %collective-permute-done.10.refs_2_), channel_id=1, source_target_pairs={{0,1},{1,0},{2,3},{3,2},{4,5},{5,4},{6,7},{7,6},{8,9},{9,8},{10,11... | collective-permute-start | bytes 24584 | tf_op jit(solution)/shard_map/ppermute | solution.py:251
